TPU v7x, 32 devices: a whole 2x2x4 slice. The times are simulated.
32 devices in a mesh: section: 4 (over x, core), ctx: 8 (over z, y).
Axes of the slice: x: 2, y: 2, z: 4, core: 2. Of those that a mesh axis runs over, the one named last changes fastest.
Arguments:
- queries: bfloat16 [4, 1024, 4096], P('section', 'ctx'), may hold values from -8 to 8
- keys: bfloat16 [4, 1024, 512], P('section', 'ctx'), may hold values from -8 to 8
- values: bfloat16 [4, 1024, 512], P('section', 'ctx'), may hold values from -6 to 6
- token_pos: int32 [1024], P('ctx'), may hold values from 0 to 1023, as said below
- segment: int32 [1024], replicated, may hold values from 0 to 7, never falling along the last dimension, each value on 1 to 256 neighbouring positions
Outputs:
- handed: bfloat16 [4, 1024, 4096], P('section', 'ctx')
Inputs may be any that keep to these rules, and one draw needn't show every extreme that they name: `token_pos`: a permutation of the 1024 positions; the 128 rows of one index of ctx are two runs of 64 consecutive positions, starting at b * 64 and at (15 - b) * 64, each b used by one index. `segment`: document numbers never fall along the positions; each document covers 1 to 256 positions, one exactly that many.
All inputs are finite; a program needn't handle non-finite values.
Results may differ from a plain program's by a relative error of at most 0.0059.
Values may be sent and summed in bfloat16 or wider, within the bound.
No kernel may reach another device: no remote copies, remote signals or barrier semaphores. Data moves between devices by JAX's collectives and lax.ppermute only.
A program may use at most 64 MiB of HBM per device.

v0:
```python
import functools
import math

import jax
import jax.numpy as jnp
from jax import lax
from jax.experimental import pallas as pl
from jax.experimental.pallas import tpu as pltpu
from jax.sharding import PartitionSpec as P

HEAD_SIZE = 128
QUERY_HEADS = 32
KEY_VALUE_HEADS = 4
GROUP = QUERY_HEADS // KEY_VALUE_HEADS
RUN = 64
TOK_DEV = 2 * RUN
QUERY_COLUMNS = QUERY_HEADS * HEAD_SIZE
KV_COLUMNS = KEY_VALUE_HEADS * HEAD_SIZE
TAG_ROWS = 16

masked_fill = -1e30


def run_numbers(pos_ref, key_refs):
    numbers = [(lax.div(pos_ref[0], RUN), lax.div(pos_ref[RUN], RUN))]
    for key_ref in key_refs[:-2] + key_refs[-1:]:
        tag = jnp.max(key_ref[key_ref.shape[0] - TAG_ROWS :, :TOK_DEV].astype(jnp.float32), axis=0, keepdims=True)
        column = lax.broadcasted_iota(jnp.int32, (1, TOK_DEV), 1)
        first = jnp.max(jnp.where(column < RUN, tag, 0.0)).astype(jnp.int32)
        second = jnp.max(jnp.where(column < RUN, 0.0, tag)).astype(jnp.int32)
        numbers.append((first, second))
    return numbers


def sort_runs(numbers, own_ref, own_column, block_refs, sorted_buf):
    halves = [(ref, ref, RUN) for ref in block_refs[:-2]] + [(block_refs[-2], block_refs[-1], 0)]
    for (first, second), (first_ref, second_ref, at) in zip(numbers[1:], halves):
        sorted_buf[first] = first_ref[:RUN, :]
        sorted_buf[second] = second_ref[at : at + RUN, :]
    for half, number in enumerate(numbers[0]):
        sorted_buf[number] = own_ref[half * RUN : (half + 1) * RUN, own_column : own_column + KV_COLUMNS]


def span_start(own, half, reach):
    return jnp.maximum(own[half] - reach, 0)


def weights_kernel(runs, pos_ref, segment_ref, own_ref, *refs):
    key_refs, (weights_ref, key_buf) = refs[:-2], refs[-2:]
    reach = runs // 4
    span = (reach + 1) * RUN
    numbers = run_numbers(pos_ref, key_refs)
    sort_runs(numbers, own_ref, QUERY_COLUMNS, key_refs, key_buf)
    segment = segment_ref[...].astype(jnp.float32)
    scale = math.log2(math.e) / math.sqrt(HEAD_SIZE)
    for half in range(2):
        start = span_start(numbers[0], half, reach)
        row_pos = numbers[0][half] * RUN + lax.broadcasted_iota(jnp.int32, (RUN, 1), 0)
        at = lax.broadcasted_iota(jnp.int32, (RUN, runs * RUN), 1) == row_pos
        row_doc = jnp.sum(jnp.where(at, segment, 0.0), axis=1, keepdims=True)
        doc_start = jnp.sum(jnp.where(segment < row_doc, 1.0, 0.0), axis=1, keepdims=True).astype(jnp.int32)
        key_pos = start * RUN + lax.broadcasted_iota(jnp.int32, (RUN, span), 1)
        bias = jnp.where((key_pos <= row_pos) & (key_pos >= doc_start), 0.0, masked_fill)
        bias = jnp.concatenate([bias] * GROUP, axis=0)
        for kv in range(KEY_VALUE_HEADS):
            query = jnp.concatenate(
                [
                    own_ref[half * RUN : (half + 1) * RUN, h * HEAD_SIZE : (h + 1) * HEAD_SIZE]
                    for h in range(kv * GROUP, (kv + 1) * GROUP)
                ],
                axis=0,
            )
            key = key_buf[pl.ds(start, reach + 1), :, kv * HEAD_SIZE : (kv + 1) * HEAD_SIZE]
            scores = bias + lax.dot_general(
                query,
                key.reshape(span, HEAD_SIZE),
                (((1,), (1,)), ((), ())),
                preferred_element_type=jnp.float32,
            )
            row_max = jnp.max(scores, axis=1, keepdims=True)
            weights_ref[half * KEY_VALUE_HEADS + kv] = jnp.exp2((scores - row_max) * scale).astype(jnp.bfloat16)


def values_kernel(runs, pos_ref, weights_ref, own_ref, *refs):
    blocks = runs // 2
    key_refs, value_refs, (out_ref, value_buf) = refs[:blocks], refs[blocks:-2], refs[-2:]
    reach = runs // 4
    span = (reach + 1) * RUN
    numbers = run_numbers(pos_ref, key_refs)
    sort_runs(numbers, own_ref, QUERY_COLUMNS + KV_COLUMNS, value_refs, value_buf)
    ones = jnp.ones((span, HEAD_SIZE), jnp.bfloat16)
    for half in range(2):
        start = span_start(numbers[0], half, reach)
        for kv in range(KEY_VALUE_HEADS):
            value = value_buf[pl.ds(start, reach + 1), :, kv * HEAD_SIZE : (kv + 1) * HEAD_SIZE]
            summed = jnp.dot(
                weights_ref[half * KEY_VALUE_HEADS + kv],
                jnp.concatenate([value.reshape(span, HEAD_SIZE), ones], axis=1),
                preferred_element_type=jnp.float32,
            )
            result = (summed[:, :HEAD_SIZE] / summed[:, HEAD_SIZE:]).astype(jnp.bfloat16)
            for i in range(GROUP):
                h = kv * GROUP + i
                out_ref[half * RUN : (half + 1) * RUN, h * HEAD_SIZE : (h + 1) * HEAD_SIZE] = result[
                    i * RUN : (i + 1) * RUN
                ]


def per_device(queries, keys, values, token_pos, segment):
    sections, places = lax.axis_size("section"), lax.axis_size("ctx")
    runs = segment.shape[0] // RUN
    depth = places // 2
    ring = [z * 2 for z in range(depth)] + [z * 2 + 1 for z in reversed(range(depth))]

    def shift(block, section_by, ring_by):
        pairs = []
        for s in range(sections):
            for i in range(places):
                target = (s + section_by) % sections * places + ring[(i + ring_by) % places]
                pairs.append((s * places + ring[i], target))
        return lax.ppermute(block, ("section", "ctx"), pairs)

    def around(block):
        ahead, back = shift(block, 1, 1), shift(block, 1, -1)
        held = [ahead, back]
        for _ in range(2, places // 2):
            ahead, back = shift(ahead, 0, 1), shift(back, 0, -1)
            held.extend([ahead, back])
        return held + [shift(ahead[:RUN], 0, 1), shift(back[RUN:], 0, -1)]

    tag = jnp.tile((token_pos >> (RUN.bit_length() - 1)).astype(jnp.bfloat16)[None], (TAG_ROWS, KEY_VALUE_HEADS))
    all_keys = around(jnp.concatenate([keys[0], tag], axis=0))
    all_values = around(values[0])
    own = shift(jnp.concatenate([queries[0], keys[0], values[0]], axis=1), 1, 0)

    smem, vmem = pl.BlockSpec(memory_space=pltpu.SMEM), pl.BlockSpec(memory_space=pltpu.VMEM)
    params = pltpu.CompilerParams(vmem_limit_bytes=40 * 1024 * 1024)
    sorted_buf = pltpu.VMEM((runs, RUN, KV_COLUMNS), jnp.bfloat16)
    weights = pl.pallas_call(
        functools.partial(weights_kernel, runs),
        out_shape=jax.ShapeDtypeStruct((2 * KEY_VALUE_HEADS, GROUP * RUN, (runs // 4 + 1) * RUN), jnp.bfloat16),
        in_specs=[smem] + [vmem] * (2 + len(all_keys)),
        out_specs=vmem,
        scratch_shapes=[sorted_buf],
        compiler_params=params,
        cost_estimate=pl.CostEstimate(flops=1 << 26, bytes_accessed=1 << 20, transcendentals=0),
    )(token_pos, segment.reshape(1, -1), own, *all_keys)
    out = pl.pallas_call(
        functools.partial(values_kernel, runs),
        out_shape=jax.ShapeDtypeStruct((TOK_DEV, QUERY_COLUMNS), jnp.bfloat16),
        in_specs=[smem] + [vmem] * (2 + len(all_keys) + len(all_values)),
        out_specs=vmem,
        scratch_shapes=[sorted_buf],
        compiler_params=params,
        cost_estimate=pl.CostEstimate(flops=1 << 26, bytes_accessed=1 << 20, transcendentals=0),
    )(token_pos, weights, own, *all_keys, *all_values)
    return out[None]


def solution(mesh):
    return jax.shard_map(
        per_device,
        mesh=mesh,
        in_specs=(
            P("section", "ctx", None),
            P("section", "ctx", None),
            P("section", "ctx", None),
            P("ctx"),
            P(),
        ),
        out_specs=P("section", "ctx", None),
        check_vma=False,
    )
```

profile of v0, /device:TPU:0, one launch (start us, length us, event | category | flops | bytes accessed | tf_op | source)
XLA Modules:
  0.0 47.7 jit_solution(2715320942024309649)
XLA Ops:
  0.0 0.0 copy-start.3
  0.0 0.0 copy-start.2
  0.0 0.0 copy-start.1
  0.0 0.0 copy-start
  0.0 1.5 %pad_maximum_fusion = bf16[128,5120]{1,0:T(8,128)(2,1)S(1)} fusion(bf16[128,512]{1,0:T(8,128)(2,1)} %bitcast.11, bf16[128,512]{1,0:T(8,128)(2,1)} %bitcast.9, bf16[128,4096]{1,0:T(8,128)(2,1)} %bitcast.8), kind=kLoop, calls=%fused_computation | loop fusion | flops 3932160 | bytes 2621440 | tf_op jit(solution)/shard_map/concatenate | solution.py:134
  1.5 0.5 %collective-permute-start = (bf16[128,5120]{1,0:T(8,128)(2,1)S(1)}, bf16[128,5120]{1,0:T(8,128)(2,1)S(1)}, u32[]{:S(2)}, u32[]{:S(2)}) collective-permute-start(bf16[128,5120]{1,0:T(8,128)(2,1)S(1)} %pad_maximum_fusion), channel_id=1, source_target_pairs={{0,8},{2,10},{4,12},{6,14},{7,15},{5,13},{3,11},{1,9},{8,16},{10,1... | collective-permute-start | bytes 3932168 | tf_op jit(solution)/shard_map/ppermute | solution.py:121
  2.0 0.0 copy-done.1
  2.0 0.0 copy-done.2
  2.1 3.8 %collective-permute-start.2 = (bf16[144,512]{1,0:T(8,128)(2,1)S(1)}, bf16[144,512]{1,0:T(8,128)(2,1)S(1)}, u32[]{:S(2)}, u32[]{:S(2)}) collective-permute-start(bf16[144,512]{1,0:T(8,128)(2,1)S(1)} %pad_maximum_fusion.1), channel_id=1, source_target_pairs={{0,9},{2,8},{4,10},{6,12},{7,14},{5,15},{3,13},{1,11},{8,17},{10,1... | collective-permute-start | bytes 442376 | tf_op jit(solution)/shard_map/ppermute | solution.py:121
  5.8 0.1 collective-permute-start.1
  6.0 0.0 copy-done.3
  6.0 1.6 %collective-permute-start.10 = (bf16[128,512]{1,0:T(8,128)(2,1)S(1)}, bf16[128,512]{1,0:T(8,128)(2,1)S(1)}, u32[]{:S(2)}, u32[]{:S(2)}) collective-permute-start(bf16[128,512]{1,0:T(8,128)(2,1)S(1)} %bitcast.12), channel_id=1, source_target_pairs={{0,9},{2,8},{4,10},{6,12},{7,14},{5,15},{3,13},{1,11},{8,17},{10,1... | collective-permute-start | bytes 393224 | tf_op jit(solution)/shard_map/ppermute | solution.py:121
  7.6 0.1 collective-permute-start.9
  7.7 2.5 %collective-permute-done.2.refs_1_ = bf16[144,512]{1,0:T(8,128)(2,1)S(1)} collective-permute-done((bf16[144,512]{1,0:T(8,128)(2,1)S(1)}, bf16[144,512]{1,0:T(8,128)(2,1)S(1)}, u32[]{:S(2)}, u32[]{:S(2)}) %collective-permute-start.2) | collective-permute-done | bytes 147488 | tf_op jit(solution)/shard_map/ppermute | solution.py:121
  10.2 15.1 %collective-permute-start.4 = (bf16[144,512]{1,0:T(8,128)(2,1)S(1)}, bf16[144,512]{1,0:T(8,128)(2,1)S(1)}, u32[]{:S(2)}, u32[]{:S(2)}) collective-permute-start(bf16[144,512]{1,0:T(8,128)(2,1)S(1)} %collective-permute-done.2.refs_1_), channel_id=1, source_target_pairs={{0,1},{2,0},{4,2},{6,4},{7,6},{5,7},{3,5},{1,3},{8,9},{10,8},{12,1... | collective-permute-start | bytes 442376 | tf_op jit(solution)/shard_map/ppermute | solution.py:121
  25.3 0.3 collective-permute-done.1.refs_0_
  25.6 0.0 collective-permute-start.3
  25.6 0.0 collective-permute-done.10.refs_9_
  25.6 2.0 %collective-permute-start.12 = (bf16[128,512]{1,0:T(8,128)(2,1)S(1)}, bf16[128,512]{1,0:T(8,128)(2,1)S(1)}, u32[]{:S(2)}, u32[]{:S(2)}) collective-permute-start(bf16[128,512]{1,0:T(8,128)(2,1)S(1)} %collective-permute-done.10.refs_9_), channel_id=1, source_target_pairs={{0,1},{2,0},{4,2},{6,4},{7,6},{5,7},{3,5},{1,3},{8,9},{10,8},{12,1... | collective-permute-start | bytes 393224 | tf_op jit(solution)/shard_map/ppermute | solution.py:121
  27.6 0.0 collective-permute-done.9.refs_8_
  27.6 0.0 collective-permute-start.11
  27.6 1.6 %collective-permute-done.4.refs_3_ = bf16[144,512]{1,0:T(8,128)(2,1)S(1)} collective-permute-done((bf16[144,512]{1,0:T(8,128)(2,1)S(1)}, bf16[144,512]{1,0:T(8,128)(2,1)S(1)}, u32[]{:S(2)}, u32[]{:S(2)}) %collective-permute-start.4) | collective-permute-done | bytes 147488 | tf_op jit(solution)/shard_map/ppermute | solution.py:121
  29.2 2.5 %collective-permute-start.6 = (bf16[144,512]{1,0:T(8,128)(2,1)S(1)}, bf16[144,512]{1,0:T(8,128)(2,1)S(1)}, u32[]{:S(2)}, u32[]{:S(2)}) collective-permute-start(bf16[144,512]{1,0:T(8,128)(2,1)S(1)} %collective-permute-done.4.refs_3_), channel_id=1, source_target_pairs={{0,1},{2,0},{4,2},{6,4},{7,6},{5,7},{3,5},{1,3},{8,9},{10,8},{12,1... | collective-permute-start | bytes 442376 | tf_op jit(solution)/shard_map/ppermute | solution.py:121
  31.7 0.3 collective-permute-done.3.refs_2_
  32.0 0.3 collective-permute-start.5
  32.3 0.0 collective-permute-done.12.refs_11_
  32.3 2.2 %collective-permute-start.14 = (bf16[128,512]{1,0:T(8,128)(2,1)S(1)}, bf16[128,512]{1,0:T(8,128)(2,1)S(1)}, u32[]{:S(2)}, u32[]{:S(2)}) collective-permute-start(bf16[128,512]{1,0:T(8,128)(2,1)S(1)} %collective-permute-done.12.refs_11_), channel_id=1, source_target_pairs={{0,1},{2,0},{4,2},{6,4},{7,6},{5,7},{3,5},{1,3},{8,9},{10,8},{12,1... | collective-permute-start | bytes 393224 | tf_op jit(solution)/shard_map/ppermute | solution.py:121
  34.5 0.3 collective-permute-done.11.refs_10_
  34.8 0.3 collective-permute-start.13
  35.1 0.5 %collective-permute-done.6.refs_5_ = bf16[144,512]{1,0:T(8,128)(2,1)S(1)} collective-permute-done((bf16[144,512]{1,0:T(8,128)(2,1)S(1)}, bf16[144,512]{1,0:T(8,128)(2,1)S(1)}, u32[]{:S(2)}, u32[]{:S(2)}) %collective-permute-start.6) | collective-permute-done | bytes 147488 | tf_op jit(solution)/shard_map/ppermute | solution.py:121
  35.6 2.1 %collective-permute-start.8 = (bf16[80,512]{1,0:T(8,128)(2,1)S(1)}, bf16[80,512]{1,0:T(8,128)(2,1)S(1)}, u32[]{:S(2)}, u32[]{:S(2)}) collective-permute-start(bf16[80,512]{1,0:T(8,128)(2,1)S(1)} %slice.17), channel_id=1, source_target_pairs={{0,1},{2,0},{4,2},{6,4},{7,6},{5,7},{3,5},{1,3},{8,9},{10,8},{12,1... | collective-permute-start | bytes 245768 | tf_op jit(solution)/shard_map/ppermute | solution.py:121
  37.8 0.3 collective-permute-done.5.refs_4_
  38.0 1.0 %collective-permute-start.7 = (bf16[64,512]{1,0:T(8,128)(2,1)S(1)}, bf16[64,512]{1,0:T(8,128)(2,1)S(1)}, u32[]{:S(2)}, u32[]{:S(2)}) collective-permute-start(bf16[64,512]{1,0:T(8,128)(2,1)S(1)} %slice.16), channel_id=1, source_target_pairs={{0,2},{2,4},{4,6},{6,7},{7,5},{5,3},{3,1},{1,0},{8,10},{10,12},{12... | collective-permute-start | bytes 196616 | tf_op jit(solution)/shard_map/ppermute | solution.py:121
  39.0 0.0 collective-permute-done.14.refs_13_
  39.0 1.2 %collective-permute-start.16 = (bf16[64,512]{1,0:T(8,128)(2,1)S(1)}, bf16[64,512]{1,0:T(8,128)(2,1)S(1)}, u32[]{:S(2)}, u32[]{:S(2)}) collective-permute-start(bf16[64,512]{1,0:T(8,128)(2,1)S(1)} %slice.19), channel_id=1, source_target_pairs={{0,1},{2,0},{4,2},{6,4},{7,6},{5,7},{3,5},{1,3},{8,9},{10,8},{12,1... | collective-permute-start | bytes 196616 | tf_op jit(solution)/shard_map/ppermute | solution.py:121
  40.2 0.0 collective-permute-done.13.refs_12_
  40.2 0.9 %collective-permute-start.15 = (bf16[64,512]{1,0:T(8,128)(2,1)S(1)}, bf16[64,512]{1,0:T(8,128)(2,1)S(1)}, u32[]{:S(2)}, u32[]{:S(2)}) collective-permute-start(bf16[64,512]{1,0:T(8,128)(2,1)S(1)} %slice.18), channel_id=1, source_target_pairs={{0,2},{2,4},{4,6},{6,7},{7,5},{5,3},{3,1},{1,0},{8,10},{10,12},{12... | collective-permute-start | bytes 196616 | tf_op jit(solution)/shard_map/ppermute | solution.py:121
  41.2 1.1 %collective-permute-done.7.refs_6_ = bf16[64,512]{1,0:T(8,128)(2,1)S(1)} collective-permute-done((bf16[64,512]{1,0:T(8,128)(2,1)S(1)}, bf16[64,512]{1,0:T(8,128)(2,1)S(1)}, u32[]{:S(2)}, u32[]{:S(2)}) %collective-permute-start.7) | collective-permute-done | bytes 65568 | tf_op jit(solution)/shard_map/ppermute | solution.py:121
  42.3 0.0 collective-permute-done.8.refs_7_
  42.3 0.0 collective-permute-done.own_ref
  42.3 0.0 copy-done
  42.3 2.4 %shard_map.55.weights_ref = bf16[8,512,320]{2,1,0:T(8,128)(2,1)S(1)} custom-call(s32[128]{0:T(128)S(1)} %copy-done.1, s32[1,1024]{1,0:T(1,128)S(1)} %bitcast.7, bf16[128,5120]{1,0:T(8,128)(2,1)S(1)} %collective-permute-done.own_ref, bf16[144,512]{1,0:T(8,128)(2,1)S(1)} %collective-permute-done.1.refs_0_, ...), custom_call_target="tpu_custom_call" | custom-call | flops 67108864 | bytes 1048576 | tf_op jit(solution)/shard_map/pallas_call | solution.py:139
  44.7 0.0 collective-permute-done.16.refs_15_
  44.7 0.0 collective-permute-done.15.refs_14_
  44.7 3.0 %shard_map.56 = bf16[128,4096]{1,0:T(8,128)(2,1)} custom-call(s32[128]{0:T(128)S(1)} %copy-done.1, bf16[8,512,320]{2,1,0:T(8,128)(2,1)S(1)} %shard_map.55.weights_ref, bf16[128,5120]{1,0:T(8,128)(2,1)S(1)} %collective-permute-done.own_ref, bf16[144,512]{1,0:T(8,128)(2,1)S(1)} %collective-permute-done.1.refs_0_, ...), custom_call_target="tpu_custom_call" | custom-call | flops 67108864 | bytes 1048576 | tf_op jit(solution)/shard_map/pallas_call | solution.py:148
  (8 shorter events, 0.1 us)
Async XLA Ops:
  0.0 6.0 %copy-start.3 = (bf16[1,128,512]{2,1,0:T(8,128)(2,1)S(1)}, bf16[1,128,512]{2,1,0:T(8,128)(2,1)}, u32[]{:S(2)}) copy-start(bf16[1,128,512]{2,1,0:T(8,128)(2,1)} %param.7) | copy-start | bytes 393220
  0.0 2.0 %copy-start.2 = (bf16[1,128,512]{2,1,0:T(8,128)(2,1)S(1)}, bf16[1,128,512]{2,1,0:T(8,128)(2,1)}, u32[]{:S(2)}) copy-start(bf16[1,128,512]{2,1,0:T(8,128)(2,1)} %param.6) | copy-start | bytes 393220
  0.0 2.0 %copy-start.1 = (s32[128]{0:T(128)S(1)}, s32[128]{0:T(128)}, u32[]{:S(2)}) copy-start(s32[128]{0:T(128)} %pos_ref.3) | copy-start | bytes 1540
  0.0 42.3 %copy-start = (s32[1024]{0:T(1024)S(1)}, s32[1024]{0:T(1024)}, u32[]{:S(2)}) copy-start(s32[1024]{0:T(1024)} %param.9) | copy-start | bytes 12292
  1.5 40.8 %collective-permute-start = (bf16[128,5120]{1,0:T(8,128)(2,1)S(1)}, bf16[128,5120]{1,0:T(8,128)(2,1)S(1)}, u32[]{:S(2)}, u32[]{:S(2)}) collective-permute-start(bf16[128,5120]{1,0:T(8,128)(2,1)S(1)} %pad_maximum_fusion), channel_id=1, source_target_pairs={{0,8},{2,10},{4,12},{6,14},{7,15},{5,13},{3,11},{1,9},{8,16},{10,1... | collective-permute-start | bytes 3932168 | tf_op jit(solution)/shard_map/ppermute | solution.py:121
  2.1 8.1 %collective-permute-start.2 = (bf16[144,512]{1,0:T(8,128)(2,1)S(1)}, bf16[144,512]{1,0:T(8,128)(2,1)S(1)}, u32[]{:S(2)}, u32[]{:S(2)}) collective-permute-start(bf16[144,512]{1,0:T(8,128)(2,1)S(1)} %pad_maximum_fusion.1), channel_id=1, source_target_pairs={{0,9},{2,8},{4,10},{6,12},{7,14},{5,15},{3,13},{1,11},{8,17},{10,1... | collective-permute-start | bytes 442376 | tf_op jit(solution)/shard_map/ppermute | solution.py:121
  5.8 19.7 %collective-permute-start.1 = (bf16[144,512]{1,0:T(8,128)(2,1)S(1)}, bf16[144,512]{1,0:T(8,128)(2,1)S(1)}, u32[]{:S(2)}, u32[]{:S(2)}) collective-permute-start(bf16[144,512]{1,0:T(8,128)(2,1)S(1)} %pad_maximum_fusion.1), channel_id=1, source_target_pairs={{0,10},{2,12},{4,14},{6,15},{7,13},{5,11},{3,9},{1,8},{8,18},{10,2... | collective-permute-start | bytes 442376 | tf_op jit(solution)/shard_map/ppermute | solution.py:121
  6.0 19.6 %collective-permute-start.10 = (bf16[128,512]{1,0:T(8,128)(2,1)S(1)}, bf16[128,512]{1,0:T(8,128)(2,1)S(1)}, u32[]{:S(2)}, u32[]{:S(2)}) collective-permute-start(bf16[128,512]{1,0:T(8,128)(2,1)S(1)} %bitcast.12), channel_id=1, source_target_pairs={{0,9},{2,8},{4,10},{6,12},{7,14},{5,15},{3,13},{1,11},{8,17},{10,1... | collective-permute-start | bytes 393224 | tf_op jit(solution)/shard_map/ppermute | solution.py:121
  7.6 20.0 %collective-permute-start.9 = (bf16[128,512]{1,0:T(8,128)(2,1)S(1)}, bf16[128,512]{1,0:T(8,128)(2,1)S(1)}, u32[]{:S(2)}, u32[]{:S(2)}) collective-permute-start(bf16[128,512]{1,0:T(8,128)(2,1)S(1)} %bitcast.13), channel_id=1, source_target_pairs={{0,10},{2,12},{4,14},{6,15},{7,13},{5,11},{3,9},{1,8},{8,18},{10,2... | collective-permute-start | bytes 393224 | tf_op jit(solution)/shard_map/ppermute | solution.py:121
  10.2 19.0 %collective-permute-start.4 = (bf16[144,512]{1,0:T(8,128)(2,1)S(1)}, bf16[144,512]{1,0:T(8,128)(2,1)S(1)}, u32[]{:S(2)}, u32[]{:S(2)}) collective-permute-start(bf16[144,512]{1,0:T(8,128)(2,1)S(1)} %collective-permute-done.2.refs_1_), channel_id=1, source_target_pairs={{0,1},{2,0},{4,2},{6,4},{7,6},{5,7},{3,5},{1,3},{8,9},{10,8},{12,1... | collective-permute-start | bytes 442376 | tf_op jit(solution)/shard_map/ppermute | solution.py:121
  25.6 6.4 %collective-permute-start.3 = (bf16[144,512]{1,0:T(8,128)(2,1)S(1)}, bf16[144,512]{1,0:T(8,128)(2,1)S(1)}, u32[]{:S(2)}, u32[]{:S(2)}) collective-permute-start(bf16[144,512]{1,0:T(8,128)(2,1)S(1)} %collective-permute-done.1.refs_0_), channel_id=1, source_target_pairs={{0,2},{2,4},{4,6},{6,7},{7,5},{5,3},{3,1},{1,0},{8,10},{10,12},{12... | collective-permute-start | bytes 442376 | tf_op jit(solution)/shard_map/ppermute | solution.py:121
  25.6 6.7 %collective-permute-start.12 = (bf16[128,512]{1,0:T(8,128)(2,1)S(1)}, bf16[128,512]{1,0:T(8,128)(2,1)S(1)}, u32[]{:S(2)}, u32[]{:S(2)}) collective-permute-start(bf16[128,512]{1,0:T(8,128)(2,1)S(1)} %collective-permute-done.10.refs_9_), channel_id=1, source_target_pairs={{0,1},{2,0},{4,2},{6,4},{7,6},{5,7},{3,5},{1,3},{8,9},{10,8},{12,1... | collective-permute-start | bytes 393224 | tf_op jit(solution)/shard_map/ppermute | solution.py:121
  27.6 7.2 %collective-permute-start.11 = (bf16[128,512]{1,0:T(8,128)(2,1)S(1)}, bf16[128,512]{1,0:T(8,128)(2,1)S(1)}, u32[]{:S(2)}, u32[]{:S(2)}) collective-permute-start(bf16[128,512]{1,0:T(8,128)(2,1)S(1)} %collective-permute-done.9.refs_8_), channel_id=1, source_target_pairs={{0,2},{2,4},{4,6},{6,7},{7,5},{5,3},{3,1},{1,0},{8,10},{10,12},{12... | collective-permute-start | bytes 393224 | tf_op jit(solution)/shard_map/ppermute | solution.py:121
  29.2 6.4 %collective-permute-start.6 = (bf16[144,512]{1,0:T(8,128)(2,1)S(1)}, bf16[144,512]{1,0:T(8,128)(2,1)S(1)}, u32[]{:S(2)}, u32[]{:S(2)}) collective-permute-start(bf16[144,512]{1,0:T(8,128)(2,1)S(1)} %collective-permute-done.4.refs_3_), channel_id=1, source_target_pairs={{0,1},{2,0},{4,2},{6,4},{7,6},{5,7},{3,5},{1,3},{8,9},{10,8},{12,1... | collective-permute-start | bytes 442376 | tf_op jit(solution)/shard_map/ppermute | solution.py:121
  32.0 6.0 %collective-permute-start.5 = (bf16[144,512]{1,0:T(8,128)(2,1)S(1)}, bf16[144,512]{1,0:T(8,128)(2,1)S(1)}, u32[]{:S(2)}, u32[]{:S(2)}) collective-permute-start(bf16[144,512]{1,0:T(8,128)(2,1)S(1)} %collective-permute-done.3.refs_2_), channel_id=1, source_target_pairs={{0,2},{2,4},{4,6},{6,7},{7,5},{5,3},{3,1},{1,0},{8,10},{10,12},{12... | collective-permute-start | bytes 442376 | tf_op jit(solution)/shard_map/ppermute | solution.py:121
  32.3 6.7 %collective-permute-start.14 = (bf16[128,512]{1,0:T(8,128)(2,1)S(1)}, bf16[128,512]{1,0:T(8,128)(2,1)S(1)}, u32[]{:S(2)}, u32[]{:S(2)}) collective-permute-start(bf16[128,512]{1,0:T(8,128)(2,1)S(1)} %collective-permute-done.12.refs_11_), channel_id=1, source_target_pairs={{0,1},{2,0},{4,2},{6,4},{7,6},{5,7},{3,5},{1,3},{8,9},{10,8},{12,1... | collective-permute-start | bytes 393224 | tf_op jit(solution)/shard_map/ppermute | solution.py:121
  34.8 5.4 %collective-permute-start.13 = (bf16[128,512]{1,0:T(8,128)(2,1)S(1)}, bf16[128,512]{1,0:T(8,128)(2,1)S(1)}, u32[]{:S(2)}, u32[]{:S(2)}) collective-permute-start(bf16[128,512]{1,0:T(8,128)(2,1)S(1)} %collective-permute-done.11.refs_10_), channel_id=1, source_target_pairs={{0,2},{2,4},{4,6},{6,7},{7,5},{5,3},{3,1},{1,0},{8,10},{10,12},{12... | collective-permute-start | bytes 393224 | tf_op jit(solution)/shard_map/ppermute | solution.py:121
  35.6 6.6 %collective-permute-start.8 = (bf16[80,512]{1,0:T(8,128)(2,1)S(1)}, bf16[80,512]{1,0:T(8,128)(2,1)S(1)}, u32[]{:S(2)}, u32[]{:S(2)}) collective-permute-start(bf16[80,512]{1,0:T(8,128)(2,1)S(1)} %slice.17), channel_id=1, source_target_pairs={{0,1},{2,0},{4,2},{6,4},{7,6},{5,7},{3,5},{1,3},{8,9},{10,8},{12,1... | collective-permute-start | bytes 245768 | tf_op jit(solution)/shard_map/ppermute | solution.py:121
  38.0 4.3 %collective-permute-start.7 = (bf16[64,512]{1,0:T(8,128)(2,1)S(1)}, bf16[64,512]{1,0:T(8,128)(2,1)S(1)}, u32[]{:S(2)}, u32[]{:S(2)}) collective-permute-start(bf16[64,512]{1,0:T(8,128)(2,1)S(1)} %slice.16), channel_id=1, source_target_pairs={{0,2},{2,4},{4,6},{6,7},{7,5},{5,3},{3,1},{1,0},{8,10},{10,12},{12... | collective-permute-start | bytes 196616 | tf_op jit(solution)/shard_map/ppermute | solution.py:121
  39.0 5.6 %collective-permute-start.16 = (bf16[64,512]{1,0:T(8,128)(2,1)S(1)}, bf16[64,512]{1,0:T(8,128)(2,1)S(1)}, u32[]{:S(2)}, u32[]{:S(2)}) collective-permute-start(bf16[64,512]{1,0:T(8,128)(2,1)S(1)} %slice.19), channel_id=1, source_target_pairs={{0,1},{2,0},{4,2},{6,4},{7,6},{5,7},{3,5},{1,3},{8,9},{10,8},{12,1... | collective-permute-start | bytes 196616 | tf_op jit(solution)/shard_map/ppermute | solution.py:121
  40.2 4.5 %collective-permute-start.15 = (bf16[64,512]{1,0:T(8,128)(2,1)S(1)}, bf16[64,512]{1,0:T(8,128)(2,1)S(1)}, u32[]{:S(2)}, u32[]{:S(2)}) collective-permute-start(bf16[64,512]{1,0:T(8,128)(2,1)S(1)} %slice.18), channel_id=1, source_target_pairs={{0,2},{2,4},{4,6},{6,7},{7,5},{5,3},{3,1},{1,0},{8,10},{10,12},{12... | collective-permute-start | bytes 196616 | tf_op jit(solution)/shard_map/ppermute | solution.py:121
where the time goes:
time: 47.8 us; the launch traced here: 47.7 us
  starting transfers between devices  33.7 us (71%)
  waiting for transfers between devices  6.96 us (15%)
  Pallas kernels  5.34 us (11%)
  other arithmetic  1.51 us (3%)
    ppermute x17, starting transfers between devices, shift(): return lax.ppermute(block, ('section', 'ctx'), pairs)  33.7 us
    ppermute x17, waiting for transfers between devices, shift(): return lax.ppermute(block, ('section', 'ctx'), pairs)  6.96 us
    pallas_call x1, Pallas kernels, per_device(): pl.pallas_call(functools.partial(values_kernel, runs), out_shape=jax.Shap...  2.99 us
    pallas_call x1, Pallas kernels, per_device(): pl.pallas_call(functools.partial(weights_kernel, runs), out_shape=jax.Sha...  2.35 us
    concatenate x1, other arithmetic, per_device(): own = shift(jnp.concatenate([queries[0], keys[0], values[0]], axis=1), 1, 0)  1.49 us
  transfers between devices with their start and end apart: 17, of which 8 were waited for; matrix products, arithmetic and copies ran while one was open for 0% of the time, Pallas kernels for 5%

commit v1 on v0

--- a/solution.py
+++ b/solution.py
@@ -131,7 +131,9 @@
     tag = jnp.tile((token_pos >> (RUN.bit_length() - 1)).astype(jnp.bfloat16)[None], (TAG_ROWS, KEY_VALUE_HEADS))
     all_keys = around(jnp.concatenate([keys[0], tag], axis=0))
     all_values = around(values[0])
-    own = shift(jnp.concatenate([queries[0], keys[0], values[0]], axis=1), 1, 0)
+
+    own = jnp.concatenate([queries[0], keys[0], values[0]], axis=1)
+    own = shift(lax.optimization_barrier((own, *all_keys[:2], *all_values[:2]))[0], 1, 0)
 
     smem, vmem = pl.BlockSpec(memory_space=pltpu.SMEM), pl.BlockSpec(memory_space=pltpu.VMEM)
     params = pltpu.CompilerParams(vmem_limit_bytes=40 * 1024 * 1024)

time: 47.8 us -> 38.2 us (0.80)
  starting transfers between devices: 33.7 us -> 17.8 us
  waiting for transfers between devices: 6.96 us -> 11.8 us
  other arithmetic: 1.51 us -> 3.03 us
    ppermute x17, starting transfers between devices: 33.7 us -> 17.8 us  [shift(): return lax.ppermute(block, ('section', 'ctx'), pairs)]
    ppermute x17, waiting for transfers between devices: 6.96 us -> 11.8 us  [shift(): return lax.ppermute(block, ('section', 'ctx'), pairs)]
    concatenate x1, other arithmetic: 0.01 us -> 0.91 us  [per_device(): all_keys = around(jnp.concatenate([keys[0], tag], axis=0))]
    convert_element_type x1, other arithmetic: 0.01 us -> 0.66 us  [per_device(): (token_pos >> RUN.bit_length() - 1).astype(jnp.bfloat16)[None]]
  transfers between devices with their start and end apart: 17 -> 17, of which waited for: 8 -> 8; matrix products, arithmetic and copies ran while one was open for 0% -> 8% of each run, Pallas kernels for 5% -> 6%
where the time goes in v1:
time: 38.2 us; the launch traced here: 38.1 us
  starting transfers between devices  17.8 us (47%)
  waiting for transfers between devices  11.8 us (31%)
  Pallas kernels  5.33 us (14%)
  other arithmetic  3.03 us (8%)
    ppermute x17, starting transfers between devices, shift(): return lax.ppermute(block, ('section', 'ctx'), pairs)  17.8 us
    ppermute x17, waiting for transfers between devices, shift(): return lax.ppermute(block, ('section', 'ctx'), pairs)  11.8 us
    pallas_call x1, Pallas kernels, per_device(): pl.pallas_call(functools.partial(values_kernel, runs), out_shape=jax.Shap...  2.98 us
    pallas_call x1, Pallas kernels, per_device(): pl.pallas_call(functools.partial(weights_kernel, runs), out_shape=jax.Sha...  2.35 us
    concatenate x1, other arithmetic, per_device(): own = jnp.concatenate([queries[0], keys[0], values[0]], axis=1)  1.46 us
    concatenate x1, other arithmetic, per_device(): all_keys = around(jnp.concatenate([keys[0], tag], axis=0))  0.91 us
  transfers between devices with their start and end apart: 17, of which 8 were waited for; matrix products, arithmetic and copies ran while one was open for 8% of the time, Pallas kernels for 6%

profile of v1, /device:TPU:0, one launch (start us, length us, event | category | flops | bytes accessed | tf_op | source)
XLA Modules:
  0.0 38.1 jit_solution(13328066360809695806)
XLA Ops:
  0.0 0.0 copy-start.1
  0.0 0.0 copy-start
  0.0 2.4 %collective-permute-start.3 = (bf16[128,512]{1,0:T(8,128)(2,1)}, bf16[128,512]{1,0:T(8,128)(2,1)S(1)}, u32[]{:S(2)}, u32[]{:S(2)}) collective-permute-start(bf16[128,512]{1,0:T(8,128)(2,1)} %bitcast.11), channel_id=1, source_target_pairs={{0,9},{2,8},{4,10},{6,12},{7,14},{5,15},{3,13},{1,11},{8,17},{10,1... | collective-permute-start | bytes 393224 | tf_op jit(solution)/shard_map/ppermute | solution.py:121
  2.4 1.7 %collective-permute-start.2 = (bf16[128,512]{1,0:T(8,128)(2,1)}, bf16[128,512]{1,0:T(8,128)(2,1)S(1)}, u32[]{:S(2)}, u32[]{:S(2)}) collective-permute-start(bf16[128,512]{1,0:T(8,128)(2,1)} %bitcast.12), channel_id=1, source_target_pairs={{0,10},{2,12},{4,14},{6,15},{7,13},{5,11},{3,9},{1,8},{8,18},{10,2... | collective-permute-start | bytes 393224 | tf_op jit(solution)/shard_map/ppermute | solution.py:121
  4.1 0.7 %shift-right-arithmetic_convert_fusion = bf16[128]{0:T(256)(128)(2,1)S(1)} fusion(s32[128]{0:T(128)} %pos_ref.3), kind=kLoop, calls=%fused_computation.3 | loop fusion | flops 256 | bytes 768 | tf_op jit(solution)/shard_map/convert_element_type | solution.py:131
  4.8 0.9 %pad_maximum_fusion.1 = bf16[144,512]{1,0:T(8,128)(2,1)S(1)} fusion(bf16[16,512]{1,0:T(8,128)(2,1)S(1)} %tile.12, bf16[128,512]{1,0:T(8,128)(2,1)} %bitcast.9), kind=kLoop, calls=%fused_computation.1 | loop fusion | flops 294912 | bytes 294912 | tf_op jit(solution)/shard_map/concatenate | solution.py:132
  5.7 1.1 %collective-permute-start.1 = (bf16[144,512]{1,0:T(8,128)(2,1)S(1)}, bf16[144,512]{1,0:T(8,128)(2,1)S(1)}, u32[]{:S(2)}, u32[]{:S(2)}) collective-permute-start(bf16[144,512]{1,0:T(8,128)(2,1)S(1)} %pad_maximum_fusion.1), channel_id=1, source_target_pairs={{0,9},{2,8},{4,10},{6,12},{7,14},{5,15},{3,13},{1,11},{8,17},{10,1... | collective-permute-start | bytes 442376 | tf_op jit(solution)/shard_map/ppermute | solution.py:121
  6.8 0.2 collective-permute-start
  7.0 1.5 %pad_maximum_fusion = bf16[128,5120]{1,0:T(8,128)(2,1)S(1)} fusion(bf16[128,512]{1,0:T(8,128)(2,1)} %bitcast.13, bf16[128,512]{1,0:T(8,128)(2,1)} %bitcast.10, bf16[128,4096]{1,0:T(8,128)(2,1)} %bitcast.8), kind=kLoop, calls=%fused_computation | loop fusion | flops 3932160 | bytes 2621440 | tf_op jit(solution)/shard_map/concatenate | solution.py:135
  8.5 0.0 collective-permute-done.3.refs_9_
  8.5 0.6 %collective-permute-done.2.refs_8_ = bf16[128,512]{1,0:T(8,128)(2,1)S(1)} collective-permute-done((bf16[128,512]{1,0:T(8,128)(2,1)}, bf16[128,512]{1,0:T(8,128)(2,1)S(1)}, u32[]{:S(2)}, u32[]{:S(2)}) %collective-permute-start.2) | collective-permute-done | bytes 131104 | tf_op jit(solution)/shard_map/ppermute | solution.py:121
  9.1 3.1 %collective-permute-done.1.refs_1_ = bf16[144,512]{1,0:T(8,128)(2,1)S(1)} collective-permute-done((bf16[144,512]{1,0:T(8,128)(2,1)S(1)}, bf16[144,512]{1,0:T(8,128)(2,1)S(1)}, u32[]{:S(2)}, u32[]{:S(2)}) %collective-permute-start.1) | collective-permute-done | bytes 147488 | tf_op jit(solution)/shard_map/ppermute | solution.py:121
  12.2 1.5 %collective-permute-done.refs_0_ = bf16[144,512]{1,0:T(8,128)(2,1)S(1)} collective-permute-done((bf16[144,512]{1,0:T(8,128)(2,1)S(1)}, bf16[144,512]{1,0:T(8,128)(2,1)S(1)}, u32[]{:S(2)}, u32[]{:S(2)}) %collective-permute-start) | collective-permute-done | bytes 147488 | tf_op jit(solution)/shard_map/ppermute | solution.py:121
  13.7 0.1 collective-permute-start.4
  13.8 1.0 %collective-permute-start.6 = (bf16[144,512]{1,0:T(8,128)(2,1)S(1)}, bf16[144,512]{1,0:T(8,128)(2,1)S(1)}, u32[]{:S(2)}, u32[]{:S(2)}) collective-permute-start(bf16[144,512]{1,0:T(8,128)(2,1)S(1)} %collective-permute-done.1.refs_1_), channel_id=1, source_target_pairs={{0,1},{2,0},{4,2},{6,4},{7,6},{5,7},{3,5},{1,3},{8,9},{10,8},{12,1... | collective-permute-start | bytes 442376 | tf_op jit(solution)/shard_map/ppermute | solution.py:121
  14.8 1.0 %collective-permute-start.5 = (bf16[144,512]{1,0:T(8,128)(2,1)S(1)}, bf16[144,512]{1,0:T(8,128)(2,1)S(1)}, u32[]{:S(2)}, u32[]{:S(2)}) collective-permute-start(bf16[144,512]{1,0:T(8,128)(2,1)S(1)} %collective-permute-done.refs_0_), channel_id=1, source_target_pairs={{0,2},{2,4},{4,6},{6,7},{7,5},{5,3},{3,1},{1,0},{8,10},{10,12},{12... | collective-permute-start | bytes 442376 | tf_op jit(solution)/shard_map/ppermute | solution.py:121
  15.8 1.0 %collective-permute-start.12 = (bf16[128,512]{1,0:T(8,128)(2,1)S(1)}, bf16[128,512]{1,0:T(8,128)(2,1)S(1)}, u32[]{:S(2)}, u32[]{:S(2)}) collective-permute-start(bf16[128,512]{1,0:T(8,128)(2,1)S(1)} %collective-permute-done.3.refs_9_), channel_id=1, source_target_pairs={{0,1},{2,0},{4,2},{6,4},{7,6},{5,7},{3,5},{1,3},{8,9},{10,8},{12,1... | collective-permute-start | bytes 393224 | tf_op jit(solution)/shard_map/ppermute | solution.py:121
  16.8 1.0 %collective-permute-start.11 = (bf16[128,512]{1,0:T(8,128)(2,1)S(1)}, bf16[128,512]{1,0:T(8,128)(2,1)S(1)}, u32[]{:S(2)}, u32[]{:S(2)}) collective-permute-start(bf16[128,512]{1,0:T(8,128)(2,1)S(1)} %collective-permute-done.2.refs_8_), channel_id=1, source_target_pairs={{0,2},{2,4},{4,6},{6,7},{7,5},{5,3},{3,1},{1,0},{8,10},{10,12},{12... | collective-permute-start | bytes 393224 | tf_op jit(solution)/shard_map/ppermute | solution.py:121
  17.8 2.6 %collective-permute-done.6.refs_3_ = bf16[144,512]{1,0:T(8,128)(2,1)S(1)} collective-permute-done((bf16[144,512]{1,0:T(8,128)(2,1)S(1)}, bf16[144,512]{1,0:T(8,128)(2,1)S(1)}, u32[]{:S(2)}, u32[]{:S(2)}) %collective-permute-start.6) | collective-permute-done | bytes 147488 | tf_op jit(solution)/shard_map/ppermute | solution.py:121
  20.4 1.1 %collective-permute-start.8 = (bf16[144,512]{1,0:T(8,128)(2,1)S(1)}, bf16[144,512]{1,0:T(8,128)(2,1)S(1)}, u32[]{:S(2)}, u32[]{:S(2)}) collective-permute-start(bf16[144,512]{1,0:T(8,128)(2,1)S(1)} %collective-permute-done.6.refs_3_), channel_id=1, source_target_pairs={{0,1},{2,0},{4,2},{6,4},{7,6},{5,7},{3,5},{1,3},{8,9},{10,8},{12,1... | collective-permute-start | bytes 442376 | tf_op jit(solution)/shard_map/ppermute | solution.py:121
  21.5 0.0 collective-permute-done.5.refs_2_
  21.5 1.0 %collective-permute-start.7 = (bf16[144,512]{1,0:T(8,128)(2,1)S(1)}, bf16[144,512]{1,0:T(8,128)(2,1)S(1)}, u32[]{:S(2)}, u32[]{:S(2)}) collective-permute-start(bf16[144,512]{1,0:T(8,128)(2,1)S(1)} %collective-permute-done.5.refs_2_), channel_id=1, source_target_pairs={{0,2},{2,4},{4,6},{6,7},{7,5},{5,3},{3,1},{1,0},{8,10},{10,12},{12... | collective-permute-start | bytes 442376 | tf_op jit(solution)/shard_map/ppermute | solution.py:121
  22.5 0.7 %collective-permute-done.12.refs_11_ = bf16[128,512]{1,0:T(8,128)(2,1)S(1)} collective-permute-done((bf16[128,512]{1,0:T(8,128)(2,1)S(1)}, bf16[128,512]{1,0:T(8,128)(2,1)S(1)}, u32[]{:S(2)}, u32[]{:S(2)}) %collective-permute-start.12) | collective-permute-done | bytes 131104 | tf_op jit(solution)/shard_map/ppermute | solution.py:121
  23.2 1.1 %collective-permute-start.14 = (bf16[128,512]{1,0:T(8,128)(2,1)S(1)}, bf16[128,512]{1,0:T(8,128)(2,1)S(1)}, u32[]{:S(2)}, u32[]{:S(2)}) collective-permute-start(bf16[128,512]{1,0:T(8,128)(2,1)S(1)} %collective-permute-done.12.refs_11_), channel_id=1, source_target_pairs={{0,1},{2,0},{4,2},{6,4},{7,6},{5,7},{3,5},{1,3},{8,9},{10,8},{12,1... | collective-permute-start | bytes 393224 | tf_op jit(solution)/shard_map/ppermute | solution.py:121
  24.3 0.0 collective-permute-done.11.refs_10_
  24.3 1.0 %collective-permute-start.13 = (bf16[128,512]{1,0:T(8,128)(2,1)S(1)}, bf16[128,512]{1,0:T(8,128)(2,1)S(1)}, u32[]{:S(2)}, u32[]{:S(2)}) collective-permute-start(bf16[128,512]{1,0:T(8,128)(2,1)S(1)} %collective-permute-done.11.refs_10_), channel_id=1, source_target_pairs={{0,2},{2,4},{4,6},{6,7},{7,5},{5,3},{3,1},{1,0},{8,10},{10,12},{12... | collective-permute-start | bytes 393224 | tf_op jit(solution)/shard_map/ppermute | solution.py:121
  25.3 1.6 %collective-permute-done.8.refs_5_ = bf16[144,512]{1,0:T(8,128)(2,1)S(1)} collective-permute-done((bf16[144,512]{1,0:T(8,128)(2,1)S(1)}, bf16[144,512]{1,0:T(8,128)(2,1)S(1)}, u32[]{:S(2)}, u32[]{:S(2)}) %collective-permute-start.8) | collective-permute-done | bytes 147488 | tf_op jit(solution)/shard_map/ppermute | solution.py:121
  26.8 1.0 %collective-permute-start.10 = (bf16[80,512]{1,0:T(8,128)(2,1)S(1)}, bf16[80,512]{1,0:T(8,128)(2,1)S(1)}, u32[]{:S(2)}, u32[]{:S(2)}) collective-permute-start(bf16[80,512]{1,0:T(8,128)(2,1)S(1)} %slice.17), channel_id=1, source_target_pairs={{0,1},{2,0},{4,2},{6,4},{7,6},{5,7},{3,5},{1,3},{8,9},{10,8},{12,1... | collective-permute-start | bytes 245768 | tf_op jit(solution)/shard_map/ppermute | solution.py:121
  27.9 0.0 collective-permute-done.7.refs_4_
  27.9 1.0 %collective-permute-start.9 = (bf16[64,512]{1,0:T(8,128)(2,1)S(1)}, bf16[64,512]{1,0:T(8,128)(2,1)S(1)}, u32[]{:S(2)}, u32[]{:S(2)}) collective-permute-start(bf16[64,512]{1,0:T(8,128)(2,1)S(1)} %slice.16), channel_id=1, source_target_pairs={{0,2},{2,4},{4,6},{6,7},{7,5},{5,3},{3,1},{1,0},{8,10},{10,12},{12... | collective-permute-start | bytes 196616 | tf_op jit(solution)/shard_map/ppermute | solution.py:121
  28.9 0.7 %collective-permute-done.14.refs_13_ = bf16[128,512]{1,0:T(8,128)(2,1)S(1)} collective-permute-done((bf16[128,512]{1,0:T(8,128)(2,1)S(1)}, bf16[128,512]{1,0:T(8,128)(2,1)S(1)}, u32[]{:S(2)}, u32[]{:S(2)}) %collective-permute-start.14) | collective-permute-done | bytes 131104 | tf_op jit(solution)/shard_map/ppermute | solution.py:121
  29.6 1.0 %collective-permute-start.16 = (bf16[64,512]{1,0:T(8,128)(2,1)S(1)}, bf16[64,512]{1,0:T(8,128)(2,1)S(1)}, u32[]{:S(2)}, u32[]{:S(2)}) collective-permute-start(bf16[64,512]{1,0:T(8,128)(2,1)S(1)} %slice.19), channel_id=1, source_target_pairs={{0,1},{2,0},{4,2},{6,4},{7,6},{5,7},{3,5},{1,3},{8,9},{10,8},{12,1... | collective-permute-start | bytes 196616 | tf_op jit(solution)/shard_map/ppermute | solution.py:121
  30.7 0.0 collective-permute-done.13.refs_12_
  30.7 1.0 %collective-permute-start.15 = (bf16[64,512]{1,0:T(8,128)(2,1)S(1)}, bf16[64,512]{1,0:T(8,128)(2,1)S(1)}, u32[]{:S(2)}, u32[]{:S(2)}) collective-permute-start(bf16[64,512]{1,0:T(8,128)(2,1)S(1)} %slice.18), channel_id=1, source_target_pairs={{0,2},{2,4},{4,6},{6,7},{7,5},{5,3},{3,1},{1,0},{8,10},{10,12},{12... | collective-permute-start | bytes 196616 | tf_op jit(solution)/shard_map/ppermute | solution.py:121
  31.7 1.0 %collective-permute-done.9.refs_6_ = bf16[64,512]{1,0:T(8,128)(2,1)S(1)} collective-permute-done((bf16[64,512]{1,0:T(8,128)(2,1)S(1)}, bf16[64,512]{1,0:T(8,128)(2,1)S(1)}, u32[]{:S(2)}, u32[]{:S(2)}) %collective-permute-start.9) | collective-permute-done | bytes 65568 | tf_op jit(solution)/shard_map/ppermute | solution.py:121
  32.7 0.0 collective-permute-done.10.refs_7_
  32.7 0.0 collective-permute-done.4.own_ref
  32.7 0.0 copy-done.1
  32.7 0.0 copy-done
  32.7 2.4 %shard_map.55.weights_ref = bf16[8,512,320]{2,1,0:T(8,128)(2,1)S(1)} custom-call(s32[128]{0:T(128)S(1)} %copy-done.1, s32[1,1024]{1,0:T(1,128)S(1)} %bitcast.7, bf16[128,5120]{1,0:T(8,128)(2,1)S(1)} %collective-permute-done.4.own_ref, bf16[144,512]{1,0:T(8,128)(2,1)S(1)} %collective-permute-done.refs_0_, ...), custom_call_target="tpu_custom_call" | custom-call | flops 67108864 | bytes 1048576 | tf_op jit(solution)/shard_map/pallas_call | solution.py:141
  35.1 0.0 collective-permute-done.16.refs_15_
  35.1 0.0 collective-permute-done.15.refs_14_
  35.1 3.0 %shard_map.56 = bf16[128,4096]{1,0:T(8,128)(2,1)} custom-call(s32[128]{0:T(128)S(1)} %copy-done.1, bf16[8,512,320]{2,1,0:T(8,128)(2,1)S(1)} %shard_map.55.weights_ref, bf16[128,5120]{1,0:T(8,128)(2,1)S(1)} %collective-permute-done.4.own_ref, bf16[144,512]{1,0:T(8,128)(2,1)S(1)} %collective-permute-done.refs_0_, ...), custom_call_target="tpu_custom_call" | custom-call | flops 67108864 | bytes 1048576 | tf_op jit(solution)/shard_map/pallas_call | solution.py:150
  (6 shorter events, 0.0 us)
Async XLA Ops:
  0.0 32.7 %copy-start.1 = (s32[128]{0:T(128)S(1)}, s32[128]{0:T(128)}, u32[]{:S(2)}) copy-start(s32[128]{0:T(128)} %pos_ref.3) | copy-start | bytes 1540
  0.0 32.7 %copy-start = (s32[1024]{0:T(1024)S(1)}, s32[1024]{0:T(1024)}, u32[]{:S(2)}) copy-start(s32[1024]{0:T(1024)} %param.9) | copy-start | bytes 12292
  0.0 8.5 %collective-permute-start.3 = (bf16[128,512]{1,0:T(8,128)(2,1)}, bf16[128,512]{1,0:T(8,128)(2,1)S(1)}, u32[]{:S(2)}, u32[]{:S(2)}) collective-permute-start(bf16[128,512]{1,0:T(8,128)(2,1)} %bitcast.11), channel_id=1, source_target_pairs={{0,9},{2,8},{4,10},{6,12},{7,14},{5,15},{3,13},{1,11},{8,17},{10,1... | collective-permute-start | bytes 393224 | tf_op jit(solution)/shard_map/ppermute | solution.py:121
  2.4 6.7 %collective-permute-start.2 = (bf16[128,512]{1,0:T(8,128)(2,1)}, bf16[128,512]{1,0:T(8,128)(2,1)S(1)}, u32[]{:S(2)}, u32[]{:S(2)}) collective-permute-start(bf16[128,512]{1,0:T(8,128)(2,1)} %bitcast.12), channel_id=1, source_target_pairs={{0,10},{2,12},{4,14},{6,15},{7,13},{5,11},{3,9},{1,8},{8,18},{10,2... | collective-permute-start | bytes 393224 | tf_op jit(solution)/shard_map/ppermute | solution.py:121
  5.7 6.5 %collective-permute-start.1 = (bf16[144,512]{1,0:T(8,128)(2,1)S(1)}, bf16[144,512]{1,0:T(8,128)(2,1)S(1)}, u32[]{:S(2)}, u32[]{:S(2)}) collective-permute-start(bf16[144,512]{1,0:T(8,128)(2,1)S(1)} %pad_maximum_fusion.1), channel_id=1, source_target_pairs={{0,9},{2,8},{4,10},{6,12},{7,14},{5,15},{3,13},{1,11},{8,17},{10,1... | collective-permute-start | bytes 442376 | tf_op jit(solution)/shard_map/ppermute | solution.py:121
  6.8 6.8 %collective-permute-start = (bf16[144,512]{1,0:T(8,128)(2,1)S(1)}, bf16[144,512]{1,0:T(8,128)(2,1)S(1)}, u32[]{:S(2)}, u32[]{:S(2)}) collective-permute-start(bf16[144,512]{1,0:T(8,128)(2,1)S(1)} %pad_maximum_fusion.1), channel_id=1, source_target_pairs={{0,10},{2,12},{4,14},{6,15},{7,13},{5,11},{3,9},{1,8},{8,18},{10,2... | collective-permute-start | bytes 442376 | tf_op jit(solution)/shard_map/ppermute | solution.py:121
  13.7 19.0 %collective-permute-start.4 = (bf16[128,5120]{1,0:T(8,128)(2,1)S(1)}, bf16[128,5120]{1,0:T(8,128)(2,1)S(1)}, u32[]{:S(2)}, u32[]{:S(2)}) collective-permute-start(bf16[128,5120]{1,0:T(8,128)(2,1)S(1)} %pad_maximum_fusion), channel_id=1, source_target_pairs={{0,8},{2,10},{4,12},{6,14},{7,15},{5,13},{3,11},{1,9},{8,16},{10,1... | collective-permute-start | bytes 3932168 | tf_op jit(solution)/shard_map/ppermute | solution.py:121
  13.8 6.6 %collective-permute-start.6 = (bf16[144,512]{1,0:T(8,128)(2,1)S(1)}, bf16[144,512]{1,0:T(8,128)(2,1)S(1)}, u32[]{:S(2)}, u32[]{:S(2)}) collective-permute-start(bf16[144,512]{1,0:T(8,128)(2,1)S(1)} %collective-permute-done.1.refs_1_), channel_id=1, source_target_pairs={{0,1},{2,0},{4,2},{6,4},{7,6},{5,7},{3,5},{1,3},{8,9},{10,8},{12,1... | collective-permute-start | bytes 442376 | tf_op jit(solution)/shard_map/ppermute | solution.py:121
  14.8 6.7 %collective-permute-start.5 = (bf16[144,512]{1,0:T(8,128)(2,1)S(1)}, bf16[144,512]{1,0:T(8,128)(2,1)S(1)}, u32[]{:S(2)}, u32[]{:S(2)}) collective-permute-start(bf16[144,512]{1,0:T(8,128)(2,1)S(1)} %collective-permute-done.refs_0_), channel_id=1, source_target_pairs={{0,2},{2,4},{4,6},{6,7},{7,5},{5,3},{3,1},{1,0},{8,10},{10,12},{12... | collective-permute-start | bytes 442376 | tf_op jit(solution)/shard_map/ppermute | solution.py:121
  15.8 7.4 %collective-permute-start.12 = (bf16[128,512]{1,0:T(8,128)(2,1)S(1)}, bf16[128,512]{1,0:T(8,128)(2,1)S(1)}, u32[]{:S(2)}, u32[]{:S(2)}) collective-permute-start(bf16[128,512]{1,0:T(8,128)(2,1)S(1)} %collective-permute-done.3.refs_9_), channel_id=1, source_target_pairs={{0,1},{2,0},{4,2},{6,4},{7,6},{5,7},{3,5},{1,3},{8,9},{10,8},{12,1... | collective-permute-start | bytes 393224 | tf_op jit(solution)/shard_map/ppermute | solution.py:121
  16.8 7.5 %collective-permute-start.11 = (bf16[128,512]{1,0:T(8,128)(2,1)S(1)}, bf16[128,512]{1,0:T(8,128)(2,1)S(1)}, u32[]{:S(2)}, u32[]{:S(2)}) collective-permute-start(bf16[128,512]{1,0:T(8,128)(2,1)S(1)} %collective-permute-done.2.refs_8_), channel_id=1, source_target_pairs={{0,2},{2,4},{4,6},{6,7},{7,5},{5,3},{3,1},{1,0},{8,10},{10,12},{12... | collective-permute-start | bytes 393224 | tf_op jit(solution)/shard_map/ppermute | solution.py:121
  20.4 6.4 %collective-permute-start.8 = (bf16[144,512]{1,0:T(8,128)(2,1)S(1)}, bf16[144,512]{1,0:T(8,128)(2,1)S(1)}, u32[]{:S(2)}, u32[]{:S(2)}) collective-permute-start(bf16[144,512]{1,0:T(8,128)(2,1)S(1)} %collective-permute-done.6.refs_3_), channel_id=1, source_target_pairs={{0,1},{2,0},{4,2},{6,4},{7,6},{5,7},{3,5},{1,3},{8,9},{10,8},{12,1... | collective-permute-start | bytes 442376 | tf_op jit(solution)/shard_map/ppermute | solution.py:121
  21.5 6.4 %collective-permute-start.7 = (bf16[144,512]{1,0:T(8,128)(2,1)S(1)}, bf16[144,512]{1,0:T(8,128)(2,1)S(1)}, u32[]{:S(2)}, u32[]{:S(2)}) collective-permute-start(bf16[144,512]{1,0:T(8,128)(2,1)S(1)} %collective-permute-done.5.refs_2_), channel_id=1, source_target_pairs={{0,2},{2,4},{4,6},{6,7},{7,5},{5,3},{3,1},{1,0},{8,10},{10,12},{12... | collective-permute-start | bytes 442376 | tf_op jit(solution)/shard_map/ppermute | solution.py:121
  23.2 6.4 %collective-permute-start.14 = (bf16[128,512]{1,0:T(8,128)(2,1)S(1)}, bf16[128,512]{1,0:T(8,128)(2,1)S(1)}, u32[]{:S(2)}, u32[]{:S(2)}) collective-permute-start(bf16[128,512]{1,0:T(8,128)(2,1)S(1)} %collective-permute-done.12.refs_11_), channel_id=1, source_target_pairs={{0,1},{2,0},{4,2},{6,4},{7,6},{5,7},{3,5},{1,3},{8,9},{10,8},{12,1... | collective-permute-start | bytes 393224 | tf_op jit(solution)/shard_map/ppermute | solution.py:121
  24.3 6.4 %collective-permute-start.13 = (bf16[128,512]{1,0:T(8,128)(2,1)S(1)}, bf16[128,512]{1,0:T(8,128)(2,1)S(1)}, u32[]{:S(2)}, u32[]{:S(2)}) collective-permute-start(bf16[128,512]{1,0:T(8,128)(2,1)S(1)} %collective-permute-done.11.refs_10_), channel_id=1, source_target_pairs={{0,2},{2,4},{4,6},{6,7},{7,5},{5,3},{3,1},{1,0},{8,10},{10,12},{12... | collective-permute-start | bytes 393224 | tf_op jit(solution)/shard_map/ppermute | solution.py:121
  26.8 5.9 %collective-permute-start.10 = (bf16[80,512]{1,0:T(8,128)(2,1)S(1)}, bf16[80,512]{1,0:T(8,128)(2,1)S(1)}, u32[]{:S(2)}, u32[]{:S(2)}) collective-permute-start(bf16[80,512]{1,0:T(8,128)(2,1)S(1)} %slice.17), channel_id=1, source_target_pairs={{0,1},{2,0},{4,2},{6,4},{7,6},{5,7},{3,5},{1,3},{8,9},{10,8},{12,1... | collective-permute-start | bytes 245768 | tf_op jit(solution)/shard_map/ppermute | solution.py:121
  27.9 4.8 %collective-permute-start.9 = (bf16[64,512]{1,0:T(8,128)(2,1)S(1)}, bf16[64,512]{1,0:T(8,128)(2,1)S(1)}, u32[]{:S(2)}, u32[]{:S(2)}) collective-permute-start(bf16[64,512]{1,0:T(8,128)(2,1)S(1)} %slice.16), channel_id=1, source_target_pairs={{0,2},{2,4},{4,6},{6,7},{7,5},{5,3},{3,1},{1,0},{8,10},{10,12},{12... | collective-permute-start | bytes 196616 | tf_op jit(solution)/shard_map/ppermute | solution.py:121
  29.6 5.4 %collective-permute-start.16 = (bf16[64,512]{1,0:T(8,128)(2,1)S(1)}, bf16[64,512]{1,0:T(8,128)(2,1)S(1)}, u32[]{:S(2)}, u32[]{:S(2)}) collective-permute-start(bf16[64,512]{1,0:T(8,128)(2,1)S(1)} %slice.19), channel_id=1, source_target_pairs={{0,1},{2,0},{4,2},{6,4},{7,6},{5,7},{3,5},{1,3},{8,9},{10,8},{12,1... | collective-permute-start | bytes 196616 | tf_op jit(solution)/shard_map/ppermute | solution.py:121
  30.7 4.4 %collective-permute-start.15 = (bf16[64,512]{1,0:T(8,128)(2,1)S(1)}, bf16[64,512]{1,0:T(8,128)(2,1)S(1)}, u32[]{:S(2)}, u32[]{:S(2)}) collective-permute-start(bf16[64,512]{1,0:T(8,128)(2,1)S(1)} %slice.18), channel_id=1, source_target_pairs={{0,2},{2,4},{4,6},{6,7},{7,5},{5,3},{3,1},{1,0},{8,10},{10,12},{12... | collective-permute-start | bytes 196616 | tf_op jit(solution)/shard_map/ppermute | solution.py:121

commit v2 on v0

--- a/solution.py
+++ b/solution.py
@@ -45,23 +45,29 @@
     return jnp.maximum(own[half] - reach, 0)
 
 
-def weights_kernel(runs, pos_ref, segment_ref, own_ref, *refs):
+def bias_kernel(runs, pos_ref, segment_ref, bias_ref):
+    reach = runs // 4
+    segment = segment_ref[...].astype(jnp.float32)
+    for half in range(2):
+        run = lax.div(pos_ref[half * RUN], RUN)
+        row_pos = run * RUN + lax.broadcasted_iota(jnp.int32, (RUN, 1), 0)
+        at = lax.broadcasted_iota(jnp.int32, (RUN, runs * RUN), 1) == row_pos
+        row_doc = jnp.sum(jnp.where(at, segment, 0.0), axis=1, keepdims=True)
+        doc_start = jnp.sum(jnp.where(segment < row_doc, 1.0, 0.0), axis=1, keepdims=True).astype(jnp.int32)
+        key_pos = jnp.maximum(run - reach, 0) * RUN + lax.broadcasted_iota(jnp.int32, bias_ref.shape[1:], 1)
+        bias_ref[half] = jnp.where((key_pos <= row_pos) & (key_pos >= doc_start), 0.0, masked_fill)
+
+
+def weights_kernel(runs, pos_ref, bias_ref, own_ref, *refs):
     key_refs, (weights_ref, key_buf) = refs[:-2], refs[-2:]
     reach = runs // 4
     span = (reach + 1) * RUN
     numbers = run_numbers(pos_ref, key_refs)
     sort_runs(numbers, own_ref, QUERY_COLUMNS, key_refs, key_buf)
-    segment = segment_ref[...].astype(jnp.float32)
     scale = math.log2(math.e) / math.sqrt(HEAD_SIZE)
     for half in range(2):
         start = span_start(numbers[0], half, reach)
-        row_pos = numbers[0][half] * RUN + lax.broadcasted_iota(jnp.int32, (RUN, 1), 0)
-        at = lax.broadcasted_iota(jnp.int32, (RUN, runs * RUN), 1) == row_pos
-        row_doc = jnp.sum(jnp.where(at, segment, 0.0), axis=1, keepdims=True)
-        doc_start = jnp.sum(jnp.where(segment < row_doc, 1.0, 0.0), axis=1, keepdims=True).astype(jnp.int32)
-        key_pos = start * RUN + lax.broadcasted_iota(jnp.int32, (RUN, span), 1)
-        bias = jnp.where((key_pos <= row_pos) & (key_pos >= doc_start), 0.0, masked_fill)
-        bias = jnp.concatenate([bias] * GROUP, axis=0)
+        bias = jnp.concatenate([bias_ref[half]] * GROUP, axis=0)
         for kv in range(KEY_VALUE_HEADS):
             query = jnp.concatenate(
                 [
@@ -131,11 +137,20 @@
     tag = jnp.tile((token_pos >> (RUN.bit_length() - 1)).astype(jnp.bfloat16)[None], (TAG_ROWS, KEY_VALUE_HEADS))
     all_keys = around(jnp.concatenate([keys[0], tag], axis=0))
     all_values = around(values[0])
+
     own = shift(jnp.concatenate([queries[0], keys[0], values[0]], axis=1), 1, 0)
+    late_segment, _, _ = lax.optimization_barrier((segment, all_keys[-2:], all_values[-4:-2]))
 
     smem, vmem = pl.BlockSpec(memory_space=pltpu.SMEM), pl.BlockSpec(memory_space=pltpu.VMEM)
     params = pltpu.CompilerParams(vmem_limit_bytes=40 * 1024 * 1024)
     sorted_buf = pltpu.VMEM((runs, RUN, KV_COLUMNS), jnp.bfloat16)
+    bias = pl.pallas_call(
+        functools.partial(bias_kernel, runs),
+        out_shape=jax.ShapeDtypeStruct((2, RUN, (runs // 4 + 1) * RUN), jnp.float32),
+        in_specs=[smem, vmem],
+        out_specs=vmem,
+        cost_estimate=pl.CostEstimate(flops=10<<30, bytes_accessed=0, transcendentals=0),
+    )(token_pos, late_segment.reshape(1, -1))
     weights = pl.pallas_call(
         functools.partial(weights_kernel, runs),
         out_shape=jax.ShapeDtypeStruct((2 * KEY_VALUE_HEADS, GROUP * RUN, (runs // 4 + 1) * RUN), jnp.bfloat16),
@@ -144,7 +159,7 @@
         scratch_shapes=[sorted_buf],
         compiler_params=params,
         cost_estimate=pl.CostEstimate(flops=1 << 26, bytes_accessed=1 << 20, transcendentals=0),
-    )(token_pos, segment.reshape(1, -1), own, *all_keys)
+    )(token_pos, bias, own, *all_keys)
     out = pl.pallas_call(
         functools.partial(values_kernel, runs),
         out_shape=jax.ShapeDtypeStruct((TOK_DEV, QUERY_COLUMNS), jnp.bfloat16),

time: 47.8 us -> 38.5 us (0.81)
  starting transfers between devices: 33.7 us -> 18.6 us
  other arithmetic: 1.51 us -> 4.14 us
  Pallas kernels: 5.34 us -> 7.08 us
  local copies, waits for them, and re-layouts: 0.05 us -> 0.96 us
  waiting for transfers between devices: 6.96 us -> 7.47 us
    ppermute x17, starting transfers between devices: 33.7 us -> 18.6 us  [shift(): return lax.ppermute(block, ('section', 'ctx'), pairs)]
    pallas_call x0 -> x1, Pallas kernels: none -> 1.7 us  [per_device(): pl.pallas_call(functools.partial(bias_kernel, runs), out_shape=jax.ShapeD...]
    concatenate x1, other arithmetic: 1.49 us -> 2.57 us  [per_device(): own = shift(jnp.concatenate([queries[0], keys[0], values[0]], axis=1), 1, 0)]
    unnamed x8 -> x4, local copies, waits for them, and re-layouts: 0.01 us -> 0.93 us
    concatenate x1, other arithmetic: 0.01 us -> 0.91 us  [per_device(): all_keys = around(jnp.concatenate([keys[0], tag], axis=0))]
    convert_element_type x1, other arithmetic: 0.01 us -> 0.66 us  [per_device(): (token_pos >> RUN.bit_length() - 1).astype(jnp.bfloat16)[None]]
    ppermute x17, waiting for transfers between devices: 6.96 us -> 7.47 us  [shift(): return lax.ppermute(block, ('section', 'ctx'), pairs)]
  transfers between devices with their start and end apart: 17 -> 17, of which waited for: 8 -> 6; matrix products, arithmetic and copies ran while one was open for 0% -> 7% of each run, Pallas kernels for 5% -> 11%
where the time goes in v2:
time: 38.5 us; the launch traced here: 38.3 us
  starting transfers between devices  18.6 us (48%)
  waiting for transfers between devices  7.47 us (19%)
  Pallas kernels  7.08 us (18%)
  other arithmetic  4.14 us (11%)
  local copies, waits for them, and re-layouts  0.96 us (2%)
    ppermute x17, starting transfers between devices, shift(): return lax.ppermute(block, ('section', 'ctx'), pairs)  18.6 us
    ppermute x17, waiting for transfers between devices, shift(): return lax.ppermute(block, ('section', 'ctx'), pairs)  7.47 us
    pallas_call x1, Pallas kernels, per_device(): pl.pallas_call(functools.partial(values_kernel, runs), out_shape=jax.Shap...  2.98 us
    concatenate x1, other arithmetic, per_device(): own = shift(jnp.concatenate([queries[0], keys[0], values[0]], axis=1), 1, 0)  2.57 us
    pallas_call x1, Pallas kernels, per_device(): pl.pallas_call(functools.partial(weights_kernel, runs), out_shape=jax.Sha...  2.4 us
    pallas_call x1, Pallas kernels, per_device(): pl.pallas_call(functools.partial(bias_kernel, runs), out_shape=jax.ShapeD...  1.7 us
    unnamed x4, local copies, waits for them, and re-layouts  0.93 us
    concatenate x1, other arithmetic, per_device(): all_keys = around(jnp.concatenate([keys[0], tag], axis=0))  0.91 us
  transfers between devices with their start and end apart: 17, of which 6 were waited for; matrix products, arithmetic and copies ran while one was open for 7% of the time, Pallas kernels for 11%

profile of v2, /device:TPU:0, one launch (start us, length us, event | category | flops | bytes accessed | tf_op | source)
XLA Modules:
  0.0 38.3 jit_solution(1271415610221056885)
XLA Ops:
  0.0 0.7 %shift-right-arithmetic_convert_fusion = bf16[128]{0:T(256)(128)(2,1)S(1)} fusion(s32[128]{0:T(128)} %pos_ref.5), kind=kLoop, calls=%fused_computation.3 | loop fusion | flops 256 | bytes 768 | tf_op jit(solution)/shard_map/convert_element_type | solution.py:137
  0.7 0.9 %pad_maximum_fusion.1 = bf16[144,512]{1,0:T(8,128)(2,1)S(1)} fusion(bf16[16,512]{1,0:T(8,128)(2,1)S(1)} %tile.12, bf16[128,512]{1,0:T(8,128)(2,1)} %bitcast.8), kind=kLoop, calls=%fused_computation.1 | loop fusion | flops 294912 | bytes 294912 | tf_op jit(solution)/shard_map/concatenate | solution.py:138
  1.6 2.5 %collective-permute-start.4 = (bf16[144,512]{1,0:T(8,128)(2,1)S(1)}, bf16[144,512]{1,0:T(8,128)(2,1)S(1)}, u32[]{:S(2)}, u32[]{:S(2)}) collective-permute-start(bf16[144,512]{1,0:T(8,128)(2,1)S(1)} %pad_maximum_fusion.1), channel_id=1, source_target_pairs={{0,9},{2,8},{4,10},{6,12},{7,14},{5,15},{3,13},{1,11},{8,17},{10,1... | collective-permute-start | bytes 442376 | tf_op jit(solution)/shard_map/ppermute | solution.py:127
  4.0 1.7 %collective-permute-start = (bf16[144,512]{1,0:T(8,128)(2,1)S(1)}, bf16[144,512]{1,0:T(8,128)(2,1)S(1)}, u32[]{:S(2)}, u32[]{:S(2)}) collective-permute-start(bf16[144,512]{1,0:T(8,128)(2,1)S(1)} %pad_maximum_fusion.1), channel_id=1, source_target_pairs={{0,10},{2,12},{4,14},{6,15},{7,13},{5,11},{3,9},{1,8},{8,18},{10,2... | collective-permute-start | bytes 442376 | tf_op jit(solution)/shard_map/ppermute | solution.py:127
  5.8 1.1 %collective-permute-start.11 = (bf16[128,512]{1,0:T(8,128)(2,1)}, bf16[128,512]{1,0:T(8,128)(2,1)S(1)}, u32[]{:S(2)}, u32[]{:S(2)}) collective-permute-start(bf16[128,512]{1,0:T(8,128)(2,1)} %bitcast.10), channel_id=1, source_target_pairs={{0,9},{2,8},{4,10},{6,12},{7,14},{5,15},{3,13},{1,11},{8,17},{10,1... | collective-permute-start | bytes 393224 | tf_op jit(solution)/shard_map/ppermute | solution.py:127
  6.8 0.1 collective-permute-start.8
  7.0 1.6 %collective-permute-done.4.refs_1_ = bf16[144,512]{1,0:T(8,128)(2,1)S(1)} collective-permute-done((bf16[144,512]{1,0:T(8,128)(2,1)S(1)}, bf16[144,512]{1,0:T(8,128)(2,1)S(1)}, u32[]{:S(2)}, u32[]{:S(2)}) %collective-permute-start.4) | collective-permute-done | bytes 147488 | tf_op jit(solution)/shard_map/ppermute | solution.py:127
  8.6 2.3 %collective-permute-start.5 = (bf16[144,512]{1,0:T(8,128)(2,1)S(1)}, bf16[144,512]{1,0:T(8,128)(2,1)S(1)}, u32[]{:S(2)}, u32[]{:S(2)}) collective-permute-start(bf16[144,512]{1,0:T(8,128)(2,1)S(1)} %collective-permute-done.4.refs_1_), channel_id=1, source_target_pairs={{0,1},{2,0},{4,2},{6,4},{7,6},{5,7},{3,5},{1,3},{8,9},{10,8},{12,1... | collective-permute-start | bytes 442376 | tf_op jit(solution)/shard_map/ppermute | solution.py:127
  10.9 0.0 collective-permute-done.refs_0_
  10.9 0.9 %collective-permute-start.1 = (bf16[144,512]{1,0:T(8,128)(2,1)S(1)}, bf16[144,512]{1,0:T(8,128)(2,1)S(1)}, u32[]{:S(2)}, u32[]{:S(2)}) collective-permute-start(bf16[144,512]{1,0:T(8,128)(2,1)S(1)} %collective-permute-done.refs_0_), channel_id=1, source_target_pairs={{0,2},{2,4},{4,6},{6,7},{7,5},{5,3},{3,1},{1,0},{8,10},{10,12},{12... | collective-permute-start | bytes 442376 | tf_op jit(solution)/shard_map/ppermute | solution.py:127
  11.8 2.6 %pad_maximum_fusion = bf16[128,5120]{1,0:T(8,128)(2,1)} fusion(bf16[128,512]{1,0:T(8,128)(2,1)} %bitcast.12, bf16[128,512]{1,0:T(8,128)(2,1)} %bitcast.9, bf16[128,4096]{1,0:T(8,128)(2,1)} %bitcast.7), kind=kLoop, calls=%fused_computation | loop fusion | flops 3932160 | bytes 2621440 | tf_op jit(solution)/shard_map/concatenate | solution.py:141
  14.4 0.5 %collective-permute-start.14 = (bf16[128,5120]{1,0:T(8,128)(2,1)}, bf16[128,5120]{1,0:T(8,128)(2,1)S(1)}, u32[]{:S(2)}, u32[]{:S(2)}) collective-permute-start(bf16[128,5120]{1,0:T(8,128)(2,1)} %pad_maximum_fusion), channel_id=1, source_target_pairs={{0,8},{2,10},{4,12},{6,14},{7,15},{5,13},{3,11},{1,9},{8,16},{10,1... | collective-permute-start | bytes 3932168 | tf_op jit(solution)/shard_map/ppermute | solution.py:127
  14.8 0.0 collective-permute-done.11.refs_9_
  14.8 1.4 %collective-permute-start.12 = (bf16[128,512]{1,0:T(8,128)(2,1)S(1)}, bf16[128,512]{1,0:T(8,128)(2,1)S(1)}, u32[]{:S(2)}, u32[]{:S(2)}) collective-permute-start(bf16[128,512]{1,0:T(8,128)(2,1)S(1)} %collective-permute-done.11.refs_9_), channel_id=1, source_target_pairs={{0,1},{2,0},{4,2},{6,4},{7,6},{5,7},{3,5},{1,3},{8,9},{10,8},{12,1... | collective-permute-start | bytes 393224 | tf_op jit(solution)/shard_map/ppermute | solution.py:127
  16.2 0.0 collective-permute-done.8.refs_8_
  16.2 0.7 %collective-permute-start.9 = (bf16[128,512]{1,0:T(8,128)(2,1)S(1)}, bf16[128,512]{1,0:T(8,128)(2,1)S(1)}, u32[]{:S(2)}, u32[]{:S(2)}) collective-permute-start(bf16[128,512]{1,0:T(8,128)(2,1)S(1)} %collective-permute-done.8.refs_8_), channel_id=1, source_target_pairs={{0,2},{2,4},{4,6},{6,7},{7,5},{5,3},{3,1},{1,0},{8,10},{10,12},{12... | collective-permute-start | bytes 393224 | tf_op jit(solution)/shard_map/ppermute | solution.py:127
  16.9 0.0 collective-permute-done.5.refs_3_
  16.9 1.4 %collective-permute-start.6 = (bf16[144,512]{1,0:T(8,128)(2,1)S(1)}, bf16[144,512]{1,0:T(8,128)(2,1)S(1)}, u32[]{:S(2)}, u32[]{:S(2)}) collective-permute-start(bf16[144,512]{1,0:T(8,128)(2,1)S(1)} %collective-permute-done.5.refs_3_), channel_id=1, source_target_pairs={{0,1},{2,0},{4,2},{6,4},{7,6},{5,7},{3,5},{1,3},{8,9},{10,8},{12,1... | collective-permute-start | bytes 442376 | tf_op jit(solution)/shard_map/ppermute | solution.py:127
  18.2 0.0 collective-permute-done.1.refs_2_
  18.2 0.7 %collective-permute-start.2 = (bf16[144,512]{1,0:T(8,128)(2,1)S(1)}, bf16[144,512]{1,0:T(8,128)(2,1)S(1)}, u32[]{:S(2)}, u32[]{:S(2)}) collective-permute-start(bf16[144,512]{1,0:T(8,128)(2,1)S(1)} %collective-permute-done.1.refs_2_), channel_id=1, source_target_pairs={{0,2},{2,4},{4,6},{6,7},{7,5},{5,3},{3,1},{1,0},{8,10},{10,12},{12... | collective-permute-start | bytes 442376 | tf_op jit(solution)/shard_map/ppermute | solution.py:127
  18.9 1.7 %collective-permute-done.12.refs_11_ = bf16[128,512]{1,0:T(8,128)(2,1)S(1)} collective-permute-done((bf16[128,512]{1,0:T(8,128)(2,1)S(1)}, bf16[128,512]{1,0:T(8,128)(2,1)S(1)}, u32[]{:S(2)}, u32[]{:S(2)}) %collective-permute-start.12) | collective-permute-done | bytes 131104 | tf_op jit(solution)/shard_map/ppermute | solution.py:127
  20.6 1.2 %collective-permute-start.13 = (bf16[128,512]{1,0:T(8,128)(2,1)S(1)}, bf16[128,512]{1,0:T(8,128)(2,1)S(1)}, u32[]{:S(2)}, u32[]{:S(2)}) collective-permute-start(bf16[128,512]{1,0:T(8,128)(2,1)S(1)} %collective-permute-done.12.refs_11_), channel_id=1, source_target_pairs={{0,1},{2,0},{4,2},{6,4},{7,6},{5,7},{3,5},{1,3},{8,9},{10,8},{12,1... | collective-permute-start | bytes 393224 | tf_op jit(solution)/shard_map/ppermute | solution.py:127
  21.8 0.0 collective-permute-done.9.refs_10_
  21.8 0.9 %collective-permute-start.10 = (bf16[128,512]{1,0:T(8,128)(2,1)S(1)}, bf16[128,512]{1,0:T(8,128)(2,1)S(1)}, u32[]{:S(2)}, u32[]{:S(2)}) collective-permute-start(bf16[128,512]{1,0:T(8,128)(2,1)S(1)} %collective-permute-done.9.refs_10_), channel_id=1, source_target_pairs={{0,2},{2,4},{4,6},{6,7},{7,5},{5,3},{3,1},{1,0},{8,10},{10,12},{12... | collective-permute-start | bytes 393224 | tf_op jit(solution)/shard_map/ppermute | solution.py:127
  22.7 1.1 %collective-permute-done.6.refs_5_ = bf16[144,512]{1,0:T(8,128)(2,1)S(1)} collective-permute-done((bf16[144,512]{1,0:T(8,128)(2,1)S(1)}, bf16[144,512]{1,0:T(8,128)(2,1)S(1)}, u32[]{:S(2)}, u32[]{:S(2)}) %collective-permute-start.6) | collective-permute-done | bytes 147488 | tf_op jit(solution)/shard_map/ppermute | solution.py:127
  23.8 1.2 %collective-permute-start.7 = (bf16[80,512]{1,0:T(8,128)(2,1)S(1)}, bf16[80,512]{1,0:T(8,128)(2,1)S(1)}, u32[]{:S(2)}, u32[]{:S(2)}) collective-permute-start(bf16[80,512]{1,0:T(8,128)(2,1)S(1)} %slice.17), channel_id=1, source_target_pairs={{0,1},{2,0},{4,2},{6,4},{7,6},{5,7},{3,5},{1,3},{8,9},{10,8},{12,1... | collective-permute-start | bytes 245768 | tf_op jit(solution)/shard_map/ppermute | solution.py:127
  24.9 0.0 collective-permute-done.2.refs_4_
  25.0 0.9 %collective-permute-start.3 = (bf16[64,512]{1,0:T(8,128)(2,1)S(1)}, bf16[64,512]{1,0:T(8,128)(2,1)S(1)}, u32[]{:S(2)}, u32[]{:S(2)}) collective-permute-start(bf16[64,512]{1,0:T(8,128)(2,1)S(1)} %slice.16), channel_id=1, source_target_pairs={{0,2},{2,4},{4,6},{6,7},{7,5},{5,3},{3,1},{1,0},{8,10},{10,12},{12... | collective-permute-start | bytes 196616 | tf_op jit(solution)/shard_map/ppermute | solution.py:127
  25.9 1.2 %collective-permute-done.13.refs_13_ = bf16[128,512]{1,0:T(8,128)(2,1)S(1)} collective-permute-done((bf16[128,512]{1,0:T(8,128)(2,1)S(1)}, bf16[128,512]{1,0:T(8,128)(2,1)S(1)}, u32[]{:S(2)}, u32[]{:S(2)}) %collective-permute-start.13) | collective-permute-done | bytes 131104 | tf_op jit(solution)/shard_map/ppermute | solution.py:127
  27.1 1.2 %collective-permute-start.16 = (bf16[64,512]{1,0:T(8,128)(2,1)S(1)}, bf16[64,512]{1,0:T(8,128)(2,1)S(1)}, u32[]{:S(2)}, u32[]{:S(2)}) collective-permute-start(bf16[64,512]{1,0:T(8,128)(2,1)S(1)} %slice.19), channel_id=1, source_target_pairs={{0,1},{2,0},{4,2},{6,4},{7,6},{5,7},{3,5},{1,3},{8,9},{10,8},{12,1... | collective-permute-start | bytes 196616 | tf_op jit(solution)/shard_map/ppermute | solution.py:127
  28.2 0.6 %collective-permute-done.10.refs_12_ = bf16[128,512]{1,0:T(8,128)(2,1)S(1)} collective-permute-done((bf16[128,512]{1,0:T(8,128)(2,1)S(1)}, bf16[128,512]{1,0:T(8,128)(2,1)S(1)}, u32[]{:S(2)}, u32[]{:S(2)}) %collective-permute-start.10) | collective-permute-done | bytes 131104 | tf_op jit(solution)/shard_map/ppermute | solution.py:127
  28.9 0.3 collective-permute-start.15
  29.1 1.1 %collective-permute-done.3.refs_6_ = bf16[64,512]{1,0:T(8,128)(2,1)S(1)} collective-permute-done((bf16[64,512]{1,0:T(8,128)(2,1)S(1)}, bf16[64,512]{1,0:T(8,128)(2,1)S(1)}, u32[]{:S(2)}, u32[]{:S(2)}) %collective-permute-start.3) | collective-permute-done | bytes 65568 | tf_op jit(solution)/shard_map/ppermute | solution.py:127
  30.3 0.0 collective-permute-done.7.refs_7_
  30.3 0.0 copy-start.1
  30.3 1.7 %shard_map.55.bias_ref = f32[2,64,320]{2,1,0:T(8,128)} custom-call(s32[128]{0:T(128)} %pos_ref.5, s32[1,1024]{1,0:T(1,128)} %bitcast.13), custom_call_target="tpu_custom_call" | custom-call | flops 10737418240 | tf_op jit(solution)/shard_map/pallas_call | solution.py:147
  32.0 0.0 collective-permute-done.14.own_ref
  32.0 0.0 copy-done.1
  32.0 0.0 copy-start
  32.0 0.9 %copy-done = f32[2,64,320]{2,1,0:T(8,128)S(1)} copy-done((f32[2,64,320]{2,1,0:T(8,128)S(1)}, f32[2,64,320]{2,1,0:T(8,128)}, u32[]{:S(2)}) %copy-start) | copy-done | bytes 163864
  32.9 2.4 %shard_map.56.weights_ref = bf16[8,512,320]{2,1,0:T(8,128)(2,1)S(1)} custom-call(s32[128]{0:T(128)S(1)} %copy-done.1, f32[2,64,320]{2,1,0:T(8,128)S(1)} %copy-done, bf16[128,5120]{1,0:T(8,128)(2,1)S(1)} %collective-permute-done.14.own_ref, bf16[144,512]{1,0:T(8,128)(2,1)S(1)} %collective-permute-done.refs_0_, ...), custom_call_target="tpu_custom_call" | custom-call | flops 67108864 | bytes 1048576 | tf_op jit(solution)/shard_map/pallas_call | solution.py:154
  35.3 0.0 collective-permute-done.16.refs_15_
  35.3 0.0 collective-permute-done.15.refs_14_
  35.3 3.0 %shard_map.57 = bf16[128,4096]{1,0:T(8,128)(2,1)} custom-call(s32[128]{0:T(128)S(1)} %copy-done.1, bf16[8,512,320]{2,1,0:T(8,128)(2,1)S(1)} %shard_map.56.weights_ref, bf16[128,5120]{1,0:T(8,128)(2,1)S(1)} %collective-permute-done.14.own_ref, bf16[144,512]{1,0:T(8,128)(2,1)S(1)} %collective-permute-done.refs_0_, ...), custom_call_target="tpu_custom_call" | custom-call | flops 67108864 | bytes 1048576 | tf_op jit(solution)/shard_map/pallas_call | solution.py:163
  (6 shorter events, 0.0 us)
Async XLA Ops:
  1.6 7.0 %collective-permute-start.4 = (bf16[144,512]{1,0:T(8,128)(2,1)S(1)}, bf16[144,512]{1,0:T(8,128)(2,1)S(1)}, u32[]{:S(2)}, u32[]{:S(2)}) collective-permute-start(bf16[144,512]{1,0:T(8,128)(2,1)S(1)} %pad_maximum_fusion.1), channel_id=1, source_target_pairs={{0,9},{2,8},{4,10},{6,12},{7,14},{5,15},{3,13},{1,11},{8,17},{10,1... | collective-permute-start | bytes 442376 | tf_op jit(solution)/shard_map/ppermute | solution.py:127
  4.0 6.9 %collective-permute-start = (bf16[144,512]{1,0:T(8,128)(2,1)S(1)}, bf16[144,512]{1,0:T(8,128)(2,1)S(1)}, u32[]{:S(2)}, u32[]{:S(2)}) collective-permute-start(bf16[144,512]{1,0:T(8,128)(2,1)S(1)} %pad_maximum_fusion.1), channel_id=1, source_target_pairs={{0,10},{2,12},{4,14},{6,15},{7,13},{5,11},{3,9},{1,8},{8,18},{10,2... | collective-permute-start | bytes 442376 | tf_op jit(solution)/shard_map/ppermute | solution.py:127
  5.8 9.1 %collective-permute-start.11 = (bf16[128,512]{1,0:T(8,128)(2,1)}, bf16[128,512]{1,0:T(8,128)(2,1)S(1)}, u32[]{:S(2)}, u32[]{:S(2)}) collective-permute-start(bf16[128,512]{1,0:T(8,128)(2,1)} %bitcast.10), channel_id=1, source_target_pairs={{0,9},{2,8},{4,10},{6,12},{7,14},{5,15},{3,13},{1,11},{8,17},{10,1... | collective-permute-start | bytes 393224 | tf_op jit(solution)/shard_map/ppermute | solution.py:127
  6.8 9.4 %collective-permute-start.8 = (bf16[128,512]{1,0:T(8,128)(2,1)}, bf16[128,512]{1,0:T(8,128)(2,1)S(1)}, u32[]{:S(2)}, u32[]{:S(2)}) collective-permute-start(bf16[128,512]{1,0:T(8,128)(2,1)} %bitcast.11), channel_id=1, source_target_pairs={{0,10},{2,12},{4,14},{6,15},{7,13},{5,11},{3,9},{1,8},{8,18},{10,2... | collective-permute-start | bytes 393224 | tf_op jit(solution)/shard_map/ppermute | solution.py:127
  8.6 8.3 %collective-permute-start.5 = (bf16[144,512]{1,0:T(8,128)(2,1)S(1)}, bf16[144,512]{1,0:T(8,128)(2,1)S(1)}, u32[]{:S(2)}, u32[]{:S(2)}) collective-permute-start(bf16[144,512]{1,0:T(8,128)(2,1)S(1)} %collective-permute-done.4.refs_1_), channel_id=1, source_target_pairs={{0,1},{2,0},{4,2},{6,4},{7,6},{5,7},{3,5},{1,3},{8,9},{10,8},{12,1... | collective-permute-start | bytes 442376 | tf_op jit(solution)/shard_map/ppermute | solution.py:127
  10.9 7.3 %collective-permute-start.1 = (bf16[144,512]{1,0:T(8,128)(2,1)S(1)}, bf16[144,512]{1,0:T(8,128)(2,1)S(1)}, u32[]{:S(2)}, u32[]{:S(2)}) collective-permute-start(bf16[144,512]{1,0:T(8,128)(2,1)S(1)} %collective-permute-done.refs_0_), channel_id=1, source_target_pairs={{0,2},{2,4},{4,6},{6,7},{7,5},{5,3},{3,1},{1,0},{8,10},{10,12},{12... | collective-permute-start | bytes 442376 | tf_op jit(solution)/shard_map/ppermute | solution.py:127
  14.4 17.6 %collective-permute-start.14 = (bf16[128,5120]{1,0:T(8,128)(2,1)}, bf16[128,5120]{1,0:T(8,128)(2,1)S(1)}, u32[]{:S(2)}, u32[]{:S(2)}) collective-permute-start(bf16[128,5120]{1,0:T(8,128)(2,1)} %pad_maximum_fusion), channel_id=1, source_target_pairs={{0,8},{2,10},{4,12},{6,14},{7,15},{5,13},{3,11},{1,9},{8,16},{10,1... | collective-permute-start | bytes 3932168 | tf_op jit(solution)/shard_map/ppermute | solution.py:127
  14.8 5.8 %collective-permute-start.12 = (bf16[128,512]{1,0:T(8,128)(2,1)S(1)}, bf16[128,512]{1,0:T(8,128)(2,1)S(1)}, u32[]{:S(2)}, u32[]{:S(2)}) collective-permute-start(bf16[128,512]{1,0:T(8,128)(2,1)S(1)} %collective-permute-done.11.refs_9_), channel_id=1, source_target_pairs={{0,1},{2,0},{4,2},{6,4},{7,6},{5,7},{3,5},{1,3},{8,9},{10,8},{12,1... | collective-permute-start | bytes 393224 | tf_op jit(solution)/shard_map/ppermute | solution.py:127
  16.2 5.6 %collective-permute-start.9 = (bf16[128,512]{1,0:T(8,128)(2,1)S(1)}, bf16[128,512]{1,0:T(8,128)(2,1)S(1)}, u32[]{:S(2)}, u32[]{:S(2)}) collective-permute-start(bf16[128,512]{1,0:T(8,128)(2,1)S(1)} %collective-permute-done.8.refs_8_), channel_id=1, source_target_pairs={{0,2},{2,4},{4,6},{6,7},{7,5},{5,3},{3,1},{1,0},{8,10},{10,12},{12... | collective-permute-start | bytes 393224 | tf_op jit(solution)/shard_map/ppermute | solution.py:127
  16.9 6.9 %collective-permute-start.6 = (bf16[144,512]{1,0:T(8,128)(2,1)S(1)}, bf16[144,512]{1,0:T(8,128)(2,1)S(1)}, u32[]{:S(2)}, u32[]{:S(2)}) collective-permute-start(bf16[144,512]{1,0:T(8,128)(2,1)S(1)} %collective-permute-done.5.refs_3_), channel_id=1, source_target_pairs={{0,1},{2,0},{4,2},{6,4},{7,6},{5,7},{3,5},{1,3},{8,9},{10,8},{12,1... | collective-permute-start | bytes 442376 | tf_op jit(solution)/shard_map/ppermute | solution.py:127
  18.2 6.7 %collective-permute-start.2 = (bf16[144,512]{1,0:T(8,128)(2,1)S(1)}, bf16[144,512]{1,0:T(8,128)(2,1)S(1)}, u32[]{:S(2)}, u32[]{:S(2)}) collective-permute-start(bf16[144,512]{1,0:T(8,128)(2,1)S(1)} %collective-permute-done.1.refs_2_), channel_id=1, source_target_pairs={{0,2},{2,4},{4,6},{6,7},{7,5},{5,3},{3,1},{1,0},{8,10},{10,12},{12... | collective-permute-start | bytes 442376 | tf_op jit(solution)/shard_map/ppermute | solution.py:127
  20.6 6.4 %collective-permute-start.13 = (bf16[128,512]{1,0:T(8,128)(2,1)S(1)}, bf16[128,512]{1,0:T(8,128)(2,1)S(1)}, u32[]{:S(2)}, u32[]{:S(2)}) collective-permute-start(bf16[128,512]{1,0:T(8,128)(2,1)S(1)} %collective-permute-done.12.refs_11_), channel_id=1, source_target_pairs={{0,1},{2,0},{4,2},{6,4},{7,6},{5,7},{3,5},{1,3},{8,9},{10,8},{12,1... | collective-permute-start | bytes 393224 | tf_op jit(solution)/shard_map/ppermute | solution.py:127
  21.8 7.1 %collective-permute-start.10 = (bf16[128,512]{1,0:T(8,128)(2,1)S(1)}, bf16[128,512]{1,0:T(8,128)(2,1)S(1)}, u32[]{:S(2)}, u32[]{:S(2)}) collective-permute-start(bf16[128,512]{1,0:T(8,128)(2,1)S(1)} %collective-permute-done.9.refs_10_), channel_id=1, source_target_pairs={{0,2},{2,4},{4,6},{6,7},{7,5},{5,3},{3,1},{1,0},{8,10},{10,12},{12... | collective-permute-start | bytes 393224 | tf_op jit(solution)/shard_map/ppermute | solution.py:127
  23.8 6.5 %collective-permute-start.7 = (bf16[80,512]{1,0:T(8,128)(2,1)S(1)}, bf16[80,512]{1,0:T(8,128)(2,1)S(1)}, u32[]{:S(2)}, u32[]{:S(2)}) collective-permute-start(bf16[80,512]{1,0:T(8,128)(2,1)S(1)} %slice.17), channel_id=1, source_target_pairs={{0,1},{2,0},{4,2},{6,4},{7,6},{5,7},{3,5},{1,3},{8,9},{10,8},{12,1... | collective-permute-start | bytes 245768 | tf_op jit(solution)/shard_map/ppermute | solution.py:127
  25.0 5.3 %collective-permute-start.3 = (bf16[64,512]{1,0:T(8,128)(2,1)S(1)}, bf16[64,512]{1,0:T(8,128)(2,1)S(1)}, u32[]{:S(2)}, u32[]{:S(2)}) collective-permute-start(bf16[64,512]{1,0:T(8,128)(2,1)S(1)} %slice.16), channel_id=1, source_target_pairs={{0,2},{2,4},{4,6},{6,7},{7,5},{5,3},{3,1},{1,0},{8,10},{10,12},{12... | collective-permute-start | bytes 196616 | tf_op jit(solution)/shard_map/ppermute | solution.py:127
  27.1 8.3 %collective-permute-start.16 = (bf16[64,512]{1,0:T(8,128)(2,1)S(1)}, bf16[64,512]{1,0:T(8,128)(2,1)S(1)}, u32[]{:S(2)}, u32[]{:S(2)}) collective-permute-start(bf16[64,512]{1,0:T(8,128)(2,1)S(1)} %slice.19), channel_id=1, source_target_pairs={{0,1},{2,0},{4,2},{6,4},{7,6},{5,7},{3,5},{1,3},{8,9},{10,8},{12,1... | collective-permute-start | bytes 196616 | tf_op jit(solution)/shard_map/ppermute | solution.py:127
  28.9 6.5 %collective-permute-start.15 = (bf16[64,512]{1,0:T(8,128)(2,1)S(1)}, bf16[64,512]{1,0:T(8,128)(2,1)S(1)}, u32[]{:S(2)}, u32[]{:S(2)}) collective-permute-start(bf16[64,512]{1,0:T(8,128)(2,1)S(1)} %slice.18), channel_id=1, source_target_pairs={{0,2},{2,4},{4,6},{6,7},{7,5},{5,3},{3,1},{1,0},{8,10},{10,12},{12... | collective-permute-start | bytes 196616 | tf_op jit(solution)/shard_map/ppermute | solution.py:127
  30.3 1.7 %copy-start.1 = (s32[128]{0:T(128)S(1)}, s32[128]{0:T(128)}, u32[]{:S(2)}) copy-start(s32[128]{0:T(128)} %pos_ref.5) | copy-start | bytes 1540
  32.0 0.9 %copy-start = (f32[2,64,320]{2,1,0:T(8,128)S(1)}, f32[2,64,320]{2,1,0:T(8,128)}, u32[]{:S(2)}) copy-start(f32[2,64,320]{2,1,0:T(8,128)} %shard_map.55.bias_ref) | copy-start | bytes 491524

commit v3 on v2

v3 whole, which is shorter than its diff:
```python
import functools
import math

import jax
import jax.numpy as jnp
from jax import lax
from jax.experimental import pallas as pl
from jax.experimental.pallas import tpu as pltpu
from jax.sharding import PartitionSpec as P

HEAD_SIZE = 128
QUERY_HEADS = 32
KEY_VALUE_HEADS = 4
GROUP = QUERY_HEADS // KEY_VALUE_HEADS
RUN = 64
TOK_DEV = 2 * RUN
QUERY_COLUMNS = QUERY_HEADS * HEAD_SIZE
KV_COLUMNS = KEY_VALUE_HEADS * HEAD_SIZE
TAG_ROWS = 16

masked_fill = -1e30


def first_run(pos):
    return jnp.min(pos.astype(jnp.float32)).astype(jnp.int32) // RUN


def run_numbers(runs, pos_ref, tagged_refs):
    firsts = [first_run(pos_ref[...])]
    for ref in tagged_refs:
        firsts.append(jnp.max(ref[TOK_DEV:, :HEAD_SIZE].astype(jnp.float32)).astype(jnp.int32))
    places = runs // 2
    firsts.append(places * (places - 1) // 2 - sum(firsts))
    return [(first, runs - 1 - first) for first in firsts]


def sort_runs(numbers, own_ref, own_column, block_refs, sorted_buf):
    for half, number in enumerate(numbers[0]):
        sorted_buf[number] = own_ref[half * RUN : (half + 1) * RUN, own_column : own_column + KV_COLUMNS]
    halves = [(ref, ref, RUN) for ref in block_refs[:-2]] + [(block_refs[-2], block_refs[-1], 0)]
    for (first, second), (first_ref, second_ref, at) in zip(numbers[1:], halves):
        sorted_buf[first] = first_ref[:RUN, :]
        sorted_buf[second] = second_ref[at : at + RUN, :]


def bias_kernel(runs, pos_ref, segment_ref, bias_ref):
    reach = runs // 4
    segment = segment_ref[...].astype(jnp.float32)
    first = first_run(pos_ref[...])
    for half, run in enumerate((first, runs - 1 - first)):
        row_pos = run * RUN + lax.broadcasted_iota(jnp.int32, (RUN, 1), 0)
        at = lax.broadcasted_iota(jnp.int32, (RUN, runs * RUN), 1) == row_pos
        row_doc = jnp.sum(jnp.where(at, segment, 0.0), axis=1, keepdims=True)
        doc_start = jnp.sum(jnp.where(segment < row_doc, 1.0, 0.0), axis=1, keepdims=True).astype(jnp.int32)
        key_pos = jnp.maximum(run - reach, 0) * RUN + lax.broadcasted_iota(jnp.int32, bias_ref.shape[1:], 1)
        bias_ref[half] = jnp.where((key_pos <= row_pos) & (key_pos >= doc_start), 0.0, masked_fill)


def weights_kernel(runs, pos_ref, bias_ref, own_ref, *refs):
    blocks = runs // 2
    key_refs, tagged_refs, (weights_ref, key_buf) = refs[:blocks], refs[blocks:-2], refs[-2:]
    reach = runs // 4
    span = (reach + 1) * RUN
    numbers = run_numbers(runs, pos_ref, tagged_refs)
    sort_runs(numbers, own_ref, QUERY_COLUMNS, key_refs, key_buf)
    scale = math.log2(math.e) / math.sqrt(HEAD_SIZE)
    for half in range(2):
        start = jnp.maximum(numbers[0][half] - reach, 0)
        bias = jnp.concatenate([bias_ref[half]] * GROUP, axis=0)
        for kv in range(KEY_VALUE_HEADS):
            query = jnp.concatenate(
                [
                    own_ref[half * RUN : (half + 1) * RUN, h * HEAD_SIZE : (h + 1) * HEAD_SIZE]
                    for h in range(kv * GROUP, (kv + 1) * GROUP)
                ],
                axis=0,
            )
            key = key_buf[pl.ds(start, reach + 1), :, kv * HEAD_SIZE : (kv + 1) * HEAD_SIZE]
            scores = bias + lax.dot_general(
                query,
                key.reshape(span, HEAD_SIZE),
                (((1,), (1,)), ((), ())),
                preferred_element_type=jnp.float32,
            )
            row_max = jnp.max(scores, axis=1, keepdims=True)
            weights_ref[half * KEY_VALUE_HEADS + kv] = jnp.exp2((scores - row_max) * scale).astype(jnp.bfloat16)


def values_kernel(runs, pos_ref, weights_ref, own_ref, *refs):
    value_refs, (out_ref, value_buf, result_buf, out_sems) = refs[:-4], refs[-4:]
    reach = runs // 4
    span = (reach + 1) * RUN
    numbers = run_numbers(runs, pos_ref, value_refs[:-2])
    sort_runs(numbers, own_ref, QUERY_COLUMNS + KV_COLUMNS, value_refs, value_buf)
    ones = jnp.ones((span, HEAD_SIZE), jnp.bfloat16)
    copies = []
    for half in range(2):
        start = jnp.maximum(numbers[0][half] - reach, 0)
        for kv in range(KEY_VALUE_HEADS):
            value = value_buf[pl.ds(start, reach + 1), :, kv * HEAD_SIZE : (kv + 1) * HEAD_SIZE]
            summed = jnp.dot(
                weights_ref[half * KEY_VALUE_HEADS + kv],
                jnp.concatenate([value.reshape(span, HEAD_SIZE), ones], axis=1),
                preferred_element_type=jnp.float32,
            )
            result = (summed[:, :HEAD_SIZE] / summed[:, HEAD_SIZE:]).astype(jnp.bfloat16)
            for i in range(GROUP):
                h = kv * GROUP + i
                result_buf[half, :, h * HEAD_SIZE : (h + 1) * HEAD_SIZE] = result[i * RUN : (i + 1) * RUN]
        copies.append(
            pltpu.make_async_copy(result_buf.at[half], out_ref.at[pl.ds(half * RUN, RUN), :], out_sems.at[half])
        )
        copies[-1].start()
    for copy in copies:
        copy.wait()


def per_device(queries, keys, values, token_pos, segment):
    sections, places = lax.axis_size("section"), lax.axis_size("ctx")
    runs = segment.shape[0] // RUN
    depth = places // 2
    ring = [z * 2 for z in range(depth)] + [z * 2 + 1 for z in reversed(range(depth))]

    def shift(block, section_by, ring_by):
        pairs = []
        for s in range(sections):
            for i in range(places):
                target = (s + section_by) % sections * places + ring[(i + ring_by) % places]
                pairs.append((s * places + ring[i], target))
        return lax.ppermute(block, ("section", "ctx"), pairs)

    own = jnp.concatenate([queries[0], keys[0], values[0]], axis=1)

    def around(block, early=None):
        ahead, back = shift(block, 1, 1), shift(block, 1, -1)
        held = [ahead, back]
        if early is not None:
            ahead, early = lax.optimization_barrier((ahead, early))
        for _ in range(2, places // 2):
            ahead, back = shift(ahead, 0, 1), shift(back, 0, -1)
            held.extend([ahead, back])
        return held + [shift(ahead[:RUN], 0, 1), shift(back[RUN:TOK_DEV], 0, -1)], early

    first = jnp.broadcast_to((token_pos[:TOK_DEV] >> (RUN.bit_length() - 1))[:1], (KV_COLUMNS,))
    tag = jnp.broadcast_to(first.astype(jnp.bfloat16)[None], (TAG_ROWS, KV_COLUMNS))
    all_keys, own = around(keys[0], own)
    all_values, _ = around(jnp.concatenate([values[0], tag], axis=0))
    own = shift(own, 1, 0)
    late_segment, _, _ = lax.optimization_barrier((segment, all_keys[-2:], all_values[:2]))

    pos = token_pos.reshape(1, -1)
    vmem = pl.BlockSpec(memory_space=pltpu.VMEM)
    params = pltpu.CompilerParams(vmem_limit_bytes=40 * 1024 * 1024)
    sorted_buf = pltpu.VMEM((runs, RUN, KV_COLUMNS), jnp.bfloat16)
    bias = pl.pallas_call(
        functools.partial(bias_kernel, runs),
        out_shape=jax.ShapeDtypeStruct((2, RUN, (runs // 4 + 1) * RUN), jnp.float32),
        in_specs=[vmem] * 2,
        out_specs=vmem,
        cost_estimate=pl.CostEstimate(flops=10 << 30, bytes_accessed=0, transcendentals=0),
    )(pos, late_segment.reshape(1, -1))
    weights = pl.pallas_call(
        functools.partial(weights_kernel, runs),
        out_shape=jax.ShapeDtypeStruct((2 * KEY_VALUE_HEADS, GROUP * RUN, (runs // 4 + 1) * RUN), jnp.bfloat16),
        in_specs=[vmem] * (3 + len(all_keys) + len(all_values[:-2])),
        out_specs=vmem,
        scratch_shapes=[sorted_buf],
        compiler_params=params,
        cost_estimate=pl.CostEstimate(flops=1 << 26, bytes_accessed=1 << 20, transcendentals=0),
    )(pos, bias, own, *all_keys, *all_values[:-2])
    out = pl.pallas_call(
        functools.partial(values_kernel, runs),
        out_shape=jax.ShapeDtypeStruct((TOK_DEV, QUERY_COLUMNS), jnp.bfloat16),
        in_specs=[vmem] * (3 + len(all_values)),
        out_specs=pl.BlockSpec(memory_space=pl.ANY),
        scratch_shapes=[
            sorted_buf,
            pltpu.VMEM((2, RUN, QUERY_COLUMNS), jnp.bfloat16),
            pltpu.SemaphoreType.DMA((2,)),
        ],
        compiler_params=params,
        cost_estimate=pl.CostEstimate(flops=1 << 26, bytes_accessed=1 << 20, transcendentals=0),
    )(pos, weights, own, *all_values)
    return out[None]


def solution(mesh):
    return jax.shard_map(
        per_device,
        mesh=mesh,
        in_specs=(
            P("section", "ctx", None),
            P("section", "ctx", None),
            P("section", "ctx", None),
            P("ctx"),
            P(),
        ),
        out_specs=P("section", "ctx", None),
        check_vma=False,
    )
```

time: 38.5 us -> 35.3 us (0.917)
  waiting for transfers between devices: 7.47 us -> 4.62 us
  Pallas kernels: 7.08 us -> 5.89 us
  local copies, waits for them, and re-layouts: 0.96 us -> 1.9 us
  other arithmetic: 4.14 us -> 3.23 us
  starting transfers between devices: 18.6 us -> 19.3 us
    ppermute x17, waiting for transfers between devices: 7.47 us -> 4.62 us  [shift(): return lax.ppermute(block, ('section', 'ctx'), pairs)]
    concatenate x0 -> x1, local copies, waits for them, and re-layouts: none -> 0.95 us  [per_device(): all_values, _ = around(jnp.concatenate([values[0], tag], axis=0))]
    concatenate x2 -> x1, other arithmetic: 3.48 us -> 2.57 us  [per_device(): own = jnp.concatenate([queries[0], keys[0], values[0]], axis=1)]
    ppermute x17, starting transfers between devices: 18.6 us -> 19.3 us  [shift(): return lax.ppermute(block, ('section', 'ctx'), pairs)]
    pallas_call x1, Pallas kernels: 2.98 us -> 2.27 us  [per_device(): pl.pallas_call(functools.partial(values_kernel, runs), out_shape=jax.Shap...]
    another operation x0 -> x1, other arithmetic: none -> 0.66 us
    convert_element_type x1 -> x0, other arithmetic: 0.66 us -> none  [per_device(): (token_pos >> RUN.bit_length() - 1).astype(jnp.bfloat16)[None]]
    pallas_call x1, Pallas kernels: 2.4 us -> 1.86 us  [per_device(): pl.pallas_call(functools.partial(weights_kernel, runs), out_shape=jax.Sha...]
  transfers between devices with their start and end apart: 17 -> 17, of which waited for: 6 -> 6; matrix products, arithmetic and copies ran while one was open for 7% -> 12% of each run, Pallas kernels for 11% -> 10%
where the time goes in v3:
time: 35.3 us; the launch traced here: 35.1 us
  starting transfers between devices  19.3 us (55%)
  Pallas kernels  5.89 us (17%)
  waiting for transfers between devices  4.62 us (13%)
  other arithmetic  3.23 us (9%)
  local copies, waits for them, and re-layouts  1.9 us (5%)
    ppermute x17, starting transfers between devices, shift(): return lax.ppermute(block, ('section', 'ctx'), pairs)  19.3 us
    ppermute x17, waiting for transfers between devices, shift(): return lax.ppermute(block, ('section', 'ctx'), pairs)  4.62 us
    concatenate x1, other arithmetic, per_device(): own = jnp.concatenate([queries[0], keys[0], values[0]], axis=1)  2.57 us
    pallas_call x1, Pallas kernels, per_device(): pl.pallas_call(functools.partial(values_kernel, runs), out_shape=jax.Shap...  2.27 us
    pallas_call x1, Pallas kernels, per_device(): pl.pallas_call(functools.partial(weights_kernel, runs), out_shape=jax.Sha...  1.86 us
    pallas_call x1, Pallas kernels, per_device(): pl.pallas_call(functools.partial(bias_kernel, runs), out_shape=jax.ShapeD...  1.75 us
    concatenate x1, local copies, waits for them, and re-layouts, per_device(): all_values, _ = around(jnp.concatenate([values[0], tag], axis=0))  0.95 us
    unnamed x4, local copies, waits for them, and re-layouts  0.93 us
  transfers between devices with their start and end apart: 17, of which 6 were waited for; matrix products, arithmetic and copies ran while one was open for 12% of the time, Pallas kernels for 10%

profile of v3, /device:TPU:0, one launch (start us, length us, event | category | flops | bytes accessed | tf_op | source)
XLA Modules:
  0.0 35.1 jit_solution(6860300058426600779)
XLA Ops:
  0.0 2.5 %collective-permute-start = (bf16[128,512]{1,0:T(8,128)(2,1)}, bf16[128,512]{1,0:T(8,128)(2,1)S(1)}, u32[]{:S(2)}, u32[]{:S(2)}) collective-permute-start(bf16[128,512]{1,0:T(8,128)(2,1)} %bitcast.14), channel_id=1, source_target_pairs={{0,10},{2,12},{4,14},{6,15},{7,13},{5,11},{3,9},{1,8},{8,18},{10,2... | collective-permute-start | bytes 393224 | tf_op jit(solution)/shard_map/ppermute | solution.py:130
  2.5 1.7 %collective-permute-start.4 = (bf16[128,512]{1,0:T(8,128)(2,1)}, bf16[128,512]{1,0:T(8,128)(2,1)S(1)}, u32[]{:S(2)}, u32[]{:S(2)}) collective-permute-start(bf16[128,512]{1,0:T(8,128)(2,1)} %bitcast.15), channel_id=1, source_target_pairs={{0,9},{2,8},{4,10},{6,12},{7,14},{5,15},{3,13},{1,11},{8,17},{10,1... | collective-permute-start | bytes 393224 | tf_op jit(solution)/shard_map/ppermute | solution.py:130
  4.1 0.7 %shift-right-arithmetic_convert_fusion = bf16[128]{0:T(256)(128)(2,1)S(1)} fusion(s32[128]{0:T(128)} %param.8), kind=kLoop, calls=%fused_computation.1 | loop fusion | flops 256 | bytes 768 | tf_op jit(solution)/shard_map/convert
  4.8 1.0 %concatenate.7 = bf16[144,512]{1,0:T(8,128)(2,1)S(1)} pad(bf16[128,512]{1,0:T(8,128)(2,1)} %bitcast.12, bf16[]{:T(256)S(1)} %bitcast.17), padding=0_16x0_0 | pad | bytes 278530 | tf_op jit(solution)/shard_map/concatenate | solution.py:147
  5.7 1.2 %collective-permute-start.8 = (bf16[144,512]{1,0:T(8,128)(2,1)S(1)}, bf16[144,512]{1,0:T(8,128)(2,1)S(1)}, u32[]{:S(2)}, u32[]{:S(2)}) collective-permute-start(bf16[144,512]{1,0:T(8,128)(2,1)S(1)} %concatenate.7), channel_id=1, source_target_pairs={{0,10},{2,12},{4,14},{6,15},{7,13},{5,11},{3,9},{1,8},{8,18},{10,2... | collective-permute-start | bytes 442376 | tf_op jit(solution)/shard_map/ppermute | solution.py:130
  6.9 0.0 collective-permute-start.9
  6.9 2.6 %pad_maximum_fusion = bf16[128,5120]{1,0:T(8,128)(2,1)} fusion(bf16[128,512]{1,0:T(8,128)(2,1)} %bitcast.13, bf16[128,512]{1,0:T(8,128)(2,1)} %bitcast.16, bf16[128,4096]{1,0:T(8,128)(2,1)} %bitcast.11), kind=kLoop, calls=%fused_computation | loop fusion | flops 3932160 | bytes 2621440 | tf_op jit(solution)/shard_map/concatenate | solution.py:132
  9.5 0.0 collective-permute-done.refs_0_
  9.5 2.2 %collective-permute-start.1 = (bf16[128,512]{1,0:T(8,128)(2,1)S(1)}, bf16[128,512]{1,0:T(8,128)(2,1)S(1)}, u32[]{:S(2)}, u32[]{:S(2)}) collective-permute-start(bf16[128,512]{1,0:T(8,128)(2,1)S(1)} %collective-permute-done.refs_0_), channel_id=1, source_target_pairs={{0,2},{2,4},{4,6},{6,7},{7,5},{5,3},{3,1},{1,0},{8,10},{10,12},{12... | collective-permute-start | bytes 393224 | tf_op jit(solution)/shard_map/ppermute | solution.py:130
  11.7 0.0 collective-permute-done.4.refs_1_
  11.7 0.0 collective-permute-start.5
  11.7 0.0 collective-permute-start.10
  11.7 0.2 collective-permute-done.8.refs_8_.refs_0_
  11.9 2.4 %collective-permute-start.11 = (bf16[144,512]{1,0:T(8,128)(2,1)S(1)}, bf16[144,512]{1,0:T(8,128)(2,1)S(1)}, u32[]{:S(2)}, u32[]{:S(2)}) collective-permute-start(bf16[144,512]{1,0:T(8,128)(2,1)S(1)} %collective-permute-done.8.refs_8_.refs_0_), channel_id=1, source_target_pairs={{0,2},{2,4},{4,6},{6,7},{7,5},{5,3},{3,1},{1,0},{8,10},{10,12},{12... | collective-permute-start | bytes 442376 | tf_op jit(solution)/shard_map/ppermute | solution.py:130
  14.3 0.0 collective-permute-done.9.refs_9_.refs_1_
  14.4 0.0 collective-permute-start.12
  14.4 1.1 %collective-permute-done.1.refs_2_ = bf16[128,512]{1,0:T(8,128)(2,1)S(1)} collective-permute-done((bf16[128,512]{1,0:T(8,128)(2,1)S(1)}, bf16[128,512]{1,0:T(8,128)(2,1)S(1)}, u32[]{:S(2)}, u32[]{:S(2)}) %collective-permute-start.1) | collective-permute-done | bytes 131104 | tf_op jit(solution)/shard_map/ppermute | solution.py:130
  15.4 1.6 %collective-permute-start.2 = (bf16[128,512]{1,0:T(8,128)(2,1)S(1)}, bf16[128,512]{1,0:T(8,128)(2,1)S(1)}, u32[]{:S(2)}, u32[]{:S(2)}) collective-permute-start(bf16[128,512]{1,0:T(8,128)(2,1)S(1)} %collective-permute-done.1.refs_2_), channel_id=1, source_target_pairs={{0,2},{2,4},{4,6},{6,7},{7,5},{5,3},{3,1},{1,0},{8,10},{10,12},{12... | collective-permute-start | bytes 393224 | tf_op jit(solution)/shard_map/ppermute | solution.py:130
  17.0 0.0 collective-permute-done.5.refs_3_
  17.0 0.5 %collective-permute-start.6 = (bf16[128,512]{1,0:T(8,128)(2,1)S(1)}, bf16[128,512]{1,0:T(8,128)(2,1)S(1)}, u32[]{:S(2)}, u32[]{:S(2)}) collective-permute-start(bf16[128,512]{1,0:T(8,128)(2,1)S(1)} %collective-permute-done.5.refs_3_), channel_id=1, source_target_pairs={{0,1},{2,0},{4,2},{6,4},{7,6},{5,7},{3,5},{1,3},{8,9},{10,8},{12,1... | collective-permute-start | bytes 393224 | tf_op jit(solution)/shard_map/ppermute | solution.py:130
  17.5 1.1 %collective-permute-done.11.refs_10_.refs_2_ = bf16[144,512]{1,0:T(8,128)(2,1)S(1)} collective-permute-done((bf16[144,512]{1,0:T(8,128)(2,1)S(1)}, bf16[144,512]{1,0:T(8,128)(2,1)S(1)}, u32[]{:S(2)}, u32[]{:S(2)}) %collective-permute-start.11) | collective-permute-done | bytes 147488 | tf_op jit(solution)/shard_map/ppermute | solution.py:130
  18.6 2.5 %collective-permute-start.13 = (bf16[144,512]{1,0:T(8,128)(2,1)S(1)}, bf16[144,512]{1,0:T(8,128)(2,1)S(1)}, u32[]{:S(2)}, u32[]{:S(2)}) collective-permute-start(bf16[144,512]{1,0:T(8,128)(2,1)S(1)} %collective-permute-done.11.refs_10_.refs_2_), channel_id=1, source_target_pairs={{0,2},{2,4},{4,6},{6,7},{7,5},{5,3},{3,1},{1,0},{8,10},{10,12},{12... | collective-permute-start | bytes 442376 | tf_op jit(solution)/shard_map/ppermute | solution.py:130
  21.1 0.0 collective-permute-done.12.refs_11_.refs_3_
  21.1 0.0 collective-permute-start.14
  21.1 0.4 %collective-permute-done.2.refs_4_ = bf16[128,512]{1,0:T(8,128)(2,1)S(1)} collective-permute-done((bf16[128,512]{1,0:T(8,128)(2,1)S(1)}, bf16[128,512]{1,0:T(8,128)(2,1)S(1)}, u32[]{:S(2)}, u32[]{:S(2)}) %collective-permute-start.2) | collective-permute-done | bytes 131104 | tf_op jit(solution)/shard_map/ppermute | solution.py:130
  21.5 2.4 %collective-permute-start.3 = (bf16[64,512]{1,0:T(8,128)(2,1)S(1)}, bf16[64,512]{1,0:T(8,128)(2,1)S(1)}, u32[]{:S(2)}, u32[]{:S(2)}) collective-permute-start(bf16[64,512]{1,0:T(8,128)(2,1)S(1)} %slice.21), channel_id=1, source_target_pairs={{0,2},{2,4},{4,6},{6,7},{7,5},{5,3},{3,1},{1,0},{8,10},{10,12},{12... | collective-permute-start | bytes 196616 | tf_op jit(solution)/shard_map/ppermute | solution.py:130
  23.9 0.0 collective-permute-done.6.refs_5_
  23.9 0.1 collective-permute-start.7
  24.0 1.1 %collective-permute-done.13.refs_12_.refs_4_ = bf16[144,512]{1,0:T(8,128)(2,1)S(1)} collective-permute-done((bf16[144,512]{1,0:T(8,128)(2,1)S(1)}, bf16[144,512]{1,0:T(8,128)(2,1)S(1)}, u32[]{:S(2)}, u32[]{:S(2)}) %collective-permute-start.13) | collective-permute-done | bytes 147488 | tf_op jit(solution)/shard_map/ppermute | solution.py:130
  25.1 2.4 %collective-permute-start.15 = (bf16[64,512]{1,0:T(8,128)(2,1)S(1)}, bf16[64,512]{1,0:T(8,128)(2,1)S(1)}, u32[]{:S(2)}, u32[]{:S(2)}) collective-permute-start(bf16[64,512]{1,0:T(8,128)(2,1)S(1)} %slice.23), channel_id=1, source_target_pairs={{0,2},{2,4},{4,6},{6,7},{7,5},{5,3},{3,1},{1,0},{8,10},{10,12},{12... | collective-permute-start | bytes 196616 | tf_op jit(solution)/shard_map/ppermute | solution.py:130
  27.4 0.0 collective-permute-done.14.refs_13_.refs_5_
  27.4 0.1 collective-permute-start.16
  27.5 0.0 collective-permute-done.3.refs_6_
  27.5 0.7 %collective-permute-done.7.refs_7_ = bf16[64,512]{1,0:T(8,128)(2,1)S(1)} collective-permute-done((bf16[64,512]{1,0:T(8,128)(2,1)S(1)}, bf16[64,512]{1,0:T(8,128)(2,1)S(1)}, u32[]{:S(2)}, u32[]{:S(2)}) %collective-permute-start.7) | collective-permute-done | bytes 65568 | tf_op jit(solution)/shard_map/ppermute | solution.py:130
  28.2 0.0 copy-start.1
  28.2 1.7 %shard_map.55.bias_ref = f32[2,64,320]{2,1,0:T(8,128)} custom-call(s32[1,128]{1,0:T(1,128)} %bitcast.8, s32[1,1024]{1,0:T(1,128)} %bitcast.18), custom_call_target="tpu_custom_call" | custom-call | flops 10737418240 | tf_op jit(solution)/shard_map/pallas_call | solution.py:155
  30.0 0.0 collective-permute-done.10.own_ref
  30.0 0.0 copy-done.1
  30.0 0.0 copy-start
  30.0 0.9 %copy-done = f32[2,64,320]{2,1,0:T(8,128)S(1)} copy-done((f32[2,64,320]{2,1,0:T(8,128)S(1)}, f32[2,64,320]{2,1,0:T(8,128)}, u32[]{:S(2)}) %copy-start) | copy-done | bytes 163864
  30.9 1.9 %shard_map.56.weights_ref = bf16[8,512,320]{2,1,0:T(8,128)(2,1)S(1)} custom-call(s32[1,128]{1,0:T(1,128)S(1)} %bitcast.9, f32[2,64,320]{2,1,0:T(8,128)S(1)} %copy-done, bf16[128,5120]{1,0:T(8,128)(2,1)S(1)} %collective-permute-done.10.own_ref, bf16[128,512]{1,0:T(8,128)(2,1)S(1)} %collective-permute-done.refs_0_, ...), custom_call_target="tpu_custom_call" | custom-call | flops 67108864 | bytes 1048576 | tf_op jit(solution)/shard_map/pallas_call | solution.py:162
  32.8 0.0 collective-permute-done.15.refs_6_
  32.8 0.0 collective-permute-done.16.refs_7_
  32.8 2.3 %shard_map.57 = bf16[128,4096]{1,0:T(8,128)(2,1)} custom-call(s32[1,128]{1,0:T(1,128)S(1)} %bitcast.10, bf16[8,512,320]{2,1,0:T(8,128)(2,1)S(1)} %shard_map.56.weights_ref, bf16[128,5120]{1,0:T(8,128)(2,1)S(1)} %collective-permute-done.10.own_ref, bf16[144,512]{1,0:T(8,128)(2,1)S(1)} %collective-permute-done.8.refs_8_.refs_0_, ...), custom_call_target="tpu_custom_call" | custom-call | flops 67108864 | bytes 1048576 | tf_op jit(solution)/shard_map/pallas_call | solution.py:171
  (4 shorter events, 0.0 us)
Async XLA Ops:
  0.0 9.5 %collective-permute-start = (bf16[128,512]{1,0:T(8,128)(2,1)}, bf16[128,512]{1,0:T(8,128)(2,1)S(1)}, u32[]{:S(2)}, u32[]{:S(2)}) collective-permute-start(bf16[128,512]{1,0:T(8,128)(2,1)} %bitcast.14), channel_id=1, source_target_pairs={{0,10},{2,12},{4,14},{6,15},{7,13},{5,11},{3,9},{1,8},{8,18},{10,2... | collective-permute-start | bytes 393224 | tf_op jit(solution)/shard_map/ppermute | solution.py:130
  2.5 9.2 %collective-permute-start.4 = (bf16[128,512]{1,0:T(8,128)(2,1)}, bf16[128,512]{1,0:T(8,128)(2,1)S(1)}, u32[]{:S(2)}, u32[]{:S(2)}) collective-permute-start(bf16[128,512]{1,0:T(8,128)(2,1)} %bitcast.15), channel_id=1, source_target_pairs={{0,9},{2,8},{4,10},{6,12},{7,14},{5,15},{3,13},{1,11},{8,17},{10,1... | collective-permute-start | bytes 393224 | tf_op jit(solution)/shard_map/ppermute | solution.py:130
  5.7 6.2 %collective-permute-start.8 = (bf16[144,512]{1,0:T(8,128)(2,1)S(1)}, bf16[144,512]{1,0:T(8,128)(2,1)S(1)}, u32[]{:S(2)}, u32[]{:S(2)}) collective-permute-start(bf16[144,512]{1,0:T(8,128)(2,1)S(1)} %concatenate.7), channel_id=1, source_target_pairs={{0,10},{2,12},{4,14},{6,15},{7,13},{5,11},{3,9},{1,8},{8,18},{10,2... | collective-permute-start | bytes 442376 | tf_op jit(solution)/shard_map/ppermute | solution.py:130
  6.9 7.4 %collective-permute-start.9 = (bf16[144,512]{1,0:T(8,128)(2,1)S(1)}, bf16[144,512]{1,0:T(8,128)(2,1)S(1)}, u32[]{:S(2)}, u32[]{:S(2)}) collective-permute-start(bf16[144,512]{1,0:T(8,128)(2,1)S(1)} %concatenate.7), channel_id=1, source_target_pairs={{0,9},{2,8},{4,10},{6,12},{7,14},{5,15},{3,13},{1,11},{8,17},{10,1... | collective-permute-start | bytes 442376 | tf_op jit(solution)/shard_map/ppermute | solution.py:130
  9.5 5.9 %collective-permute-start.1 = (bf16[128,512]{1,0:T(8,128)(2,1)S(1)}, bf16[128,512]{1,0:T(8,128)(2,1)S(1)}, u32[]{:S(2)}, u32[]{:S(2)}) collective-permute-start(bf16[128,512]{1,0:T(8,128)(2,1)S(1)} %collective-permute-done.refs_0_), channel_id=1, source_target_pairs={{0,2},{2,4},{4,6},{6,7},{7,5},{5,3},{3,1},{1,0},{8,10},{10,12},{12... | collective-permute-start | bytes 393224 | tf_op jit(solution)/shard_map/ppermute | solution.py:130
  11.7 5.4 %collective-permute-start.5 = (bf16[128,512]{1,0:T(8,128)(2,1)S(1)}, bf16[128,512]{1,0:T(8,128)(2,1)S(1)}, u32[]{:S(2)}, u32[]{:S(2)}) collective-permute-start(bf16[128,512]{1,0:T(8,128)(2,1)S(1)} %collective-permute-done.4.refs_1_), channel_id=1, source_target_pairs={{0,1},{2,0},{4,2},{6,4},{7,6},{5,7},{3,5},{1,3},{8,9},{10,8},{12,1... | collective-permute-start | bytes 393224 | tf_op jit(solution)/shard_map/ppermute | solution.py:130
  11.7 18.3 %collective-permute-start.10 = (bf16[128,5120]{1,0:T(8,128)(2,1)}, bf16[128,5120]{1,0:T(8,128)(2,1)S(1)}, u32[]{:S(2)}, u32[]{:S(2)}) collective-permute-start(bf16[128,5120]{1,0:T(8,128)(2,1)} %pad_maximum_fusion), channel_id=1, source_target_pairs={{0,8},{2,10},{4,12},{6,14},{7,15},{5,13},{3,11},{1,9},{8,16},{10,1... | collective-permute-start | bytes 3932168 | tf_op jit(solution)/shard_map/ppermute | solution.py:130
  11.9 6.7 %collective-permute-start.11 = (bf16[144,512]{1,0:T(8,128)(2,1)S(1)}, bf16[144,512]{1,0:T(8,128)(2,1)S(1)}, u32[]{:S(2)}, u32[]{:S(2)}) collective-permute-start(bf16[144,512]{1,0:T(8,128)(2,1)S(1)} %collective-permute-done.8.refs_8_.refs_0_), channel_id=1, source_target_pairs={{0,2},{2,4},{4,6},{6,7},{7,5},{5,3},{3,1},{1,0},{8,10},{10,12},{12... | collective-permute-start | bytes 442376 | tf_op jit(solution)/shard_map/ppermute | solution.py:130
  14.4 6.7 %collective-permute-start.12 = (bf16[144,512]{1,0:T(8,128)(2,1)S(1)}, bf16[144,512]{1,0:T(8,128)(2,1)S(1)}, u32[]{:S(2)}, u32[]{:S(2)}) collective-permute-start(bf16[144,512]{1,0:T(8,128)(2,1)S(1)} %collective-permute-done.9.refs_9_.refs_1_), channel_id=1, source_target_pairs={{0,1},{2,0},{4,2},{6,4},{7,6},{5,7},{3,5},{1,3},{8,9},{10,8},{12,1... | collective-permute-start | bytes 442376 | tf_op jit(solution)/shard_map/ppermute | solution.py:130
  15.4 6.0 %collective-permute-start.2 = (bf16[128,512]{1,0:T(8,128)(2,1)S(1)}, bf16[128,512]{1,0:T(8,128)(2,1)S(1)}, u32[]{:S(2)}, u32[]{:S(2)}) collective-permute-start(bf16[128,512]{1,0:T(8,128)(2,1)S(1)} %collective-permute-done.1.refs_2_), channel_id=1, source_target_pairs={{0,2},{2,4},{4,6},{6,7},{7,5},{5,3},{3,1},{1,0},{8,10},{10,12},{12... | collective-permute-start | bytes 393224 | tf_op jit(solution)/shard_map/ppermute | solution.py:130
  17.0 6.9 %collective-permute-start.6 = (bf16[128,512]{1,0:T(8,128)(2,1)S(1)}, bf16[128,512]{1,0:T(8,128)(2,1)S(1)}, u32[]{:S(2)}, u32[]{:S(2)}) collective-permute-start(bf16[128,512]{1,0:T(8,128)(2,1)S(1)} %collective-permute-done.5.refs_3_), channel_id=1, source_target_pairs={{0,1},{2,0},{4,2},{6,4},{7,6},{5,7},{3,5},{1,3},{8,9},{10,8},{12,1... | collective-permute-start | bytes 393224 | tf_op jit(solution)/shard_map/ppermute | solution.py:130
  18.6 6.5 %collective-permute-start.13 = (bf16[144,512]{1,0:T(8,128)(2,1)S(1)}, bf16[144,512]{1,0:T(8,128)(2,1)S(1)}, u32[]{:S(2)}, u32[]{:S(2)}) collective-permute-start(bf16[144,512]{1,0:T(8,128)(2,1)S(1)} %collective-permute-done.11.refs_10_.refs_2_), channel_id=1, source_target_pairs={{0,2},{2,4},{4,6},{6,7},{7,5},{5,3},{3,1},{1,0},{8,10},{10,12},{12... | collective-permute-start | bytes 442376 | tf_op jit(solution)/shard_map/ppermute | solution.py:130
  21.1 6.4 %collective-permute-start.14 = (bf16[144,512]{1,0:T(8,128)(2,1)S(1)}, bf16[144,512]{1,0:T(8,128)(2,1)S(1)}, u32[]{:S(2)}, u32[]{:S(2)}) collective-permute-start(bf16[144,512]{1,0:T(8,128)(2,1)S(1)} %collective-permute-done.12.refs_11_.refs_3_), channel_id=1, source_target_pairs={{0,1},{2,0},{4,2},{6,4},{7,6},{5,7},{3,5},{1,3},{8,9},{10,8},{12,1... | collective-permute-start | bytes 442376 | tf_op jit(solution)/shard_map/ppermute | solution.py:130
  21.5 6.1 %collective-permute-start.3 = (bf16[64,512]{1,0:T(8,128)(2,1)S(1)}, bf16[64,512]{1,0:T(8,128)(2,1)S(1)}, u32[]{:S(2)}, u32[]{:S(2)}) collective-permute-start(bf16[64,512]{1,0:T(8,128)(2,1)S(1)} %slice.21), channel_id=1, source_target_pairs={{0,2},{2,4},{4,6},{6,7},{7,5},{5,3},{3,1},{1,0},{8,10},{10,12},{12... | collective-permute-start | bytes 196616 | tf_op jit(solution)/shard_map/ppermute | solution.py:130
  23.9 4.3 %collective-permute-start.7 = (bf16[64,512]{1,0:T(8,128)(2,1)S(1)}, bf16[64,512]{1,0:T(8,128)(2,1)S(1)}, u32[]{:S(2)}, u32[]{:S(2)}) collective-permute-start(bf16[64,512]{1,0:T(8,128)(2,1)S(1)} %slice.22), channel_id=1, source_target_pairs={{0,1},{2,0},{4,2},{6,4},{7,6},{5,7},{3,5},{1,3},{8,9},{10,8},{12,1... | collective-permute-start | bytes 196616 | tf_op jit(solution)/shard_map/ppermute | solution.py:130
  25.1 7.7 %collective-permute-start.15 = (bf16[64,512]{1,0:T(8,128)(2,1)S(1)}, bf16[64,512]{1,0:T(8,128)(2,1)S(1)}, u32[]{:S(2)}, u32[]{:S(2)}) collective-permute-start(bf16[64,512]{1,0:T(8,128)(2,1)S(1)} %slice.23), channel_id=1, source_target_pairs={{0,2},{2,4},{4,6},{6,7},{7,5},{5,3},{3,1},{1,0},{8,10},{10,12},{12... | collective-permute-start | bytes 196616 | tf_op jit(solution)/shard_map/ppermute | solution.py:130
  27.4 5.3 %collective-permute-start.16 = (bf16[64,512]{1,0:T(8,128)(2,1)S(1)}, bf16[64,512]{1,0:T(8,128)(2,1)S(1)}, u32[]{:S(2)}, u32[]{:S(2)}) collective-permute-start(bf16[64,512]{1,0:T(8,128)(2,1)S(1)} %slice.24), channel_id=1, source_target_pairs={{0,1},{2,0},{4,2},{6,4},{7,6},{5,7},{3,5},{1,3},{8,9},{10,8},{12,1... | collective-permute-start | bytes 196616 | tf_op jit(solution)/shard_map/ppermute | solution.py:130
  28.2 1.8 %copy-start.1 = (s32[128]{0:T(128)S(1)}, s32[128]{0:T(128)}, u32[]{:S(2)}) copy-start(s32[128]{0:T(128)} %param.8) | copy-start | bytes 1540
  30.0 0.9 %copy-start = (f32[2,64,320]{2,1,0:T(8,128)S(1)}, f32[2,64,320]{2,1,0:T(8,128)}, u32[]{:S(2)}) copy-start(f32[2,64,320]{2,1,0:T(8,128)} %shard_map.55.bias_ref) | copy-start | bytes 491524

commit v4 on v3

--- a/solution.py
+++ b/solution.py
@@ -21,12 +21,12 @@
 masked_fill = -1e30
 
 
-def first_run(pos):
-    return jnp.min(pos.astype(jnp.float32)).astype(jnp.int32) // RUN
+def first_run(pos_ref):
+    return lax.div(jnp.min(pos_ref[:, :TOK_DEV]).astype(jnp.int32), RUN)
 
 
 def run_numbers(runs, pos_ref, tagged_refs):
-    firsts = [first_run(pos_ref[...])]
+    firsts = [first_run(pos_ref)]
     for ref in tagged_refs:
         firsts.append(jnp.max(ref[TOK_DEV:, :HEAD_SIZE].astype(jnp.float32)).astype(jnp.int32))
     places = runs // 2
@@ -43,10 +43,11 @@
         sorted_buf[second] = second_ref[at : at + RUN, :]
 
 
-def bias_kernel(runs, pos_ref, segment_ref, bias_ref):
+def bias_kernel(runs, pos_ref, *refs):
+    bias_ref = refs[-1]
     reach = runs // 4
-    segment = segment_ref[...].astype(jnp.float32)
-    first = first_run(pos_ref[...])
+    segment = pos_ref[:, TOK_DEV:]
+    first = first_run(pos_ref)
     for half, run in enumerate((first, runs - 1 - first)):
         row_pos = run * RUN + lax.broadcasted_iota(jnp.int32, (RUN, 1), 0)
         at = lax.broadcasted_iota(jnp.int32, (RUN, runs * RUN), 1) == row_pos
@@ -141,24 +142,23 @@
             held.extend([ahead, back])
         return held + [shift(ahead[:RUN], 0, 1), shift(back[RUN:TOK_DEV], 0, -1)], early
 
-    first = jnp.broadcast_to((token_pos[:TOK_DEV] >> (RUN.bit_length() - 1))[:1], (KV_COLUMNS,))
-    tag = jnp.broadcast_to(first.astype(jnp.bfloat16)[None], (TAG_ROWS, KV_COLUMNS))
+    pos = lax.optimization_barrier(jnp.concatenate([token_pos, segment]).astype(jnp.float32)[None])
+    tag = jnp.broadcast_to((pos[:, :1] / RUN).astype(jnp.bfloat16), (TAG_ROWS, KV_COLUMNS))
     all_keys, own = around(keys[0], own)
     all_values, _ = around(jnp.concatenate([values[0], tag], axis=0))
     own = shift(own, 1, 0)
-    late_segment, _, _ = lax.optimization_barrier((segment, all_keys[-2:], all_values[:2]))
-
-    pos = token_pos.reshape(1, -1)
     vmem = pl.BlockSpec(memory_space=pltpu.VMEM)
-    params = pltpu.CompilerParams(vmem_limit_bytes=40 * 1024 * 1024)
+    params = pltpu.CompilerParams(vmem_limit_bytes=(12 + runs // 4) * 1024 * 1024)
     sorted_buf = pltpu.VMEM((runs, RUN, KV_COLUMNS), jnp.bfloat16)
+    before_mask = all_keys[-2:]
     bias = pl.pallas_call(
         functools.partial(bias_kernel, runs),
         out_shape=jax.ShapeDtypeStruct((2, RUN, (runs // 4 + 1) * RUN), jnp.float32),
-        in_specs=[vmem] * 2,
+        in_specs=[vmem] * (1 + len(before_mask)),
         out_specs=vmem,
+        compiler_params=pltpu.CompilerParams(vmem_limit_bytes=8 * 1024 * 1024),
         cost_estimate=pl.CostEstimate(flops=10 << 30, bytes_accessed=0, transcendentals=0),
-    )(pos, late_segment.reshape(1, -1))
+    )(pos, *before_mask)
     weights = pl.pallas_call(
         functools.partial(weights_kernel, runs),
         out_shape=jax.ShapeDtypeStruct((2 * KEY_VALUE_HEADS, GROUP * RUN, (runs // 4 + 1) * RUN), jnp.bfloat16),

time: 35.3 us -> 34.7 us (0.983)
  waiting for transfers between devices: 4.62 us -> 6.67 us
  Pallas kernels: 5.89 us -> 4.49 us
  other arithmetic: 3.23 us -> 2.16 us
  between operations: 0.09 us -> 0.74 us
  local copies, waits for them, and re-layouts: 1.9 us -> 1.45 us
    ppermute x17, waiting for transfers between devices: 4.62 us -> 6.67 us  [shift(): return lax.ppermute(block, ('section', 'ctx'), pairs)]
    pallas_call x1, Pallas kernels: 1.75 us -> 0.34 us  [per_device(): pl.pallas_call(functools.partial(bias_kernel, runs), out_shape=jax.ShapeD...]
    concatenate x1, other arithmetic: 2.57 us -> 1.47 us  [per_device(): own = jnp.concatenate([queries[0], keys[0], values[0]], axis=1)]
    unnamed x4 -> x0, local copies, waits for them, and re-layouts: 0.93 us -> none
    convert_element_type x0 -> x1, other arithmetic: none -> 0.69 us  [per_device(): jnp.concatenate([token_pos, segment]).astype(jnp.float32)[None]]
    another operation x1 -> x0, other arithmetic: 0.66 us -> none
    slice x0 -> x1, local copies, waits for them, and re-layouts: none -> 0.51 us  [per_device(): pos[:, :1] / RUN]
  transfers between devices with their start and end apart: 17 -> 17, of which waited for: 6 -> 7; matrix products, arithmetic and copies ran while one was open for 12% -> 10% of each run, Pallas kernels for 10% -> 6%
where the time goes in v4:
time: 34.7 us; the launch traced here: 34.5 us
  starting transfers between devices  19 us (55%)
  waiting for transfers between devices  6.67 us (19%)
  Pallas kernels  4.49 us (13%)
  other arithmetic  2.16 us (6%)
  local copies, waits for them, and re-layouts  1.45 us (4%)
  between operations  0.74 us (2%)
    ppermute x17, starting transfers between devices, shift(): return lax.ppermute(block, ('section', 'ctx'), pairs)  19 us
    ppermute x17, waiting for transfers between devices, shift(): return lax.ppermute(block, ('section', 'ctx'), pairs)  6.67 us
    pallas_call x1, Pallas kernels, per_device(): pl.pallas_call(functools.partial(values_kernel, runs), out_shape=jax.Shap...  2.26 us
    pallas_call x1, Pallas kernels, per_device(): pl.pallas_call(functools.partial(weights_kernel, runs), out_shape=jax.Sha...  1.89 us
    concatenate x1, other arithmetic, per_device(): own = jnp.concatenate([queries[0], keys[0], values[0]], axis=1)  1.47 us
    concatenate x1, local copies, waits for them, and re-layouts, per_device(): all_values, _ = around(jnp.concatenate([values[0], tag], axis=0))  0.92 us
  transfers between devices with their start and end apart: 17, of which 7 were waited for; matrix products, arithmetic and copies ran while one was open for 10% of the time, Pallas kernels for 6%

profile of v4, /device:TPU:0, one launch (start us, length us, event | category | flops | bytes accessed | tf_op | source)
XLA Modules:
  0.0 34.5 jit_solution(13490726772778730128)
XLA Ops:
  0.0 2.5 %collective-permute-start = (bf16[128,512]{1,0:T(8,128)(2,1)}, bf16[128,512]{1,0:T(8,128)(2,1)S(1)}, u32[]{:S(2)}, u32[]{:S(2)}) collective-permute-start(bf16[128,512]{1,0:T(8,128)(2,1)} %bitcast.10), channel_id=1, source_target_pairs={{0,10},{2,12},{4,14},{6,15},{7,13},{5,11},{3,9},{1,8},{8,18},{10,2... | collective-permute-start | bytes 393224 | tf_op jit(solution)/shard_map/ppermute | solution.py:131
  2.5 1.7 %collective-permute-start.4 = (bf16[128,512]{1,0:T(8,128)(2,1)}, bf16[128,512]{1,0:T(8,128)(2,1)S(1)}, u32[]{:S(2)}, u32[]{:S(2)}) collective-permute-start(bf16[128,512]{1,0:T(8,128)(2,1)} %bitcast.11), channel_id=1, source_target_pairs={{0,9},{2,8},{4,10},{6,12},{7,14},{5,15},{3,13},{1,11},{8,17},{10,1... | collective-permute-start | bytes 393224 | tf_op jit(solution)/shard_map/ppermute | solution.py:131
  4.1 0.7 %add_convert_fusion.pos_ref = f32[1,1152]{1,0:T(1,128)S(1)} fusion(s32[1,1024]{1,0:T(1,128)} %bitcast.13, s32[1,128]{1,0:T(1,128)} %bitcast.14), kind=kLoop, calls=%fused_computation.1 | loop fusion | flops 2304 | bytes 9216 | tf_op jit(solution)/shard_map/convert_element_type | solution.py:145
  4.8 0.5 %slice.22 = f32[1,1]{1,0:T(1,128)} slice(f32[1,1152]{1,0:T(1,128)S(1)} %add_convert_fusion.pos_ref), slice={[0:1], [0:1]} | slice | bytes 8 | tf_op jit(solution)/shard_map/slice | solution.py:146
  6.0 0.9 %concatenate.24 = bf16[144,512]{1,0:T(8,128)(2,1)S(1)} pad(bf16[128,512]{1,0:T(8,128)(2,1)} %bitcast.8, bf16[]{:T(256)} %bitcast.5), padding=0_16x0_0 | pad | bytes 278530 | tf_op jit(solution)/shard_map/concatenate | solution.py:148
  6.9 1.2 %collective-permute-start.9 = (bf16[144,512]{1,0:T(8,128)(2,1)S(1)}, bf16[144,512]{1,0:T(8,128)(2,1)S(1)}, u32[]{:S(2)}, u32[]{:S(2)}) collective-permute-start(bf16[144,512]{1,0:T(8,128)(2,1)S(1)} %concatenate.24), channel_id=1, source_target_pairs={{0,10},{2,12},{4,14},{6,15},{7,13},{5,11},{3,9},{1,8},{8,18},{10,2... | collective-permute-start | bytes 442376 | tf_op jit(solution)/shard_map/ppermute | solution.py:131
  8.1 0.0 collective-permute-start.10
  8.1 1.5 %pad_maximum_fusion = bf16[128,5120]{1,0:T(8,128)(2,1)S(1)} fusion(bf16[128,512]{1,0:T(8,128)(2,1)} %bitcast.9, bf16[128,512]{1,0:T(8,128)(2,1)} %bitcast.12, bf16[128,4096]{1,0:T(8,128)(2,1)} %bitcast.7), kind=kLoop, calls=%fused_computation | loop fusion | flops 3932160 | bytes 2621440 | tf_op jit(solution)/shard_map/concatenate | solution.py:133
  9.6 0.0 collective-permute-done.refs_0_
  9.6 2.2 %collective-permute-start.1 = (bf16[128,512]{1,0:T(8,128)(2,1)S(1)}, bf16[128,512]{1,0:T(8,128)(2,1)S(1)}, u32[]{:S(2)}, u32[]{:S(2)}) collective-permute-start(bf16[128,512]{1,0:T(8,128)(2,1)S(1)} %collective-permute-done.refs_0_), channel_id=1, source_target_pairs={{0,2},{2,4},{4,6},{6,7},{7,5},{5,3},{3,1},{1,0},{8,10},{10,12},{12... | collective-permute-start | bytes 393224 | tf_op jit(solution)/shard_map/ppermute | solution.py:131
  11.8 0.0 collective-permute-done.4.refs_1_
  11.8 0.0 collective-permute-start.5
  11.8 0.0 collective-permute-start.8
  11.8 1.3 %collective-permute-done.9.refs_8_.refs_0_ = bf16[144,512]{1,0:T(8,128)(2,1)S(1)} collective-permute-done((bf16[144,512]{1,0:T(8,128)(2,1)S(1)}, bf16[144,512]{1,0:T(8,128)(2,1)S(1)}, u32[]{:S(2)}, u32[]{:S(2)}) %collective-permute-start.9) | collective-permute-done | bytes 147488 | tf_op jit(solution)/shard_map/ppermute | solution.py:131
  13.1 2.4 %collective-permute-start.11 = (bf16[144,512]{1,0:T(8,128)(2,1)S(1)}, bf16[144,512]{1,0:T(8,128)(2,1)S(1)}, u32[]{:S(2)}, u32[]{:S(2)}) collective-permute-start(bf16[144,512]{1,0:T(8,128)(2,1)S(1)} %collective-permute-done.9.refs_8_.refs_0_), channel_id=1, source_target_pairs={{0,2},{2,4},{4,6},{6,7},{7,5},{5,3},{3,1},{1,0},{8,10},{10,12},{12... | collective-permute-start | bytes 442376 | tf_op jit(solution)/shard_map/ppermute | solution.py:131
  15.5 0.0 collective-permute-done.10.refs_9_.refs_1_
  15.5 0.0 collective-permute-start.12
  15.5 0.5 %collective-permute-done.1.refs_2_ = bf16[128,512]{1,0:T(8,128)(2,1)S(1)} collective-permute-done((bf16[128,512]{1,0:T(8,128)(2,1)S(1)}, bf16[128,512]{1,0:T(8,128)(2,1)S(1)}, u32[]{:S(2)}, u32[]{:S(2)}) %collective-permute-start.1) | collective-permute-done | bytes 131104 | tf_op jit(solution)/shard_map/ppermute | solution.py:131
  16.0 1.5 %collective-permute-start.2 = (bf16[128,512]{1,0:T(8,128)(2,1)S(1)}, bf16[128,512]{1,0:T(8,128)(2,1)S(1)}, u32[]{:S(2)}, u32[]{:S(2)}) collective-permute-start(bf16[128,512]{1,0:T(8,128)(2,1)S(1)} %collective-permute-done.1.refs_2_), channel_id=1, source_target_pairs={{0,2},{2,4},{4,6},{6,7},{7,5},{5,3},{3,1},{1,0},{8,10},{10,12},{12... | collective-permute-start | bytes 393224 | tf_op jit(solution)/shard_map/ppermute | solution.py:131
  17.6 0.0 collective-permute-done.5.refs_3_
  17.6 0.5 %collective-permute-start.6 = (bf16[128,512]{1,0:T(8,128)(2,1)S(1)}, bf16[128,512]{1,0:T(8,128)(2,1)S(1)}, u32[]{:S(2)}, u32[]{:S(2)}) collective-permute-start(bf16[128,512]{1,0:T(8,128)(2,1)S(1)} %collective-permute-done.5.refs_3_), channel_id=1, source_target_pairs={{0,1},{2,0},{4,2},{6,4},{7,6},{5,7},{3,5},{1,3},{8,9},{10,8},{12,1... | collective-permute-start | bytes 393224 | tf_op jit(solution)/shard_map/ppermute | solution.py:131
  18.1 1.7 %collective-permute-done.11.refs_10_.refs_2_ = bf16[144,512]{1,0:T(8,128)(2,1)S(1)} collective-permute-done((bf16[144,512]{1,0:T(8,128)(2,1)S(1)}, bf16[144,512]{1,0:T(8,128)(2,1)S(1)}, u32[]{:S(2)}, u32[]{:S(2)}) %collective-permute-start.11) | collective-permute-done | bytes 147488 | tf_op jit(solution)/shard_map/ppermute | solution.py:131
  19.8 2.4 %collective-permute-start.13 = (bf16[144,512]{1,0:T(8,128)(2,1)S(1)}, bf16[144,512]{1,0:T(8,128)(2,1)S(1)}, u32[]{:S(2)}, u32[]{:S(2)}) collective-permute-start(bf16[144,512]{1,0:T(8,128)(2,1)S(1)} %collective-permute-done.11.refs_10_.refs_2_), channel_id=1, source_target_pairs={{0,2},{2,4},{4,6},{6,7},{7,5},{5,3},{3,1},{1,0},{8,10},{10,12},{12... | collective-permute-start | bytes 442376 | tf_op jit(solution)/shard_map/ppermute | solution.py:131
  22.2 0.0 collective-permute-done.12.refs_11_.refs_3_
  22.3 0.0 collective-permute-start.14
  22.3 0.3 collective-permute-done.2.refs_4_
  22.6 2.4 %collective-permute-start.3 = (bf16[64,512]{1,0:T(8,128)(2,1)S(1)}, bf16[64,512]{1,0:T(8,128)(2,1)S(1)}, u32[]{:S(2)}, u32[]{:S(2)}) collective-permute-start(bf16[64,512]{1,0:T(8,128)(2,1)S(1)} %slice.20), channel_id=1, source_target_pairs={{0,2},{2,4},{4,6},{6,7},{7,5},{5,3},{3,1},{1,0},{8,10},{10,12},{12... | collective-permute-start | bytes 196616 | tf_op jit(solution)/shard_map/ppermute | solution.py:131
  25.1 0.0 collective-permute-done.6.refs_5_
  25.1 0.1 collective-permute-start.7
  25.1 1.0 %collective-permute-done.13.refs_12_.refs_4_ = bf16[144,512]{1,0:T(8,128)(2,1)S(1)} collective-permute-done((bf16[144,512]{1,0:T(8,128)(2,1)S(1)}, bf16[144,512]{1,0:T(8,128)(2,1)S(1)}, u32[]{:S(2)}, u32[]{:S(2)}) %collective-permute-start.13) | collective-permute-done | bytes 147488 | tf_op jit(solution)/shard_map/ppermute | solution.py:131
  26.2 1.8 %collective-permute-start.15 = (bf16[64,512]{1,0:T(8,128)(2,1)S(1)}, bf16[64,512]{1,0:T(8,128)(2,1)S(1)}, u32[]{:S(2)}, u32[]{:S(2)}) collective-permute-start(bf16[64,512]{1,0:T(8,128)(2,1)S(1)} %slice.23), channel_id=1, source_target_pairs={{0,2},{2,4},{4,6},{6,7},{7,5},{5,3},{3,1},{1,0},{8,10},{10,12},{12... | collective-permute-start | bytes 196616 | tf_op jit(solution)/shard_map/ppermute | solution.py:131
  27.9 0.0 collective-permute-done.14.refs_13_.refs_5_
  27.9 0.3 collective-permute-start.16
  28.3 0.0 collective-permute-done.3.refs_0_.refs_6_
  28.3 1.2 %collective-permute-done.7.refs_1_.refs_7_ = bf16[64,512]{1,0:T(8,128)(2,1)S(1)} collective-permute-done((bf16[64,512]{1,0:T(8,128)(2,1)S(1)}, bf16[64,512]{1,0:T(8,128)(2,1)S(1)}, u32[]{:S(2)}, u32[]{:S(2)}) %collective-permute-start.7) | collective-permute-done | bytes 65568 | tf_op jit(solution)/shard_map/ppermute | solution.py:131
  29.5 0.3 shard_map.55.bias_ref
  29.8 0.0 collective-permute-done.8.own_ref
  29.8 1.9 %shard_map.56.weights_ref = bf16[8,512,320]{2,1,0:T(8,128)(2,1)S(1)} custom-call(f32[1,1152]{1,0:T(1,128)S(1)} %add_convert_fusion.pos_ref, f32[2,64,320]{2,1,0:T(8,128)S(1)} %shard_map.55.bias_ref, bf16[128,5120]{1,0:T(8,128)(2,1)S(1)} %collective-permute-done.8.own_ref, bf16[128,512]{1,0:T(8,128)(2,1)S(1)} %collective-permute-done.refs_0_, ...), custom_call_target="tpu_custom_call" | custom-call | flops 67108864 | bytes 1048576 | tf_op jit(solution)/shard_map/pallas_call | solution.py:162
  31.7 0.0 collective-permute-done.15.refs_6_
  31.7 0.5 %collective-permute-done.16.refs_7_ = bf16[64,512]{1,0:T(8,128)(2,1)S(1)} collective-permute-done((bf16[64,512]{1,0:T(8,128)(2,1)S(1)}, bf16[64,512]{1,0:T(8,128)(2,1)S(1)}, u32[]{:S(2)}, u32[]{:S(2)}) %collective-permute-start.16) | collective-permute-done | bytes 65568 | tf_op jit(solution)/shard_map/ppermute | solution.py:131
  32.3 2.3 %shard_map.57 = bf16[128,4096]{1,0:T(8,128)(2,1)} custom-call(f32[1,1152]{1,0:T(1,128)S(1)} %add_convert_fusion.pos_ref, bf16[8,512,320]{2,1,0:T(8,128)(2,1)S(1)} %shard_map.56.weights_ref, bf16[128,5120]{1,0:T(8,128)(2,1)S(1)} %collective-permute-done.8.own_ref, bf16[144,512]{1,0:T(8,128)(2,1)S(1)} %collective-permute-done.9.refs_8_.refs_0_, ...), custom_call_target="tpu_custom_call" | custom-call | flops 67108864 | bytes 1048576 | tf_op jit(solution)/shard_map/pallas_call | solution.py:171
  (4 shorter events, 0.0 us)
Async XLA Ops:
  0.0 9.6 %collective-permute-start = (bf16[128,512]{1,0:T(8,128)(2,1)}, bf16[128,512]{1,0:T(8,128)(2,1)S(1)}, u32[]{:S(2)}, u32[]{:S(2)}) collective-permute-start(bf16[128,512]{1,0:T(8,128)(2,1)} %bitcast.10), channel_id=1, source_target_pairs={{0,10},{2,12},{4,14},{6,15},{7,13},{5,11},{3,9},{1,8},{8,18},{10,2... | collective-permute-start | bytes 393224 | tf_op jit(solution)/shard_map/ppermute | solution.py:131
  2.5 9.3 %collective-permute-start.4 = (bf16[128,512]{1,0:T(8,128)(2,1)}, bf16[128,512]{1,0:T(8,128)(2,1)S(1)}, u32[]{:S(2)}, u32[]{:S(2)}) collective-permute-start(bf16[128,512]{1,0:T(8,128)(2,1)} %bitcast.11), channel_id=1, source_target_pairs={{0,9},{2,8},{4,10},{6,12},{7,14},{5,15},{3,13},{1,11},{8,17},{10,1... | collective-permute-start | bytes 393224 | tf_op jit(solution)/shard_map/ppermute | solution.py:131
  6.9 6.2 %collective-permute-start.9 = (bf16[144,512]{1,0:T(8,128)(2,1)S(1)}, bf16[144,512]{1,0:T(8,128)(2,1)S(1)}, u32[]{:S(2)}, u32[]{:S(2)}) collective-permute-start(bf16[144,512]{1,0:T(8,128)(2,1)S(1)} %concatenate.24), channel_id=1, source_target_pairs={{0,10},{2,12},{4,14},{6,15},{7,13},{5,11},{3,9},{1,8},{8,18},{10,2... | collective-permute-start | bytes 442376 | tf_op jit(solution)/shard_map/ppermute | solution.py:131
  8.1 7.4 %collective-permute-start.10 = (bf16[144,512]{1,0:T(8,128)(2,1)S(1)}, bf16[144,512]{1,0:T(8,128)(2,1)S(1)}, u32[]{:S(2)}, u32[]{:S(2)}) collective-permute-start(bf16[144,512]{1,0:T(8,128)(2,1)S(1)} %concatenate.24), channel_id=1, source_target_pairs={{0,9},{2,8},{4,10},{6,12},{7,14},{5,15},{3,13},{1,11},{8,17},{10,1... | collective-permute-start | bytes 442376 | tf_op jit(solution)/shard_map/ppermute | solution.py:131
  9.6 6.5 %collective-permute-start.1 = (bf16[128,512]{1,0:T(8,128)(2,1)S(1)}, bf16[128,512]{1,0:T(8,128)(2,1)S(1)}, u32[]{:S(2)}, u32[]{:S(2)}) collective-permute-start(bf16[128,512]{1,0:T(8,128)(2,1)S(1)} %collective-permute-done.refs_0_), channel_id=1, source_target_pairs={{0,2},{2,4},{4,6},{6,7},{7,5},{5,3},{3,1},{1,0},{8,10},{10,12},{12... | collective-permute-start | bytes 393224 | tf_op jit(solution)/shard_map/ppermute | solution.py:131
  11.8 5.8 %collective-permute-start.5 = (bf16[128,512]{1,0:T(8,128)(2,1)S(1)}, bf16[128,512]{1,0:T(8,128)(2,1)S(1)}, u32[]{:S(2)}, u32[]{:S(2)}) collective-permute-start(bf16[128,512]{1,0:T(8,128)(2,1)S(1)} %collective-permute-done.4.refs_1_), channel_id=1, source_target_pairs={{0,1},{2,0},{4,2},{6,4},{7,6},{5,7},{3,5},{1,3},{8,9},{10,8},{12,1... | collective-permute-start | bytes 393224 | tf_op jit(solution)/shard_map/ppermute | solution.py:131
  11.8 18.0 %collective-permute-start.8 = (bf16[128,5120]{1,0:T(8,128)(2,1)S(1)}, bf16[128,5120]{1,0:T(8,128)(2,1)S(1)}, u32[]{:S(2)}, u32[]{:S(2)}) collective-permute-start(bf16[128,5120]{1,0:T(8,128)(2,1)S(1)} %pad_maximum_fusion), channel_id=1, source_target_pairs={{0,8},{2,10},{4,12},{6,14},{7,15},{5,13},{3,11},{1,9},{8,16},{10,1... | collective-permute-start | bytes 3932168 | tf_op jit(solution)/shard_map/ppermute | solution.py:131
  13.1 6.7 %collective-permute-start.11 = (bf16[144,512]{1,0:T(8,128)(2,1)S(1)}, bf16[144,512]{1,0:T(8,128)(2,1)S(1)}, u32[]{:S(2)}, u32[]{:S(2)}) collective-permute-start(bf16[144,512]{1,0:T(8,128)(2,1)S(1)} %collective-permute-done.9.refs_8_.refs_0_), channel_id=1, source_target_pairs={{0,2},{2,4},{4,6},{6,7},{7,5},{5,3},{3,1},{1,0},{8,10},{10,12},{12... | collective-permute-start | bytes 442376 | tf_op jit(solution)/shard_map/ppermute | solution.py:131
  15.5 6.8 %collective-permute-start.12 = (bf16[144,512]{1,0:T(8,128)(2,1)S(1)}, bf16[144,512]{1,0:T(8,128)(2,1)S(1)}, u32[]{:S(2)}, u32[]{:S(2)}) collective-permute-start(bf16[144,512]{1,0:T(8,128)(2,1)S(1)} %collective-permute-done.10.refs_9_.refs_1_), channel_id=1, source_target_pairs={{0,1},{2,0},{4,2},{6,4},{7,6},{5,7},{3,5},{1,3},{8,9},{10,8},{12,1... | collective-permute-start | bytes 442376 | tf_op jit(solution)/shard_map/ppermute | solution.py:131
  16.0 6.6 %collective-permute-start.2 = (bf16[128,512]{1,0:T(8,128)(2,1)S(1)}, bf16[128,512]{1,0:T(8,128)(2,1)S(1)}, u32[]{:S(2)}, u32[]{:S(2)}) collective-permute-start(bf16[128,512]{1,0:T(8,128)(2,1)S(1)} %collective-permute-done.1.refs_2_), channel_id=1, source_target_pairs={{0,2},{2,4},{4,6},{6,7},{7,5},{5,3},{3,1},{1,0},{8,10},{10,12},{12... | collective-permute-start | bytes 393224 | tf_op jit(solution)/shard_map/ppermute | solution.py:131
  17.6 7.5 %collective-permute-start.6 = (bf16[128,512]{1,0:T(8,128)(2,1)S(1)}, bf16[128,512]{1,0:T(8,128)(2,1)S(1)}, u32[]{:S(2)}, u32[]{:S(2)}) collective-permute-start(bf16[128,512]{1,0:T(8,128)(2,1)S(1)} %collective-permute-done.5.refs_3_), channel_id=1, source_target_pairs={{0,1},{2,0},{4,2},{6,4},{7,6},{5,7},{3,5},{1,3},{8,9},{10,8},{12,1... | collective-permute-start | bytes 393224 | tf_op jit(solution)/shard_map/ppermute | solution.py:131
  19.8 6.4 %collective-permute-start.13 = (bf16[144,512]{1,0:T(8,128)(2,1)S(1)}, bf16[144,512]{1,0:T(8,128)(2,1)S(1)}, u32[]{:S(2)}, u32[]{:S(2)}) collective-permute-start(bf16[144,512]{1,0:T(8,128)(2,1)S(1)} %collective-permute-done.11.refs_10_.refs_2_), channel_id=1, source_target_pairs={{0,2},{2,4},{4,6},{6,7},{7,5},{5,3},{3,1},{1,0},{8,10},{10,12},{12... | collective-permute-start | bytes 442376 | tf_op jit(solution)/shard_map/ppermute | solution.py:131
  22.3 5.6 %collective-permute-start.14 = (bf16[144,512]{1,0:T(8,128)(2,1)S(1)}, bf16[144,512]{1,0:T(8,128)(2,1)S(1)}, u32[]{:S(2)}, u32[]{:S(2)}) collective-permute-start(bf16[144,512]{1,0:T(8,128)(2,1)S(1)} %collective-permute-done.12.refs_11_.refs_3_), channel_id=1, source_target_pairs={{0,1},{2,0},{4,2},{6,4},{7,6},{5,7},{3,5},{1,3},{8,9},{10,8},{12,1... | collective-permute-start | bytes 442376 | tf_op jit(solution)/shard_map/ppermute | solution.py:131
  22.6 5.6 %collective-permute-start.3 = (bf16[64,512]{1,0:T(8,128)(2,1)S(1)}, bf16[64,512]{1,0:T(8,128)(2,1)S(1)}, u32[]{:S(2)}, u32[]{:S(2)}) collective-permute-start(bf16[64,512]{1,0:T(8,128)(2,1)S(1)} %slice.20), channel_id=1, source_target_pairs={{0,2},{2,4},{4,6},{6,7},{7,5},{5,3},{3,1},{1,0},{8,10},{10,12},{12... | collective-permute-start | bytes 196616 | tf_op jit(solution)/shard_map/ppermute | solution.py:131
  25.1 4.4 %collective-permute-start.7 = (bf16[64,512]{1,0:T(8,128)(2,1)S(1)}, bf16[64,512]{1,0:T(8,128)(2,1)S(1)}, u32[]{:S(2)}, u32[]{:S(2)}) collective-permute-start(bf16[64,512]{1,0:T(8,128)(2,1)S(1)} %slice.21), channel_id=1, source_target_pairs={{0,1},{2,0},{4,2},{6,4},{7,6},{5,7},{3,5},{1,3},{8,9},{10,8},{12,1... | collective-permute-start | bytes 196616 | tf_op jit(solution)/shard_map/ppermute | solution.py:131
  26.2 5.6 %collective-permute-start.15 = (bf16[64,512]{1,0:T(8,128)(2,1)S(1)}, bf16[64,512]{1,0:T(8,128)(2,1)S(1)}, u32[]{:S(2)}, u32[]{:S(2)}) collective-permute-start(bf16[64,512]{1,0:T(8,128)(2,1)S(1)} %slice.23), channel_id=1, source_target_pairs={{0,2},{2,4},{4,6},{6,7},{7,5},{5,3},{3,1},{1,0},{8,10},{10,12},{12... | collective-permute-start | bytes 196616 | tf_op jit(solution)/shard_map/ppermute | solution.py:131
  27.9 4.3 %collective-permute-start.16 = (bf16[64,512]{1,0:T(8,128)(2,1)S(1)}, bf16[64,512]{1,0:T(8,128)(2,1)S(1)}, u32[]{:S(2)}, u32[]{:S(2)}) collective-permute-start(bf16[64,512]{1,0:T(8,128)(2,1)S(1)} %slice.24), channel_id=1, source_target_pairs={{0,1},{2,0},{4,2},{6,4},{7,6},{5,7},{3,5},{1,3},{8,9},{10,8},{12,1... | collective-permute-start | bytes 196616 | tf_op jit(solution)/shard_map/ppermute | solution.py:131

commit v5 on v4

--- a/solution.py
+++ b/solution.py
@@ -28,19 +28,18 @@
 def run_numbers(runs, pos_ref, tagged_refs):
     firsts = [first_run(pos_ref)]
     for ref in tagged_refs:
-        firsts.append(jnp.max(ref[TOK_DEV:, :HEAD_SIZE].astype(jnp.float32)).astype(jnp.int32))
+        firsts.append(jnp.min(ref[TOK_DEV:, :TOK_DEV].astype(jnp.float32)).astype(jnp.int32))
     places = runs // 2
     firsts.append(places * (places - 1) // 2 - sum(firsts))
     return [(first, runs - 1 - first) for first in firsts]
 
 
-def sort_runs(numbers, own_ref, own_column, block_refs, sorted_buf):
+def sort_runs(numbers, own_ref, own_column, block_refs, sorted_ref):
     for half, number in enumerate(numbers[0]):
-        sorted_buf[number] = own_ref[half * RUN : (half + 1) * RUN, own_column : own_column + KV_COLUMNS]
-    halves = [(ref, ref, RUN) for ref in block_refs[:-2]] + [(block_refs[-2], block_refs[-1], 0)]
-    for (first, second), (first_ref, second_ref, at) in zip(numbers[1:], halves):
-        sorted_buf[first] = first_ref[:RUN, :]
-        sorted_buf[second] = second_ref[at : at + RUN, :]
+        sorted_ref[number] = own_ref[half * RUN : (half + 1) * RUN, own_column : own_column + KV_COLUMNS]
+    for (first, second), ref in zip(numbers[1:], block_refs):
+        sorted_ref[first] = ref[:RUN, :]
+        sorted_ref[second] = ref[RUN:TOK_DEV, :]
 
 
 def bias_kernel(runs, pos_ref, *refs):
@@ -59,11 +58,16 @@
 
 def weights_kernel(runs, pos_ref, bias_ref, own_ref, *refs):
     blocks = runs // 2
-    key_refs, tagged_refs, (weights_ref, key_buf) = refs[:blocks], refs[blocks:-2], refs[-2:]
+    key_refs, tagged_refs = refs[:blocks], refs[blocks:-4]
+    weights_ref, inverse_ref, sorted_ref, key_buf = refs[-4:]
     reach = runs // 4
     span = (reach + 1) * RUN
     numbers = run_numbers(runs, pos_ref, tagged_refs)
-    sort_runs(numbers, own_ref, QUERY_COLUMNS, key_refs, key_buf)
+    sort_runs(numbers, own_ref, QUERY_COLUMNS, key_refs[:-2], key_buf)
+    for number, ref in zip(numbers[-1], key_refs[-2:]):
+        key_buf[number] = ref[...]
+    sort_runs(numbers, own_ref, QUERY_COLUMNS + KV_COLUMNS, tagged_refs, sorted_ref)
+    ones = jnp.ones((span, HEAD_SIZE), jnp.bfloat16)
     scale = math.log2(math.e) / math.sqrt(HEAD_SIZE)
     for half in range(2):
         start = jnp.maximum(numbers[0][half] - reach, 0)
@@ -84,27 +88,33 @@
                 preferred_element_type=jnp.float32,
             )
             row_max = jnp.max(scores, axis=1, keepdims=True)
-            weights_ref[half * KEY_VALUE_HEADS + kv] = jnp.exp2((scores - row_max) * scale).astype(jnp.bfloat16)
-
-
-def values_kernel(runs, pos_ref, weights_ref, own_ref, *refs):
-    value_refs, (out_ref, value_buf, result_buf, out_sems) = refs[:-4], refs[-4:]
+            weights = jnp.exp2((scores - row_max) * scale).astype(jnp.bfloat16)
+            weights_ref[half * KEY_VALUE_HEADS + kv] = weights
+            total = jnp.dot(weights, ones, preferred_element_type=jnp.float32)
+            inverse_ref[half * KEY_VALUE_HEADS + kv] = 1.0 / total
+
+
+def values_kernel(runs, pos_ref, weights_ref, inverse_ref, sorted_ref, *refs):
+    tagged_refs, last_refs, (out_ref, result_buf, out_sems) = refs[:-5], refs[-5:-3], refs[-3:]
     reach = runs // 4
-    span = (reach + 1) * RUN
-    numbers = run_numbers(runs, pos_ref, value_refs[:-2])
-    sort_runs(numbers, own_ref, QUERY_COLUMNS + KV_COLUMNS, value_refs, value_buf)
-    ones = jnp.ones((span, HEAD_SIZE), jnp.bfloat16)
+    numbers = run_numbers(runs, pos_ref, tagged_refs)
     copies = []
     for half in range(2):
         start = jnp.maximum(numbers[0][half] - reach, 0)
         for kv in range(KEY_VALUE_HEADS):
-            value = value_buf[pl.ds(start, reach + 1), :, kv * HEAD_SIZE : (kv + 1) * HEAD_SIZE]
+            columns = slice(kv * HEAD_SIZE, (kv + 1) * HEAD_SIZE)
+            parts = []
+            for i in range(reach + 1):
+                part = sorted_ref[start + i, :, columns]
+                for number, last_ref in zip(numbers[-1], last_refs):
+                    part = jnp.where(start + i == number, last_ref[:, columns], part)
+                parts.append(part)
             summed = jnp.dot(
                 weights_ref[half * KEY_VALUE_HEADS + kv],
-                jnp.concatenate([value.reshape(span, HEAD_SIZE), ones], axis=1),
+                jnp.concatenate(parts, axis=0),
                 preferred_element_type=jnp.float32,
             )
-            result = (summed[:, :HEAD_SIZE] / summed[:, HEAD_SIZE:]).astype(jnp.bfloat16)
+            result = (summed * inverse_ref[half * KEY_VALUE_HEADS + kv]).astype(jnp.bfloat16)
             for i in range(GROUP):
                 h = kv * GROUP + i
                 result_buf[half, :, h * HEAD_SIZE : (h + 1) * HEAD_SIZE] = result[i * RUN : (i + 1) * RUN]
@@ -142,14 +152,14 @@
             held.extend([ahead, back])
         return held + [shift(ahead[:RUN], 0, 1), shift(back[RUN:TOK_DEV], 0, -1)], early
 
-    pos = lax.optimization_barrier(jnp.concatenate([token_pos, segment]).astype(jnp.float32)[None])
-    tag = jnp.broadcast_to((pos[:, :1] / RUN).astype(jnp.bfloat16), (TAG_ROWS, KV_COLUMNS))
+    tag = jnp.broadcast_to((token_pos >> (RUN.bit_length() - 1)).astype(jnp.bfloat16)[None], (TAG_ROWS, TOK_DEV))
+    tag = jnp.pad(tag, ((0, 0), (0, KV_COLUMNS - TOK_DEV)))
     all_keys, own = around(keys[0], own)
     all_values, _ = around(jnp.concatenate([values[0], tag], axis=0))
     own = shift(own, 1, 0)
+    pos = lax.optimization_barrier(jnp.concatenate([token_pos, segment]).astype(jnp.float32)[None])
     vmem = pl.BlockSpec(memory_space=pltpu.VMEM)
     params = pltpu.CompilerParams(vmem_limit_bytes=(12 + runs // 4) * 1024 * 1024)
-    sorted_buf = pltpu.VMEM((runs, RUN, KV_COLUMNS), jnp.bfloat16)
     before_mask = all_keys[-2:]
     bias = pl.pallas_call(
         functools.partial(bias_kernel, runs),
@@ -157,30 +167,33 @@
         in_specs=[vmem] * (1 + len(before_mask)),
         out_specs=vmem,
         compiler_params=pltpu.CompilerParams(vmem_limit_bytes=8 * 1024 * 1024),
-        cost_estimate=pl.CostEstimate(flops=10 << 30, bytes_accessed=0, transcendentals=0),
+        cost_estimate=pl.CostEstimate(flops=35 << 28, bytes_accessed=0, transcendentals=0),
     )(pos, *before_mask)
-    weights = pl.pallas_call(
+    weights, inverse, sorted_values = pl.pallas_call(
         functools.partial(weights_kernel, runs),
-        out_shape=jax.ShapeDtypeStruct((2 * KEY_VALUE_HEADS, GROUP * RUN, (runs // 4 + 1) * RUN), jnp.bfloat16),
+        out_shape=(
+            jax.ShapeDtypeStruct((2 * KEY_VALUE_HEADS, GROUP * RUN, (runs // 4 + 1) * RUN), jnp.bfloat16),
+            jax.ShapeDtypeStruct((2 * KEY_VALUE_HEADS, GROUP * RUN, HEAD_SIZE), jnp.float32),
+            jax.ShapeDtypeStruct((runs, RUN, KV_COLUMNS), jnp.bfloat16),
+        ),
         in_specs=[vmem] * (3 + len(all_keys) + len(all_values[:-2])),
-        out_specs=vmem,
-        scratch_shapes=[sorted_buf],
+        out_specs=(vmem,) * 3,
+        scratch_shapes=[pltpu.VMEM((runs, RUN, KV_COLUMNS), jnp.bfloat16)],
         compiler_params=params,
         cost_estimate=pl.CostEstimate(flops=1 << 26, bytes_accessed=1 << 20, transcendentals=0),
     )(pos, bias, own, *all_keys, *all_values[:-2])
     out = pl.pallas_call(
         functools.partial(values_kernel, runs),
         out_shape=jax.ShapeDtypeStruct((TOK_DEV, QUERY_COLUMNS), jnp.bfloat16),
-        in_specs=[vmem] * (3 + len(all_values)),
+        in_specs=[vmem] * (4 + len(all_values)),
         out_specs=pl.BlockSpec(memory_space=pl.ANY),
         scratch_shapes=[
-            sorted_buf,
             pltpu.VMEM((2, RUN, QUERY_COLUMNS), jnp.bfloat16),
             pltpu.SemaphoreType.DMA((2,)),
         ],
         compiler_params=params,
         cost_estimate=pl.CostEstimate(flops=1 << 26, bytes_accessed=1 << 20, transcendentals=0),
-    )(pos, weights, own, *all_values)
+    )(pos, weights, inverse, sorted_values, *all_values)
     return out[None]
 
 

time: 34.7 us -> 34.1 us (0.983)
  local copies, waits for them, and re-layouts: 1.45 us -> 0.04 us
  Pallas kernels: 4.49 us -> 5.62 us
  other arithmetic: 2.16 us -> 3.04 us
  between operations: 0.74 us -> 0.11 us
  waiting for transfers between devices: 6.67 us -> 6.12 us
    pallas_call x1, Pallas kernels: 1.89 us -> 3.35 us  [per_device(): pl.pallas_call(functools.partial(weights_kernel, runs), out_shape=(jax.Sh...]
    concatenate x1 -> x0, local copies, waits for them, and re-layouts: 0.92 us -> none  [per_device(): all_values, _ = around(jnp.concatenate([values[0], tag], axis=0))]
    concatenate x0 -> x1, other arithmetic: none -> 0.91 us  [per_device(): all_values, _ = around(jnp.concatenate([values[0], tag], axis=0))]
    convert_element_type x1, other arithmetic: 0.69 us -> 0.01 us  [per_device(): jnp.concatenate([token_pos, segment]).astype(jnp.float32)[None]]
    convert_element_type x0 -> x1, other arithmetic: none -> 0.66 us  [per_device(): (token_pos >> RUN.bit_length() - 1).astype(jnp.bfloat16)[None]]
    ppermute x17, waiting for transfers between devices: 6.67 us -> 6.12 us  [shift(): return lax.ppermute(block, ('section', 'ctx'), pairs)]
    slice x1 -> x0, local copies, waits for them, and re-layouts: 0.51 us -> none  [per_device(): pos[:, :1] / RUN]
  transfers between devices with their start and end apart: 17 -> 17, of which waited for: 7 -> 6; matrix products, arithmetic and copies ran while one was open for 10% -> 9% of each run, Pallas kernels for 6% -> 11%
where the time goes in v5:
time: 34.1 us; the launch traced here: 33.9 us
  starting transfers between devices  19 us (56%)
  waiting for transfers between devices  6.12 us (18%)
  Pallas kernels  5.62 us (16%)
  other arithmetic  3.04 us (9%)
    ppermute x17, starting transfers between devices, shift(): return lax.ppermute(block, ('section', 'ctx'), pairs)  19 us
    ppermute x17, waiting for transfers between devices, shift(): return lax.ppermute(block, ('section', 'ctx'), pairs)  6.12 us
    pallas_call x1, Pallas kernels, per_device(): pl.pallas_call(functools.partial(weights_kernel, runs), out_shape=(jax.Sh...  3.35 us
    pallas_call x1, Pallas kernels, per_device(): pl.pallas_call(functools.partial(values_kernel, runs), out_shape=jax.Shap...  1.93 us
    concatenate x1, other arithmetic, per_device(): own = jnp.concatenate([queries[0], keys[0], values[0]], axis=1)  1.46 us
    concatenate x1, other arithmetic, per_device(): all_values, _ = around(jnp.concatenate([values[0], tag], axis=0))  0.91 us
  transfers between devices with their start and end apart: 17, of which 6 were waited for; matrix products, arithmetic and copies ran while one was open for 9% of the time, Pallas kernels for 11%

profile of v5, /device:TPU:0, one launch (start us, length us, event | category | flops | bytes accessed | tf_op | source)
XLA Modules:
  0.0 33.9 jit_solution(10621750410669325437)
XLA Ops:
  0.0 0.0 copy-start.1
  0.0 0.0 copy-start
  0.0 2.5 %collective-permute-start = (bf16[128,512]{1,0:T(8,128)(2,1)}, bf16[128,512]{1,0:T(8,128)(2,1)S(1)}, u32[]{:S(2)}, u32[]{:S(2)}) collective-permute-start(bf16[128,512]{1,0:T(8,128)(2,1)} %bitcast.9), channel_id=1, source_target_pairs={{0,10},{2,12},{4,14},{6,15},{7,13},{5,11},{3,9},{1,8},{8,18},{10,2... | collective-permute-start | bytes 393224 | tf_op jit(solution)/shard_map/ppermute | solution.py:141
  2.5 1.7 %collective-permute-start.4 = (bf16[128,512]{1,0:T(8,128)(2,1)}, bf16[128,512]{1,0:T(8,128)(2,1)S(1)}, u32[]{:S(2)}, u32[]{:S(2)}) collective-permute-start(bf16[128,512]{1,0:T(8,128)(2,1)} %bitcast.10), channel_id=1, source_target_pairs={{0,9},{2,8},{4,10},{6,12},{7,14},{5,15},{3,13},{1,11},{8,17},{10,1... | collective-permute-start | bytes 393224 | tf_op jit(solution)/shard_map/ppermute | solution.py:141
  4.1 0.7 %shift-right-arithmetic_convert_fusion = bf16[128]{0:T(256)(128)(2,1)S(1)} fusion(s32[128]{0:T(128)} %param.8), kind=kLoop, calls=%fused_computation.3 | loop fusion | flops 256 | bytes 768 | tf_op jit(solution)/shard_map/convert_element_type | solution.py:155
  4.8 0.9 %pad_maximum_fusion.1 = bf16[144,512]{1,0:T(8,128)(2,1)S(1)} fusion(bf16[16,512]{1,0:T(8,128)(2,1)S(1)} %pad.7, bf16[128,512]{1,0:T(8,128)(2,1)} %bitcast.7), kind=kLoop, calls=%fused_computation.1 | loop fusion | flops 294912 | bytes 294912 | tf_op jit(solution)/shard_map/concatenate | solution.py:158
  5.7 1.2 %collective-permute-start.9 = (bf16[144,512]{1,0:T(8,128)(2,1)S(1)}, bf16[144,512]{1,0:T(8,128)(2,1)S(1)}, u32[]{:S(2)}, u32[]{:S(2)}) collective-permute-start(bf16[144,512]{1,0:T(8,128)(2,1)S(1)} %pad_maximum_fusion.1), channel_id=1, source_target_pairs={{0,10},{2,12},{4,14},{6,15},{7,13},{5,11},{3,9},{1,8},{8,18},{10,2... | collective-permute-start | bytes 442376 | tf_op jit(solution)/shard_map/ppermute | solution.py:141
  6.9 0.1 collective-permute-start.10
  7.0 1.5 %pad_maximum_fusion = bf16[128,5120]{1,0:T(8,128)(2,1)S(1)} fusion(bf16[128,512]{1,0:T(8,128)(2,1)} %bitcast.8, bf16[128,512]{1,0:T(8,128)(2,1)} %bitcast.11, bf16[128,4096]{1,0:T(8,128)(2,1)} %bitcast.6), kind=kLoop, calls=%fused_computation | loop fusion | flops 3932160 | bytes 2621440 | tf_op jit(solution)/shard_map/concatenate | solution.py:143
  8.4 0.0 collective-permute-done.refs_0_
  8.4 2.1 %collective-permute-start.1 = (bf16[128,512]{1,0:T(8,128)(2,1)S(1)}, bf16[128,512]{1,0:T(8,128)(2,1)S(1)}, u32[]{:S(2)}, u32[]{:S(2)}) collective-permute-start(bf16[128,512]{1,0:T(8,128)(2,1)S(1)} %collective-permute-done.refs_0_), channel_id=1, source_target_pairs={{0,2},{2,4},{4,6},{6,7},{7,5},{5,3},{3,1},{1,0},{8,10},{10,12},{12... | collective-permute-start | bytes 393224 | tf_op jit(solution)/shard_map/ppermute | solution.py:141
  10.6 0.0 collective-permute-done.4.refs_1_
  10.6 0.0 collective-permute-start.5
  10.6 0.0 collective-permute-start.8
  10.6 1.3 %collective-permute-done.9.refs_8_.refs_0_ = bf16[144,512]{1,0:T(8,128)(2,1)S(1)} collective-permute-done((bf16[144,512]{1,0:T(8,128)(2,1)S(1)}, bf16[144,512]{1,0:T(8,128)(2,1)S(1)}, u32[]{:S(2)}, u32[]{:S(2)}) %collective-permute-start.9) | collective-permute-done | bytes 147488 | tf_op jit(solution)/shard_map/ppermute | solution.py:141
  11.9 2.4 %collective-permute-start.11 = (bf16[144,512]{1,0:T(8,128)(2,1)S(1)}, bf16[144,512]{1,0:T(8,128)(2,1)S(1)}, u32[]{:S(2)}, u32[]{:S(2)}) collective-permute-start(bf16[144,512]{1,0:T(8,128)(2,1)S(1)} %collective-permute-done.9.refs_8_.refs_0_), channel_id=1, source_target_pairs={{0,2},{2,4},{4,6},{6,7},{7,5},{5,3},{3,1},{1,0},{8,10},{10,12},{12... | collective-permute-start | bytes 442376 | tf_op jit(solution)/shard_map/ppermute | solution.py:141
  14.3 0.0 collective-permute-done.10.refs_9_.refs_1_
  14.3 0.0 collective-permute-start.12
  14.3 0.5 %collective-permute-done.1.refs_2_ = bf16[128,512]{1,0:T(8,128)(2,1)S(1)} collective-permute-done((bf16[128,512]{1,0:T(8,128)(2,1)S(1)}, bf16[128,512]{1,0:T(8,128)(2,1)S(1)}, u32[]{:S(2)}, u32[]{:S(2)}) %collective-permute-start.1) | collective-permute-done | bytes 131104 | tf_op jit(solution)/shard_map/ppermute | solution.py:141
  14.9 1.5 %collective-permute-start.2 = (bf16[128,512]{1,0:T(8,128)(2,1)S(1)}, bf16[128,512]{1,0:T(8,128)(2,1)S(1)}, u32[]{:S(2)}, u32[]{:S(2)}) collective-permute-start(bf16[128,512]{1,0:T(8,128)(2,1)S(1)} %collective-permute-done.1.refs_2_), channel_id=1, source_target_pairs={{0,2},{2,4},{4,6},{6,7},{7,5},{5,3},{3,1},{1,0},{8,10},{10,12},{12... | collective-permute-start | bytes 393224 | tf_op jit(solution)/shard_map/ppermute | solution.py:141
  16.4 0.0 collective-permute-done.5.refs_3_
  16.4 0.5 %collective-permute-start.6 = (bf16[128,512]{1,0:T(8,128)(2,1)S(1)}, bf16[128,512]{1,0:T(8,128)(2,1)S(1)}, u32[]{:S(2)}, u32[]{:S(2)}) collective-permute-start(bf16[128,512]{1,0:T(8,128)(2,1)S(1)} %collective-permute-done.5.refs_3_), channel_id=1, source_target_pairs={{0,1},{2,0},{4,2},{6,4},{7,6},{5,7},{3,5},{1,3},{8,9},{10,8},{12,1... | collective-permute-start | bytes 393224 | tf_op jit(solution)/shard_map/ppermute | solution.py:141
  16.9 1.7 %collective-permute-done.11.refs_10_.refs_2_ = bf16[144,512]{1,0:T(8,128)(2,1)S(1)} collective-permute-done((bf16[144,512]{1,0:T(8,128)(2,1)S(1)}, bf16[144,512]{1,0:T(8,128)(2,1)S(1)}, u32[]{:S(2)}, u32[]{:S(2)}) %collective-permute-start.11) | collective-permute-done | bytes 147488 | tf_op jit(solution)/shard_map/ppermute | solution.py:141
  18.6 2.4 %collective-permute-start.13 = (bf16[144,512]{1,0:T(8,128)(2,1)S(1)}, bf16[144,512]{1,0:T(8,128)(2,1)S(1)}, u32[]{:S(2)}, u32[]{:S(2)}) collective-permute-start(bf16[144,512]{1,0:T(8,128)(2,1)S(1)} %collective-permute-done.11.refs_10_.refs_2_), channel_id=1, source_target_pairs={{0,2},{2,4},{4,6},{6,7},{7,5},{5,3},{3,1},{1,0},{8,10},{10,12},{12... | collective-permute-start | bytes 442376 | tf_op jit(solution)/shard_map/ppermute | solution.py:141
  21.1 0.0 collective-permute-done.12.refs_11_.refs_3_
  21.1 0.0 collective-permute-start.14
  21.1 0.3 collective-permute-done.2.refs_4_
  21.4 2.4 %collective-permute-start.3 = (bf16[64,512]{1,0:T(8,128)(2,1)S(1)}, bf16[64,512]{1,0:T(8,128)(2,1)S(1)}, u32[]{:S(2)}, u32[]{:S(2)}) collective-permute-start(bf16[64,512]{1,0:T(8,128)(2,1)S(1)} %slice.16), channel_id=1, source_target_pairs={{0,2},{2,4},{4,6},{6,7},{7,5},{5,3},{3,1},{1,0},{8,10},{10,12},{12... | collective-permute-start | bytes 196616 | tf_op jit(solution)/shard_map/ppermute | solution.py:141
  23.9 0.0 collective-permute-done.6.refs_5_
  23.9 0.1 collective-permute-start.7
  24.0 0.0 copy-done.1
  24.0 0.0 copy-done
  24.0 1.0 %collective-permute-done.13.refs_12_.refs_4_ = bf16[144,512]{1,0:T(8,128)(2,1)S(1)} collective-permute-done((bf16[144,512]{1,0:T(8,128)(2,1)S(1)}, bf16[144,512]{1,0:T(8,128)(2,1)S(1)}, u32[]{:S(2)}, u32[]{:S(2)}) %collective-permute-start.13) | collective-permute-done | bytes 147488 | tf_op jit(solution)/shard_map/ppermute | solution.py:141
  25.0 1.7 %collective-permute-start.15 = (bf16[64,512]{1,0:T(8,128)(2,1)S(1)}, bf16[64,512]{1,0:T(8,128)(2,1)S(1)}, u32[]{:S(2)}, u32[]{:S(2)}) collective-permute-start(bf16[64,512]{1,0:T(8,128)(2,1)S(1)} %slice.18), channel_id=1, source_target_pairs={{0,2},{2,4},{4,6},{6,7},{7,5},{5,3},{3,1},{1,0},{8,10},{10,12},{12... | collective-permute-start | bytes 196616 | tf_op jit(solution)/shard_map/ppermute | solution.py:141
  26.7 0.0 collective-permute-done.14.refs_13_.refs_5_
  26.7 0.3 collective-permute-start.16
  27.1 0.0 collective-permute-done.3.refs_0_.refs_6_
  27.1 1.2 %collective-permute-done.7.refs_1_.refs_7_ = bf16[64,512]{1,0:T(8,128)(2,1)S(1)} collective-permute-done((bf16[64,512]{1,0:T(8,128)(2,1)S(1)}, bf16[64,512]{1,0:T(8,128)(2,1)S(1)}, u32[]{:S(2)}, u32[]{:S(2)}) %collective-permute-start.7) | collective-permute-done | bytes 65568 | tf_op jit(solution)/shard_map/ppermute | solution.py:141
  28.3 0.3 %shard_map.55.bias_ref = f32[2,64,320]{2,1,0:T(8,128)S(1)} custom-call(f32[1,1152]{1,0:T(1,128)S(1)} %add_convert_fusion.pos_ref, bf16[64,512]{1,0:T(8,128)(2,1)S(1)} %collective-permute-done.3.refs_0_.refs_6_, bf16[64,512]{1,0:T(8,128)(2,1)S(1)} %collective-permute-done.7.refs_1_.refs_7_), custom_call_target="tpu_custom_call" | custom-call | flops 9395240960 | tf_op jit(solution)/shard_map/pallas_call | solution.py:164
  28.6 0.0 collective-permute-done.8.own_ref
  28.6 3.4 %shard_map.56 = (bf16[8,512,320]{2,1,0:T(8,128)(2,1)S(1)}, f32[8,512,128]{2,1,0:T(8,128)S(1)}, bf16[16,64,512]{2,1,0:T(8,128)(2,1)S(1)}) custom-call(f32[1,1152]{1,0:T(1,128)S(1)} %add_convert_fusion.pos_ref, f32[2,64,320]{2,1,0:T(8,128)S(1)} %shard_map.55.bias_ref, bf16[128,5120]{1,0:T(8,128)(2,1)S(1)} %collective-permute-done.8.own_ref, ...), custom_call_target="tpu_custom_call" | custom-call | flops 67108864 | bytes 1048576 | tf_op jit(solution)/shard_map/pallas_call | solution.py:172
  32.0 0.0 collective-permute-done.15.refs_6_
  32.0 0.0 collective-permute-done.16.refs_7_
  32.0 1.9 %shard_map.57 = bf16[128,4096]{1,0:T(8,128)(2,1)} custom-call(f32[1,1152]{1,0:T(1,128)S(1)} %add_convert_fusion.pos_ref, bf16[8,512,320]{2,1,0:T(8,128)(2,1)S(1)} %get-tuple-element.12.weights_ref, f32[8,512,128]{2,1,0:T(8,128)S(1)} %get-tuple-element.13.inverse_ref, bf16[16,64,512]{2,1,0:T(8,128)(2,1)S(1)} %get-tuple-element.14.sorted_ref, ...), custom_call_target="tpu_custom_call" | custom-call | flops 67108864 | bytes 1048576 | tf_op jit(solution)/shard_map/pallas_call | solution.py:185
  (7 shorter events, 0.0 us)
Async XLA Ops:
  0.0 24.0 %copy-start.1 = (s32[128]{0:T(128)S(1)}, s32[128]{0:T(128)}, u32[]{:S(2)}) copy-start(s32[128]{0:T(128)} %param.8) | copy-start | bytes 1540
  0.0 24.0 %copy-start = (s32[1024]{0:T(1024)S(1)}, s32[1024]{0:T(1024)}, u32[]{:S(2)}) copy-start(s32[1024]{0:T(1024)} %param.9) | copy-start | bytes 12292
  0.0 8.4 %collective-permute-start = (bf16[128,512]{1,0:T(8,128)(2,1)}, bf16[128,512]{1,0:T(8,128)(2,1)S(1)}, u32[]{:S(2)}, u32[]{:S(2)}) collective-permute-start(bf16[128,512]{1,0:T(8,128)(2,1)} %bitcast.9), channel_id=1, source_target_pairs={{0,10},{2,12},{4,14},{6,15},{7,13},{5,11},{3,9},{1,8},{8,18},{10,2... | collective-permute-start | bytes 393224 | tf_op jit(solution)/shard_map/ppermute | solution.py:141
  2.5 8.1 %collective-permute-start.4 = (bf16[128,512]{1,0:T(8,128)(2,1)}, bf16[128,512]{1,0:T(8,128)(2,1)S(1)}, u32[]{:S(2)}, u32[]{:S(2)}) collective-permute-start(bf16[128,512]{1,0:T(8,128)(2,1)} %bitcast.10), channel_id=1, source_target_pairs={{0,9},{2,8},{4,10},{6,12},{7,14},{5,15},{3,13},{1,11},{8,17},{10,1... | collective-permute-start | bytes 393224 | tf_op jit(solution)/shard_map/ppermute | solution.py:141
  5.7 6.2 %collective-permute-start.9 = (bf16[144,512]{1,0:T(8,128)(2,1)S(1)}, bf16[144,512]{1,0:T(8,128)(2,1)S(1)}, u32[]{:S(2)}, u32[]{:S(2)}) collective-permute-start(bf16[144,512]{1,0:T(8,128)(2,1)S(1)} %pad_maximum_fusion.1), channel_id=1, source_target_pairs={{0,10},{2,12},{4,14},{6,15},{7,13},{5,11},{3,9},{1,8},{8,18},{10,2... | collective-permute-start | bytes 442376 | tf_op jit(solution)/shard_map/ppermute | solution.py:141
  6.9 7.4 %collective-permute-start.10 = (bf16[144,512]{1,0:T(8,128)(2,1)S(1)}, bf16[144,512]{1,0:T(8,128)(2,1)S(1)}, u32[]{:S(2)}, u32[]{:S(2)}) collective-permute-start(bf16[144,512]{1,0:T(8,128)(2,1)S(1)} %pad_maximum_fusion.1), channel_id=1, source_target_pairs={{0,9},{2,8},{4,10},{6,12},{7,14},{5,15},{3,13},{1,11},{8,17},{10,1... | collective-permute-start | bytes 442376 | tf_op jit(solution)/shard_map/ppermute | solution.py:141
  8.4 6.4 %collective-permute-start.1 = (bf16[128,512]{1,0:T(8,128)(2,1)S(1)}, bf16[128,512]{1,0:T(8,128)(2,1)S(1)}, u32[]{:S(2)}, u32[]{:S(2)}) collective-permute-start(bf16[128,512]{1,0:T(8,128)(2,1)S(1)} %collective-permute-done.refs_0_), channel_id=1, source_target_pairs={{0,2},{2,4},{4,6},{6,7},{7,5},{5,3},{3,1},{1,0},{8,10},{10,12},{12... | collective-permute-start | bytes 393224 | tf_op jit(solution)/shard_map/ppermute | solution.py:141
  10.6 5.8 %collective-permute-start.5 = (bf16[128,512]{1,0:T(8,128)(2,1)S(1)}, bf16[128,512]{1,0:T(8,128)(2,1)S(1)}, u32[]{:S(2)}, u32[]{:S(2)}) collective-permute-start(bf16[128,512]{1,0:T(8,128)(2,1)S(1)} %collective-permute-done.4.refs_1_), channel_id=1, source_target_pairs={{0,1},{2,0},{4,2},{6,4},{7,6},{5,7},{3,5},{1,3},{8,9},{10,8},{12,1... | collective-permute-start | bytes 393224 | tf_op jit(solution)/shard_map/ppermute | solution.py:141
  10.6 18.0 %collective-permute-start.8 = (bf16[128,5120]{1,0:T(8,128)(2,1)S(1)}, bf16[128,5120]{1,0:T(8,128)(2,1)S(1)}, u32[]{:S(2)}, u32[]{:S(2)}) collective-permute-start(bf16[128,5120]{1,0:T(8,128)(2,1)S(1)} %pad_maximum_fusion), channel_id=1, source_target_pairs={{0,8},{2,10},{4,12},{6,14},{7,15},{5,13},{3,11},{1,9},{8,16},{10,1... | collective-permute-start | bytes 3932168 | tf_op jit(solution)/shard_map/ppermute | solution.py:141
  11.9 6.7 %collective-permute-start.11 = (bf16[144,512]{1,0:T(8,128)(2,1)S(1)}, bf16[144,512]{1,0:T(8,128)(2,1)S(1)}, u32[]{:S(2)}, u32[]{:S(2)}) collective-permute-start(bf16[144,512]{1,0:T(8,128)(2,1)S(1)} %collective-permute-done.9.refs_8_.refs_0_), channel_id=1, source_target_pairs={{0,2},{2,4},{4,6},{6,7},{7,5},{5,3},{3,1},{1,0},{8,10},{10,12},{12... | collective-permute-start | bytes 442376 | tf_op jit(solution)/shard_map/ppermute | solution.py:141
  14.3 6.8 %collective-permute-start.12 = (bf16[144,512]{1,0:T(8,128)(2,1)S(1)}, bf16[144,512]{1,0:T(8,128)(2,1)S(1)}, u32[]{:S(2)}, u32[]{:S(2)}) collective-permute-start(bf16[144,512]{1,0:T(8,128)(2,1)S(1)} %collective-permute-done.10.refs_9_.refs_1_), channel_id=1, source_target_pairs={{0,1},{2,0},{4,2},{6,4},{7,6},{5,7},{3,5},{1,3},{8,9},{10,8},{12,1... | collective-permute-start | bytes 442376 | tf_op jit(solution)/shard_map/ppermute | solution.py:141
  14.9 6.6 %collective-permute-start.2 = (bf16[128,512]{1,0:T(8,128)(2,1)S(1)}, bf16[128,512]{1,0:T(8,128)(2,1)S(1)}, u32[]{:S(2)}, u32[]{:S(2)}) collective-permute-start(bf16[128,512]{1,0:T(8,128)(2,1)S(1)} %collective-permute-done.1.refs_2_), channel_id=1, source_target_pairs={{0,2},{2,4},{4,6},{6,7},{7,5},{5,3},{3,1},{1,0},{8,10},{10,12},{12... | collective-permute-start | bytes 393224 | tf_op jit(solution)/shard_map/ppermute | solution.py:141
  16.4 7.5 %collective-permute-start.6 = (bf16[128,512]{1,0:T(8,128)(2,1)S(1)}, bf16[128,512]{1,0:T(8,128)(2,1)S(1)}, u32[]{:S(2)}, u32[]{:S(2)}) collective-permute-start(bf16[128,512]{1,0:T(8,128)(2,1)S(1)} %collective-permute-done.5.refs_3_), channel_id=1, source_target_pairs={{0,1},{2,0},{4,2},{6,4},{7,6},{5,7},{3,5},{1,3},{8,9},{10,8},{12,1... | collective-permute-start | bytes 393224 | tf_op jit(solution)/shard_map/ppermute | solution.py:141
  18.6 6.4 %collective-permute-start.13 = (bf16[144,512]{1,0:T(8,128)(2,1)S(1)}, bf16[144,512]{1,0:T(8,128)(2,1)S(1)}, u32[]{:S(2)}, u32[]{:S(2)}) collective-permute-start(bf16[144,512]{1,0:T(8,128)(2,1)S(1)} %collective-permute-done.11.refs_10_.refs_2_), channel_id=1, source_target_pairs={{0,2},{2,4},{4,6},{6,7},{7,5},{5,3},{3,1},{1,0},{8,10},{10,12},{12... | collective-permute-start | bytes 442376 | tf_op jit(solution)/shard_map/ppermute | solution.py:141
  21.1 5.6 %collective-permute-start.14 = (bf16[144,512]{1,0:T(8,128)(2,1)S(1)}, bf16[144,512]{1,0:T(8,128)(2,1)S(1)}, u32[]{:S(2)}, u32[]{:S(2)}) collective-permute-start(bf16[144,512]{1,0:T(8,128)(2,1)S(1)} %collective-permute-done.12.refs_11_.refs_3_), channel_id=1, source_target_pairs={{0,1},{2,0},{4,2},{6,4},{7,6},{5,7},{3,5},{1,3},{8,9},{10,8},{12,1... | collective-permute-start | bytes 442376 | tf_op jit(solution)/shard_map/ppermute | solution.py:141
  21.4 5.6 %collective-permute-start.3 = (bf16[64,512]{1,0:T(8,128)(2,1)S(1)}, bf16[64,512]{1,0:T(8,128)(2,1)S(1)}, u32[]{:S(2)}, u32[]{:S(2)}) collective-permute-start(bf16[64,512]{1,0:T(8,128)(2,1)S(1)} %slice.16), channel_id=1, source_target_pairs={{0,2},{2,4},{4,6},{6,7},{7,5},{5,3},{3,1},{1,0},{8,10},{10,12},{12... | collective-permute-start | bytes 196616 | tf_op jit(solution)/shard_map/ppermute | solution.py:141
  23.9 4.4 %collective-permute-start.7 = (bf16[64,512]{1,0:T(8,128)(2,1)S(1)}, bf16[64,512]{1,0:T(8,128)(2,1)S(1)}, u32[]{:S(2)}, u32[]{:S(2)}) collective-permute-start(bf16[64,512]{1,0:T(8,128)(2,1)S(1)} %slice.17), channel_id=1, source_target_pairs={{0,1},{2,0},{4,2},{6,4},{7,6},{5,7},{3,5},{1,3},{8,9},{10,8},{12,1... | collective-permute-start | bytes 196616 | tf_op jit(solution)/shard_map/ppermute | solution.py:141
  25.0 7.0 %collective-permute-start.15 = (bf16[64,512]{1,0:T(8,128)(2,1)S(1)}, bf16[64,512]{1,0:T(8,128)(2,1)S(1)}, u32[]{:S(2)}, u32[]{:S(2)}) collective-permute-start(bf16[64,512]{1,0:T(8,128)(2,1)S(1)} %slice.18), channel_id=1, source_target_pairs={{0,2},{2,4},{4,6},{6,7},{7,5},{5,3},{3,1},{1,0},{8,10},{10,12},{12... | collective-permute-start | bytes 196616 | tf_op jit(solution)/shard_map/ppermute | solution.py:141
  26.7 5.3 %collective-permute-start.16 = (bf16[64,512]{1,0:T(8,128)(2,1)S(1)}, bf16[64,512]{1,0:T(8,128)(2,1)S(1)}, u32[]{:S(2)}, u32[]{:S(2)}) collective-permute-start(bf16[64,512]{1,0:T(8,128)(2,1)S(1)} %slice.19), channel_id=1, source_target_pairs={{0,1},{2,0},{4,2},{6,4},{7,6},{5,7},{3,5},{1,3},{8,9},{10,8},{12,1... | collective-permute-start | bytes 196616 | tf_op jit(solution)/shard_map/ppermute | solution.py:141

commit v6 on v5

--- a/solution.py
+++ b/solution.py
@@ -40,6 +40,23 @@
     for (first, second), ref in zip(numbers[1:], block_refs):
         sorted_ref[first] = ref[:RUN, :]
         sorted_ref[second] = ref[RUN:TOK_DEV, :]
+
+
+def pack_kernel(pos_ref, query_ref, key_ref, value_ref, tagged_ref, own_ref, pos_buf, sems):
+    sources = [(pos_ref, pos_buf), (value_ref, tagged_ref.at[pl.ds(0, TOK_DEV), :])]
+    column = 0
+    for ref in (query_ref, key_ref, value_ref):
+        sources.append((ref, own_ref.at[:, pl.ds(column, ref.shape[1])]))
+        column += ref.shape[1]
+    copies = [pltpu.make_async_copy(source, target, sems.at[i]) for i, (source, target) in enumerate(sources)]
+    for copy in copies:
+        copy.start()
+    copies[0].wait()
+    tag = jnp.floor(pos_buf[...].astype(jnp.float32) * (1.0 / RUN)).astype(jnp.bfloat16)
+    for i in range(KEY_VALUE_HEADS):
+        tagged_ref[TOK_DEV:, i * TOK_DEV : (i + 1) * TOK_DEV] = jnp.broadcast_to(tag, (TAG_ROWS, TOK_DEV))
+    for copy in copies[1:]:
+        copy.wait()
 
 
 def bias_kernel(runs, pos_ref, *refs):
@@ -58,8 +75,8 @@
 
 def weights_kernel(runs, pos_ref, bias_ref, own_ref, *refs):
     blocks = runs // 2
-    key_refs, tagged_refs = refs[:blocks], refs[blocks:-4]
-    weights_ref, inverse_ref, sorted_ref, key_buf = refs[-4:]
+    key_refs, tagged_refs = refs[:blocks], refs[blocks:-3]
+    weights_ref, sorted_ref, key_buf = refs[-3:]
     reach = runs // 4
     span = (reach + 1) * RUN
     numbers = run_numbers(runs, pos_ref, tagged_refs)
@@ -67,7 +84,6 @@
     for number, ref in zip(numbers[-1], key_refs[-2:]):
         key_buf[number] = ref[...]
     sort_runs(numbers, own_ref, QUERY_COLUMNS + KV_COLUMNS, tagged_refs, sorted_ref)
-    ones = jnp.ones((span, HEAD_SIZE), jnp.bfloat16)
     scale = math.log2(math.e) / math.sqrt(HEAD_SIZE)
     for half in range(2):
         start = jnp.maximum(numbers[0][half] - reach, 0)
@@ -88,16 +104,14 @@
                 preferred_element_type=jnp.float32,
             )
             row_max = jnp.max(scores, axis=1, keepdims=True)
-            weights = jnp.exp2((scores - row_max) * scale).astype(jnp.bfloat16)
-            weights_ref[half * KEY_VALUE_HEADS + kv] = weights
-            total = jnp.dot(weights, ones, preferred_element_type=jnp.float32)
-            inverse_ref[half * KEY_VALUE_HEADS + kv] = 1.0 / total
-
-
-def values_kernel(runs, pos_ref, weights_ref, inverse_ref, sorted_ref, *refs):
+            weights_ref[half * KEY_VALUE_HEADS + kv] = jnp.exp2((scores - row_max) * scale).astype(jnp.bfloat16)
+
+
+def values_kernel(runs, pos_ref, weights_ref, sorted_ref, *refs):
     tagged_refs, last_refs, (out_ref, result_buf, out_sems) = refs[:-5], refs[-5:-3], refs[-3:]
     reach = runs // 4
     numbers = run_numbers(runs, pos_ref, tagged_refs)
+    ones = jnp.ones(((reach + 1) * RUN, HEAD_SIZE), jnp.bfloat16)
     copies = []
     for half in range(2):
         start = jnp.maximum(numbers[0][half] - reach, 0)
@@ -111,10 +125,10 @@
                 parts.append(part)
             summed = jnp.dot(
                 weights_ref[half * KEY_VALUE_HEADS + kv],
-                jnp.concatenate(parts, axis=0),
+                jnp.concatenate([jnp.concatenate(parts, axis=0), ones], axis=1),
                 preferred_element_type=jnp.float32,
             )
-            result = (summed * inverse_ref[half * KEY_VALUE_HEADS + kv]).astype(jnp.bfloat16)
+            result = (summed[:, :HEAD_SIZE] / summed[:, HEAD_SIZE:]).astype(jnp.bfloat16)
             for i in range(GROUP):
                 h = kv * GROUP + i
                 result_buf[half, :, h * HEAD_SIZE : (h + 1) * HEAD_SIZE] = result[i * RUN : (i + 1) * RUN]
@@ -140,25 +154,30 @@
                 pairs.append((s * places + ring[i], target))
         return lax.ppermute(block, ("section", "ctx"), pairs)
 
-    own = jnp.concatenate([queries[0], keys[0], values[0]], axis=1)
-
-    def around(block, early=None):
+    def around(block):
         ahead, back = shift(block, 1, 1), shift(block, 1, -1)
         held = [ahead, back]
-        if early is not None:
-            ahead, early = lax.optimization_barrier((ahead, early))
         for _ in range(2, places // 2):
             ahead, back = shift(ahead, 0, 1), shift(back, 0, -1)
             held.extend([ahead, back])
-        return held + [shift(ahead[:RUN], 0, 1), shift(back[RUN:TOK_DEV], 0, -1)], early
-
-    tag = jnp.broadcast_to((token_pos >> (RUN.bit_length() - 1)).astype(jnp.bfloat16)[None], (TAG_ROWS, TOK_DEV))
-    tag = jnp.pad(tag, ((0, 0), (0, KV_COLUMNS - TOK_DEV)))
-    all_keys, own = around(keys[0], own)
-    all_values, _ = around(jnp.concatenate([values[0], tag], axis=0))
+        return held + [shift(ahead[:RUN], 0, 1), shift(back[RUN:TOK_DEV], 0, -1)]
+
+    vmem, anywhere = pl.BlockSpec(memory_space=pltpu.VMEM), pl.BlockSpec(memory_space=pl.ANY)
+    tagged, own = pl.pallas_call(
+        pack_kernel,
+        out_shape=(
+            jax.ShapeDtypeStruct((TOK_DEV + TAG_ROWS, KV_COLUMNS), jnp.bfloat16),
+            jax.ShapeDtypeStruct((TOK_DEV, QUERY_COLUMNS + 2 * KV_COLUMNS), jnp.bfloat16),
+        ),
+        in_specs=[anywhere] * 4,
+        out_specs=(vmem,) * 2,
+        scratch_shapes=[pltpu.VMEM((1, TOK_DEV), jnp.int32), pltpu.SemaphoreType.DMA((5,))],
+        compiler_params=pltpu.CompilerParams(vmem_limit_bytes=58 * 1024 * 1024),
+        cost_estimate=pl.CostEstimate(flops=0, bytes_accessed=1 << 22, transcendentals=0),
+    )(token_pos[None], queries[0], keys[0], values[0])
+    all_keys, all_values = around(keys[0]), around(tagged)
     own = shift(own, 1, 0)
     pos = lax.optimization_barrier(jnp.concatenate([token_pos, segment]).astype(jnp.float32)[None])
-    vmem = pl.BlockSpec(memory_space=pltpu.VMEM)
     params = pltpu.CompilerParams(vmem_limit_bytes=(12 + runs // 4) * 1024 * 1024)
     before_mask = all_keys[-2:]
     bias = pl.pallas_call(
@@ -169,15 +188,14 @@
         compiler_params=pltpu.CompilerParams(vmem_limit_bytes=8 * 1024 * 1024),
         cost_estimate=pl.CostEstimate(flops=35 << 28, bytes_accessed=0, transcendentals=0),
     )(pos, *before_mask)
-    weights, inverse, sorted_values = pl.pallas_call(
+    weights, sorted_values = pl.pallas_call(
         functools.partial(weights_kernel, runs),
         out_shape=(
             jax.ShapeDtypeStruct((2 * KEY_VALUE_HEADS, GROUP * RUN, (runs // 4 + 1) * RUN), jnp.bfloat16),
-            jax.ShapeDtypeStruct((2 * KEY_VALUE_HEADS, GROUP * RUN, HEAD_SIZE), jnp.float32),
             jax.ShapeDtypeStruct((runs, RUN, KV_COLUMNS), jnp.bfloat16),
         ),
         in_specs=[vmem] * (3 + len(all_keys) + len(all_values[:-2])),
-        out_specs=(vmem,) * 3,
+        out_specs=(vmem,) * 2,
         scratch_shapes=[pltpu.VMEM((runs, RUN, KV_COLUMNS), jnp.bfloat16)],
         compiler_params=params,
         cost_estimate=pl.CostEstimate(flops=1 << 26, bytes_accessed=1 << 20, transcendentals=0),
@@ -185,15 +203,15 @@
     out = pl.pallas_call(
         functools.partial(values_kernel, runs),
         out_shape=jax.ShapeDtypeStruct((TOK_DEV, QUERY_COLUMNS), jnp.bfloat16),
-        in_specs=[vmem] * (4 + len(all_values)),
-        out_specs=pl.BlockSpec(memory_space=pl.ANY),
+        in_specs=[vmem] * (3 + len(all_values)),
+        out_specs=anywhere,
         scratch_shapes=[
             pltpu.VMEM((2, RUN, QUERY_COLUMNS), jnp.bfloat16),
             pltpu.SemaphoreType.DMA((2,)),
         ],
         compiler_params=params,
         cost_estimate=pl.CostEstimate(flops=1 << 26, bytes_accessed=1 << 20, transcendentals=0),
-    )(pos, weights, inverse, sorted_values, *all_values)
+    )(pos, weights, sorted_values, *all_values)
     return out[None]
 
 

time: 34.1 us -> 34.3 us (level)
  other arithmetic: 3.04 us -> 0.01 us
  waiting for transfers between devices: 6.12 us -> 9.13 us
  Pallas kernels: 5.62 us -> 7.03 us
  starting transfers between devices: 19 us -> 17.9 us
    ppermute x17, waiting for transfers between devices: 6.12 us -> 9.13 us  [shift(): return lax.ppermute(block, ('section', 'ctx'), pairs)]
    pallas_call x0 -> x1, Pallas kernels: none -> 2.51 us  [per_device(): pl.pallas_call(pack_kernel, out_shape=(jax.ShapeDtypeStruct((TOK_DEV + TA...]
    concatenate x2 -> x0, other arithmetic: 2.37 us -> none  [the longest x1 1.46 us: per_device(): own = jnp.concatenate([queries[0], keys[0], values[0]], axis=1)]
    pallas_call x1, Pallas kernels: 3.35 us -> 1.96 us  [per_device(): pl.pallas_call(functools.partial(weights_kernel, runs), out_shape=(jax.Sh...]
    ppermute x17, starting transfers between devices: 19 us -> 17.9 us  [shift(): return lax.ppermute(block, ('section', 'ctx'), pairs)]
    convert_element_type x1 -> x0, other arithmetic: 0.66 us -> none  [per_device(): (token_pos >> RUN.bit_length() - 1).astype(jnp.bfloat16)[None]]
  transfers between devices with their start and end apart: 17 -> 17, of which waited for: 6 -> 10; matrix products, arithmetic and copies ran while one was open for 9% -> 0% of each run, Pallas kernels for 11% -> 14%
where the time goes in v6:
time: 34.3 us; the launch traced here: 34.1 us
  starting transfers between devices  17.9 us (52%)
  waiting for transfers between devices  9.13 us (27%)
  Pallas kernels  7.03 us (20%)
    ppermute x17, starting transfers between devices, shift(): return lax.ppermute(block, ('section', 'ctx'), pairs)  17.9 us
    ppermute x17, waiting for transfers between devices, shift(): return lax.ppermute(block, ('section', 'ctx'), pairs)  9.13 us
    pallas_call x1, Pallas kernels, per_device(): pl.pallas_call(pack_kernel, out_shape=(jax.ShapeDtypeStruct((TOK_DEV + TA...  2.51 us
    pallas_call x1, Pallas kernels, per_device(): pl.pallas_call(functools.partial(values_kernel, runs), out_shape=jax.Shap...  2.22 us
    pallas_call x1, Pallas kernels, per_device(): pl.pallas_call(functools.partial(weights_kernel, runs), out_shape=(jax.Sh...  1.96 us
  transfers between devices with their start and end apart: 17, of which 10 were waited for; matrix products, arithmetic and copies ran while one was open for 0% of the time, Pallas kernels for 14%

profile of v6, /device:TPU:0, one launch (start us, length us, event | category | flops | bytes accessed | tf_op | source)
XLA Modules:
  0.0 34.1 jit_solution(18135799334975240347)
XLA Ops:
  0.0 0.0 copy-start.1
  0.0 0.0 copy-start
  0.0 2.5 %collective-permute-start = (bf16[128,512]{1,0:T(8,128)(2,1)}, bf16[128,512]{1,0:T(8,128)(2,1)S(1)}, u32[]{:S(2)}, u32[]{:S(2)}) collective-permute-start(bf16[128,512]{1,0:T(8,128)(2,1)} %bitcast.8), channel_id=1, source_target_pairs={{0,10},{2,12},{4,14},{6,15},{7,13},{5,11},{3,9},{1,8},{8,18},{10,2... | collective-permute-start | bytes 393224 | tf_op jit(solution)/shard_map/ppermute | solution.py:155
  2.5 1.7 %collective-permute-start.4 = (bf16[128,512]{1,0:T(8,128)(2,1)}, bf16[128,512]{1,0:T(8,128)(2,1)S(1)}, u32[]{:S(2)}, u32[]{:S(2)}) collective-permute-start(bf16[128,512]{1,0:T(8,128)(2,1)} %bitcast.9), channel_id=1, source_target_pairs={{0,9},{2,8},{4,10},{6,12},{7,14},{5,15},{3,13},{1,11},{8,17},{10,1... | collective-permute-start | bytes 393224 | tf_op jit(solution)/shard_map/ppermute | solution.py:155
  4.1 2.5 %shard_map.56 = (bf16[144,512]{1,0:T(8,128)(2,1)}, bf16[128,5120]{1,0:T(8,128)(2,1)}) custom-call(s32[1,128]{1,0:T(1,128)} %bitcast.12, bf16[128,4096]{1,0:T(8,128)(2,1)} %bitcast.6, bf16[128,512]{1,0:T(8,128)(2,1)} %bitcast.10, bf16[128,512]{1,0:T(8,128)(2,1)} %bitcast.7), custom_call_target="tpu_custom_call" | custom-call | bytes 4194304 | tf_op jit(solution)/shard_map/pallas_call | solution.py:166
  6.6 1.2 %collective-permute-start.9 = (bf16[144,512]{1,0:T(8,128)(2,1)}, bf16[144,512]{1,0:T(8,128)(2,1)S(1)}, u32[]{:S(2)}, u32[]{:S(2)}) collective-permute-start(bf16[144,512]{1,0:T(8,128)(2,1)} %get-tuple-element.10), channel_id=1, source_target_pairs={{0,10},{2,12},{4,14},{6,15},{7,13},{5,11},{3,9},{1,8},{8,18},{10,2... | collective-permute-start | bytes 442376 | tf_op jit(solution)/shard_map/ppermute | solution.py:155
  7.8 0.1 collective-permute-start.10
  7.9 0.0 collective-permute-done.refs_0_
  7.9 2.3 %collective-permute-start.1 = (bf16[128,512]{1,0:T(8,128)(2,1)S(1)}, bf16[128,512]{1,0:T(8,128)(2,1)S(1)}, u32[]{:S(2)}, u32[]{:S(2)}) collective-permute-start(bf16[128,512]{1,0:T(8,128)(2,1)S(1)} %collective-permute-done.refs_0_), channel_id=1, source_target_pairs={{0,2},{2,4},{4,6},{6,7},{7,5},{5,3},{3,1},{1,0},{8,10},{10,12},{12... | collective-permute-start | bytes 393224 | tf_op jit(solution)/shard_map/ppermute | solution.py:155
  10.2 0.0 collective-permute-done.4.refs_1_
  10.2 0.0 collective-permute-start.5
  10.2 0.0 collective-permute-start.8
  10.2 2.8 %collective-permute-done.9.refs_8_.refs_0_ = bf16[144,512]{1,0:T(8,128)(2,1)S(1)} collective-permute-done((bf16[144,512]{1,0:T(8,128)(2,1)}, bf16[144,512]{1,0:T(8,128)(2,1)S(1)}, u32[]{:S(2)}, u32[]{:S(2)}) %collective-permute-start.9) | collective-permute-done | bytes 147488 | tf_op jit(solution)/shard_map/ppermute | solution.py:155
  13.0 2.5 %collective-permute-start.11 = (bf16[144,512]{1,0:T(8,128)(2,1)S(1)}, bf16[144,512]{1,0:T(8,128)(2,1)S(1)}, u32[]{:S(2)}, u32[]{:S(2)}) collective-permute-start(bf16[144,512]{1,0:T(8,128)(2,1)S(1)} %collective-permute-done.9.refs_8_.refs_0_), channel_id=1, source_target_pairs={{0,2},{2,4},{4,6},{6,7},{7,5},{5,3},{3,1},{1,0},{8,10},{10,12},{12... | collective-permute-start | bytes 442376 | tf_op jit(solution)/shard_map/ppermute | solution.py:155
  15.5 0.0 collective-permute-done.10.refs_9_.refs_1_
  15.5 0.0 collective-permute-start.12
  15.6 0.4 %collective-permute-done.1.refs_2_ = bf16[128,512]{1,0:T(8,128)(2,1)S(1)} collective-permute-done((bf16[128,512]{1,0:T(8,128)(2,1)S(1)}, bf16[128,512]{1,0:T(8,128)(2,1)S(1)}, u32[]{:S(2)}, u32[]{:S(2)}) %collective-permute-start.1) | collective-permute-done | bytes 131104 | tf_op jit(solution)/shard_map/ppermute | solution.py:155
  16.0 1.6 %collective-permute-start.2 = (bf16[128,512]{1,0:T(8,128)(2,1)S(1)}, bf16[128,512]{1,0:T(8,128)(2,1)S(1)}, u32[]{:S(2)}, u32[]{:S(2)}) collective-permute-start(bf16[128,512]{1,0:T(8,128)(2,1)S(1)} %collective-permute-done.1.refs_2_), channel_id=1, source_target_pairs={{0,2},{2,4},{4,6},{6,7},{7,5},{5,3},{3,1},{1,0},{8,10},{10,12},{12... | collective-permute-start | bytes 393224 | tf_op jit(solution)/shard_map/ppermute | solution.py:155
  17.6 0.0 collective-permute-done.5.refs_3_
  17.6 0.4 %collective-permute-start.6 = (bf16[128,512]{1,0:T(8,128)(2,1)S(1)}, bf16[128,512]{1,0:T(8,128)(2,1)S(1)}, u32[]{:S(2)}, u32[]{:S(2)}) collective-permute-start(bf16[128,512]{1,0:T(8,128)(2,1)S(1)} %collective-permute-done.5.refs_3_), channel_id=1, source_target_pairs={{0,1},{2,0},{4,2},{6,4},{7,6},{5,7},{3,5},{1,3},{8,9},{10,8},{12,1... | collective-permute-start | bytes 393224 | tf_op jit(solution)/shard_map/ppermute | solution.py:155
  18.0 1.7 %collective-permute-done.11.refs_10_.refs_2_ = bf16[144,512]{1,0:T(8,128)(2,1)S(1)} collective-permute-done((bf16[144,512]{1,0:T(8,128)(2,1)S(1)}, bf16[144,512]{1,0:T(8,128)(2,1)S(1)}, u32[]{:S(2)}, u32[]{:S(2)}) %collective-permute-start.11) | collective-permute-done | bytes 147488 | tf_op jit(solution)/shard_map/ppermute | solution.py:155
  19.7 1.7 %collective-permute-start.13 = (bf16[144,512]{1,0:T(8,128)(2,1)S(1)}, bf16[144,512]{1,0:T(8,128)(2,1)S(1)}, u32[]{:S(2)}, u32[]{:S(2)}) collective-permute-start(bf16[144,512]{1,0:T(8,128)(2,1)S(1)} %collective-permute-done.11.refs_10_.refs_2_), channel_id=1, source_target_pairs={{0,2},{2,4},{4,6},{6,7},{7,5},{5,3},{3,1},{1,0},{8,10},{10,12},{12... | collective-permute-start | bytes 442376 | tf_op jit(solution)/shard_map/ppermute | solution.py:155
  21.4 0.4 %collective-permute-done.12.refs_11_.refs_3_ = bf16[144,512]{1,0:T(8,128)(2,1)S(1)} collective-permute-done((bf16[144,512]{1,0:T(8,128)(2,1)S(1)}, bf16[144,512]{1,0:T(8,128)(2,1)S(1)}, u32[]{:S(2)}, u32[]{:S(2)}) %collective-permute-start.12) | collective-permute-done | bytes 147488 | tf_op jit(solution)/shard_map/ppermute | solution.py:155
  21.8 0.4 %collective-permute-start.14 = (bf16[144,512]{1,0:T(8,128)(2,1)S(1)}, bf16[144,512]{1,0:T(8,128)(2,1)S(1)}, u32[]{:S(2)}, u32[]{:S(2)}) collective-permute-start(bf16[144,512]{1,0:T(8,128)(2,1)S(1)} %collective-permute-done.12.refs_11_.refs_3_), channel_id=1, source_target_pairs={{0,1},{2,0},{4,2},{6,4},{7,6},{5,7},{3,5},{1,3},{8,9},{10,8},{12,1... | collective-permute-start | bytes 442376 | tf_op jit(solution)/shard_map/ppermute | solution.py:155
  22.2 0.3 collective-permute-done.2.refs_4_
  22.6 1.6 %collective-permute-start.3 = (bf16[64,512]{1,0:T(8,128)(2,1)S(1)}, bf16[64,512]{1,0:T(8,128)(2,1)S(1)}, u32[]{:S(2)}, u32[]{:S(2)}) collective-permute-start(bf16[64,512]{1,0:T(8,128)(2,1)S(1)} %slice.16), channel_id=1, source_target_pairs={{0,2},{2,4},{4,6},{6,7},{7,5},{5,3},{3,1},{1,0},{8,10},{10,12},{12... | collective-permute-start | bytes 196616 | tf_op jit(solution)/shard_map/ppermute | solution.py:155
  24.2 0.3 collective-permute-done.6.refs_5_
  24.5 0.1 collective-permute-start.7
  24.7 0.0 copy-done.1
  24.7 0.0 copy-done
  24.7 1.4 %collective-permute-done.13.refs_12_.refs_4_ = bf16[144,512]{1,0:T(8,128)(2,1)S(1)} collective-permute-done((bf16[144,512]{1,0:T(8,128)(2,1)S(1)}, bf16[144,512]{1,0:T(8,128)(2,1)S(1)}, u32[]{:S(2)}, u32[]{:S(2)}) %collective-permute-start.13) | collective-permute-done | bytes 147488 | tf_op jit(solution)/shard_map/ppermute | solution.py:155
  26.1 1.2 %collective-permute-start.15 = (bf16[64,512]{1,0:T(8,128)(2,1)S(1)}, bf16[64,512]{1,0:T(8,128)(2,1)S(1)}, u32[]{:S(2)}, u32[]{:S(2)}) collective-permute-start(bf16[64,512]{1,0:T(8,128)(2,1)S(1)} %slice.18), channel_id=1, source_target_pairs={{0,2},{2,4},{4,6},{6,7},{7,5},{5,3},{3,1},{1,0},{8,10},{10,12},{12... | collective-permute-start | bytes 196616 | tf_op jit(solution)/shard_map/ppermute | solution.py:155
  27.4 0.3 collective-permute-done.14.refs_13_.refs_5_
  27.7 0.5 %collective-permute-start.16 = (bf16[64,512]{1,0:T(8,128)(2,1)S(1)}, bf16[64,512]{1,0:T(8,128)(2,1)S(1)}, u32[]{:S(2)}, u32[]{:S(2)}) collective-permute-start(bf16[64,512]{1,0:T(8,128)(2,1)S(1)} %slice.19), channel_id=1, source_target_pairs={{0,1},{2,0},{4,2},{6,4},{7,6},{5,7},{3,5},{1,3},{8,9},{10,8},{12,1... | collective-permute-start | bytes 196616 | tf_op jit(solution)/shard_map/ppermute | solution.py:155
  28.2 0.0 collective-permute-done.3.refs_0_.refs_6_
  28.2 1.2 %collective-permute-done.7.refs_1_.refs_7_ = bf16[64,512]{1,0:T(8,128)(2,1)S(1)} collective-permute-done((bf16[64,512]{1,0:T(8,128)(2,1)S(1)}, bf16[64,512]{1,0:T(8,128)(2,1)S(1)}, u32[]{:S(2)}, u32[]{:S(2)}) %collective-permute-start.7) | collective-permute-done | bytes 65568 | tf_op jit(solution)/shard_map/ppermute | solution.py:155
  29.4 0.3 shard_map.55.bias_ref
  29.8 0.0 collective-permute-done.8.own_ref
  29.8 2.0 %shard_map.57 = (bf16[8,512,320]{2,1,0:T(8,128)(2,1)S(1)}, bf16[16,64,512]{2,1,0:T(8,128)(2,1)S(1)}) custom-call(f32[1,1152]{1,0:T(1,128)S(1)} %add_convert_fusion.pos_ref, f32[2,64,320]{2,1,0:T(8,128)S(1)} %shard_map.55.bias_ref, bf16[128,5120]{1,0:T(8,128)(2,1)S(1)} %collective-permute-done.8.own_ref, bf16[128,512]{1,0:T(8,128)(2,1)S(1)} %collective-permute-done.refs_0_, ...), custom_call_target="tpu_custom_call" | custom-call | flops 67108864 | bytes 1048576 | tf_op jit(solution)/shard_map/pallas_call | solution.py:191
  31.7 0.0 collective-permute-done.15.refs_6_
  31.7 0.2 collective-permute-done.16.refs_7_
  31.9 2.2 %shard_map.58 = bf16[128,4096]{1,0:T(8,128)(2,1)} custom-call(f32[1,1152]{1,0:T(1,128)S(1)} %add_convert_fusion.pos_ref, bf16[8,512,320]{2,1,0:T(8,128)(2,1)S(1)} %get-tuple-element.11.weights_ref, bf16[16,64,512]{2,1,0:T(8,128)(2,1)S(1)} %get-tuple-element.12.sorted_ref, bf16[144,512]{1,0:T(8,128)(2,1)S(1)} %collective-permute-done.9.refs_8_.refs_0_, ...), custom_call_target="tpu_custom_call" | custom-call | flops 67108864 | bytes 1048576 | tf_op jit(solution)/shard_map/pallas_call | solution.py:203
  (5 shorter events, 0.0 us)
Async XLA Ops:
  0.0 24.7 %copy-start.1 = (s32[128]{0:T(128)S(1)}, s32[128]{0:T(128)}, u32[]{:S(2)}) copy-start(s32[128]{0:T(128)} %param.8) | copy-start | bytes 1540
  0.0 24.7 %copy-start = (s32[1024]{0:T(1024)S(1)}, s32[1024]{0:T(1024)}, u32[]{:S(2)}) copy-start(s32[1024]{0:T(1024)} %param.9) | copy-start | bytes 12292
  0.0 7.9 %collective-permute-start = (bf16[128,512]{1,0:T(8,128)(2,1)}, bf16[128,512]{1,0:T(8,128)(2,1)S(1)}, u32[]{:S(2)}, u32[]{:S(2)}) collective-permute-start(bf16[128,512]{1,0:T(8,128)(2,1)} %bitcast.8), channel_id=1, source_target_pairs={{0,10},{2,12},{4,14},{6,15},{7,13},{5,11},{3,9},{1,8},{8,18},{10,2... | collective-permute-start | bytes 393224 | tf_op jit(solution)/shard_map/ppermute | solution.py:155
  2.5 7.8 %collective-permute-start.4 = (bf16[128,512]{1,0:T(8,128)(2,1)}, bf16[128,512]{1,0:T(8,128)(2,1)S(1)}, u32[]{:S(2)}, u32[]{:S(2)}) collective-permute-start(bf16[128,512]{1,0:T(8,128)(2,1)} %bitcast.9), channel_id=1, source_target_pairs={{0,9},{2,8},{4,10},{6,12},{7,14},{5,15},{3,13},{1,11},{8,17},{10,1... | collective-permute-start | bytes 393224 | tf_op jit(solution)/shard_map/ppermute | solution.py:155
  6.6 6.4 %collective-permute-start.9 = (bf16[144,512]{1,0:T(8,128)(2,1)}, bf16[144,512]{1,0:T(8,128)(2,1)S(1)}, u32[]{:S(2)}, u32[]{:S(2)}) collective-permute-start(bf16[144,512]{1,0:T(8,128)(2,1)} %get-tuple-element.10), channel_id=1, source_target_pairs={{0,10},{2,12},{4,14},{6,15},{7,13},{5,11},{3,9},{1,8},{8,18},{10,2... | collective-permute-start | bytes 442376 | tf_op jit(solution)/shard_map/ppermute | solution.py:155
  7.8 7.7 %collective-permute-start.10 = (bf16[144,512]{1,0:T(8,128)(2,1)}, bf16[144,512]{1,0:T(8,128)(2,1)S(1)}, u32[]{:S(2)}, u32[]{:S(2)}) collective-permute-start(bf16[144,512]{1,0:T(8,128)(2,1)} %get-tuple-element.10), channel_id=1, source_target_pairs={{0,9},{2,8},{4,10},{6,12},{7,14},{5,15},{3,13},{1,11},{8,17},{10,1... | collective-permute-start | bytes 442376 | tf_op jit(solution)/shard_map/ppermute | solution.py:155
  7.9 8.1 %collective-permute-start.1 = (bf16[128,512]{1,0:T(8,128)(2,1)S(1)}, bf16[128,512]{1,0:T(8,128)(2,1)S(1)}, u32[]{:S(2)}, u32[]{:S(2)}) collective-permute-start(bf16[128,512]{1,0:T(8,128)(2,1)S(1)} %collective-permute-done.refs_0_), channel_id=1, source_target_pairs={{0,2},{2,4},{4,6},{6,7},{7,5},{5,3},{3,1},{1,0},{8,10},{10,12},{12... | collective-permute-start | bytes 393224 | tf_op jit(solution)/shard_map/ppermute | solution.py:155
  10.2 7.4 %collective-permute-start.5 = (bf16[128,512]{1,0:T(8,128)(2,1)S(1)}, bf16[128,512]{1,0:T(8,128)(2,1)S(1)}, u32[]{:S(2)}, u32[]{:S(2)}) collective-permute-start(bf16[128,512]{1,0:T(8,128)(2,1)S(1)} %collective-permute-done.4.refs_1_), channel_id=1, source_target_pairs={{0,1},{2,0},{4,2},{6,4},{7,6},{5,7},{3,5},{1,3},{8,9},{10,8},{12,1... | collective-permute-start | bytes 393224 | tf_op jit(solution)/shard_map/ppermute | solution.py:155
  10.2 19.5 %collective-permute-start.8 = (bf16[128,5120]{1,0:T(8,128)(2,1)}, bf16[128,5120]{1,0:T(8,128)(2,1)S(1)}, u32[]{:S(2)}, u32[]{:S(2)}) collective-permute-start(bf16[128,5120]{1,0:T(8,128)(2,1)} %get-tuple-element.9), channel_id=1, source_target_pairs={{0,8},{2,10},{4,12},{6,14},{7,15},{5,13},{3,11},{1,9},{8,16},{10,1... | collective-permute-start | bytes 3932168 | tf_op jit(solution)/shard_map/ppermute | solution.py:155
  13.0 6.7 %collective-permute-start.11 = (bf16[144,512]{1,0:T(8,128)(2,1)S(1)}, bf16[144,512]{1,0:T(8,128)(2,1)S(1)}, u32[]{:S(2)}, u32[]{:S(2)}) collective-permute-start(bf16[144,512]{1,0:T(8,128)(2,1)S(1)} %collective-permute-done.9.refs_8_.refs_0_), channel_id=1, source_target_pairs={{0,2},{2,4},{4,6},{6,7},{7,5},{5,3},{3,1},{1,0},{8,10},{10,12},{12... | collective-permute-start | bytes 442376 | tf_op jit(solution)/shard_map/ppermute | solution.py:155
  15.5 6.3 %collective-permute-start.12 = (bf16[144,512]{1,0:T(8,128)(2,1)S(1)}, bf16[144,512]{1,0:T(8,128)(2,1)S(1)}, u32[]{:S(2)}, u32[]{:S(2)}) collective-permute-start(bf16[144,512]{1,0:T(8,128)(2,1)S(1)} %collective-permute-done.10.refs_9_.refs_1_), channel_id=1, source_target_pairs={{0,1},{2,0},{4,2},{6,4},{7,6},{5,7},{3,5},{1,3},{8,9},{10,8},{12,1... | collective-permute-start | bytes 442376 | tf_op jit(solution)/shard_map/ppermute | solution.py:155
  16.0 6.6 %collective-permute-start.2 = (bf16[128,512]{1,0:T(8,128)(2,1)S(1)}, bf16[128,512]{1,0:T(8,128)(2,1)S(1)}, u32[]{:S(2)}, u32[]{:S(2)}) collective-permute-start(bf16[128,512]{1,0:T(8,128)(2,1)S(1)} %collective-permute-done.1.refs_2_), channel_id=1, source_target_pairs={{0,2},{2,4},{4,6},{6,7},{7,5},{5,3},{3,1},{1,0},{8,10},{10,12},{12... | collective-permute-start | bytes 393224 | tf_op jit(solution)/shard_map/ppermute | solution.py:155
  17.6 6.9 %collective-permute-start.6 = (bf16[128,512]{1,0:T(8,128)(2,1)S(1)}, bf16[128,512]{1,0:T(8,128)(2,1)S(1)}, u32[]{:S(2)}, u32[]{:S(2)}) collective-permute-start(bf16[128,512]{1,0:T(8,128)(2,1)S(1)} %collective-permute-done.5.refs_3_), channel_id=1, source_target_pairs={{0,1},{2,0},{4,2},{6,4},{7,6},{5,7},{3,5},{1,3},{8,9},{10,8},{12,1... | collective-permute-start | bytes 393224 | tf_op jit(solution)/shard_map/ppermute | solution.py:155
  19.7 6.4 %collective-permute-start.13 = (bf16[144,512]{1,0:T(8,128)(2,1)S(1)}, bf16[144,512]{1,0:T(8,128)(2,1)S(1)}, u32[]{:S(2)}, u32[]{:S(2)}) collective-permute-start(bf16[144,512]{1,0:T(8,128)(2,1)S(1)} %collective-permute-done.11.refs_10_.refs_2_), channel_id=1, source_target_pairs={{0,2},{2,4},{4,6},{6,7},{7,5},{5,3},{3,1},{1,0},{8,10},{10,12},{12... | collective-permute-start | bytes 442376 | tf_op jit(solution)/shard_map/ppermute | solution.py:155
  21.8 5.8 %collective-permute-start.14 = (bf16[144,512]{1,0:T(8,128)(2,1)S(1)}, bf16[144,512]{1,0:T(8,128)(2,1)S(1)}, u32[]{:S(2)}, u32[]{:S(2)}) collective-permute-start(bf16[144,512]{1,0:T(8,128)(2,1)S(1)} %collective-permute-done.12.refs_11_.refs_3_), channel_id=1, source_target_pairs={{0,1},{2,0},{4,2},{6,4},{7,6},{5,7},{3,5},{1,3},{8,9},{10,8},{12,1... | collective-permute-start | bytes 442376 | tf_op jit(solution)/shard_map/ppermute | solution.py:155
  22.6 5.6 %collective-permute-start.3 = (bf16[64,512]{1,0:T(8,128)(2,1)S(1)}, bf16[64,512]{1,0:T(8,128)(2,1)S(1)}, u32[]{:S(2)}, u32[]{:S(2)}) collective-permute-start(bf16[64,512]{1,0:T(8,128)(2,1)S(1)} %slice.16), channel_id=1, source_target_pairs={{0,2},{2,4},{4,6},{6,7},{7,5},{5,3},{3,1},{1,0},{8,10},{10,12},{12... | collective-permute-start | bytes 196616 | tf_op jit(solution)/shard_map/ppermute | solution.py:155
  24.5 4.9 %collective-permute-start.7 = (bf16[64,512]{1,0:T(8,128)(2,1)S(1)}, bf16[64,512]{1,0:T(8,128)(2,1)S(1)}, u32[]{:S(2)}, u32[]{:S(2)}) collective-permute-start(bf16[64,512]{1,0:T(8,128)(2,1)S(1)} %slice.17), channel_id=1, source_target_pairs={{0,1},{2,0},{4,2},{6,4},{7,6},{5,7},{3,5},{1,3},{8,9},{10,8},{12,1... | collective-permute-start | bytes 196616 | tf_op jit(solution)/shard_map/ppermute | solution.py:155
  26.1 5.6 %collective-permute-start.15 = (bf16[64,512]{1,0:T(8,128)(2,1)S(1)}, bf16[64,512]{1,0:T(8,128)(2,1)S(1)}, u32[]{:S(2)}, u32[]{:S(2)}) collective-permute-start(bf16[64,512]{1,0:T(8,128)(2,1)S(1)} %slice.18), channel_id=1, source_target_pairs={{0,2},{2,4},{4,6},{6,7},{7,5},{5,3},{3,1},{1,0},{8,10},{10,12},{12... | collective-permute-start | bytes 196616 | tf_op jit(solution)/shard_map/ppermute | solution.py:155
  27.7 4.3 %collective-permute-start.16 = (bf16[64,512]{1,0:T(8,128)(2,1)S(1)}, bf16[64,512]{1,0:T(8,128)(2,1)S(1)}, u32[]{:S(2)}, u32[]{:S(2)}) collective-permute-start(bf16[64,512]{1,0:T(8,128)(2,1)S(1)} %slice.19), channel_id=1, source_target_pairs={{0,1},{2,0},{4,2},{6,4},{7,6},{5,7},{3,5},{1,3},{8,9},{10,8},{12,1... | collective-permute-start | bytes 196616 | tf_op jit(solution)/shard_map/ppermute | solution.py:155

commit v7 on v6

--- a/solution.py
+++ b/solution.py
@@ -40,23 +40,6 @@
     for (first, second), ref in zip(numbers[1:], block_refs):
         sorted_ref[first] = ref[:RUN, :]
         sorted_ref[second] = ref[RUN:TOK_DEV, :]
-
-
-def pack_kernel(pos_ref, query_ref, key_ref, value_ref, tagged_ref, own_ref, pos_buf, sems):
-    sources = [(pos_ref, pos_buf), (value_ref, tagged_ref.at[pl.ds(0, TOK_DEV), :])]
-    column = 0
-    for ref in (query_ref, key_ref, value_ref):
-        sources.append((ref, own_ref.at[:, pl.ds(column, ref.shape[1])]))
-        column += ref.shape[1]
-    copies = [pltpu.make_async_copy(source, target, sems.at[i]) for i, (source, target) in enumerate(sources)]
-    for copy in copies:
-        copy.start()
-    copies[0].wait()
-    tag = jnp.floor(pos_buf[...].astype(jnp.float32) * (1.0 / RUN)).astype(jnp.bfloat16)
-    for i in range(KEY_VALUE_HEADS):
-        tagged_ref[TOK_DEV:, i * TOK_DEV : (i + 1) * TOK_DEV] = jnp.broadcast_to(tag, (TAG_ROWS, TOK_DEV))
-    for copy in copies[1:]:
-        copy.wait()
 
 
 def bias_kernel(runs, pos_ref, *refs):
@@ -162,23 +145,14 @@
             held.extend([ahead, back])
         return held + [shift(ahead[:RUN], 0, 1), shift(back[RUN:TOK_DEV], 0, -1)]
 
-    vmem, anywhere = pl.BlockSpec(memory_space=pltpu.VMEM), pl.BlockSpec(memory_space=pl.ANY)
-    tagged, own = pl.pallas_call(
-        pack_kernel,
-        out_shape=(
-            jax.ShapeDtypeStruct((TOK_DEV + TAG_ROWS, KV_COLUMNS), jnp.bfloat16),
-            jax.ShapeDtypeStruct((TOK_DEV, QUERY_COLUMNS + 2 * KV_COLUMNS), jnp.bfloat16),
-        ),
-        in_specs=[anywhere] * 4,
-        out_specs=(vmem,) * 2,
-        scratch_shapes=[pltpu.VMEM((1, TOK_DEV), jnp.int32), pltpu.SemaphoreType.DMA((5,))],
-        compiler_params=pltpu.CompilerParams(vmem_limit_bytes=58 * 1024 * 1024),
-        cost_estimate=pl.CostEstimate(flops=0, bytes_accessed=1 << 22, transcendentals=0),
-    )(token_pos[None], queries[0], keys[0], values[0])
+    own = shift(jnp.concatenate([queries[0], keys[0], values[0]], axis=1), 1, 0)
+    tag = jnp.broadcast_to((token_pos >> (RUN.bit_length() - 1)).astype(jnp.bfloat16)[None], (TAG_ROWS, TOK_DEV))
+    tag = jnp.pad(tag, ((0, 0), (0, KV_COLUMNS - TOK_DEV)))
+    tagged = jnp.concatenate([values[0], tag], axis=0)
     all_keys, all_values = around(keys[0]), around(tagged)
-    own = shift(own, 1, 0)
     pos = lax.optimization_barrier(jnp.concatenate([token_pos, segment]).astype(jnp.float32)[None])
     params = pltpu.CompilerParams(vmem_limit_bytes=(12 + runs // 4) * 1024 * 1024)
+    vmem = pl.BlockSpec(memory_space=pltpu.VMEM)
     before_mask = all_keys[-2:]
     bias = pl.pallas_call(
         functools.partial(bias_kernel, runs),
@@ -204,7 +178,7 @@
         functools.partial(values_kernel, runs),
         out_shape=jax.ShapeDtypeStruct((TOK_DEV, QUERY_COLUMNS), jnp.bfloat16),
         in_specs=[vmem] * (3 + len(all_values)),
-        out_specs=anywhere,
+        out_specs=pl.BlockSpec(memory_space=pl.ANY),
         scratch_shapes=[
             pltpu.VMEM((2, RUN, QUERY_COLUMNS), jnp.bfloat16),
             pltpu.SemaphoreType.DMA((2,)),

time: 34.3 us -> 34 us (level)
  waiting for transfers between devices: 9.13 us -> 5.86 us
  other arithmetic: 0.01 us -> 3.04 us
  Pallas kernels: 7.03 us -> 4.51 us
  starting transfers between devices: 17.9 us -> 20.3 us
    ppermute x17, waiting for transfers between devices: 9.13 us -> 5.86 us  [shift(): return lax.ppermute(block, ('section', 'ctx'), pairs)]
    pallas_call x1 -> x0, Pallas kernels: 2.51 us -> none  [per_device(): pl.pallas_call(pack_kernel, out_shape=(jax.ShapeDtypeStruct((TOK_DEV + TA...]
    ppermute x17, starting transfers between devices: 17.9 us -> 20.3 us  [shift(): return lax.ppermute(block, ('section', 'ctx'), pairs)]
    concatenate x0 -> x2, other arithmetic: none -> 2.37 us  [the longest x1 1.46 us: per_device(): own = shift(jnp.concatenate([queries[0], keys[0], values[0]], axis=1), 1, 0)]
    convert_element_type x0 -> x1, other arithmetic: none -> 0.66 us  [per_device(): (token_pos >> RUN.bit_length() - 1).astype(jnp.bfloat16)[None]]
  transfers between devices with their start and end apart: 17 -> 17, of which waited for: 10 -> 8; matrix products, arithmetic and copies ran while one was open for 0% -> 9% of each run, Pallas kernels for 14% -> 7%
where the time goes in v7:
time: 34 us; the launch traced here: 33.9 us
  starting transfers between devices  20.3 us (60%)
  waiting for transfers between devices  5.86 us (17%)
  Pallas kernels  4.51 us (13%)
  other arithmetic  3.04 us (9%)
    ppermute x17, starting transfers between devices, shift(): return lax.ppermute(block, ('section', 'ctx'), pairs)  20.3 us
    ppermute x17, waiting for transfers between devices, shift(): return lax.ppermute(block, ('section', 'ctx'), pairs)  5.86 us
    pallas_call x1, Pallas kernels, per_device(): pl.pallas_call(functools.partial(values_kernel, runs), out_shape=jax.Shap...  2.22 us
    pallas_call x1, Pallas kernels, per_device(): pl.pallas_call(functools.partial(weights_kernel, runs), out_shape=(jax.Sh...  1.95 us
    concatenate x1, other arithmetic, per_device(): own = shift(jnp.concatenate([queries[0], keys[0], values[0]], axis=1), 1, 0)  1.46 us
    concatenate x1, other arithmetic, per_device(): tagged = jnp.concatenate([values[0], tag], axis=0)  0.91 us
  transfers between devices with their start and end apart: 17, of which 8 were waited for; matrix products, arithmetic and copies ran while one was open for 9% of the time, Pallas kernels for 7%

profile of v7, /device:TPU:0, one launch (start us, length us, event | category | flops | bytes accessed | tf_op | source)
XLA Modules:
  0.0 33.9 jit_solution(5444281083717777015)
XLA Ops:
  0.0 0.0 copy-start.1
  0.0 0.0 copy-start
  0.0 2.5 %collective-permute-start = (bf16[128,512]{1,0:T(8,128)(2,1)}, bf16[128,512]{1,0:T(8,128)(2,1)S(1)}, u32[]{:S(2)}, u32[]{:S(2)}) collective-permute-start(bf16[128,512]{1,0:T(8,128)(2,1)} %bitcast.9), channel_id=1, source_target_pairs={{0,10},{2,12},{4,14},{6,15},{7,13},{5,11},{3,9},{1,8},{8,18},{10,2... | collective-permute-start | bytes 393224 | tf_op jit(solution)/shard_map/ppermute | solution.py:138
  2.5 1.7 %collective-permute-start.4 = (bf16[128,512]{1,0:T(8,128)(2,1)}, bf16[128,512]{1,0:T(8,128)(2,1)S(1)}, u32[]{:S(2)}, u32[]{:S(2)}) collective-permute-start(bf16[128,512]{1,0:T(8,128)(2,1)} %bitcast.10), channel_id=1, source_target_pairs={{0,9},{2,8},{4,10},{6,12},{7,14},{5,15},{3,13},{1,11},{8,17},{10,1... | collective-permute-start | bytes 393224 | tf_op jit(solution)/shard_map/ppermute | solution.py:138
  4.1 0.7 %shift-right-arithmetic_convert_fusion = bf16[128]{0:T(256)(128)(2,1)S(1)} fusion(s32[128]{0:T(128)} %param.8), kind=kLoop, calls=%fused_computation.3 | loop fusion | flops 256 | bytes 768 | tf_op jit(solution)/shard_map/convert_element_type | solution.py:149
  4.8 0.9 %pad_maximum_fusion.1 = bf16[144,512]{1,0:T(8,128)(2,1)S(1)} fusion(bf16[16,512]{1,0:T(8,128)(2,1)S(1)} %pad.7, bf16[128,512]{1,0:T(8,128)(2,1)} %bitcast.7), kind=kLoop, calls=%fused_computation.1 | loop fusion | flops 294912 | bytes 294912 | tf_op jit(solution)/shard_map/concatenate | solution.py:151
  5.7 1.2 %collective-permute-start.9 = (bf16[144,512]{1,0:T(8,128)(2,1)S(1)}, bf16[144,512]{1,0:T(8,128)(2,1)S(1)}, u32[]{:S(2)}, u32[]{:S(2)}) collective-permute-start(bf16[144,512]{1,0:T(8,128)(2,1)S(1)} %pad_maximum_fusion.1), channel_id=1, source_target_pairs={{0,10},{2,12},{4,14},{6,15},{7,13},{5,11},{3,9},{1,8},{8,18},{10,2... | collective-permute-start | bytes 442376 | tf_op jit(solution)/shard_map/ppermute | solution.py:138
  6.9 0.1 collective-permute-start.10
  7.0 0.0 collective-permute-done.refs_0_
  7.0 3.3 %collective-permute-start.1 = (bf16[128,512]{1,0:T(8,128)(2,1)S(1)}, bf16[128,512]{1,0:T(8,128)(2,1)S(1)}, u32[]{:S(2)}, u32[]{:S(2)}) collective-permute-start(bf16[128,512]{1,0:T(8,128)(2,1)S(1)} %collective-permute-done.refs_0_), channel_id=1, source_target_pairs={{0,2},{2,4},{4,6},{6,7},{7,5},{5,3},{3,1},{1,0},{8,10},{10,12},{12... | collective-permute-start | bytes 393224 | tf_op jit(solution)/shard_map/ppermute | solution.py:138
  10.2 0.0 collective-permute-done.4.refs_1_
  10.2 0.0 collective-permute-start.5
  10.2 1.5 %pad_maximum_fusion = bf16[128,5120]{1,0:T(8,128)(2,1)S(1)} fusion(bf16[128,512]{1,0:T(8,128)(2,1)} %bitcast.8, bf16[128,512]{1,0:T(8,128)(2,1)} %bitcast.11, bf16[128,4096]{1,0:T(8,128)(2,1)} %bitcast.6), kind=kLoop, calls=%fused_computation | loop fusion | flops 3932160 | bytes 2621440 | tf_op jit(solution)/shard_map/concatenate | solution.py:148
  11.7 0.1 collective-permute-start.8
  11.8 0.1 collective-permute-done.9.refs_8_.refs_0_
  11.9 2.4 %collective-permute-start.11 = (bf16[144,512]{1,0:T(8,128)(2,1)S(1)}, bf16[144,512]{1,0:T(8,128)(2,1)S(1)}, u32[]{:S(2)}, u32[]{:S(2)}) collective-permute-start(bf16[144,512]{1,0:T(8,128)(2,1)S(1)} %collective-permute-done.9.refs_8_.refs_0_), channel_id=1, source_target_pairs={{0,2},{2,4},{4,6},{6,7},{7,5},{5,3},{3,1},{1,0},{8,10},{10,12},{12... | collective-permute-start | bytes 442376 | tf_op jit(solution)/shard_map/ppermute | solution.py:138
  14.3 0.0 collective-permute-done.10.refs_9_.refs_1_
  14.3 0.0 collective-permute-start.12
  14.3 0.5 %collective-permute-done.1.refs_2_ = bf16[128,512]{1,0:T(8,128)(2,1)S(1)} collective-permute-done((bf16[128,512]{1,0:T(8,128)(2,1)S(1)}, bf16[128,512]{1,0:T(8,128)(2,1)S(1)}, u32[]{:S(2)}, u32[]{:S(2)}) %collective-permute-start.1) | collective-permute-done | bytes 131104 | tf_op jit(solution)/shard_map/ppermute | solution.py:138
  14.9 1.5 %collective-permute-start.2 = (bf16[128,512]{1,0:T(8,128)(2,1)S(1)}, bf16[128,512]{1,0:T(8,128)(2,1)S(1)}, u32[]{:S(2)}, u32[]{:S(2)}) collective-permute-start(bf16[128,512]{1,0:T(8,128)(2,1)S(1)} %collective-permute-done.1.refs_2_), channel_id=1, source_target_pairs={{0,2},{2,4},{4,6},{6,7},{7,5},{5,3},{3,1},{1,0},{8,10},{10,12},{12... | collective-permute-start | bytes 393224 | tf_op jit(solution)/shard_map/ppermute | solution.py:138
  16.4 0.0 collective-permute-done.5.refs_3_
  16.4 0.5 %collective-permute-start.6 = (bf16[128,512]{1,0:T(8,128)(2,1)S(1)}, bf16[128,512]{1,0:T(8,128)(2,1)S(1)}, u32[]{:S(2)}, u32[]{:S(2)}) collective-permute-start(bf16[128,512]{1,0:T(8,128)(2,1)S(1)} %collective-permute-done.5.refs_3_), channel_id=1, source_target_pairs={{0,1},{2,0},{4,2},{6,4},{7,6},{5,7},{3,5},{1,3},{8,9},{10,8},{12,1... | collective-permute-start | bytes 393224 | tf_op jit(solution)/shard_map/ppermute | solution.py:138
  16.9 1.7 %collective-permute-done.11.refs_10_.refs_2_ = bf16[144,512]{1,0:T(8,128)(2,1)S(1)} collective-permute-done((bf16[144,512]{1,0:T(8,128)(2,1)S(1)}, bf16[144,512]{1,0:T(8,128)(2,1)S(1)}, u32[]{:S(2)}, u32[]{:S(2)}) %collective-permute-start.11) | collective-permute-done | bytes 147488 | tf_op jit(solution)/shard_map/ppermute | solution.py:138
  18.6 2.3 %collective-permute-start.13 = (bf16[144,512]{1,0:T(8,128)(2,1)S(1)}, bf16[144,512]{1,0:T(8,128)(2,1)S(1)}, u32[]{:S(2)}, u32[]{:S(2)}) collective-permute-start(bf16[144,512]{1,0:T(8,128)(2,1)S(1)} %collective-permute-done.11.refs_10_.refs_2_), channel_id=1, source_target_pairs={{0,2},{2,4},{4,6},{6,7},{7,5},{5,3},{3,1},{1,0},{8,10},{10,12},{12... | collective-permute-start | bytes 442376 | tf_op jit(solution)/shard_map/ppermute | solution.py:138
  21.0 0.0 collective-permute-done.12.refs_11_.refs_3_
  21.0 0.0 collective-permute-start.14
  21.0 0.4 %collective-permute-done.2.refs_4_ = bf16[128,512]{1,0:T(8,128)(2,1)S(1)} collective-permute-done((bf16[128,512]{1,0:T(8,128)(2,1)S(1)}, bf16[128,512]{1,0:T(8,128)(2,1)S(1)}, u32[]{:S(2)}, u32[]{:S(2)}) %collective-permute-start.2) | collective-permute-done | bytes 131104 | tf_op jit(solution)/shard_map/ppermute | solution.py:138
  21.4 2.3 %collective-permute-start.3 = (bf16[64,512]{1,0:T(8,128)(2,1)S(1)}, bf16[64,512]{1,0:T(8,128)(2,1)S(1)}, u32[]{:S(2)}, u32[]{:S(2)}) collective-permute-start(bf16[64,512]{1,0:T(8,128)(2,1)S(1)} %slice.16), channel_id=1, source_target_pairs={{0,2},{2,4},{4,6},{6,7},{7,5},{5,3},{3,1},{1,0},{8,10},{10,12},{12... | collective-permute-start | bytes 196616 | tf_op jit(solution)/shard_map/ppermute | solution.py:138
  23.8 0.0 collective-permute-done.6.refs_5_
  23.8 0.1 collective-permute-start.7
  23.9 0.0 copy-done.1
  23.9 0.0 copy-done
  23.9 1.1 %collective-permute-done.13.refs_12_.refs_4_ = bf16[144,512]{1,0:T(8,128)(2,1)S(1)} collective-permute-done((bf16[144,512]{1,0:T(8,128)(2,1)S(1)}, bf16[144,512]{1,0:T(8,128)(2,1)S(1)}, u32[]{:S(2)}, u32[]{:S(2)}) %collective-permute-start.13) | collective-permute-done | bytes 147488 | tf_op jit(solution)/shard_map/ppermute | solution.py:138
  25.0 2.4 %collective-permute-start.15 = (bf16[64,512]{1,0:T(8,128)(2,1)S(1)}, bf16[64,512]{1,0:T(8,128)(2,1)S(1)}, u32[]{:S(2)}, u32[]{:S(2)}) collective-permute-start(bf16[64,512]{1,0:T(8,128)(2,1)S(1)} %slice.18), channel_id=1, source_target_pairs={{0,2},{2,4},{4,6},{6,7},{7,5},{5,3},{3,1},{1,0},{8,10},{10,12},{12... | collective-permute-start | bytes 196616 | tf_op jit(solution)/shard_map/ppermute | solution.py:138
  27.3 0.0 collective-permute-done.14.refs_13_.refs_5_
  27.3 0.1 collective-permute-start.16
  27.4 0.0 collective-permute-done.3.refs_0_.refs_6_
  27.4 0.9 %collective-permute-done.7.refs_1_.refs_7_ = bf16[64,512]{1,0:T(8,128)(2,1)S(1)} collective-permute-done((bf16[64,512]{1,0:T(8,128)(2,1)S(1)}, bf16[64,512]{1,0:T(8,128)(2,1)S(1)}, u32[]{:S(2)}, u32[]{:S(2)}) %collective-permute-start.7) | collective-permute-done | bytes 65568 | tf_op jit(solution)/shard_map/ppermute | solution.py:138
  28.3 0.3 %shard_map.55.bias_ref = f32[2,64,320]{2,1,0:T(8,128)S(1)} custom-call(f32[1,1152]{1,0:T(1,128)S(1)} %add_convert_fusion.pos_ref, bf16[64,512]{1,0:T(8,128)(2,1)S(1)} %collective-permute-done.3.refs_0_.refs_6_, bf16[64,512]{1,0:T(8,128)(2,1)S(1)} %collective-permute-done.7.refs_1_.refs_7_), custom_call_target="tpu_custom_call" | custom-call | flops 9395240960 | tf_op jit(solution)/shard_map/pallas_call | solution.py:157
  28.6 0.1 collective-permute-done.8.own_ref
  28.8 1.9 %shard_map.56 = (bf16[8,512,320]{2,1,0:T(8,128)(2,1)S(1)}, bf16[16,64,512]{2,1,0:T(8,128)(2,1)S(1)}) custom-call(f32[1,1152]{1,0:T(1,128)S(1)} %add_convert_fusion.pos_ref, f32[2,64,320]{2,1,0:T(8,128)S(1)} %shard_map.55.bias_ref, bf16[128,5120]{1,0:T(8,128)(2,1)S(1)} %collective-permute-done.8.own_ref, bf16[128,512]{1,0:T(8,128)(2,1)S(1)} %collective-permute-done.refs_0_, ...), custom_call_target="tpu_custom_call" | custom-call | flops 67108864 | bytes 1048576 | tf_op jit(solution)/shard_map/pallas_call | solution.py:165
  30.7 0.0 collective-permute-done.15.refs_6_
  30.8 0.9 %collective-permute-done.16.refs_7_ = bf16[64,512]{1,0:T(8,128)(2,1)S(1)} collective-permute-done((bf16[64,512]{1,0:T(8,128)(2,1)S(1)}, bf16[64,512]{1,0:T(8,128)(2,1)S(1)}, u32[]{:S(2)}, u32[]{:S(2)}) %collective-permute-start.16) | collective-permute-done | bytes 65568 | tf_op jit(solution)/shard_map/ppermute | solution.py:138
  31.7 2.2 %shard_map.57 = bf16[128,4096]{1,0:T(8,128)(2,1)} custom-call(f32[1,1152]{1,0:T(1,128)S(1)} %add_convert_fusion.pos_ref, bf16[8,512,320]{2,1,0:T(8,128)(2,1)S(1)} %get-tuple-element.7.weights_ref, bf16[16,64,512]{2,1,0:T(8,128)(2,1)S(1)} %get-tuple-element.8.sorted_ref, bf16[144,512]{1,0:T(8,128)(2,1)S(1)} %collective-permute-done.9.refs_8_.refs_0_, ...), custom_call_target="tpu_custom_call" | custom-call | flops 67108864 | bytes 1048576 | tf_op jit(solution)/shard_map/pallas_call | solution.py:177
  (7 shorter events, 0.0 us)
Async XLA Ops:
  0.0 23.9 %copy-start.1 = (s32[128]{0:T(128)S(1)}, s32[128]{0:T(128)}, u32[]{:S(2)}) copy-start(s32[128]{0:T(128)} %param.8) | copy-start | bytes 1540
  0.0 23.9 %copy-start = (s32[1024]{0:T(1024)S(1)}, s32[1024]{0:T(1024)}, u32[]{:S(2)}) copy-start(s32[1024]{0:T(1024)} %param.9) | copy-start | bytes 12292
  0.0 7.0 %collective-permute-start = (bf16[128,512]{1,0:T(8,128)(2,1)}, bf16[128,512]{1,0:T(8,128)(2,1)S(1)}, u32[]{:S(2)}, u32[]{:S(2)}) collective-permute-start(bf16[128,512]{1,0:T(8,128)(2,1)} %bitcast.9), channel_id=1, source_target_pairs={{0,10},{2,12},{4,14},{6,15},{7,13},{5,11},{3,9},{1,8},{8,18},{10,2... | collective-permute-start | bytes 393224 | tf_op jit(solution)/shard_map/ppermute | solution.py:138
  2.5 7.8 %collective-permute-start.4 = (bf16[128,512]{1,0:T(8,128)(2,1)}, bf16[128,512]{1,0:T(8,128)(2,1)S(1)}, u32[]{:S(2)}, u32[]{:S(2)}) collective-permute-start(bf16[128,512]{1,0:T(8,128)(2,1)} %bitcast.10), channel_id=1, source_target_pairs={{0,9},{2,8},{4,10},{6,12},{7,14},{5,15},{3,13},{1,11},{8,17},{10,1... | collective-permute-start | bytes 393224 | tf_op jit(solution)/shard_map/ppermute | solution.py:138
  5.7 6.2 %collective-permute-start.9 = (bf16[144,512]{1,0:T(8,128)(2,1)S(1)}, bf16[144,512]{1,0:T(8,128)(2,1)S(1)}, u32[]{:S(2)}, u32[]{:S(2)}) collective-permute-start(bf16[144,512]{1,0:T(8,128)(2,1)S(1)} %pad_maximum_fusion.1), channel_id=1, source_target_pairs={{0,10},{2,12},{4,14},{6,15},{7,13},{5,11},{3,9},{1,8},{8,18},{10,2... | collective-permute-start | bytes 442376 | tf_op jit(solution)/shard_map/ppermute | solution.py:138
  6.9 7.4 %collective-permute-start.10 = (bf16[144,512]{1,0:T(8,128)(2,1)S(1)}, bf16[144,512]{1,0:T(8,128)(2,1)S(1)}, u32[]{:S(2)}, u32[]{:S(2)}) collective-permute-start(bf16[144,512]{1,0:T(8,128)(2,1)S(1)} %pad_maximum_fusion.1), channel_id=1, source_target_pairs={{0,9},{2,8},{4,10},{6,12},{7,14},{5,15},{3,13},{1,11},{8,17},{10,1... | collective-permute-start | bytes 442376 | tf_op jit(solution)/shard_map/ppermute | solution.py:138
  7.0 7.9 %collective-permute-start.1 = (bf16[128,512]{1,0:T(8,128)(2,1)S(1)}, bf16[128,512]{1,0:T(8,128)(2,1)S(1)}, u32[]{:S(2)}, u32[]{:S(2)}) collective-permute-start(bf16[128,512]{1,0:T(8,128)(2,1)S(1)} %collective-permute-done.refs_0_), channel_id=1, source_target_pairs={{0,2},{2,4},{4,6},{6,7},{7,5},{5,3},{3,1},{1,0},{8,10},{10,12},{12... | collective-permute-start | bytes 393224 | tf_op jit(solution)/shard_map/ppermute | solution.py:138
  10.2 6.1 %collective-permute-start.5 = (bf16[128,512]{1,0:T(8,128)(2,1)S(1)}, bf16[128,512]{1,0:T(8,128)(2,1)S(1)}, u32[]{:S(2)}, u32[]{:S(2)}) collective-permute-start(bf16[128,512]{1,0:T(8,128)(2,1)S(1)} %collective-permute-done.4.refs_1_), channel_id=1, source_target_pairs={{0,1},{2,0},{4,2},{6,4},{7,6},{5,7},{3,5},{1,3},{8,9},{10,8},{12,1... | collective-permute-start | bytes 393224 | tf_op jit(solution)/shard_map/ppermute | solution.py:138
  11.7 17.1 %collective-permute-start.8 = (bf16[128,5120]{1,0:T(8,128)(2,1)S(1)}, bf16[128,5120]{1,0:T(8,128)(2,1)S(1)}, u32[]{:S(2)}, u32[]{:S(2)}) collective-permute-start(bf16[128,5120]{1,0:T(8,128)(2,1)S(1)} %pad_maximum_fusion), channel_id=1, source_target_pairs={{0,8},{2,10},{4,12},{6,14},{7,15},{5,13},{3,11},{1,9},{8,16},{10,1... | collective-permute-start | bytes 3932168 | tf_op jit(solution)/shard_map/ppermute | solution.py:138
  11.9 6.7 %collective-permute-start.11 = (bf16[144,512]{1,0:T(8,128)(2,1)S(1)}, bf16[144,512]{1,0:T(8,128)(2,1)S(1)}, u32[]{:S(2)}, u32[]{:S(2)}) collective-permute-start(bf16[144,512]{1,0:T(8,128)(2,1)S(1)} %collective-permute-done.9.refs_8_.refs_0_), channel_id=1, source_target_pairs={{0,2},{2,4},{4,6},{6,7},{7,5},{5,3},{3,1},{1,0},{8,10},{10,12},{12... | collective-permute-start | bytes 442376 | tf_op jit(solution)/shard_map/ppermute | solution.py:138
  14.3 6.7 %collective-permute-start.12 = (bf16[144,512]{1,0:T(8,128)(2,1)S(1)}, bf16[144,512]{1,0:T(8,128)(2,1)S(1)}, u32[]{:S(2)}, u32[]{:S(2)}) collective-permute-start(bf16[144,512]{1,0:T(8,128)(2,1)S(1)} %collective-permute-done.10.refs_9_.refs_1_), channel_id=1, source_target_pairs={{0,1},{2,0},{4,2},{6,4},{7,6},{5,7},{3,5},{1,3},{8,9},{10,8},{12,1... | collective-permute-start | bytes 442376 | tf_op jit(solution)/shard_map/ppermute | solution.py:138
  14.9 6.6 %collective-permute-start.2 = (bf16[128,512]{1,0:T(8,128)(2,1)S(1)}, bf16[128,512]{1,0:T(8,128)(2,1)S(1)}, u32[]{:S(2)}, u32[]{:S(2)}) collective-permute-start(bf16[128,512]{1,0:T(8,128)(2,1)S(1)} %collective-permute-done.1.refs_2_), channel_id=1, source_target_pairs={{0,2},{2,4},{4,6},{6,7},{7,5},{5,3},{3,1},{1,0},{8,10},{10,12},{12... | collective-permute-start | bytes 393224 | tf_op jit(solution)/shard_map/ppermute | solution.py:138
  16.4 7.4 %collective-permute-start.6 = (bf16[128,512]{1,0:T(8,128)(2,1)S(1)}, bf16[128,512]{1,0:T(8,128)(2,1)S(1)}, u32[]{:S(2)}, u32[]{:S(2)}) collective-permute-start(bf16[128,512]{1,0:T(8,128)(2,1)S(1)} %collective-permute-done.5.refs_3_), channel_id=1, source_target_pairs={{0,1},{2,0},{4,2},{6,4},{7,6},{5,7},{3,5},{1,3},{8,9},{10,8},{12,1... | collective-permute-start | bytes 393224 | tf_op jit(solution)/shard_map/ppermute | solution.py:138
  18.6 6.3 %collective-permute-start.13 = (bf16[144,512]{1,0:T(8,128)(2,1)S(1)}, bf16[144,512]{1,0:T(8,128)(2,1)S(1)}, u32[]{:S(2)}, u32[]{:S(2)}) collective-permute-start(bf16[144,512]{1,0:T(8,128)(2,1)S(1)} %collective-permute-done.11.refs_10_.refs_2_), channel_id=1, source_target_pairs={{0,2},{2,4},{4,6},{6,7},{7,5},{5,3},{3,1},{1,0},{8,10},{10,12},{12... | collective-permute-start | bytes 442376 | tf_op jit(solution)/shard_map/ppermute | solution.py:138
  21.0 6.3 %collective-permute-start.14 = (bf16[144,512]{1,0:T(8,128)(2,1)S(1)}, bf16[144,512]{1,0:T(8,128)(2,1)S(1)}, u32[]{:S(2)}, u32[]{:S(2)}) collective-permute-start(bf16[144,512]{1,0:T(8,128)(2,1)S(1)} %collective-permute-done.12.refs_11_.refs_3_), channel_id=1, source_target_pairs={{0,1},{2,0},{4,2},{6,4},{7,6},{5,7},{3,5},{1,3},{8,9},{10,8},{12,1... | collective-permute-start | bytes 442376 | tf_op jit(solution)/shard_map/ppermute | solution.py:138
  21.4 6.0 %collective-permute-start.3 = (bf16[64,512]{1,0:T(8,128)(2,1)S(1)}, bf16[64,512]{1,0:T(8,128)(2,1)S(1)}, u32[]{:S(2)}, u32[]{:S(2)}) collective-permute-start(bf16[64,512]{1,0:T(8,128)(2,1)S(1)} %slice.16), channel_id=1, source_target_pairs={{0,2},{2,4},{4,6},{6,7},{7,5},{5,3},{3,1},{1,0},{8,10},{10,12},{12... | collective-permute-start | bytes 196616 | tf_op jit(solution)/shard_map/ppermute | solution.py:138
  23.8 4.5 %collective-permute-start.7 = (bf16[64,512]{1,0:T(8,128)(2,1)S(1)}, bf16[64,512]{1,0:T(8,128)(2,1)S(1)}, u32[]{:S(2)}, u32[]{:S(2)}) collective-permute-start(bf16[64,512]{1,0:T(8,128)(2,1)S(1)} %slice.17), channel_id=1, source_target_pairs={{0,1},{2,0},{4,2},{6,4},{7,6},{5,7},{3,5},{1,3},{8,9},{10,8},{12,1... | collective-permute-start | bytes 196616 | tf_op jit(solution)/shard_map/ppermute | solution.py:138
  25.0 5.8 %collective-permute-start.15 = (bf16[64,512]{1,0:T(8,128)(2,1)S(1)}, bf16[64,512]{1,0:T(8,128)(2,1)S(1)}, u32[]{:S(2)}, u32[]{:S(2)}) collective-permute-start(bf16[64,512]{1,0:T(8,128)(2,1)S(1)} %slice.18), channel_id=1, source_target_pairs={{0,2},{2,4},{4,6},{6,7},{7,5},{5,3},{3,1},{1,0},{8,10},{10,12},{12... | collective-permute-start | bytes 196616 | tf_op jit(solution)/shard_map/ppermute | solution.py:138
  27.3 4.3 %collective-permute-start.16 = (bf16[64,512]{1,0:T(8,128)(2,1)S(1)}, bf16[64,512]{1,0:T(8,128)(2,1)S(1)}, u32[]{:S(2)}, u32[]{:S(2)}) collective-permute-start(bf16[64,512]{1,0:T(8,128)(2,1)S(1)} %slice.19), channel_id=1, source_target_pairs={{0,1},{2,0},{4,2},{6,4},{7,6},{5,7},{3,5},{1,3},{8,9},{10,8},{12,1... | collective-permute-start | bytes 196616 | tf_op jit(solution)/shard_map/ppermute | solution.py:138

commit v8 on v7

--- a/solution.py
+++ b/solution.py
@@ -40,6 +40,10 @@
     for (first, second), ref in zip(numbers[1:], block_refs):
         sorted_ref[first] = ref[:RUN, :]
         sorted_ref[second] = ref[RUN:TOK_DEV, :]
+
+
+def blank_kernel(out_ref):
+    out_ref[...] = jnp.zeros_like(out_ref)
 
 
 def bias_kernel(runs, pos_ref, *refs):
@@ -146,13 +150,18 @@
         return held + [shift(ahead[:RUN], 0, 1), shift(back[RUN:TOK_DEV], 0, -1)]
 
     own = shift(jnp.concatenate([queries[0], keys[0], values[0]], axis=1), 1, 0)
-    tag = jnp.broadcast_to((token_pos >> (RUN.bit_length() - 1)).astype(jnp.bfloat16)[None], (TAG_ROWS, TOK_DEV))
-    tag = jnp.pad(tag, ((0, 0), (0, KV_COLUMNS - TOK_DEV)))
-    tagged = jnp.concatenate([values[0], tag], axis=0)
+    vmem = pl.BlockSpec(memory_space=pltpu.VMEM)
+    blank = pl.pallas_call(
+        blank_kernel,
+        out_shape=jax.ShapeDtypeStruct((TAG_ROWS, KV_COLUMNS), jnp.bfloat16),
+        out_specs=vmem,
+        cost_estimate=pl.CostEstimate(flops=1 << 30, bytes_accessed=0, transcendentals=0),
+    )()
+    tag = jnp.pad((token_pos >> (RUN.bit_length() - 1)).astype(jnp.bfloat16), (0, KV_COLUMNS - TOK_DEV))
+    tagged = jnp.concatenate([values[0], blank + tag[None]], axis=0)
     all_keys, all_values = around(keys[0]), around(tagged)
     pos = lax.optimization_barrier(jnp.concatenate([token_pos, segment]).astype(jnp.float32)[None])
     params = pltpu.CompilerParams(vmem_limit_bytes=(12 + runs // 4) * 1024 * 1024)
-    vmem = pl.BlockSpec(memory_space=pltpu.VMEM)
     before_mask = all_keys[-2:]
     bias = pl.pallas_call(
         functools.partial(bias_kernel, runs),

time: 34 us -> 33.1 us (0.974)
  other arithmetic: 3.04 us -> 0.83 us
  waiting for transfers between devices: 5.86 us -> 7.22 us
  Pallas kernels: 4.51 us -> 5.12 us
  starting transfers between devices: 20.3 us -> 19.7 us
    concatenate x1, other arithmetic: 1.46 us -> 0.09 us  [per_device(): own = shift(jnp.concatenate([queries[0], keys[0], values[0]], axis=1), 1, 0)]
    ppermute x17, waiting for transfers between devices: 5.86 us -> 7.22 us  [shift(): return lax.ppermute(block, ('section', 'ctx'), pairs)]
    concatenate x1, other arithmetic: 0.91 us -> 0.01 us  [per_device(): tagged = jnp.concatenate([values[0], blank + tag[None]], axis=0)]
    add x0 -> x1, other arithmetic: none -> 0.72 us  [per_device(): tagged = jnp.concatenate([values[0], blank + tag[None]], axis=0)]
    convert_element_type x1, other arithmetic: 0.66 us -> 0.01 us  [per_device(): (token_pos >> RUN.bit_length() - 1).astype(jnp.bfloat16)]
    ppermute x17, starting transfers between devices: 20.3 us -> 19.7 us  [shift(): return lax.ppermute(block, ('section', 'ctx'), pairs)]
    pallas_call x0 -> x1, Pallas kernels: none -> 0.61 us  [per_device(): pl.pallas_call(blank_kernel, out_shape=jax.ShapeDtypeStruct((TAG_ROWS, KV...]
  transfers between devices with their start and end apart: 17 -> 17, of which waited for: 8 -> 9; matrix products, arithmetic and copies ran while one was open for 9% -> 3% of each run, Pallas kernels for 7% -> 9%
where the time goes in v8:
time: 33.1 us; the launch traced here: 33 us
  starting transfers between devices  19.7 us (60%)
  waiting for transfers between devices  7.22 us (22%)
  Pallas kernels  5.12 us (15%)
  other arithmetic  0.83 us (3%)
    ppermute x17, starting transfers between devices, shift(): return lax.ppermute(block, ('section', 'ctx'), pairs)  19.7 us
    ppermute x17, waiting for transfers between devices, shift(): return lax.ppermute(block, ('section', 'ctx'), pairs)  7.22 us
    pallas_call x1, Pallas kernels, per_device(): pl.pallas_call(functools.partial(values_kernel, runs), out_shape=jax.Shap...  2.22 us
    pallas_call x1, Pallas kernels, per_device(): pl.pallas_call(functools.partial(weights_kernel, runs), out_shape=(jax.Sh...  1.96 us
    add x1, other arithmetic, per_device(): tagged = jnp.concatenate([values[0], blank + tag[None]], axis=0)  0.72 us
  transfers between devices with their start and end apart: 17, of which 9 were waited for; matrix products, arithmetic and copies ran while one was open for 3% of the time, Pallas kernels for 9%

profile of v8, /device:TPU:0, one launch (start us, length us, event | category | flops | bytes accessed | tf_op | source)
XLA Modules:
  0.0 33.0 jit_solution(8853292486426153525)
XLA Ops:
  0.0 0.0 copy-start.2
  0.0 0.0 copy-start.4
  0.0 0.0 copy-start.1
  0.0 2.5 %collective-permute-start = (bf16[128,512]{1,0:T(8,128)(2,1)}, bf16[128,512]{1,0:T(8,128)(2,1)S(1)}, u32[]{:S(2)}, u32[]{:S(2)}) collective-permute-start(bf16[128,512]{1,0:T(8,128)(2,1)} %bitcast.9), channel_id=1, source_target_pairs={{0,10},{2,12},{4,14},{6,15},{7,13},{5,11},{3,9},{1,8},{8,18},{10,2... | collective-permute-start | bytes 393224 | tf_op jit(solution)/shard_map/ppermute | solution.py:142
  2.5 1.7 %collective-permute-start.4 = (bf16[128,512]{1,0:T(8,128)(2,1)}, bf16[128,512]{1,0:T(8,128)(2,1)S(1)}, u32[]{:S(2)}, u32[]{:S(2)}) collective-permute-start(bf16[128,512]{1,0:T(8,128)(2,1)} %bitcast.10), channel_id=1, source_target_pairs={{0,9},{2,8},{4,10},{6,12},{7,14},{5,15},{3,13},{1,11},{8,17},{10,1... | collective-permute-start | bytes 393224 | tf_op jit(solution)/shard_map/ppermute | solution.py:142
  4.2 0.6 %shard_map.56 = bf16[16,512]{1,0:T(8,128)(2,1)} custom-call(), custom_call_target="tpu_custom_call" | custom-call | flops 1073741824 | tf_op jit(solution)/shard_map/pallas_call | solution.py:154
  4.8 0.0 copy-done.4
  4.8 0.7 %broadcast_add_fusion = bf16[16,512]{1,0:T(8,128)(2,1)S(1)} fusion(bf16[16,512]{1,0:T(8,128)(2,1)} %shard_map.56, bf16[512]{0:T(512)(128)(2,1)S(1)} %pad.4), kind=kLoop, calls=%fused_computation.2 | loop fusion | flops 8192 | bytes 33792 | tf_op jit(solution)/shard_map/add | solution.py:161
  5.5 0.0 copy-done.1
  5.6 1.2 %collective-permute-start.9 = (bf16[144,512]{1,0:T(8,128)(2,1)S(1)}, bf16[144,512]{1,0:T(8,128)(2,1)S(1)}, u32[]{:S(2)}, u32[]{:S(2)}) collective-permute-start(bf16[144,512]{1,0:T(8,128)(2,1)S(1)} %pad_maximum_fusion.1), channel_id=1, source_target_pairs={{0,10},{2,12},{4,14},{6,15},{7,13},{5,11},{3,9},{1,8},{8,18},{10,2... | collective-permute-start | bytes 442376 | tf_op jit(solution)/shard_map/ppermute | solution.py:142
  6.7 0.1 collective-permute-start.10
  6.8 0.0 collective-permute-done.refs_0_
  6.8 3.5 %collective-permute-start.1 = (bf16[128,512]{1,0:T(8,128)(2,1)S(1)}, bf16[128,512]{1,0:T(8,128)(2,1)S(1)}, u32[]{:S(2)}, u32[]{:S(2)}) collective-permute-start(bf16[128,512]{1,0:T(8,128)(2,1)S(1)} %collective-permute-done.refs_0_), channel_id=1, source_target_pairs={{0,2},{2,4},{4,6},{6,7},{7,5},{5,3},{3,1},{1,0},{8,10},{10,12},{12... | collective-permute-start | bytes 393224 | tf_op jit(solution)/shard_map/ppermute | solution.py:142
  10.3 0.0 collective-permute-done.4.refs_1_
  10.3 0.0 collective-permute-start.5
  10.3 0.0 copy-done.2
  10.3 0.0 copy-done
  10.3 0.1 pad_maximum_fusion
  10.4 0.1 collective-permute-start.8
  10.5 1.3 %collective-permute-done.9.refs_8_.refs_0_ = bf16[144,512]{1,0:T(8,128)(2,1)S(1)} collective-permute-done((bf16[144,512]{1,0:T(8,128)(2,1)S(1)}, bf16[144,512]{1,0:T(8,128)(2,1)S(1)}, u32[]{:S(2)}, u32[]{:S(2)}) %collective-permute-start.9) | collective-permute-done | bytes 147488 | tf_op jit(solution)/shard_map/ppermute | solution.py:142
  11.7 2.4 %collective-permute-start.11 = (bf16[144,512]{1,0:T(8,128)(2,1)S(1)}, bf16[144,512]{1,0:T(8,128)(2,1)S(1)}, u32[]{:S(2)}, u32[]{:S(2)}) collective-permute-start(bf16[144,512]{1,0:T(8,128)(2,1)S(1)} %collective-permute-done.9.refs_8_.refs_0_), channel_id=1, source_target_pairs={{0,2},{2,4},{4,6},{6,7},{7,5},{5,3},{3,1},{1,0},{8,10},{10,12},{12... | collective-permute-start | bytes 442376 | tf_op jit(solution)/shard_map/ppermute | solution.py:142
  14.2 0.0 collective-permute-done.10.refs_9_.refs_1_
  14.2 0.0 collective-permute-start.12
  14.2 0.5 %collective-permute-done.1.refs_2_ = bf16[128,512]{1,0:T(8,128)(2,1)S(1)} collective-permute-done((bf16[128,512]{1,0:T(8,128)(2,1)S(1)}, bf16[128,512]{1,0:T(8,128)(2,1)S(1)}, u32[]{:S(2)}, u32[]{:S(2)}) %collective-permute-start.1) | collective-permute-done | bytes 131104 | tf_op jit(solution)/shard_map/ppermute | solution.py:142
  14.7 1.5 %collective-permute-start.2 = (bf16[128,512]{1,0:T(8,128)(2,1)S(1)}, bf16[128,512]{1,0:T(8,128)(2,1)S(1)}, u32[]{:S(2)}, u32[]{:S(2)}) collective-permute-start(bf16[128,512]{1,0:T(8,128)(2,1)S(1)} %collective-permute-done.1.refs_2_), channel_id=1, source_target_pairs={{0,2},{2,4},{4,6},{6,7},{7,5},{5,3},{3,1},{1,0},{8,10},{10,12},{12... | collective-permute-start | bytes 393224 | tf_op jit(solution)/shard_map/ppermute | solution.py:142
  16.2 0.0 collective-permute-done.5.refs_3_
  16.2 0.5 %collective-permute-start.6 = (bf16[128,512]{1,0:T(8,128)(2,1)S(1)}, bf16[128,512]{1,0:T(8,128)(2,1)S(1)}, u32[]{:S(2)}, u32[]{:S(2)}) collective-permute-start(bf16[128,512]{1,0:T(8,128)(2,1)S(1)} %collective-permute-done.5.refs_3_), channel_id=1, source_target_pairs={{0,1},{2,0},{4,2},{6,4},{7,6},{5,7},{3,5},{1,3},{8,9},{10,8},{12,1... | collective-permute-start | bytes 393224 | tf_op jit(solution)/shard_map/ppermute | solution.py:142
  16.7 1.7 %collective-permute-done.11.refs_10_.refs_2_ = bf16[144,512]{1,0:T(8,128)(2,1)S(1)} collective-permute-done((bf16[144,512]{1,0:T(8,128)(2,1)S(1)}, bf16[144,512]{1,0:T(8,128)(2,1)S(1)}, u32[]{:S(2)}, u32[]{:S(2)}) %collective-permute-start.11) | collective-permute-done | bytes 147488 | tf_op jit(solution)/shard_map/ppermute | solution.py:142
  18.5 2.1 %collective-permute-start.13 = (bf16[144,512]{1,0:T(8,128)(2,1)S(1)}, bf16[144,512]{1,0:T(8,128)(2,1)S(1)}, u32[]{:S(2)}, u32[]{:S(2)}) collective-permute-start(bf16[144,512]{1,0:T(8,128)(2,1)S(1)} %collective-permute-done.11.refs_10_.refs_2_), channel_id=1, source_target_pairs={{0,2},{2,4},{4,6},{6,7},{7,5},{5,3},{3,1},{1,0},{8,10},{10,12},{12... | collective-permute-start | bytes 442376 | tf_op jit(solution)/shard_map/ppermute | solution.py:142
  20.6 0.1 collective-permute-done.12.refs_11_.refs_3_
  20.7 0.2 collective-permute-start.14
  20.9 0.4 %collective-permute-done.2.refs_4_ = bf16[128,512]{1,0:T(8,128)(2,1)S(1)} collective-permute-done((bf16[128,512]{1,0:T(8,128)(2,1)S(1)}, bf16[128,512]{1,0:T(8,128)(2,1)S(1)}, u32[]{:S(2)}, u32[]{:S(2)}) %collective-permute-start.2) | collective-permute-done | bytes 131104 | tf_op jit(solution)/shard_map/ppermute | solution.py:142
  21.3 1.6 %collective-permute-start.3 = (bf16[64,512]{1,0:T(8,128)(2,1)S(1)}, bf16[64,512]{1,0:T(8,128)(2,1)S(1)}, u32[]{:S(2)}, u32[]{:S(2)}) collective-permute-start(bf16[64,512]{1,0:T(8,128)(2,1)S(1)} %slice.16), channel_id=1, source_target_pairs={{0,2},{2,4},{4,6},{6,7},{7,5},{5,3},{3,1},{1,0},{8,10},{10,12},{12... | collective-permute-start | bytes 196616 | tf_op jit(solution)/shard_map/ppermute | solution.py:142
  22.9 0.2 collective-permute-done.6.refs_5_
  23.1 0.2 collective-permute-start.7
  23.4 0.0 copy-done.3
  23.4 1.4 %collective-permute-done.13.refs_12_.refs_4_ = bf16[144,512]{1,0:T(8,128)(2,1)S(1)} collective-permute-done((bf16[144,512]{1,0:T(8,128)(2,1)S(1)}, bf16[144,512]{1,0:T(8,128)(2,1)S(1)}, u32[]{:S(2)}, u32[]{:S(2)}) %collective-permute-start.13) | collective-permute-done | bytes 147488 | tf_op jit(solution)/shard_map/ppermute | solution.py:142
  24.8 1.6 %collective-permute-start.15 = (bf16[64,512]{1,0:T(8,128)(2,1)S(1)}, bf16[64,512]{1,0:T(8,128)(2,1)S(1)}, u32[]{:S(2)}, u32[]{:S(2)}) collective-permute-start(bf16[64,512]{1,0:T(8,128)(2,1)S(1)} %slice.18), channel_id=1, source_target_pairs={{0,2},{2,4},{4,6},{6,7},{7,5},{5,3},{3,1},{1,0},{8,10},{10,12},{12... | collective-permute-start | bytes 196616 | tf_op jit(solution)/shard_map/ppermute | solution.py:142
  26.4 0.0 collective-permute-done.14.refs_13_.refs_5_
  26.4 0.5 %collective-permute-start.16 = (bf16[64,512]{1,0:T(8,128)(2,1)S(1)}, bf16[64,512]{1,0:T(8,128)(2,1)S(1)}, u32[]{:S(2)}, u32[]{:S(2)}) collective-permute-start(bf16[64,512]{1,0:T(8,128)(2,1)S(1)} %slice.19), channel_id=1, source_target_pairs={{0,1},{2,0},{4,2},{6,4},{7,6},{5,7},{3,5},{1,3},{8,9},{10,8},{12,1... | collective-permute-start | bytes 196616 | tf_op jit(solution)/shard_map/ppermute | solution.py:142
  26.9 0.0 collective-permute-done.3.refs_0_.refs_6_
  26.9 0.9 %collective-permute-done.7.refs_1_.refs_7_ = bf16[64,512]{1,0:T(8,128)(2,1)S(1)} collective-permute-done((bf16[64,512]{1,0:T(8,128)(2,1)S(1)}, bf16[64,512]{1,0:T(8,128)(2,1)S(1)}, u32[]{:S(2)}, u32[]{:S(2)}) %collective-permute-start.7) | collective-permute-done | bytes 65568 | tf_op jit(solution)/shard_map/ppermute | solution.py:142
  27.8 0.3 %shard_map.55.bias_ref = f32[2,64,320]{2,1,0:T(8,128)S(1)} custom-call(f32[1,1152]{1,0:T(1,128)S(1)} %add_convert_fusion.pos_ref, bf16[64,512]{1,0:T(8,128)(2,1)S(1)} %collective-permute-done.3.refs_0_.refs_6_, bf16[64,512]{1,0:T(8,128)(2,1)S(1)} %collective-permute-done.7.refs_1_.refs_7_), custom_call_target="tpu_custom_call" | custom-call | flops 9395240960 | tf_op jit(solution)/shard_map/pallas_call | solution.py:166
  28.2 0.0 collective-permute-done.8.own_ref
  28.2 2.0 %shard_map.57 = (bf16[8,512,320]{2,1,0:T(8,128)(2,1)S(1)}, bf16[16,64,512]{2,1,0:T(8,128)(2,1)S(1)}) custom-call(f32[1,1152]{1,0:T(1,128)S(1)} %add_convert_fusion.pos_ref, f32[2,64,320]{2,1,0:T(8,128)S(1)} %shard_map.55.bias_ref, bf16[128,5120]{1,0:T(8,128)(2,1)S(1)} %collective-permute-done.8.own_ref, bf16[128,512]{1,0:T(8,128)(2,1)S(1)} %collective-permute-done.refs_0_, ...), custom_call_target="tpu_custom_call" | custom-call | flops 67108864 | bytes 1048576 | tf_op jit(solution)/shard_map/pallas_call | solution.py:174
  30.2 0.0 collective-permute-done.15.refs_6_
  30.2 0.6 %collective-permute-done.16.refs_7_ = bf16[64,512]{1,0:T(8,128)(2,1)S(1)} collective-permute-done((bf16[64,512]{1,0:T(8,128)(2,1)S(1)}, bf16[64,512]{1,0:T(8,128)(2,1)S(1)}, u32[]{:S(2)}, u32[]{:S(2)}) %collective-permute-start.16) | collective-permute-done | bytes 65568 | tf_op jit(solution)/shard_map/ppermute | solution.py:142
  30.8 2.2 %shard_map.58 = bf16[128,4096]{1,0:T(8,128)(2,1)} custom-call(f32[1,1152]{1,0:T(1,128)S(1)} %add_convert_fusion.pos_ref, bf16[8,512,320]{2,1,0:T(8,128)(2,1)S(1)} %get-tuple-element.7.weights_ref, bf16[16,64,512]{2,1,0:T(8,128)(2,1)S(1)} %get-tuple-element.8.sorted_ref, bf16[144,512]{1,0:T(8,128)(2,1)S(1)} %collective-permute-done.9.refs_8_.refs_0_, ...), custom_call_target="tpu_custom_call" | custom-call | flops 67108864 | bytes 1048576 | tf_op jit(solution)/shard_map/pallas_call | solution.py:186
  (10 shorter events, 0.1 us)
Async XLA Ops:
  0.0 10.3 %copy-start.2 = (bf16[1,128,512]{2,1,0:T(8,128)(2,1)S(1)}, bf16[1,128,512]{2,1,0:T(8,128)(2,1)}, u32[]{:S(2)}) copy-start(bf16[1,128,512]{2,1,0:T(8,128)(2,1)} %param.6) | copy-start | bytes 393220
  0.0 4.8 %copy-start.4 = (s32[128]{0:T(128)S(1)}, s32[128]{0:T(128)}, u32[]{:S(2)}) copy-start(s32[128]{0:T(128)} %param.8) | copy-start | bytes 1540
  0.0 5.5 %copy-start.1 = (bf16[1,128,512]{2,1,0:T(8,128)(2,1)S(1)}, bf16[1,128,512]{2,1,0:T(8,128)(2,1)}, u32[]{:S(2)}) copy-start(bf16[1,128,512]{2,1,0:T(8,128)(2,1)} %param.7) | copy-start | bytes 393220
  0.0 10.3 %copy-start = (bf16[1,128,4096]{2,1,0:T(8,128)(2,1)S(1)}, bf16[1,128,4096]{2,1,0:T(8,128)(2,1)}, u32[]{:S(2)}) copy-start(bf16[1,128,4096]{2,1,0:T(8,128)(2,1)} %param.5) | copy-start | bytes 3145732
  0.0 23.4 %copy-start.3 = (s32[1024]{0:T(1024)S(1)}, s32[1024]{0:T(1024)}, u32[]{:S(2)}) copy-start(s32[1024]{0:T(1024)} %param.9) | copy-start | bytes 12292
  0.0 6.8 %collective-permute-start = (bf16[128,512]{1,0:T(8,128)(2,1)}, bf16[128,512]{1,0:T(8,128)(2,1)S(1)}, u32[]{:S(2)}, u32[]{:S(2)}) collective-permute-start(bf16[128,512]{1,0:T(8,128)(2,1)} %bitcast.9), channel_id=1, source_target_pairs={{0,10},{2,12},{4,14},{6,15},{7,13},{5,11},{3,9},{1,8},{8,18},{10,2... | collective-permute-start | bytes 393224 | tf_op jit(solution)/shard_map/ppermute | solution.py:142
  2.5 7.8 %collective-permute-start.4 = (bf16[128,512]{1,0:T(8,128)(2,1)}, bf16[128,512]{1,0:T(8,128)(2,1)S(1)}, u32[]{:S(2)}, u32[]{:S(2)}) collective-permute-start(bf16[128,512]{1,0:T(8,128)(2,1)} %bitcast.10), channel_id=1, source_target_pairs={{0,9},{2,8},{4,10},{6,12},{7,14},{5,15},{3,13},{1,11},{8,17},{10,1... | collective-permute-start | bytes 393224 | tf_op jit(solution)/shard_map/ppermute | solution.py:142
  5.6 6.2 %collective-permute-start.9 = (bf16[144,512]{1,0:T(8,128)(2,1)S(1)}, bf16[144,512]{1,0:T(8,128)(2,1)S(1)}, u32[]{:S(2)}, u32[]{:S(2)}) collective-permute-start(bf16[144,512]{1,0:T(8,128)(2,1)S(1)} %pad_maximum_fusion.1), channel_id=1, source_target_pairs={{0,10},{2,12},{4,14},{6,15},{7,13},{5,11},{3,9},{1,8},{8,18},{10,2... | collective-permute-start | bytes 442376 | tf_op jit(solution)/shard_map/ppermute | solution.py:142
  6.7 7.4 %collective-permute-start.10 = (bf16[144,512]{1,0:T(8,128)(2,1)S(1)}, bf16[144,512]{1,0:T(8,128)(2,1)S(1)}, u32[]{:S(2)}, u32[]{:S(2)}) collective-permute-start(bf16[144,512]{1,0:T(8,128)(2,1)S(1)} %pad_maximum_fusion.1), channel_id=1, source_target_pairs={{0,9},{2,8},{4,10},{6,12},{7,14},{5,15},{3,13},{1,11},{8,17},{10,1... | collective-permute-start | bytes 442376 | tf_op jit(solution)/shard_map/ppermute | solution.py:142
  6.8 7.9 %collective-permute-start.1 = (bf16[128,512]{1,0:T(8,128)(2,1)S(1)}, bf16[128,512]{1,0:T(8,128)(2,1)S(1)}, u32[]{:S(2)}, u32[]{:S(2)}) collective-permute-start(bf16[128,512]{1,0:T(8,128)(2,1)S(1)} %collective-permute-done.refs_0_), channel_id=1, source_target_pairs={{0,2},{2,4},{4,6},{6,7},{7,5},{5,3},{3,1},{1,0},{8,10},{10,12},{12... | collective-permute-start | bytes 393224 | tf_op jit(solution)/shard_map/ppermute | solution.py:142
  10.3 5.9 %collective-permute-start.5 = (bf16[128,512]{1,0:T(8,128)(2,1)S(1)}, bf16[128,512]{1,0:T(8,128)(2,1)S(1)}, u32[]{:S(2)}, u32[]{:S(2)}) collective-permute-start(bf16[128,512]{1,0:T(8,128)(2,1)S(1)} %collective-permute-done.4.refs_1_), channel_id=1, source_target_pairs={{0,1},{2,0},{4,2},{6,4},{7,6},{5,7},{3,5},{1,3},{8,9},{10,8},{12,1... | collective-permute-start | bytes 393224 | tf_op jit(solution)/shard_map/ppermute | solution.py:142
  10.4 17.8 %collective-permute-start.8 = (bf16[128,5120]{1,0:T(8,128)(2,1)S(1)}, bf16[128,5120]{1,0:T(8,128)(2,1)S(1)}, u32[]{:S(2)}, u32[]{:S(2)}) collective-permute-start(bf16[128,5120]{1,0:T(8,128)(2,1)S(1)} %pad_maximum_fusion), channel_id=1, source_target_pairs={{0,8},{2,10},{4,12},{6,14},{7,15},{5,13},{3,11},{1,9},{8,16},{10,1... | collective-permute-start | bytes 3932168 | tf_op jit(solution)/shard_map/ppermute | solution.py:142
  11.7 6.7 %collective-permute-start.11 = (bf16[144,512]{1,0:T(8,128)(2,1)S(1)}, bf16[144,512]{1,0:T(8,128)(2,1)S(1)}, u32[]{:S(2)}, u32[]{:S(2)}) collective-permute-start(bf16[144,512]{1,0:T(8,128)(2,1)S(1)} %collective-permute-done.9.refs_8_.refs_0_), channel_id=1, source_target_pairs={{0,2},{2,4},{4,6},{6,7},{7,5},{5,3},{3,1},{1,0},{8,10},{10,12},{12... | collective-permute-start | bytes 442376 | tf_op jit(solution)/shard_map/ppermute | solution.py:142
  14.2 6.5 %collective-permute-start.12 = (bf16[144,512]{1,0:T(8,128)(2,1)S(1)}, bf16[144,512]{1,0:T(8,128)(2,1)S(1)}, u32[]{:S(2)}, u32[]{:S(2)}) collective-permute-start(bf16[144,512]{1,0:T(8,128)(2,1)S(1)} %collective-permute-done.10.refs_9_.refs_1_), channel_id=1, source_target_pairs={{0,1},{2,0},{4,2},{6,4},{7,6},{5,7},{3,5},{1,3},{8,9},{10,8},{12,1... | collective-permute-start | bytes 442376 | tf_op jit(solution)/shard_map/ppermute | solution.py:142
  14.7 6.6 %collective-permute-start.2 = (bf16[128,512]{1,0:T(8,128)(2,1)S(1)}, bf16[128,512]{1,0:T(8,128)(2,1)S(1)}, u32[]{:S(2)}, u32[]{:S(2)}) collective-permute-start(bf16[128,512]{1,0:T(8,128)(2,1)S(1)} %collective-permute-done.1.refs_2_), channel_id=1, source_target_pairs={{0,2},{2,4},{4,6},{6,7},{7,5},{5,3},{3,1},{1,0},{8,10},{10,12},{12... | collective-permute-start | bytes 393224 | tf_op jit(solution)/shard_map/ppermute | solution.py:142
  16.2 6.9 %collective-permute-start.6 = (bf16[128,512]{1,0:T(8,128)(2,1)S(1)}, bf16[128,512]{1,0:T(8,128)(2,1)S(1)}, u32[]{:S(2)}, u32[]{:S(2)}) collective-permute-start(bf16[128,512]{1,0:T(8,128)(2,1)S(1)} %collective-permute-done.5.refs_3_), channel_id=1, source_target_pairs={{0,1},{2,0},{4,2},{6,4},{7,6},{5,7},{3,5},{1,3},{8,9},{10,8},{12,1... | collective-permute-start | bytes 393224 | tf_op jit(solution)/shard_map/ppermute | solution.py:142
  18.5 6.4 %collective-permute-start.13 = (bf16[144,512]{1,0:T(8,128)(2,1)S(1)}, bf16[144,512]{1,0:T(8,128)(2,1)S(1)}, u32[]{:S(2)}, u32[]{:S(2)}) collective-permute-start(bf16[144,512]{1,0:T(8,128)(2,1)S(1)} %collective-permute-done.11.refs_10_.refs_2_), channel_id=1, source_target_pairs={{0,2},{2,4},{4,6},{6,7},{7,5},{5,3},{3,1},{1,0},{8,10},{10,12},{12... | collective-permute-start | bytes 442376 | tf_op jit(solution)/shard_map/ppermute | solution.py:142
  20.7 5.7 %collective-permute-start.14 = (bf16[144,512]{1,0:T(8,128)(2,1)S(1)}, bf16[144,512]{1,0:T(8,128)(2,1)S(1)}, u32[]{:S(2)}, u32[]{:S(2)}) collective-permute-start(bf16[144,512]{1,0:T(8,128)(2,1)S(1)} %collective-permute-done.12.refs_11_.refs_3_), channel_id=1, source_target_pairs={{0,1},{2,0},{4,2},{6,4},{7,6},{5,7},{3,5},{1,3},{8,9},{10,8},{12,1... | collective-permute-start | bytes 442376 | tf_op jit(solution)/shard_map/ppermute | solution.py:142
  21.3 5.6 %collective-permute-start.3 = (bf16[64,512]{1,0:T(8,128)(2,1)S(1)}, bf16[64,512]{1,0:T(8,128)(2,1)S(1)}, u32[]{:S(2)}, u32[]{:S(2)}) collective-permute-start(bf16[64,512]{1,0:T(8,128)(2,1)S(1)} %slice.16), channel_id=1, source_target_pairs={{0,2},{2,4},{4,6},{6,7},{7,5},{5,3},{3,1},{1,0},{8,10},{10,12},{12... | collective-permute-start | bytes 196616 | tf_op jit(solution)/shard_map/ppermute | solution.py:142
  23.1 4.7 %collective-permute-start.7 = (bf16[64,512]{1,0:T(8,128)(2,1)S(1)}, bf16[64,512]{1,0:T(8,128)(2,1)S(1)}, u32[]{:S(2)}, u32[]{:S(2)}) collective-permute-start(bf16[64,512]{1,0:T(8,128)(2,1)S(1)} %slice.17), channel_id=1, source_target_pairs={{0,1},{2,0},{4,2},{6,4},{7,6},{5,7},{3,5},{1,3},{8,9},{10,8},{12,1... | collective-permute-start | bytes 196616 | tf_op jit(solution)/shard_map/ppermute | solution.py:142
  24.8 5.3 %collective-permute-start.15 = (bf16[64,512]{1,0:T(8,128)(2,1)S(1)}, bf16[64,512]{1,0:T(8,128)(2,1)S(1)}, u32[]{:S(2)}, u32[]{:S(2)}) collective-permute-start(bf16[64,512]{1,0:T(8,128)(2,1)S(1)} %slice.18), channel_id=1, source_target_pairs={{0,2},{2,4},{4,6},{6,7},{7,5},{5,3},{3,1},{1,0},{8,10},{10,12},{12... | collective-permute-start | bytes 196616 | tf_op jit(solution)/shard_map/ppermute | solution.py:142
  26.4 4.3 %collective-permute-start.16 = (bf16[64,512]{1,0:T(8,128)(2,1)S(1)}, bf16[64,512]{1,0:T(8,128)(2,1)S(1)}, u32[]{:S(2)}, u32[]{:S(2)}) collective-permute-start(bf16[64,512]{1,0:T(8,128)(2,1)S(1)} %slice.19), channel_id=1, source_target_pairs={{0,1},{2,0},{4,2},{6,4},{7,6},{5,7},{3,5},{1,3},{8,9},{10,8},{12,1... | collective-permute-start | bytes 196616 | tf_op jit(solution)/shard_map/ppermute | solution.py:142

commit v9 on v8

--- a/solution.py
+++ b/solution.py
@@ -155,6 +155,7 @@
         blank_kernel,
         out_shape=jax.ShapeDtypeStruct((TAG_ROWS, KV_COLUMNS), jnp.bfloat16),
         out_specs=vmem,
+        compiler_params=pltpu.CompilerParams(vmem_limit_bytes=8 * 1024 * 1024),
         cost_estimate=pl.CostEstimate(flops=1 << 30, bytes_accessed=0, transcendentals=0),
     )()
     tag = jnp.pad((token_pos >> (RUN.bit_length() - 1)).astype(jnp.bfloat16), (0, KV_COLUMNS - TOK_DEV))

time: 33.1 us -> 32.7 us (0.988)
  other arithmetic: 0.83 us -> 0.14 us
  Pallas kernels: 5.12 us -> 4.52 us
  starting transfers between devices: 19.7 us -> 20.2 us
    add x1, other arithmetic: 0.72 us -> 0.01 us  [per_device(): tagged = jnp.concatenate([values[0], blank + tag[None]], axis=0)]
    pallas_call x1, Pallas kernels: 0.61 us -> 0.01 us  [per_device(): pl.pallas_call(blank_kernel, out_shape=jax.ShapeDtypeStruct((TAG_ROWS, KV...]
    ppermute x17, starting transfers between devices: 19.7 us -> 20.2 us  [shift(): return lax.ppermute(block, ('section', 'ctx'), pairs)]
  transfers between devices with their start and end apart: 17 -> 17, of which waited for: 9 -> 9; matrix products, arithmetic and copies ran while one was open for 3% -> 1% of each run, Pallas kernels for 9% -> 7%
where the time goes in v9:
time: 32.7 us; the launch traced here: 32.6 us
  starting transfers between devices  20.2 us (62%)
  waiting for transfers between devices  7.51 us (23%)
  Pallas kernels  4.52 us (14%)
    ppermute x17, starting transfers between devices, shift(): return lax.ppermute(block, ('section', 'ctx'), pairs)  20.2 us
    ppermute x17, waiting for transfers between devices, shift(): return lax.ppermute(block, ('section', 'ctx'), pairs)  7.51 us
    pallas_call x1, Pallas kernels, per_device(): pl.pallas_call(functools.partial(values_kernel, runs), out_shape=jax.Shap...  2.22 us
    pallas_call x1, Pallas kernels, per_device(): pl.pallas_call(functools.partial(weights_kernel, runs), out_shape=(jax.Sh...  1.96 us
  transfers between devices with their start and end apart: 17, of which 9 were waited for; matrix products, arithmetic and copies ran while one was open for 1% of the time, Pallas kernels for 7%

profile of v9, /device:TPU:0, one launch (start us, length us, event | category | flops | bytes accessed | tf_op | source)
XLA Modules:
  0.0 32.6 jit_solution(9422891788742673523)
XLA Ops:
  0.0 0.0 copy-start.2
  0.0 0.0 copy-start.4
  0.0 0.0 copy-start.1
  0.0 0.0 copy-start
  0.0 0.0 copy-start.3
  0.0 2.5 %collective-permute-start = (bf16[128,512]{1,0:T(8,128)(2,1)}, bf16[128,512]{1,0:T(8,128)(2,1)S(1)}, u32[]{:S(2)}, u32[]{:S(2)}) collective-permute-start(bf16[128,512]{1,0:T(8,128)(2,1)} %bitcast.9), channel_id=1, source_target_pairs={{0,10},{2,12},{4,14},{6,15},{7,13},{5,11},{3,9},{1,8},{8,18},{10,2... | collective-permute-start | bytes 393224 | tf_op jit(solution)/shard_map/ppermute | solution.py:142
  2.5 1.7 %collective-permute-start.4 = (bf16[128,512]{1,0:T(8,128)(2,1)}, bf16[128,512]{1,0:T(8,128)(2,1)S(1)}, u32[]{:S(2)}, u32[]{:S(2)}) collective-permute-start(bf16[128,512]{1,0:T(8,128)(2,1)} %bitcast.10), channel_id=1, source_target_pairs={{0,9},{2,8},{4,10},{6,12},{7,14},{5,15},{3,13},{1,11},{8,17},{10,1... | collective-permute-start | bytes 393224 | tf_op jit(solution)/shard_map/ppermute | solution.py:142
  4.2 0.0 copy-done.4
  4.2 0.0 copy-done.1
  4.3 1.2 %collective-permute-start.9 = (bf16[144,512]{1,0:T(8,128)(2,1)S(1)}, bf16[144,512]{1,0:T(8,128)(2,1)S(1)}, u32[]{:S(2)}, u32[]{:S(2)}) collective-permute-start(bf16[144,512]{1,0:T(8,128)(2,1)S(1)} %pad_maximum_fusion.1), channel_id=1, source_target_pairs={{0,10},{2,12},{4,14},{6,15},{7,13},{5,11},{3,9},{1,8},{8,18},{10,2... | collective-permute-start | bytes 442376 | tf_op jit(solution)/shard_map/ppermute | solution.py:142
  5.5 0.1 collective-permute-start.10
  5.5 0.9 %collective-permute-done.refs_0_ = bf16[128,512]{1,0:T(8,128)(2,1)S(1)} collective-permute-done((bf16[128,512]{1,0:T(8,128)(2,1)}, bf16[128,512]{1,0:T(8,128)(2,1)S(1)}, u32[]{:S(2)}, u32[]{:S(2)}) %collective-permute-start) | collective-permute-done | bytes 131104 | tf_op jit(solution)/shard_map/ppermute | solution.py:142
  6.4 3.9 %collective-permute-start.1 = (bf16[128,512]{1,0:T(8,128)(2,1)S(1)}, bf16[128,512]{1,0:T(8,128)(2,1)S(1)}, u32[]{:S(2)}, u32[]{:S(2)}) collective-permute-start(bf16[128,512]{1,0:T(8,128)(2,1)S(1)} %collective-permute-done.refs_0_), channel_id=1, source_target_pairs={{0,2},{2,4},{4,6},{6,7},{7,5},{5,3},{3,1},{1,0},{8,10},{10,12},{12... | collective-permute-start | bytes 393224 | tf_op jit(solution)/shard_map/ppermute | solution.py:142
  10.3 0.0 collective-permute-done.4.refs_1_
  10.3 0.0 collective-permute-start.5
  10.3 0.0 copy-done.2
  10.3 0.0 copy-done
  10.3 0.1 pad_maximum_fusion
  10.4 0.1 collective-permute-start.8
  10.6 0.8 %collective-permute-done.9.refs_8_.refs_0_ = bf16[144,512]{1,0:T(8,128)(2,1)S(1)} collective-permute-done((bf16[144,512]{1,0:T(8,128)(2,1)S(1)}, bf16[144,512]{1,0:T(8,128)(2,1)S(1)}, u32[]{:S(2)}, u32[]{:S(2)}) %collective-permute-start.9) | collective-permute-done | bytes 147488 | tf_op jit(solution)/shard_map/ppermute | solution.py:142
  11.4 2.0 %collective-permute-start.11 = (bf16[144,512]{1,0:T(8,128)(2,1)S(1)}, bf16[144,512]{1,0:T(8,128)(2,1)S(1)}, u32[]{:S(2)}, u32[]{:S(2)}) collective-permute-start(bf16[144,512]{1,0:T(8,128)(2,1)S(1)} %collective-permute-done.9.refs_8_.refs_0_), channel_id=1, source_target_pairs={{0,2},{2,4},{4,6},{6,7},{7,5},{5,3},{3,1},{1,0},{8,10},{10,12},{12... | collective-permute-start | bytes 442376 | tf_op jit(solution)/shard_map/ppermute | solution.py:142
  13.3 0.0 collective-permute-done.10.refs_9_.refs_1_
  13.4 0.0 collective-permute-start.12
  13.4 0.3 collective-permute-done.1.refs_2_
  13.7 1.7 %collective-permute-start.2 = (bf16[128,512]{1,0:T(8,128)(2,1)S(1)}, bf16[128,512]{1,0:T(8,128)(2,1)S(1)}, u32[]{:S(2)}, u32[]{:S(2)}) collective-permute-start(bf16[128,512]{1,0:T(8,128)(2,1)S(1)} %collective-permute-done.1.refs_2_), channel_id=1, source_target_pairs={{0,2},{2,4},{4,6},{6,7},{7,5},{5,3},{3,1},{1,0},{8,10},{10,12},{12... | collective-permute-start | bytes 393224 | tf_op jit(solution)/shard_map/ppermute | solution.py:142
  15.4 0.4 %collective-permute-done.5.refs_3_ = bf16[128,512]{1,0:T(8,128)(2,1)S(1)} collective-permute-done((bf16[128,512]{1,0:T(8,128)(2,1)S(1)}, bf16[128,512]{1,0:T(8,128)(2,1)S(1)}, u32[]{:S(2)}, u32[]{:S(2)}) %collective-permute-start.5) | collective-permute-done | bytes 131104 | tf_op jit(solution)/shard_map/ppermute | solution.py:142
  15.8 0.3 collective-permute-start.6
  16.1 2.0 %collective-permute-done.11.refs_10_.refs_2_ = bf16[144,512]{1,0:T(8,128)(2,1)S(1)} collective-permute-done((bf16[144,512]{1,0:T(8,128)(2,1)S(1)}, bf16[144,512]{1,0:T(8,128)(2,1)S(1)}, u32[]{:S(2)}, u32[]{:S(2)}) %collective-permute-start.11) | collective-permute-done | bytes 147488 | tf_op jit(solution)/shard_map/ppermute | solution.py:142
  18.0 2.0 %collective-permute-start.13 = (bf16[144,512]{1,0:T(8,128)(2,1)S(1)}, bf16[144,512]{1,0:T(8,128)(2,1)S(1)}, u32[]{:S(2)}, u32[]{:S(2)}) collective-permute-start(bf16[144,512]{1,0:T(8,128)(2,1)S(1)} %collective-permute-done.11.refs_10_.refs_2_), channel_id=1, source_target_pairs={{0,2},{2,4},{4,6},{6,7},{7,5},{5,3},{3,1},{1,0},{8,10},{10,12},{12... | collective-permute-start | bytes 442376 | tf_op jit(solution)/shard_map/ppermute | solution.py:142
  20.0 0.0 collective-permute-done.12.refs_11_.refs_3_
  20.1 0.0 collective-permute-start.14
  20.1 0.3 collective-permute-done.2.refs_4_
  20.4 2.5 %collective-permute-start.3 = (bf16[64,512]{1,0:T(8,128)(2,1)S(1)}, bf16[64,512]{1,0:T(8,128)(2,1)S(1)}, u32[]{:S(2)}, u32[]{:S(2)}) collective-permute-start(bf16[64,512]{1,0:T(8,128)(2,1)S(1)} %slice.16), channel_id=1, source_target_pairs={{0,2},{2,4},{4,6},{6,7},{7,5},{5,3},{3,1},{1,0},{8,10},{10,12},{12... | collective-permute-start | bytes 196616 | tf_op jit(solution)/shard_map/ppermute | solution.py:142
  22.8 0.0 collective-permute-done.6.refs_5_
  22.9 0.1 collective-permute-start.7
  22.9 0.0 copy-done.3
  22.9 1.0 %collective-permute-done.13.refs_12_.refs_4_ = bf16[144,512]{1,0:T(8,128)(2,1)S(1)} collective-permute-done((bf16[144,512]{1,0:T(8,128)(2,1)S(1)}, bf16[144,512]{1,0:T(8,128)(2,1)S(1)}, u32[]{:S(2)}, u32[]{:S(2)}) %collective-permute-start.13) | collective-permute-done | bytes 147488 | tf_op jit(solution)/shard_map/ppermute | solution.py:142
  23.9 2.1 %collective-permute-start.15 = (bf16[64,512]{1,0:T(8,128)(2,1)S(1)}, bf16[64,512]{1,0:T(8,128)(2,1)S(1)}, u32[]{:S(2)}, u32[]{:S(2)}) collective-permute-start(bf16[64,512]{1,0:T(8,128)(2,1)S(1)} %slice.18), channel_id=1, source_target_pairs={{0,2},{2,4},{4,6},{6,7},{7,5},{5,3},{3,1},{1,0},{8,10},{10,12},{12... | collective-permute-start | bytes 196616 | tf_op jit(solution)/shard_map/ppermute | solution.py:142
  26.1 0.0 collective-permute-done.14.refs_13_.refs_5_
  26.1 0.1 collective-permute-start.16
  26.1 0.0 collective-permute-done.3.refs_0_.refs_6_
  26.1 1.4 %collective-permute-done.7.refs_1_.refs_7_ = bf16[64,512]{1,0:T(8,128)(2,1)S(1)} collective-permute-done((bf16[64,512]{1,0:T(8,128)(2,1)S(1)}, bf16[64,512]{1,0:T(8,128)(2,1)S(1)}, u32[]{:S(2)}, u32[]{:S(2)}) %collective-permute-start.7) | collective-permute-done | bytes 65568 | tf_op jit(solution)/shard_map/ppermute | solution.py:142
  27.5 0.3 %shard_map.55.bias_ref = f32[2,64,320]{2,1,0:T(8,128)S(1)} custom-call(f32[1,1152]{1,0:T(1,128)S(1)} %add_convert_fusion.pos_ref, bf16[64,512]{1,0:T(8,128)(2,1)S(1)} %collective-permute-done.3.refs_0_.refs_6_, bf16[64,512]{1,0:T(8,128)(2,1)S(1)} %collective-permute-done.7.refs_1_.refs_7_), custom_call_target="tpu_custom_call" | custom-call | flops 9395240960 | tf_op jit(solution)/shard_map/pallas_call | solution.py:167
  27.9 0.0 collective-permute-done.8.own_ref
  27.9 2.0 %shard_map.57 = (bf16[8,512,320]{2,1,0:T(8,128)(2,1)S(1)}, bf16[16,64,512]{2,1,0:T(8,128)(2,1)S(1)}) custom-call(f32[1,1152]{1,0:T(1,128)S(1)} %add_convert_fusion.pos_ref, f32[2,64,320]{2,1,0:T(8,128)S(1)} %shard_map.55.bias_ref, bf16[128,5120]{1,0:T(8,128)(2,1)S(1)} %collective-permute-done.8.own_ref, bf16[128,512]{1,0:T(8,128)(2,1)S(1)} %collective-permute-done.refs_0_, ...), custom_call_target="tpu_custom_call" | custom-call | flops 67108864 | bytes 1048576 | tf_op jit(solution)/shard_map/pallas_call | solution.py:175
  29.8 0.0 collective-permute-done.15.refs_6_
  29.9 0.5 %collective-permute-done.16.refs_7_ = bf16[64,512]{1,0:T(8,128)(2,1)S(1)} collective-permute-done((bf16[64,512]{1,0:T(8,128)(2,1)S(1)}, bf16[64,512]{1,0:T(8,128)(2,1)S(1)}, u32[]{:S(2)}, u32[]{:S(2)}) %collective-permute-start.16) | collective-permute-done | bytes 65568 | tf_op jit(solution)/shard_map/ppermute | solution.py:142
  30.4 2.2 %shard_map.58 = bf16[128,4096]{1,0:T(8,128)(2,1)} custom-call(f32[1,1152]{1,0:T(1,128)S(1)} %add_convert_fusion.pos_ref, bf16[8,512,320]{2,1,0:T(8,128)(2,1)S(1)} %get-tuple-element.7.weights_ref, bf16[16,64,512]{2,1,0:T(8,128)(2,1)S(1)} %get-tuple-element.8.sorted_ref, bf16[144,512]{1,0:T(8,128)(2,1)S(1)} %collective-permute-done.9.refs_8_.refs_0_, ...), custom_call_target="tpu_custom_call" | custom-call | flops 67108864 | bytes 1048576 | tf_op jit(solution)/shard_map/pallas_call | solution.py:187
  (10 shorter events, 0.1 us)
Async XLA Ops:
  0.0 10.3 %copy-start.2 = (bf16[1,128,512]{2,1,0:T(8,128)(2,1)S(1)}, bf16[1,128,512]{2,1,0:T(8,128)(2,1)}, u32[]{:S(2)}) copy-start(bf16[1,128,512]{2,1,0:T(8,128)(2,1)} %param.6) | copy-start | bytes 393220
  0.0 4.2 %copy-start.4 = (s32[128]{0:T(128)S(1)}, s32[128]{0:T(128)}, u32[]{:S(2)}) copy-start(s32[128]{0:T(128)} %param.8) | copy-start | bytes 1540
  0.0 4.2 %copy-start.1 = (bf16[1,128,512]{2,1,0:T(8,128)(2,1)S(1)}, bf16[1,128,512]{2,1,0:T(8,128)(2,1)}, u32[]{:S(2)}) copy-start(bf16[1,128,512]{2,1,0:T(8,128)(2,1)} %param.7) | copy-start | bytes 393220
  0.0 10.3 %copy-start = (bf16[1,128,4096]{2,1,0:T(8,128)(2,1)S(1)}, bf16[1,128,4096]{2,1,0:T(8,128)(2,1)}, u32[]{:S(2)}) copy-start(bf16[1,128,4096]{2,1,0:T(8,128)(2,1)} %param.5) | copy-start | bytes 3145732
  0.0 22.9 %copy-start.3 = (s32[1024]{0:T(1024)S(1)}, s32[1024]{0:T(1024)}, u32[]{:S(2)}) copy-start(s32[1024]{0:T(1024)} %param.9) | copy-start | bytes 12292
  0.0 6.4 %collective-permute-start = (bf16[128,512]{1,0:T(8,128)(2,1)}, bf16[128,512]{1,0:T(8,128)(2,1)S(1)}, u32[]{:S(2)}, u32[]{:S(2)}) collective-permute-start(bf16[128,512]{1,0:T(8,128)(2,1)} %bitcast.9), channel_id=1, source_target_pairs={{0,10},{2,12},{4,14},{6,15},{7,13},{5,11},{3,9},{1,8},{8,18},{10,2... | collective-permute-start | bytes 393224 | tf_op jit(solution)/shard_map/ppermute | solution.py:142
  2.5 7.8 %collective-permute-start.4 = (bf16[128,512]{1,0:T(8,128)(2,1)}, bf16[128,512]{1,0:T(8,128)(2,1)S(1)}, u32[]{:S(2)}, u32[]{:S(2)}) collective-permute-start(bf16[128,512]{1,0:T(8,128)(2,1)} %bitcast.10), channel_id=1, source_target_pairs={{0,9},{2,8},{4,10},{6,12},{7,14},{5,15},{3,13},{1,11},{8,17},{10,1... | collective-permute-start | bytes 393224 | tf_op jit(solution)/shard_map/ppermute | solution.py:142
  4.3 7.1 %collective-permute-start.9 = (bf16[144,512]{1,0:T(8,128)(2,1)S(1)}, bf16[144,512]{1,0:T(8,128)(2,1)S(1)}, u32[]{:S(2)}, u32[]{:S(2)}) collective-permute-start(bf16[144,512]{1,0:T(8,128)(2,1)S(1)} %pad_maximum_fusion.1), channel_id=1, source_target_pairs={{0,10},{2,12},{4,14},{6,15},{7,13},{5,11},{3,9},{1,8},{8,18},{10,2... | collective-permute-start | bytes 442376 | tf_op jit(solution)/shard_map/ppermute | solution.py:142
  5.5 7.9 %collective-permute-start.10 = (bf16[144,512]{1,0:T(8,128)(2,1)S(1)}, bf16[144,512]{1,0:T(8,128)(2,1)S(1)}, u32[]{:S(2)}, u32[]{:S(2)}) collective-permute-start(bf16[144,512]{1,0:T(8,128)(2,1)S(1)} %pad_maximum_fusion.1), channel_id=1, source_target_pairs={{0,9},{2,8},{4,10},{6,12},{7,14},{5,15},{3,13},{1,11},{8,17},{10,1... | collective-permute-start | bytes 442376 | tf_op jit(solution)/shard_map/ppermute | solution.py:142
  6.4 7.3 %collective-permute-start.1 = (bf16[128,512]{1,0:T(8,128)(2,1)S(1)}, bf16[128,512]{1,0:T(8,128)(2,1)S(1)}, u32[]{:S(2)}, u32[]{:S(2)}) collective-permute-start(bf16[128,512]{1,0:T(8,128)(2,1)S(1)} %collective-permute-done.refs_0_), channel_id=1, source_target_pairs={{0,2},{2,4},{4,6},{6,7},{7,5},{5,3},{3,1},{1,0},{8,10},{10,12},{12... | collective-permute-start | bytes 393224 | tf_op jit(solution)/shard_map/ppermute | solution.py:142
  10.3 5.5 %collective-permute-start.5 = (bf16[128,512]{1,0:T(8,128)(2,1)S(1)}, bf16[128,512]{1,0:T(8,128)(2,1)S(1)}, u32[]{:S(2)}, u32[]{:S(2)}) collective-permute-start(bf16[128,512]{1,0:T(8,128)(2,1)S(1)} %collective-permute-done.4.refs_1_), channel_id=1, source_target_pairs={{0,1},{2,0},{4,2},{6,4},{7,6},{5,7},{3,5},{1,3},{8,9},{10,8},{12,1... | collective-permute-start | bytes 393224 | tf_op jit(solution)/shard_map/ppermute | solution.py:142
  10.4 17.4 %collective-permute-start.8 = (bf16[128,5120]{1,0:T(8,128)(2,1)S(1)}, bf16[128,5120]{1,0:T(8,128)(2,1)S(1)}, u32[]{:S(2)}, u32[]{:S(2)}) collective-permute-start(bf16[128,5120]{1,0:T(8,128)(2,1)S(1)} %pad_maximum_fusion), channel_id=1, source_target_pairs={{0,8},{2,10},{4,12},{6,14},{7,15},{5,13},{3,11},{1,9},{8,16},{10,1... | collective-permute-start | bytes 3932168 | tf_op jit(solution)/shard_map/ppermute | solution.py:142
  11.4 6.7 %collective-permute-start.11 = (bf16[144,512]{1,0:T(8,128)(2,1)S(1)}, bf16[144,512]{1,0:T(8,128)(2,1)S(1)}, u32[]{:S(2)}, u32[]{:S(2)}) collective-permute-start(bf16[144,512]{1,0:T(8,128)(2,1)S(1)} %collective-permute-done.9.refs_8_.refs_0_), channel_id=1, source_target_pairs={{0,2},{2,4},{4,6},{6,7},{7,5},{5,3},{3,1},{1,0},{8,10},{10,12},{12... | collective-permute-start | bytes 442376 | tf_op jit(solution)/shard_map/ppermute | solution.py:142
  13.4 6.7 %collective-permute-start.12 = (bf16[144,512]{1,0:T(8,128)(2,1)S(1)}, bf16[144,512]{1,0:T(8,128)(2,1)S(1)}, u32[]{:S(2)}, u32[]{:S(2)}) collective-permute-start(bf16[144,512]{1,0:T(8,128)(2,1)S(1)} %collective-permute-done.10.refs_9_.refs_1_), channel_id=1, source_target_pairs={{0,1},{2,0},{4,2},{6,4},{7,6},{5,7},{3,5},{1,3},{8,9},{10,8},{12,1... | collective-permute-start | bytes 442376 | tf_op jit(solution)/shard_map/ppermute | solution.py:142
  13.7 6.7 %collective-permute-start.2 = (bf16[128,512]{1,0:T(8,128)(2,1)S(1)}, bf16[128,512]{1,0:T(8,128)(2,1)S(1)}, u32[]{:S(2)}, u32[]{:S(2)}) collective-permute-start(bf16[128,512]{1,0:T(8,128)(2,1)S(1)} %collective-permute-done.1.refs_2_), channel_id=1, source_target_pairs={{0,2},{2,4},{4,6},{6,7},{7,5},{5,3},{3,1},{1,0},{8,10},{10,12},{12... | collective-permute-start | bytes 393224 | tf_op jit(solution)/shard_map/ppermute | solution.py:142
  15.8 7.0 %collective-permute-start.6 = (bf16[128,512]{1,0:T(8,128)(2,1)S(1)}, bf16[128,512]{1,0:T(8,128)(2,1)S(1)}, u32[]{:S(2)}, u32[]{:S(2)}) collective-permute-start(bf16[128,512]{1,0:T(8,128)(2,1)S(1)} %collective-permute-done.5.refs_3_), channel_id=1, source_target_pairs={{0,1},{2,0},{4,2},{6,4},{7,6},{5,7},{3,5},{1,3},{8,9},{10,8},{12,1... | collective-permute-start | bytes 393224 | tf_op jit(solution)/shard_map/ppermute | solution.py:142
  18.0 5.9 %collective-permute-start.13 = (bf16[144,512]{1,0:T(8,128)(2,1)S(1)}, bf16[144,512]{1,0:T(8,128)(2,1)S(1)}, u32[]{:S(2)}, u32[]{:S(2)}) collective-permute-start(bf16[144,512]{1,0:T(8,128)(2,1)S(1)} %collective-permute-done.11.refs_10_.refs_2_), channel_id=1, source_target_pairs={{0,2},{2,4},{4,6},{6,7},{7,5},{5,3},{3,1},{1,0},{8,10},{10,12},{12... | collective-permute-start | bytes 442376 | tf_op jit(solution)/shard_map/ppermute | solution.py:142
  20.1 6.0 %collective-permute-start.14 = (bf16[144,512]{1,0:T(8,128)(2,1)S(1)}, bf16[144,512]{1,0:T(8,128)(2,1)S(1)}, u32[]{:S(2)}, u32[]{:S(2)}) collective-permute-start(bf16[144,512]{1,0:T(8,128)(2,1)S(1)} %collective-permute-done.12.refs_11_.refs_3_), channel_id=1, source_target_pairs={{0,1},{2,0},{4,2},{6,4},{7,6},{5,7},{3,5},{1,3},{8,9},{10,8},{12,1... | collective-permute-start | bytes 442376 | tf_op jit(solution)/shard_map/ppermute | solution.py:142
  20.4 5.8 %collective-permute-start.3 = (bf16[64,512]{1,0:T(8,128)(2,1)S(1)}, bf16[64,512]{1,0:T(8,128)(2,1)S(1)}, u32[]{:S(2)}, u32[]{:S(2)}) collective-permute-start(bf16[64,512]{1,0:T(8,128)(2,1)S(1)} %slice.16), channel_id=1, source_target_pairs={{0,2},{2,4},{4,6},{6,7},{7,5},{5,3},{3,1},{1,0},{8,10},{10,12},{12... | collective-permute-start | bytes 196616 | tf_op jit(solution)/shard_map/ppermute | solution.py:142
  22.9 4.7 %collective-permute-start.7 = (bf16[64,512]{1,0:T(8,128)(2,1)S(1)}, bf16[64,512]{1,0:T(8,128)(2,1)S(1)}, u32[]{:S(2)}, u32[]{:S(2)}) collective-permute-start(bf16[64,512]{1,0:T(8,128)(2,1)S(1)} %slice.17), channel_id=1, source_target_pairs={{0,1},{2,0},{4,2},{6,4},{7,6},{5,7},{3,5},{1,3},{8,9},{10,8},{12,1... | collective-permute-start | bytes 196616 | tf_op jit(solution)/shard_map/ppermute | solution.py:142
  23.9 5.9 %collective-permute-start.15 = (bf16[64,512]{1,0:T(8,128)(2,1)S(1)}, bf16[64,512]{1,0:T(8,128)(2,1)S(1)}, u32[]{:S(2)}, u32[]{:S(2)}) collective-permute-start(bf16[64,512]{1,0:T(8,128)(2,1)S(1)} %slice.18), channel_id=1, source_target_pairs={{0,2},{2,4},{4,6},{6,7},{7,5},{5,3},{3,1},{1,0},{8,10},{10,12},{12... | collective-permute-start | bytes 196616 | tf_op jit(solution)/shard_map/ppermute | solution.py:142
  26.1 4.3 %collective-permute-start.16 = (bf16[64,512]{1,0:T(8,128)(2,1)S(1)}, bf16[64,512]{1,0:T(8,128)(2,1)S(1)}, u32[]{:S(2)}, u32[]{:S(2)}) collective-permute-start(bf16[64,512]{1,0:T(8,128)(2,1)S(1)} %slice.19), channel_id=1, source_target_pairs={{0,1},{2,0},{4,2},{6,4},{7,6},{5,7},{3,5},{1,3},{8,9},{10,8},{12,1... | collective-permute-start | bytes 196616 | tf_op jit(solution)/shard_map/ppermute | solution.py:142

commit v10 on v9

--- a/solution.py
+++ b/solution.py
@@ -17,6 +17,7 @@
 QUERY_COLUMNS = QUERY_HEADS * HEAD_SIZE
 KV_COLUMNS = KEY_VALUE_HEADS * HEAD_SIZE
 TAG_ROWS = 16
+VALUE_ROWS = KEY_VALUE_HEADS * TOK_DEV
 
 masked_fill = -1e30
 
@@ -28,26 +29,38 @@
 def run_numbers(runs, pos_ref, tagged_refs):
     firsts = [first_run(pos_ref)]
     for ref in tagged_refs:
-        firsts.append(jnp.min(ref[TOK_DEV:, :TOK_DEV].astype(jnp.float32)).astype(jnp.int32))
+        firsts.append(jnp.min(ref[VALUE_ROWS:, :].astype(jnp.float32)).astype(jnp.int32))
     places = runs // 2
     firsts.append(places * (places - 1) // 2 - sum(firsts))
     return [(first, runs - 1 - first) for first in firsts]
 
 
-def sort_runs(numbers, own_ref, own_column, block_refs, sorted_ref):
+def sort_keys(numbers, own_ref, block_refs, last_refs, sorted_ref):
     for half, number in enumerate(numbers[0]):
-        sorted_ref[number] = own_ref[half * RUN : (half + 1) * RUN, own_column : own_column + KV_COLUMNS]
+        sorted_ref[number] = own_ref[half * RUN : (half + 1) * RUN, QUERY_COLUMNS : QUERY_COLUMNS + KV_COLUMNS]
     for (first, second), ref in zip(numbers[1:], block_refs):
         sorted_ref[first] = ref[:RUN, :]
-        sorted_ref[second] = ref[RUN:TOK_DEV, :]
-
-
-def blank_kernel(out_ref):
-    out_ref[...] = jnp.zeros_like(out_ref)
-
-
-def bias_kernel(runs, pos_ref, *refs):
-    bias_ref = refs[-1]
+        sorted_ref[second] = ref[RUN:, :]
+    for number, ref in zip(numbers[-1], last_refs):
+        sorted_ref[number] = ref[...]
+
+
+def sort_values(numbers, own_ref, block_refs, sorted_ref):
+    for kv in range(KEY_VALUE_HEADS):
+        column = QUERY_COLUMNS + KV_COLUMNS + kv * HEAD_SIZE
+        for half, number in enumerate(numbers[0]):
+            sorted_ref[kv, number] = own_ref[half * RUN : (half + 1) * RUN, column : column + HEAD_SIZE]
+        for pair, ref in zip(numbers[1:], block_refs):
+            for half, number in enumerate(pair):
+                row = kv * TOK_DEV + half * RUN
+                sorted_ref[kv, number] = ref[row : row + RUN, :]
+
+
+def blank_kernel(*refs):
+    refs[-1][...] = jnp.zeros_like(refs[-1])
+
+
+def bias_kernel(runs, pos_ref, bias_ref):
     reach = runs // 4
     segment = pos_ref[:, TOK_DEV:]
     first = first_run(pos_ref)
@@ -60,17 +73,15 @@
         bias_ref[half] = jnp.where((key_pos <= row_pos) & (key_pos >= doc_start), 0.0, masked_fill)
 
 
-def weights_kernel(runs, pos_ref, bias_ref, own_ref, *refs):
+def weights_kernel(runs, pos_ref, bias_ref, mark_ref, own_ref, *refs):
     blocks = runs // 2
     key_refs, tagged_refs = refs[:blocks], refs[blocks:-3]
     weights_ref, sorted_ref, key_buf = refs[-3:]
     reach = runs // 4
     span = (reach + 1) * RUN
     numbers = run_numbers(runs, pos_ref, tagged_refs)
-    sort_runs(numbers, own_ref, QUERY_COLUMNS, key_refs[:-2], key_buf)
-    for number, ref in zip(numbers[-1], key_refs[-2:]):
-        key_buf[number] = ref[...]
-    sort_runs(numbers, own_ref, QUERY_COLUMNS + KV_COLUMNS, tagged_refs, sorted_ref)
+    sort_keys(numbers, own_ref, key_refs[:-2], key_refs[-2:], key_buf)
+    sort_values(numbers, own_ref, tagged_refs, sorted_ref)
     scale = math.log2(math.e) / math.sqrt(HEAD_SIZE)
     for half in range(2):
         start = jnp.maximum(numbers[0][half] - reach, 0)
@@ -103,12 +114,13 @@
     for half in range(2):
         start = jnp.maximum(numbers[0][half] - reach, 0)
         for kv in range(KEY_VALUE_HEADS):
-            columns = slice(kv * HEAD_SIZE, (kv + 1) * HEAD_SIZE)
+            last_ref = last_refs[kv * 2 // KEY_VALUE_HEADS]
             parts = []
             for i in range(reach + 1):
-                part = sorted_ref[start + i, :, columns]
-                for number, last_ref in zip(numbers[-1], last_refs):
-                    part = jnp.where(start + i == number, last_ref[:, columns], part)
+                part = sorted_ref[kv, start + i]
+                for last_half, number in enumerate(numbers[-1]):
+                    row = kv % (KEY_VALUE_HEADS // 2) * TOK_DEV + last_half * RUN
+                    part = jnp.where(start + i == number, last_ref[row : row + RUN, :], part)
                 parts.append(part)
             summed = jnp.dot(
                 weights_ref[half * KEY_VALUE_HEADS + kv],
@@ -141,49 +153,60 @@
                 pairs.append((s * places + ring[i], target))
         return lax.ppermute(block, ("section", "ctx"), pairs)
 
-    def around(block):
+    def around(block, rows, before_last=None):
         ahead, back = shift(block, 1, 1), shift(block, 1, -1)
         held = [ahead, back]
         for _ in range(2, places // 2):
             ahead, back = shift(ahead, 0, 1), shift(back, 0, -1)
             held.extend([ahead, back])
-        return held + [shift(ahead[:RUN], 0, 1), shift(back[RUN:TOK_DEV], 0, -1)]
+        if before_last is not None:
+            ahead, _ = lax.optimization_barrier((ahead, before_last))
+        return held + [shift(ahead[: rows // 2], 0, 1), shift(back[rows // 2 : rows], 0, -1)]
 
     own = shift(jnp.concatenate([queries[0], keys[0], values[0]], axis=1), 1, 0)
     vmem = pl.BlockSpec(memory_space=pltpu.VMEM)
     blank = pl.pallas_call(
         blank_kernel,
-        out_shape=jax.ShapeDtypeStruct((TAG_ROWS, KV_COLUMNS), jnp.bfloat16),
+        out_shape=jax.ShapeDtypeStruct((TAG_ROWS, TOK_DEV), jnp.bfloat16),
         out_specs=vmem,
         compiler_params=pltpu.CompilerParams(vmem_limit_bytes=8 * 1024 * 1024),
         cost_estimate=pl.CostEstimate(flops=1 << 30, bytes_accessed=0, transcendentals=0),
     )()
-    tag = jnp.pad((token_pos >> (RUN.bit_length() - 1)).astype(jnp.bfloat16), (0, KV_COLUMNS - TOK_DEV))
-    tagged = jnp.concatenate([values[0], blank + tag[None]], axis=0)
-    all_keys, all_values = around(keys[0]), around(tagged)
+    tag = (token_pos >> (RUN.bit_length() - 1)).astype(jnp.bfloat16)
+    by_head = [values[0, :, kv * HEAD_SIZE : (kv + 1) * HEAD_SIZE] for kv in range(KEY_VALUE_HEADS)]
+    tagged = jnp.concatenate([*by_head, blank + tag[None]], axis=0)
     pos = lax.optimization_barrier(jnp.concatenate([token_pos, segment]).astype(jnp.float32)[None])
-    params = pltpu.CompilerParams(vmem_limit_bytes=(12 + runs // 4) * 1024 * 1024)
-    before_mask = all_keys[-2:]
     bias = pl.pallas_call(
         functools.partial(bias_kernel, runs),
         out_shape=jax.ShapeDtypeStruct((2, RUN, (runs // 4 + 1) * RUN), jnp.float32),
-        in_specs=[vmem] * (1 + len(before_mask)),
+        in_specs=[vmem],
+        out_specs=vmem,
+        compiler_params=pltpu.CompilerParams(vmem_limit_bytes=8 * 1024 * 1024),
+        cost_estimate=pl.CostEstimate(flops=1 << 20, bytes_accessed=1 << 10, transcendentals=0),
+    )(pos)
+    all_keys = around(keys[0], TOK_DEV)
+    all_values = around(tagged, VALUE_ROWS, bias)
+    params = pltpu.CompilerParams(vmem_limit_bytes=(12 + runs // 4) * 1024 * 1024)
+    mark = pl.pallas_call(
+        blank_kernel,
+        out_shape=jax.ShapeDtypeStruct((8, HEAD_SIZE), jnp.float32),
+        in_specs=[vmem] * 2,
         out_specs=vmem,
         compiler_params=pltpu.CompilerParams(vmem_limit_bytes=8 * 1024 * 1024),
         cost_estimate=pl.CostEstimate(flops=35 << 28, bytes_accessed=0, transcendentals=0),
-    )(pos, *before_mask)
+    )(*all_keys[-2:])
     weights, sorted_values = pl.pallas_call(
         functools.partial(weights_kernel, runs),
         out_shape=(
             jax.ShapeDtypeStruct((2 * KEY_VALUE_HEADS, GROUP * RUN, (runs // 4 + 1) * RUN), jnp.bfloat16),
-            jax.ShapeDtypeStruct((runs, RUN, KV_COLUMNS), jnp.bfloat16),
+            jax.ShapeDtypeStruct((KEY_VALUE_HEADS, runs, RUN, HEAD_SIZE), jnp.bfloat16),
         ),
-        in_specs=[vmem] * (3 + len(all_keys) + len(all_values[:-2])),
+        in_specs=[vmem] * (4 + len(all_keys) + len(all_values[:-2])),
         out_specs=(vmem,) * 2,
         scratch_shapes=[pltpu.VMEM((runs, RUN, KV_COLUMNS), jnp.bfloat16)],
         compiler_params=params,
         cost_estimate=pl.CostEstimate(flops=1 << 26, bytes_accessed=1 << 20, transcendentals=0),
-    )(pos, bias, own, *all_keys, *all_values[:-2])
+    )(pos, bias, mark, own, *all_keys, *all_values[:-2])
     out = pl.pallas_call(
         functools.partial(values_kernel, runs),
         out_shape=jax.ShapeDtypeStruct((TOK_DEV, QUERY_COLUMNS), jnp.bfloat16),

time: 32.7 us -> 32.1 us (0.982)
  waiting for transfers between devices: 7.51 us -> 6.62 us
    ppermute x17, waiting for transfers between devices: 7.51 us -> 6.62 us  [shift(): return lax.ppermute(block, ('section', 'ctx'), pairs)]
  transfers between devices with their start and end apart: 17 -> 17, of which waited for: 9 -> 10; matrix products, arithmetic and copies ran while one was open for 1% -> 1% of each run, Pallas kernels for 7% -> 7%
where the time goes in v10:
time: 32.1 us; the launch traced here: 31.9 us
  starting transfers between devices  20.4 us (64%)
  waiting for transfers between devices  6.62 us (21%)
  Pallas kernels  4.53 us (14%)
    ppermute x17, starting transfers between devices, shift(): return lax.ppermute(block, ('section', 'ctx'), pairs)  20.4 us
    ppermute x17, waiting for transfers between devices, shift(): return lax.ppermute(block, ('section', 'ctx'), pairs)  6.62 us
    pallas_call x1, Pallas kernels, per_device(): pl.pallas_call(functools.partial(values_kernel, runs), out_shape=jax.Shap...  2.23 us
    pallas_call x1, Pallas kernels, per_device(): pl.pallas_call(functools.partial(weights_kernel, runs), out_shape=(jax.Sh...  1.95 us
  transfers between devices with their start and end apart: 17, of which 10 were waited for; matrix products, arithmetic and copies ran while one was open for 1% of the time, Pallas kernels for 7%

profile of v10, /device:TPU:0, one launch (start us, length us, event | category | flops | bytes accessed | tf_op | source)
XLA Modules:
  0.0 31.9 jit_solution(4878072600849436934)
XLA Ops:
  0.0 0.0 copy-start.2
  0.0 0.0 copy-start.1
  0.0 0.0 copy-start.4
  0.0 0.0 copy-start
  0.0 0.0 copy-start.3
  0.0 2.5 %collective-permute-start = (bf16[128,512]{1,0:T(8,128)(2,1)}, bf16[128,512]{1,0:T(8,128)(2,1)S(1)}, u32[]{:S(2)}, u32[]{:S(2)}) collective-permute-start(bf16[128,512]{1,0:T(8,128)(2,1)} %bitcast.16), channel_id=1, source_target_pairs={{0,10},{2,12},{4,14},{6,15},{7,13},{5,11},{3,9},{1,8},{8,18},{10,2... | collective-permute-start | bytes 393224 | tf_op jit(solution)/shard_map/ppermute | solution.py:154
  2.5 1.7 %collective-permute-start.4 = (bf16[128,512]{1,0:T(8,128)(2,1)}, bf16[128,512]{1,0:T(8,128)(2,1)S(1)}, u32[]{:S(2)}, u32[]{:S(2)}) collective-permute-start(bf16[128,512]{1,0:T(8,128)(2,1)} %bitcast.17), channel_id=1, source_target_pairs={{0,9},{2,8},{4,10},{6,12},{7,14},{5,15},{3,13},{1,11},{8,17},{10,1... | collective-permute-start | bytes 393224 | tf_op jit(solution)/shard_map/ppermute | solution.py:154
  4.2 0.0 copy-done.1
  4.3 0.0 copy-done.4
  4.3 1.2 %collective-permute-start.9 = (bf16[528,128]{1,0:T(8,128)(2,1)S(1)}, bf16[528,128]{1,0:T(8,128)(2,1)S(1)}, u32[]{:S(2)}, u32[]{:S(2)}) collective-permute-start(bf16[528,128]{1,0:T(8,128)(2,1)S(1)} %constant_dynamic-update-slice_fusion), channel_id=1, source_target_pairs={{0,10},{2,12},{4,14},{6,15},{7,13},{5,11},{3,9},{1,8},{8,18},{10,2... | collective-permute-start | bytes 405512 | tf_op jit(solution)/shard_map/ppermute | solution.py:154
  5.5 0.1 collective-permute-start.10
  5.6 0.8 %collective-permute-done.refs_0_ = bf16[128,512]{1,0:T(8,128)(2,1)S(1)} collective-permute-done((bf16[128,512]{1,0:T(8,128)(2,1)}, bf16[128,512]{1,0:T(8,128)(2,1)S(1)}, u32[]{:S(2)}, u32[]{:S(2)}) %collective-permute-start) | collective-permute-done | bytes 131104 | tf_op jit(solution)/shard_map/ppermute | solution.py:154
  6.4 3.9 %collective-permute-start.1 = (bf16[128,512]{1,0:T(8,128)(2,1)S(1)}, bf16[128,512]{1,0:T(8,128)(2,1)S(1)}, u32[]{:S(2)}, u32[]{:S(2)}) collective-permute-start(bf16[128,512]{1,0:T(8,128)(2,1)S(1)} %collective-permute-done.refs_0_), channel_id=1, source_target_pairs={{0,2},{2,4},{4,6},{6,7},{7,5},{5,3},{3,1},{1,0},{8,10},{10,12},{12... | collective-permute-start | bytes 393224 | tf_op jit(solution)/shard_map/ppermute | solution.py:154
  10.3 0.0 collective-permute-done.4.refs_1_
  10.3 0.0 collective-permute-start.5
  10.3 0.0 copy-done.2
  10.3 0.0 copy-done
  10.3 0.1 pad_maximum_fusion
  10.4 0.1 collective-permute-start.8
  10.6 0.6 %collective-permute-done.9.refs_8_.refs_0_ = bf16[528,128]{1,0:T(8,128)(2,1)S(1)} collective-permute-done((bf16[528,128]{1,0:T(8,128)(2,1)S(1)}, bf16[528,128]{1,0:T(8,128)(2,1)S(1)}, u32[]{:S(2)}, u32[]{:S(2)}) %collective-permute-start.9) | collective-permute-done | bytes 135200 | tf_op jit(solution)/shard_map/ppermute | solution.py:154
  11.1 2.0 %collective-permute-start.11 = (bf16[528,128]{1,0:T(8,128)(2,1)S(1)}, bf16[528,128]{1,0:T(8,128)(2,1)S(1)}, u32[]{:S(2)}, u32[]{:S(2)}) collective-permute-start(bf16[528,128]{1,0:T(8,128)(2,1)S(1)} %collective-permute-done.9.refs_8_.refs_0_), channel_id=1, source_target_pairs={{0,2},{2,4},{4,6},{6,7},{7,5},{5,3},{3,1},{1,0},{8,10},{10,12},{12... | collective-permute-start | bytes 405512 | tf_op jit(solution)/shard_map/ppermute | solution.py:154
  13.1 0.0 collective-permute-done.10.refs_9_.refs_1_
  13.1 0.1 collective-permute-start.12
  13.2 0.4 %collective-permute-done.1.refs_2_ = bf16[128,512]{1,0:T(8,128)(2,1)S(1)} collective-permute-done((bf16[128,512]{1,0:T(8,128)(2,1)S(1)}, bf16[128,512]{1,0:T(8,128)(2,1)S(1)}, u32[]{:S(2)}, u32[]{:S(2)}) %collective-permute-start.1) | collective-permute-done | bytes 131104 | tf_op jit(solution)/shard_map/ppermute | solution.py:154
  13.5 1.7 %collective-permute-start.2 = (bf16[128,512]{1,0:T(8,128)(2,1)S(1)}, bf16[128,512]{1,0:T(8,128)(2,1)S(1)}, u32[]{:S(2)}, u32[]{:S(2)}) collective-permute-start(bf16[128,512]{1,0:T(8,128)(2,1)S(1)} %collective-permute-done.1.refs_2_), channel_id=1, source_target_pairs={{0,2},{2,4},{4,6},{6,7},{7,5},{5,3},{3,1},{1,0},{8,10},{10,12},{12... | collective-permute-start | bytes 393224 | tf_op jit(solution)/shard_map/ppermute | solution.py:154
  15.3 0.5 %collective-permute-done.5.refs_3_ = bf16[128,512]{1,0:T(8,128)(2,1)S(1)} collective-permute-done((bf16[128,512]{1,0:T(8,128)(2,1)S(1)}, bf16[128,512]{1,0:T(8,128)(2,1)S(1)}, u32[]{:S(2)}, u32[]{:S(2)}) %collective-permute-start.5) | collective-permute-done | bytes 131104 | tf_op jit(solution)/shard_map/ppermute | solution.py:154
  15.8 0.3 collective-permute-start.6
  16.1 1.4 %collective-permute-done.11.refs_10_.refs_2_ = bf16[528,128]{1,0:T(8,128)(2,1)S(1)} collective-permute-done((bf16[528,128]{1,0:T(8,128)(2,1)S(1)}, bf16[528,128]{1,0:T(8,128)(2,1)S(1)}, u32[]{:S(2)}, u32[]{:S(2)}) %collective-permute-start.11) | collective-permute-done | bytes 135200 | tf_op jit(solution)/shard_map/ppermute | solution.py:154
  17.5 2.0 %collective-permute-start.13 = (bf16[528,128]{1,0:T(8,128)(2,1)S(1)}, bf16[528,128]{1,0:T(8,128)(2,1)S(1)}, u32[]{:S(2)}, u32[]{:S(2)}) collective-permute-start(bf16[528,128]{1,0:T(8,128)(2,1)S(1)} %collective-permute-done.11.refs_10_.refs_2_), channel_id=1, source_target_pairs={{0,2},{2,4},{4,6},{6,7},{7,5},{5,3},{3,1},{1,0},{8,10},{10,12},{12... | collective-permute-start | bytes 405512 | tf_op jit(solution)/shard_map/ppermute | solution.py:154
  19.5 0.0 collective-permute-done.12.refs_11_.refs_3_
  19.5 0.0 collective-permute-start.14
  19.6 0.4 %collective-permute-done.2.refs_4_ = bf16[128,512]{1,0:T(8,128)(2,1)S(1)} collective-permute-done((bf16[128,512]{1,0:T(8,128)(2,1)S(1)}, bf16[128,512]{1,0:T(8,128)(2,1)S(1)}, u32[]{:S(2)}, u32[]{:S(2)}) %collective-permute-start.2) | collective-permute-done | bytes 131104 | tf_op jit(solution)/shard_map/ppermute | solution.py:154
  20.0 2.3 %collective-permute-start.3 = (bf16[64,512]{1,0:T(8,128)(2,1)S(1)}, bf16[64,512]{1,0:T(8,128)(2,1)S(1)}, u32[]{:S(2)}, u32[]{:S(2)}) collective-permute-start(bf16[64,512]{1,0:T(8,128)(2,1)S(1)} %slice.32), channel_id=1, source_target_pairs={{0,2},{2,4},{4,6},{6,7},{7,5},{5,3},{3,1},{1,0},{8,10},{10,12},{12... | collective-permute-start | bytes 196616 | tf_op jit(solution)/shard_map/ppermute | solution.py:154
  22.3 0.0 collective-permute-done.6.refs_5_
  22.3 0.1 collective-permute-start.7
  22.4 0.0 copy-done.3
  22.4 0.3 %shard_map.55.bias_ref = f32[2,64,320]{2,1,0:T(8,128)S(1)} custom-call(f32[1,1152]{1,0:T(1,128)S(1)} %add_convert_fusion.pos_ref), custom_call_target="tpu_custom_call" | custom-call | flops 1048576 | bytes 1024 | tf_op jit(solution)/shard_map/pallas_call | solution.py:179
  22.7 0.2 collective-permute-done.13.refs_12_.refs_4_
  22.9 2.4 %collective-permute-start.15 = (bf16[256,128]{1,0:T(8,128)(2,1)S(1)}, bf16[256,128]{1,0:T(8,128)(2,1)S(1)}, u32[]{:S(2)}, u32[]{:S(2)}) collective-permute-start(bf16[256,128]{1,0:T(8,128)(2,1)S(1)} %slice.30), channel_id=1, source_target_pairs={{0,2},{2,4},{4,6},{6,7},{7,5},{5,3},{3,1},{1,0},{8,10},{10,12},{12... | collective-permute-start | bytes 196616 | tf_op jit(solution)/shard_map/ppermute | solution.py:154
  25.4 0.0 collective-permute-done.14.refs_13_.refs_5_
  25.4 0.1 collective-permute-start.16
  25.4 0.0 collective-permute-done.3.refs_0_.refs_6_
  25.4 1.4 %collective-permute-done.7.refs_1_.refs_7_ = bf16[64,512]{1,0:T(8,128)(2,1)S(1)} collective-permute-done((bf16[64,512]{1,0:T(8,128)(2,1)S(1)}, bf16[64,512]{1,0:T(8,128)(2,1)S(1)}, u32[]{:S(2)}, u32[]{:S(2)}) %collective-permute-start.7) | collective-permute-done | bytes 65568 | tf_op jit(solution)/shard_map/ppermute | solution.py:154
  26.8 0.7 %collective-permute-done.8.own_ref = bf16[128,5120]{1,0:T(8,128)(2,1)S(1)} collective-permute-done((bf16[128,5120]{1,0:T(8,128)(2,1)S(1)}, bf16[128,5120]{1,0:T(8,128)(2,1)S(1)}, u32[]{:S(2)}, u32[]{:S(2)}) %collective-permute-start.8) | collective-permute-done | bytes 1310752 | tf_op jit(solution)/shard_map/ppermute | solution.py:154
  27.5 2.0 %shard_map.58 = (bf16[8,512,320]{2,1,0:T(8,128)(2,1)S(1)}, bf16[4,16,64,128]{3,2,1,0:T(8,128)(2,1)S(1)}) custom-call(f32[1,1152]{1,0:T(1,128)S(1)} %add_convert_fusion.pos_ref, f32[2,64,320]{2,1,0:T(8,128)S(1)} %shard_map.55.bias_ref, f32[8,128]{1,0:T(8,128)S(1)} %shard_map.56.mark_ref, bf16[128,5120]{1,0:T(8,128)(2,1)S(1)} %collective-permute-done.8.own_ref, ...), custom_call_target="tpu_custom_call" | custom-call | flops 67108864 | bytes 1048576 | tf_op jit(solution)/shard_map/pallas_call | solution.py:198
  29.5 0.0 collective-permute-done.15.refs_6_
  29.5 0.2 collective-permute-done.16.refs_7_
  29.7 2.2 %shard_map.59 = bf16[128,4096]{1,0:T(8,128)(2,1)} custom-call(f32[1,1152]{1,0:T(1,128)S(1)} %add_convert_fusion.pos_ref, bf16[8,512,320]{2,1,0:T(8,128)(2,1)S(1)} %get-tuple-element.8.weights_ref, bf16[4,16,64,128]{3,2,1,0:T(8,128)(2,1)S(1)} %get-tuple-element.9.sorted_ref, bf16[528,128]{1,0:T(8,128)(2,1)S(1)} %collective-permute-done.9.refs_8_.refs_0_, ...), custom_call_target="tpu_custom_call" | custom-call | flops 67108864 | bytes 1048576 | tf_op jit(solution)/shard_map/pallas_call | solution.py:210
  (13 shorter events, 0.1 us)
Async XLA Ops:
  0.0 10.3 %copy-start.2 = (bf16[1,128,512]{2,1,0:T(8,128)(2,1)S(1)}, bf16[1,128,512]{2,1,0:T(8,128)(2,1)}, u32[]{:S(2)}) copy-start(bf16[1,128,512]{2,1,0:T(8,128)(2,1)} %param.6) | copy-start | bytes 393220
  0.0 4.2 %copy-start.1 = (bf16[1,128,512]{2,1,0:T(8,128)(2,1)S(1)}, bf16[1,128,512]{2,1,0:T(8,128)(2,1)}, u32[]{:S(2)}) copy-start(bf16[1,128,512]{2,1,0:T(8,128)(2,1)} %param.7) | copy-start | bytes 393220
  0.0 4.3 %copy-start.4 = (s32[128]{0:T(128)S(1)}, s32[128]{0:T(128)}, u32[]{:S(2)}) copy-start(s32[128]{0:T(128)} %param.8) | copy-start | bytes 1540
  0.0 10.3 %copy-start = (bf16[1,128,4096]{2,1,0:T(8,128)(2,1)S(1)}, bf16[1,128,4096]{2,1,0:T(8,128)(2,1)}, u32[]{:S(2)}) copy-start(bf16[1,128,4096]{2,1,0:T(8,128)(2,1)} %param.5) | copy-start | bytes 3145732
  0.0 22.4 %copy-start.3 = (s32[1024]{0:T(1024)S(1)}, s32[1024]{0:T(1024)}, u32[]{:S(2)}) copy-start(s32[1024]{0:T(1024)} %param.9) | copy-start | bytes 12292
  0.0 6.4 %collective-permute-start = (bf16[128,512]{1,0:T(8,128)(2,1)}, bf16[128,512]{1,0:T(8,128)(2,1)S(1)}, u32[]{:S(2)}, u32[]{:S(2)}) collective-permute-start(bf16[128,512]{1,0:T(8,128)(2,1)} %bitcast.16), channel_id=1, source_target_pairs={{0,10},{2,12},{4,14},{6,15},{7,13},{5,11},{3,9},{1,8},{8,18},{10,2... | collective-permute-start | bytes 393224 | tf_op jit(solution)/shard_map/ppermute | solution.py:154
  2.5 7.8 %collective-permute-start.4 = (bf16[128,512]{1,0:T(8,128)(2,1)}, bf16[128,512]{1,0:T(8,128)(2,1)S(1)}, u32[]{:S(2)}, u32[]{:S(2)}) collective-permute-start(bf16[128,512]{1,0:T(8,128)(2,1)} %bitcast.17), channel_id=1, source_target_pairs={{0,9},{2,8},{4,10},{6,12},{7,14},{5,15},{3,13},{1,11},{8,17},{10,1... | collective-permute-start | bytes 393224 | tf_op jit(solution)/shard_map/ppermute | solution.py:154
  4.3 6.8 %collective-permute-start.9 = (bf16[528,128]{1,0:T(8,128)(2,1)S(1)}, bf16[528,128]{1,0:T(8,128)(2,1)S(1)}, u32[]{:S(2)}, u32[]{:S(2)}) collective-permute-start(bf16[528,128]{1,0:T(8,128)(2,1)S(1)} %constant_dynamic-update-slice_fusion), channel_id=1, source_target_pairs={{0,10},{2,12},{4,14},{6,15},{7,13},{5,11},{3,9},{1,8},{8,18},{10,2... | collective-permute-start | bytes 405512 | tf_op jit(solution)/shard_map/ppermute | solution.py:154
  5.5 7.6 %collective-permute-start.10 = (bf16[528,128]{1,0:T(8,128)(2,1)S(1)}, bf16[528,128]{1,0:T(8,128)(2,1)S(1)}, u32[]{:S(2)}, u32[]{:S(2)}) collective-permute-start(bf16[528,128]{1,0:T(8,128)(2,1)S(1)} %constant_dynamic-update-slice_fusion), channel_id=1, source_target_pairs={{0,9},{2,8},{4,10},{6,12},{7,14},{5,15},{3,13},{1,11},{8,17},{10,1... | collective-permute-start | bytes 405512 | tf_op jit(solution)/shard_map/ppermute | solution.py:154
  6.4 7.2 %collective-permute-start.1 = (bf16[128,512]{1,0:T(8,128)(2,1)S(1)}, bf16[128,512]{1,0:T(8,128)(2,1)S(1)}, u32[]{:S(2)}, u32[]{:S(2)}) collective-permute-start(bf16[128,512]{1,0:T(8,128)(2,1)S(1)} %collective-permute-done.refs_0_), channel_id=1, source_target_pairs={{0,2},{2,4},{4,6},{6,7},{7,5},{5,3},{3,1},{1,0},{8,10},{10,12},{12... | collective-permute-start | bytes 393224 | tf_op jit(solution)/shard_map/ppermute | solution.py:154
  10.3 5.5 %collective-permute-start.5 = (bf16[128,512]{1,0:T(8,128)(2,1)S(1)}, bf16[128,512]{1,0:T(8,128)(2,1)S(1)}, u32[]{:S(2)}, u32[]{:S(2)}) collective-permute-start(bf16[128,512]{1,0:T(8,128)(2,1)S(1)} %collective-permute-done.4.refs_1_), channel_id=1, source_target_pairs={{0,1},{2,0},{4,2},{6,4},{7,6},{5,7},{3,5},{1,3},{8,9},{10,8},{12,1... | collective-permute-start | bytes 393224 | tf_op jit(solution)/shard_map/ppermute | solution.py:154
  10.4 17.1 %collective-permute-start.8 = (bf16[128,5120]{1,0:T(8,128)(2,1)S(1)}, bf16[128,5120]{1,0:T(8,128)(2,1)S(1)}, u32[]{:S(2)}, u32[]{:S(2)}) collective-permute-start(bf16[128,5120]{1,0:T(8,128)(2,1)S(1)} %pad_maximum_fusion), channel_id=1, source_target_pairs={{0,8},{2,10},{4,12},{6,14},{7,15},{5,13},{3,11},{1,9},{8,16},{10,1... | collective-permute-start | bytes 3932168 | tf_op jit(solution)/shard_map/ppermute | solution.py:154
  11.1 6.4 %collective-permute-start.11 = (bf16[528,128]{1,0:T(8,128)(2,1)S(1)}, bf16[528,128]{1,0:T(8,128)(2,1)S(1)}, u32[]{:S(2)}, u32[]{:S(2)}) collective-permute-start(bf16[528,128]{1,0:T(8,128)(2,1)S(1)} %collective-permute-done.9.refs_8_.refs_0_), channel_id=1, source_target_pairs={{0,2},{2,4},{4,6},{6,7},{7,5},{5,3},{3,1},{1,0},{8,10},{10,12},{12... | collective-permute-start | bytes 405512 | tf_op jit(solution)/shard_map/ppermute | solution.py:154
  13.1 6.4 %collective-permute-start.12 = (bf16[528,128]{1,0:T(8,128)(2,1)S(1)}, bf16[528,128]{1,0:T(8,128)(2,1)S(1)}, u32[]{:S(2)}, u32[]{:S(2)}) collective-permute-start(bf16[528,128]{1,0:T(8,128)(2,1)S(1)} %collective-permute-done.10.refs_9_.refs_1_), channel_id=1, source_target_pairs={{0,1},{2,0},{4,2},{6,4},{7,6},{5,7},{3,5},{1,3},{8,9},{10,8},{12,1... | collective-permute-start | bytes 405512 | tf_op jit(solution)/shard_map/ppermute | solution.py:154
  13.5 6.4 %collective-permute-start.2 = (bf16[128,512]{1,0:T(8,128)(2,1)S(1)}, bf16[128,512]{1,0:T(8,128)(2,1)S(1)}, u32[]{:S(2)}, u32[]{:S(2)}) collective-permute-start(bf16[128,512]{1,0:T(8,128)(2,1)S(1)} %collective-permute-done.1.refs_2_), channel_id=1, source_target_pairs={{0,2},{2,4},{4,6},{6,7},{7,5},{5,3},{3,1},{1,0},{8,10},{10,12},{12... | collective-permute-start | bytes 393224 | tf_op jit(solution)/shard_map/ppermute | solution.py:154
  15.8 6.5 %collective-permute-start.6 = (bf16[128,512]{1,0:T(8,128)(2,1)S(1)}, bf16[128,512]{1,0:T(8,128)(2,1)S(1)}, u32[]{:S(2)}, u32[]{:S(2)}) collective-permute-start(bf16[128,512]{1,0:T(8,128)(2,1)S(1)} %collective-permute-done.5.refs_3_), channel_id=1, source_target_pairs={{0,1},{2,0},{4,2},{6,4},{7,6},{5,7},{3,5},{1,3},{8,9},{10,8},{12,1... | collective-permute-start | bytes 393224 | tf_op jit(solution)/shard_map/ppermute | solution.py:154
  17.5 5.4 %collective-permute-start.13 = (bf16[528,128]{1,0:T(8,128)(2,1)S(1)}, bf16[528,128]{1,0:T(8,128)(2,1)S(1)}, u32[]{:S(2)}, u32[]{:S(2)}) collective-permute-start(bf16[528,128]{1,0:T(8,128)(2,1)S(1)} %collective-permute-done.11.refs_10_.refs_2_), channel_id=1, source_target_pairs={{0,2},{2,4},{4,6},{6,7},{7,5},{5,3},{3,1},{1,0},{8,10},{10,12},{12... | collective-permute-start | bytes 405512 | tf_op jit(solution)/shard_map/ppermute | solution.py:154
  19.5 5.8 %collective-permute-start.14 = (bf16[528,128]{1,0:T(8,128)(2,1)S(1)}, bf16[528,128]{1,0:T(8,128)(2,1)S(1)}, u32[]{:S(2)}, u32[]{:S(2)}) collective-permute-start(bf16[528,128]{1,0:T(8,128)(2,1)S(1)} %collective-permute-done.12.refs_11_.refs_3_), channel_id=1, source_target_pairs={{0,1},{2,0},{4,2},{6,4},{7,6},{5,7},{3,5},{1,3},{8,9},{10,8},{12,1... | collective-permute-start | bytes 405512 | tf_op jit(solution)/shard_map/ppermute | solution.py:154
  20.0 5.5 %collective-permute-start.3 = (bf16[64,512]{1,0:T(8,128)(2,1)S(1)}, bf16[64,512]{1,0:T(8,128)(2,1)S(1)}, u32[]{:S(2)}, u32[]{:S(2)}) collective-permute-start(bf16[64,512]{1,0:T(8,128)(2,1)S(1)} %slice.32), channel_id=1, source_target_pairs={{0,2},{2,4},{4,6},{6,7},{7,5},{5,3},{3,1},{1,0},{8,10},{10,12},{12... | collective-permute-start | bytes 196616 | tf_op jit(solution)/shard_map/ppermute | solution.py:154
  22.3 4.5 %collective-permute-start.7 = (bf16[64,512]{1,0:T(8,128)(2,1)S(1)}, bf16[64,512]{1,0:T(8,128)(2,1)S(1)}, u32[]{:S(2)}, u32[]{:S(2)}) collective-permute-start(bf16[64,512]{1,0:T(8,128)(2,1)S(1)} %slice.33), channel_id=1, source_target_pairs={{0,1},{2,0},{4,2},{6,4},{7,6},{5,7},{3,5},{1,3},{8,9},{10,8},{12,1... | collective-permute-start | bytes 196616 | tf_op jit(solution)/shard_map/ppermute | solution.py:154
  22.9 6.5 %collective-permute-start.15 = (bf16[256,128]{1,0:T(8,128)(2,1)S(1)}, bf16[256,128]{1,0:T(8,128)(2,1)S(1)}, u32[]{:S(2)}, u32[]{:S(2)}) collective-permute-start(bf16[256,128]{1,0:T(8,128)(2,1)S(1)} %slice.30), channel_id=1, source_target_pairs={{0,2},{2,4},{4,6},{6,7},{7,5},{5,3},{3,1},{1,0},{8,10},{10,12},{12... | collective-permute-start | bytes 196616 | tf_op jit(solution)/shard_map/ppermute | solution.py:154
  25.4 4.3 %collective-permute-start.16 = (bf16[256,128]{1,0:T(8,128)(2,1)S(1)}, bf16[256,128]{1,0:T(8,128)(2,1)S(1)}, u32[]{:S(2)}, u32[]{:S(2)}) collective-permute-start(bf16[256,128]{1,0:T(8,128)(2,1)S(1)} %slice.34), channel_id=1, source_target_pairs={{0,1},{2,0},{4,2},{6,4},{7,6},{5,7},{3,5},{1,3},{8,9},{10,8},{12,1... | collective-permute-start | bytes 196616 | tf_op jit(solution)/shard_map/ppermute | solution.py:154

commit v11 on v10

--- a/solution.py
+++ b/solution.py
@@ -26,6 +26,16 @@
     return lax.div(jnp.min(pos_ref[:, :TOK_DEV]).astype(jnp.int32), RUN)
 
 
+def first_in_reach(runs, pos_ref, run):
+    reach = runs // 4
+    segment = pos_ref[:, TOK_DEV:]
+    position = lax.broadcasted_iota(jnp.int32, segment.shape, 1)
+    doc = jnp.max(jnp.where(position == run * RUN, segment, -1.0))
+    far_doc = jnp.max(jnp.where(position == (run - reach + 1) * RUN - 1, segment, -1.0))
+    far = doc == far_doc
+    return jnp.where(far, run - reach, jnp.maximum(run - reach + 1, 0)), far
+
+
 def run_numbers(runs, pos_ref, tagged_refs):
     firsts = [first_run(pos_ref)]
     for ref in tagged_refs:
@@ -61,7 +71,6 @@
 
 
 def bias_kernel(runs, pos_ref, bias_ref):
-    reach = runs // 4
     segment = pos_ref[:, TOK_DEV:]
     first = first_run(pos_ref)
     for half, run in enumerate((first, runs - 1 - first)):
@@ -69,7 +78,8 @@
         at = lax.broadcasted_iota(jnp.int32, (RUN, runs * RUN), 1) == row_pos
         row_doc = jnp.sum(jnp.where(at, segment, 0.0), axis=1, keepdims=True)
         doc_start = jnp.sum(jnp.where(segment < row_doc, 1.0, 0.0), axis=1, keepdims=True).astype(jnp.int32)
-        key_pos = jnp.maximum(run - reach, 0) * RUN + lax.broadcasted_iota(jnp.int32, bias_ref.shape[1:], 1)
+        start, _ = first_in_reach(runs, pos_ref, run)
+        key_pos = start * RUN + lax.broadcasted_iota(jnp.int32, bias_ref.shape[1:], 1)
         bias_ref[half] = jnp.where((key_pos <= row_pos) & (key_pos >= doc_start), 0.0, masked_fill)
 
 
@@ -77,15 +87,14 @@
     blocks = runs // 2
     key_refs, tagged_refs = refs[:blocks], refs[blocks:-3]
     weights_ref, sorted_ref, key_buf = refs[-3:]
-    reach = runs // 4
-    span = (reach + 1) * RUN
     numbers = run_numbers(runs, pos_ref, tagged_refs)
     sort_keys(numbers, own_ref, key_refs[:-2], key_refs[-2:], key_buf)
     sort_values(numbers, own_ref, tagged_refs, sorted_ref)
     scale = math.log2(math.e) / math.sqrt(HEAD_SIZE)
-    for half in range(2):
-        start = jnp.maximum(numbers[0][half] - reach, 0)
-        bias = jnp.concatenate([bias_ref[half]] * GROUP, axis=0)
+
+    def half_weights(half, start, count):
+        span = count * RUN
+        bias = jnp.concatenate([bias_ref[half, :, :span]] * GROUP, axis=0)
         for kv in range(KEY_VALUE_HEADS):
             query = jnp.concatenate(
                 [
@@ -94,7 +103,7 @@
                 ],
                 axis=0,
             )
-            key = key_buf[pl.ds(start, reach + 1), :, kv * HEAD_SIZE : (kv + 1) * HEAD_SIZE]
+            key = key_buf[pl.ds(start, count), :, kv * HEAD_SIZE : (kv + 1) * HEAD_SIZE]
             scores = bias + lax.dot_general(
                 query,
                 key.reshape(span, HEAD_SIZE),
@@ -102,28 +111,32 @@
                 preferred_element_type=jnp.float32,
             )
             row_max = jnp.max(scores, axis=1, keepdims=True)
-            weights_ref[half * KEY_VALUE_HEADS + kv] = jnp.exp2((scores - row_max) * scale).astype(jnp.bfloat16)
+            weights = jnp.exp2((scores - row_max) * scale).astype(jnp.bfloat16)
+            weights_ref[half * KEY_VALUE_HEADS + kv, :, :span] = weights
+
+    for half in range(2):
+        start, far = first_in_reach(runs, pos_ref, numbers[0][half])
+        pl.when(far)(functools.partial(half_weights, half, start, runs // 4 + 1))
+        pl.when(jnp.logical_not(far))(functools.partial(half_weights, half, start, runs // 4))
 
 
 def values_kernel(runs, pos_ref, weights_ref, sorted_ref, *refs):
     tagged_refs, last_refs, (out_ref, result_buf, out_sems) = refs[:-5], refs[-5:-3], refs[-3:]
-    reach = runs // 4
     numbers = run_numbers(runs, pos_ref, tagged_refs)
-    ones = jnp.ones(((reach + 1) * RUN, HEAD_SIZE), jnp.bfloat16)
-    copies = []
-    for half in range(2):
-        start = jnp.maximum(numbers[0][half] - reach, 0)
+
+    def half_values(half, start, count):
+        ones = jnp.ones((count * RUN, HEAD_SIZE), jnp.bfloat16)
         for kv in range(KEY_VALUE_HEADS):
             last_ref = last_refs[kv * 2 // KEY_VALUE_HEADS]
             parts = []
-            for i in range(reach + 1):
+            for i in range(count):
                 part = sorted_ref[kv, start + i]
                 for last_half, number in enumerate(numbers[-1]):
                     row = kv % (KEY_VALUE_HEADS // 2) * TOK_DEV + last_half * RUN
                     part = jnp.where(start + i == number, last_ref[row : row + RUN, :], part)
                 parts.append(part)
             summed = jnp.dot(
-                weights_ref[half * KEY_VALUE_HEADS + kv],
+                weights_ref[half * KEY_VALUE_HEADS + kv, :, : count * RUN],
                 jnp.concatenate([jnp.concatenate(parts, axis=0), ones], axis=1),
                 preferred_element_type=jnp.float32,
             )
@@ -131,6 +144,12 @@
             for i in range(GROUP):
                 h = kv * GROUP + i
                 result_buf[half, :, h * HEAD_SIZE : (h + 1) * HEAD_SIZE] = result[i * RUN : (i + 1) * RUN]
+
+    copies = []
+    for half in range(2):
+        start, far = first_in_reach(runs, pos_ref, numbers[0][half])
+        pl.when(far)(functools.partial(half_values, half, start, runs // 4 + 1))
+        pl.when(jnp.logical_not(far))(functools.partial(half_values, half, start, runs // 4))
         copies.append(
             pltpu.make_async_copy(result_buf.at[half], out_ref.at[pl.ds(half * RUN, RUN), :], out_sems.at[half])
         )
@@ -193,7 +212,7 @@
         in_specs=[vmem] * 2,
         out_specs=vmem,
         compiler_params=pltpu.CompilerParams(vmem_limit_bytes=8 * 1024 * 1024),
-        cost_estimate=pl.CostEstimate(flops=35 << 28, bytes_accessed=0, transcendentals=0),
+        cost_estimate=pl.CostEstimate(flops=65 << 27, bytes_accessed=0, transcendentals=0),
     )(*all_keys[-2:])
     weights, sorted_values = pl.pallas_call(
         functools.partial(weights_kernel, runs),

time: 32.1 us -> 31.7 us (0.988)
  no operation moved by 1% of the time
where the time goes in v11:
time: 31.7 us; the launch traced here: 31.6 us
  starting transfers between devices  20.1 us (63%)
  waiting for transfers between devices  6.9 us (22%)
  Pallas kernels  4.21 us (13%)
    ppermute x17, starting transfers between devices, shift(): return lax.ppermute(block, ('section', 'ctx'), pairs)  20.1 us
    ppermute x17, waiting for transfers between devices, shift(): return lax.ppermute(block, ('section', 'ctx'), pairs)  6.9 us
    pallas_call x1, Pallas kernels, per_device(): pl.pallas_call(functools.partial(values_kernel, runs), out_shape=jax.Shap...  2.12 us
    pallas_call x1, Pallas kernels, per_device(): pl.pallas_call(functools.partial(weights_kernel, runs), out_shape=(jax.Sh...  1.74 us
  transfers between devices with their start and end apart: 17, of which 10 were waited for; matrix products, arithmetic and copies ran while one was open for 1% of the time, Pallas kernels for 7%

profile of v11, /device:TPU:0, one launch (start us, length us, event | category | flops | bytes accessed | tf_op | source)
XLA Modules:
  0.0 31.6 jit_solution(534099979399760711)
XLA Ops:
  0.0 0.0 copy-start.2
  0.0 0.0 copy-start.1
  0.0 0.0 copy-start.4
  0.0 0.0 copy-start
  0.0 0.0 copy-start.3
  0.0 2.5 %collective-permute-start = (bf16[128,512]{1,0:T(8,128)(2,1)}, bf16[128,512]{1,0:T(8,128)(2,1)S(1)}, u32[]{:S(2)}, u32[]{:S(2)}) collective-permute-start(bf16[128,512]{1,0:T(8,128)(2,1)} %bitcast.16), channel_id=1, source_target_pairs={{0,10},{2,12},{4,14},{6,15},{7,13},{5,11},{3,9},{1,8},{8,18},{10,2... | collective-permute-start | bytes 393224 | tf_op jit(solution)/shard_map/ppermute | solution.py:173
  2.5 1.7 %collective-permute-start.4 = (bf16[128,512]{1,0:T(8,128)(2,1)}, bf16[128,512]{1,0:T(8,128)(2,1)S(1)}, u32[]{:S(2)}, u32[]{:S(2)}) collective-permute-start(bf16[128,512]{1,0:T(8,128)(2,1)} %bitcast.17), channel_id=1, source_target_pairs={{0,9},{2,8},{4,10},{6,12},{7,14},{5,15},{3,13},{1,11},{8,17},{10,1... | collective-permute-start | bytes 393224 | tf_op jit(solution)/shard_map/ppermute | solution.py:173
  4.2 0.0 copy-done.1
  4.3 0.0 copy-done.4
  4.3 1.2 %collective-permute-start.9 = (bf16[528,128]{1,0:T(8,128)(2,1)S(1)}, bf16[528,128]{1,0:T(8,128)(2,1)S(1)}, u32[]{:S(2)}, u32[]{:S(2)}) collective-permute-start(bf16[528,128]{1,0:T(8,128)(2,1)S(1)} %constant_dynamic-update-slice_fusion), channel_id=1, source_target_pairs={{0,10},{2,12},{4,14},{6,15},{7,13},{5,11},{3,9},{1,8},{8,18},{10,2... | collective-permute-start | bytes 405512 | tf_op jit(solution)/shard_map/ppermute | solution.py:173
  5.5 0.1 collective-permute-start.10
  5.6 0.0 copy-done.2
  5.6 0.0 copy-done
  5.6 0.1 pad_maximum_fusion
  5.7 0.5 %collective-permute-start.8 = (bf16[128,5120]{1,0:T(8,128)(2,1)S(1)}, bf16[128,5120]{1,0:T(8,128)(2,1)S(1)}, u32[]{:S(2)}, u32[]{:S(2)}) collective-permute-start(bf16[128,5120]{1,0:T(8,128)(2,1)S(1)} %pad_maximum_fusion), channel_id=1, source_target_pairs={{0,8},{2,10},{4,12},{6,14},{7,15},{5,13},{3,11},{1,9},{8,16},{10,1... | collective-permute-start | bytes 3932168 | tf_op jit(solution)/shard_map/ppermute | solution.py:173
  6.2 0.2 collective-permute-done.refs_0_
  6.4 3.9 %collective-permute-start.1 = (bf16[128,512]{1,0:T(8,128)(2,1)S(1)}, bf16[128,512]{1,0:T(8,128)(2,1)S(1)}, u32[]{:S(2)}, u32[]{:S(2)}) collective-permute-start(bf16[128,512]{1,0:T(8,128)(2,1)S(1)} %collective-permute-done.refs_0_), channel_id=1, source_target_pairs={{0,2},{2,4},{4,6},{6,7},{7,5},{5,3},{3,1},{1,0},{8,10},{10,12},{12... | collective-permute-start | bytes 393224 | tf_op jit(solution)/shard_map/ppermute | solution.py:173
  10.3 0.0 collective-permute-done.4.refs_1_
  10.3 0.0 collective-permute-start.5
  10.3 0.8 %collective-permute-done.9.refs_8_.refs_0_ = bf16[528,128]{1,0:T(8,128)(2,1)S(1)} collective-permute-done((bf16[528,128]{1,0:T(8,128)(2,1)S(1)}, bf16[528,128]{1,0:T(8,128)(2,1)S(1)}, u32[]{:S(2)}, u32[]{:S(2)}) %collective-permute-start.9) | collective-permute-done | bytes 135200 | tf_op jit(solution)/shard_map/ppermute | solution.py:173
  11.1 2.1 %collective-permute-start.11 = (bf16[528,128]{1,0:T(8,128)(2,1)S(1)}, bf16[528,128]{1,0:T(8,128)(2,1)S(1)}, u32[]{:S(2)}, u32[]{:S(2)}) collective-permute-start(bf16[528,128]{1,0:T(8,128)(2,1)S(1)} %collective-permute-done.9.refs_8_.refs_0_), channel_id=1, source_target_pairs={{0,2},{2,4},{4,6},{6,7},{7,5},{5,3},{3,1},{1,0},{8,10},{10,12},{12... | collective-permute-start | bytes 405512 | tf_op jit(solution)/shard_map/ppermute | solution.py:173
  13.2 0.0 collective-permute-done.10.refs_9_.refs_1_
  13.2 0.0 collective-permute-start.12
  13.2 0.9 %collective-permute-done.1.refs_2_ = bf16[128,512]{1,0:T(8,128)(2,1)S(1)} collective-permute-done((bf16[128,512]{1,0:T(8,128)(2,1)S(1)}, bf16[128,512]{1,0:T(8,128)(2,1)S(1)}, u32[]{:S(2)}, u32[]{:S(2)}) %collective-permute-start.1) | collective-permute-done | bytes 131104 | tf_op jit(solution)/shard_map/ppermute | solution.py:173
  14.1 1.7 %collective-permute-start.2 = (bf16[128,512]{1,0:T(8,128)(2,1)S(1)}, bf16[128,512]{1,0:T(8,128)(2,1)S(1)}, u32[]{:S(2)}, u32[]{:S(2)}) collective-permute-start(bf16[128,512]{1,0:T(8,128)(2,1)S(1)} %collective-permute-done.1.refs_2_), channel_id=1, source_target_pairs={{0,2},{2,4},{4,6},{6,7},{7,5},{5,3},{3,1},{1,0},{8,10},{10,12},{12... | collective-permute-start | bytes 393224 | tf_op jit(solution)/shard_map/ppermute | solution.py:173
  15.8 0.5 %collective-permute-done.5.refs_3_ = bf16[128,512]{1,0:T(8,128)(2,1)S(1)} collective-permute-done((bf16[128,512]{1,0:T(8,128)(2,1)S(1)}, bf16[128,512]{1,0:T(8,128)(2,1)S(1)}, u32[]{:S(2)}, u32[]{:S(2)}) %collective-permute-start.5) | collective-permute-done | bytes 131104 | tf_op jit(solution)/shard_map/ppermute | solution.py:173
  16.3 0.1 collective-permute-start.6
  16.5 0.7 %collective-permute-done.11.refs_10_.refs_2_ = bf16[528,128]{1,0:T(8,128)(2,1)S(1)} collective-permute-done((bf16[528,128]{1,0:T(8,128)(2,1)S(1)}, bf16[528,128]{1,0:T(8,128)(2,1)S(1)}, u32[]{:S(2)}, u32[]{:S(2)}) %collective-permute-start.11) | collective-permute-done | bytes 135200 | tf_op jit(solution)/shard_map/ppermute | solution.py:173
  17.2 2.2 %collective-permute-start.13 = (bf16[528,128]{1,0:T(8,128)(2,1)S(1)}, bf16[528,128]{1,0:T(8,128)(2,1)S(1)}, u32[]{:S(2)}, u32[]{:S(2)}) collective-permute-start(bf16[528,128]{1,0:T(8,128)(2,1)S(1)} %collective-permute-done.11.refs_10_.refs_2_), channel_id=1, source_target_pairs={{0,2},{2,4},{4,6},{6,7},{7,5},{5,3},{3,1},{1,0},{8,10},{10,12},{12... | collective-permute-start | bytes 405512 | tf_op jit(solution)/shard_map/ppermute | solution.py:173
  19.4 0.3 collective-permute-done.12.refs_11_.refs_3_
  19.7 0.0 collective-permute-start.14
  19.7 0.8 %collective-permute-done.2.refs_4_ = bf16[128,512]{1,0:T(8,128)(2,1)S(1)} collective-permute-done((bf16[128,512]{1,0:T(8,128)(2,1)S(1)}, bf16[128,512]{1,0:T(8,128)(2,1)S(1)}, u32[]{:S(2)}, u32[]{:S(2)}) %collective-permute-start.2) | collective-permute-done | bytes 131104 | tf_op jit(solution)/shard_map/ppermute | solution.py:173
  20.5 1.7 %collective-permute-start.3 = (bf16[64,512]{1,0:T(8,128)(2,1)S(1)}, bf16[64,512]{1,0:T(8,128)(2,1)S(1)}, u32[]{:S(2)}, u32[]{:S(2)}) collective-permute-start(bf16[64,512]{1,0:T(8,128)(2,1)S(1)} %slice.32), channel_id=1, source_target_pairs={{0,2},{2,4},{4,6},{6,7},{7,5},{5,3},{3,1},{1,0},{8,10},{10,12},{12... | collective-permute-start | bytes 196616 | tf_op jit(solution)/shard_map/ppermute | solution.py:173
  22.3 0.4 %collective-permute-done.6.refs_5_ = bf16[128,512]{1,0:T(8,128)(2,1)S(1)} collective-permute-done((bf16[128,512]{1,0:T(8,128)(2,1)S(1)}, bf16[128,512]{1,0:T(8,128)(2,1)S(1)}, u32[]{:S(2)}, u32[]{:S(2)}) %collective-permute-start.6) | collective-permute-done | bytes 131104 | tf_op jit(solution)/shard_map/ppermute | solution.py:173
  22.7 0.0 collective-permute-start.7
  22.7 0.0 copy-done.3
  22.7 0.3 %shard_map.55.bias_ref = f32[2,64,320]{2,1,0:T(8,128)S(1)} custom-call(f32[1,1152]{1,0:T(1,128)S(1)} %add_convert_fusion.pos_ref), custom_call_target="tpu_custom_call" | custom-call | flops 1048576 | bytes 1024 | tf_op jit(solution)/shard_map/pallas_call | solution.py:198
  23.0 0.0 collective-permute-done.13.refs_12_.refs_4_
  23.1 2.1 %collective-permute-start.15 = (bf16[256,128]{1,0:T(8,128)(2,1)S(1)}, bf16[256,128]{1,0:T(8,128)(2,1)S(1)}, u32[]{:S(2)}, u32[]{:S(2)}) collective-permute-start(bf16[256,128]{1,0:T(8,128)(2,1)S(1)} %slice.30), channel_id=1, source_target_pairs={{0,2},{2,4},{4,6},{6,7},{7,5},{5,3},{3,1},{1,0},{8,10},{10,12},{12... | collective-permute-start | bytes 196616 | tf_op jit(solution)/shard_map/ppermute | solution.py:173
  25.1 0.0 collective-permute-done.14.refs_13_.refs_5_
  25.1 0.3 %collective-permute-start.16 = (bf16[256,128]{1,0:T(8,128)(2,1)S(1)}, bf16[256,128]{1,0:T(8,128)(2,1)S(1)}, u32[]{:S(2)}, u32[]{:S(2)}) collective-permute-start(bf16[256,128]{1,0:T(8,128)(2,1)S(1)} %slice.34), channel_id=1, source_target_pairs={{0,1},{2,0},{4,2},{6,4},{7,6},{5,7},{3,5},{1,3},{8,9},{10,8},{12,1... | collective-permute-start | bytes 196616 | tf_op jit(solution)/shard_map/ppermute | solution.py:173
  25.5 0.0 collective-permute-done.3.refs_0_.refs_6_
  25.5 1.6 %collective-permute-done.7.refs_1_.refs_7_ = bf16[64,512]{1,0:T(8,128)(2,1)S(1)} collective-permute-done((bf16[64,512]{1,0:T(8,128)(2,1)S(1)}, bf16[64,512]{1,0:T(8,128)(2,1)S(1)}, u32[]{:S(2)}, u32[]{:S(2)}) %collective-permute-start.7) | collective-permute-done | bytes 65568 | tf_op jit(solution)/shard_map/ppermute | solution.py:173
  27.1 0.0 collective-permute-done.8.own_ref
  27.1 1.7 %shard_map.58 = (bf16[8,512,320]{2,1,0:T(8,128)(2,1)S(1)}, bf16[4,16,64,128]{3,2,1,0:T(8,128)(2,1)S(1)}) custom-call(f32[1,1152]{1,0:T(1,128)S(1)} %add_convert_fusion.pos_ref, f32[2,64,320]{2,1,0:T(8,128)S(1)} %shard_map.55.bias_ref, f32[8,128]{1,0:T(8,128)S(1)} %shard_map.56.mark_ref, bf16[128,5120]{1,0:T(8,128)(2,1)S(1)} %collective-permute-done.8.own_ref, ...), custom_call_target="tpu_custom_call" | custom-call | flops 67108864 | bytes 1048576 | tf_op jit(solution)/shard_map/pallas_call | solution.py:217
  28.8 0.0 collective-permute-done.15.refs_6_
  28.9 0.6 %collective-permute-done.16.refs_7_ = bf16[256,128]{1,0:T(8,128)(2,1)S(1)} collective-permute-done((bf16[256,128]{1,0:T(8,128)(2,1)S(1)}, bf16[256,128]{1,0:T(8,128)(2,1)S(1)}, u32[]{:S(2)}, u32[]{:S(2)}) %collective-permute-start.16) | collective-permute-done | bytes 65568 | tf_op jit(solution)/shard_map/ppermute | solution.py:173
  29.4 2.1 %shard_map.59 = bf16[128,4096]{1,0:T(8,128)(2,1)} custom-call(f32[1,1152]{1,0:T(1,128)S(1)} %add_convert_fusion.pos_ref, bf16[8,512,320]{2,1,0:T(8,128)(2,1)S(1)} %get-tuple-element.8.weights_ref, bf16[4,16,64,128]{3,2,1,0:T(8,128)(2,1)S(1)} %get-tuple-element.9.sorted_ref, bf16[528,128]{1,0:T(8,128)(2,1)S(1)} %collective-permute-done.9.refs_8_.refs_0_, ...), custom_call_target="tpu_custom_call" | custom-call | flops 67108864 | bytes 1048576 | tf_op jit(solution)/shard_map/pallas_call | solution.py:229
  (13 shorter events, 0.1 us)
Async XLA Ops:
  0.0 5.6 %copy-start.2 = (bf16[1,128,512]{2,1,0:T(8,128)(2,1)S(1)}, bf16[1,128,512]{2,1,0:T(8,128)(2,1)}, u32[]{:S(2)}) copy-start(bf16[1,128,512]{2,1,0:T(8,128)(2,1)} %param.6) | copy-start | bytes 393220
  0.0 4.2 %copy-start.1 = (bf16[1,128,512]{2,1,0:T(8,128)(2,1)S(1)}, bf16[1,128,512]{2,1,0:T(8,128)(2,1)}, u32[]{:S(2)}) copy-start(bf16[1,128,512]{2,1,0:T(8,128)(2,1)} %param.7) | copy-start | bytes 393220
  0.0 4.3 %copy-start.4 = (s32[128]{0:T(128)S(1)}, s32[128]{0:T(128)}, u32[]{:S(2)}) copy-start(s32[128]{0:T(128)} %param.8) | copy-start | bytes 1540
  0.0 5.6 %copy-start = (bf16[1,128,4096]{2,1,0:T(8,128)(2,1)S(1)}, bf16[1,128,4096]{2,1,0:T(8,128)(2,1)}, u32[]{:S(2)}) copy-start(bf16[1,128,4096]{2,1,0:T(8,128)(2,1)} %param.5) | copy-start | bytes 3145732
  0.0 22.7 %copy-start.3 = (s32[1024]{0:T(1024)S(1)}, s32[1024]{0:T(1024)}, u32[]{:S(2)}) copy-start(s32[1024]{0:T(1024)} %param.9) | copy-start | bytes 12292
  0.0 6.4 %collective-permute-start = (bf16[128,512]{1,0:T(8,128)(2,1)}, bf16[128,512]{1,0:T(8,128)(2,1)S(1)}, u32[]{:S(2)}, u32[]{:S(2)}) collective-permute-start(bf16[128,512]{1,0:T(8,128)(2,1)} %bitcast.16), channel_id=1, source_target_pairs={{0,10},{2,12},{4,14},{6,15},{7,13},{5,11},{3,9},{1,8},{8,18},{10,2... | collective-permute-start | bytes 393224 | tf_op jit(solution)/shard_map/ppermute | solution.py:173
  2.5 7.8 %collective-permute-start.4 = (bf16[128,512]{1,0:T(8,128)(2,1)}, bf16[128,512]{1,0:T(8,128)(2,1)S(1)}, u32[]{:S(2)}, u32[]{:S(2)}) collective-permute-start(bf16[128,512]{1,0:T(8,128)(2,1)} %bitcast.17), channel_id=1, source_target_pairs={{0,9},{2,8},{4,10},{6,12},{7,14},{5,15},{3,13},{1,11},{8,17},{10,1... | collective-permute-start | bytes 393224 | tf_op jit(solution)/shard_map/ppermute | solution.py:173
  4.3 6.8 %collective-permute-start.9 = (bf16[528,128]{1,0:T(8,128)(2,1)S(1)}, bf16[528,128]{1,0:T(8,128)(2,1)S(1)}, u32[]{:S(2)}, u32[]{:S(2)}) collective-permute-start(bf16[528,128]{1,0:T(8,128)(2,1)S(1)} %constant_dynamic-update-slice_fusion), channel_id=1, source_target_pairs={{0,10},{2,12},{4,14},{6,15},{7,13},{5,11},{3,9},{1,8},{8,18},{10,2... | collective-permute-start | bytes 405512 | tf_op jit(solution)/shard_map/ppermute | solution.py:173
  5.5 7.7 %collective-permute-start.10 = (bf16[528,128]{1,0:T(8,128)(2,1)S(1)}, bf16[528,128]{1,0:T(8,128)(2,1)S(1)}, u32[]{:S(2)}, u32[]{:S(2)}) collective-permute-start(bf16[528,128]{1,0:T(8,128)(2,1)S(1)} %constant_dynamic-update-slice_fusion), channel_id=1, source_target_pairs={{0,9},{2,8},{4,10},{6,12},{7,14},{5,15},{3,13},{1,11},{8,17},{10,1... | collective-permute-start | bytes 405512 | tf_op jit(solution)/shard_map/ppermute | solution.py:173
  5.7 21.4 %collective-permute-start.8 = (bf16[128,5120]{1,0:T(8,128)(2,1)S(1)}, bf16[128,5120]{1,0:T(8,128)(2,1)S(1)}, u32[]{:S(2)}, u32[]{:S(2)}) collective-permute-start(bf16[128,5120]{1,0:T(8,128)(2,1)S(1)} %pad_maximum_fusion), channel_id=1, source_target_pairs={{0,8},{2,10},{4,12},{6,14},{7,15},{5,13},{3,11},{1,9},{8,16},{10,1... | collective-permute-start | bytes 3932168 | tf_op jit(solution)/shard_map/ppermute | solution.py:173
  6.4 7.7 %collective-permute-start.1 = (bf16[128,512]{1,0:T(8,128)(2,1)S(1)}, bf16[128,512]{1,0:T(8,128)(2,1)S(1)}, u32[]{:S(2)}, u32[]{:S(2)}) collective-permute-start(bf16[128,512]{1,0:T(8,128)(2,1)S(1)} %collective-permute-done.refs_0_), channel_id=1, source_target_pairs={{0,2},{2,4},{4,6},{6,7},{7,5},{5,3},{3,1},{1,0},{8,10},{10,12},{12... | collective-permute-start | bytes 393224 | tf_op jit(solution)/shard_map/ppermute | solution.py:173
  10.3 6.0 %collective-permute-start.5 = (bf16[128,512]{1,0:T(8,128)(2,1)S(1)}, bf16[128,512]{1,0:T(8,128)(2,1)S(1)}, u32[]{:S(2)}, u32[]{:S(2)}) collective-permute-start(bf16[128,512]{1,0:T(8,128)(2,1)S(1)} %collective-permute-done.4.refs_1_), channel_id=1, source_target_pairs={{0,1},{2,0},{4,2},{6,4},{7,6},{5,7},{3,5},{1,3},{8,9},{10,8},{12,1... | collective-permute-start | bytes 393224 | tf_op jit(solution)/shard_map/ppermute | solution.py:173
  11.1 6.1 %collective-permute-start.11 = (bf16[528,128]{1,0:T(8,128)(2,1)S(1)}, bf16[528,128]{1,0:T(8,128)(2,1)S(1)}, u32[]{:S(2)}, u32[]{:S(2)}) collective-permute-start(bf16[528,128]{1,0:T(8,128)(2,1)S(1)} %collective-permute-done.9.refs_8_.refs_0_), channel_id=1, source_target_pairs={{0,2},{2,4},{4,6},{6,7},{7,5},{5,3},{3,1},{1,0},{8,10},{10,12},{12... | collective-permute-start | bytes 405512 | tf_op jit(solution)/shard_map/ppermute | solution.py:173
  13.2 6.5 %collective-permute-start.12 = (bf16[528,128]{1,0:T(8,128)(2,1)S(1)}, bf16[528,128]{1,0:T(8,128)(2,1)S(1)}, u32[]{:S(2)}, u32[]{:S(2)}) collective-permute-start(bf16[528,128]{1,0:T(8,128)(2,1)S(1)} %collective-permute-done.10.refs_9_.refs_1_), channel_id=1, source_target_pairs={{0,1},{2,0},{4,2},{6,4},{7,6},{5,7},{3,5},{1,3},{8,9},{10,8},{12,1... | collective-permute-start | bytes 405512 | tf_op jit(solution)/shard_map/ppermute | solution.py:173
  14.1 6.4 %collective-permute-start.2 = (bf16[128,512]{1,0:T(8,128)(2,1)S(1)}, bf16[128,512]{1,0:T(8,128)(2,1)S(1)}, u32[]{:S(2)}, u32[]{:S(2)}) collective-permute-start(bf16[128,512]{1,0:T(8,128)(2,1)S(1)} %collective-permute-done.1.refs_2_), channel_id=1, source_target_pairs={{0,2},{2,4},{4,6},{6,7},{7,5},{5,3},{3,1},{1,0},{8,10},{10,12},{12... | collective-permute-start | bytes 393224 | tf_op jit(solution)/shard_map/ppermute | solution.py:173
  16.3 6.3 %collective-permute-start.6 = (bf16[128,512]{1,0:T(8,128)(2,1)S(1)}, bf16[128,512]{1,0:T(8,128)(2,1)S(1)}, u32[]{:S(2)}, u32[]{:S(2)}) collective-permute-start(bf16[128,512]{1,0:T(8,128)(2,1)S(1)} %collective-permute-done.5.refs_3_), channel_id=1, source_target_pairs={{0,1},{2,0},{4,2},{6,4},{7,6},{5,7},{3,5},{1,3},{8,9},{10,8},{12,1... | collective-permute-start | bytes 393224 | tf_op jit(solution)/shard_map/ppermute | solution.py:173
  17.2 5.8 %collective-permute-start.13 = (bf16[528,128]{1,0:T(8,128)(2,1)S(1)}, bf16[528,128]{1,0:T(8,128)(2,1)S(1)}, u32[]{:S(2)}, u32[]{:S(2)}) collective-permute-start(bf16[528,128]{1,0:T(8,128)(2,1)S(1)} %collective-permute-done.11.refs_10_.refs_2_), channel_id=1, source_target_pairs={{0,2},{2,4},{4,6},{6,7},{7,5},{5,3},{3,1},{1,0},{8,10},{10,12},{12... | collective-permute-start | bytes 405512 | tf_op jit(solution)/shard_map/ppermute | solution.py:173
  19.7 5.4 %collective-permute-start.14 = (bf16[528,128]{1,0:T(8,128)(2,1)S(1)}, bf16[528,128]{1,0:T(8,128)(2,1)S(1)}, u32[]{:S(2)}, u32[]{:S(2)}) collective-permute-start(bf16[528,128]{1,0:T(8,128)(2,1)S(1)} %collective-permute-done.12.refs_11_.refs_3_), channel_id=1, source_target_pairs={{0,1},{2,0},{4,2},{6,4},{7,6},{5,7},{3,5},{1,3},{8,9},{10,8},{12,1... | collective-permute-start | bytes 405512 | tf_op jit(solution)/shard_map/ppermute | solution.py:173
  20.5 4.9 %collective-permute-start.3 = (bf16[64,512]{1,0:T(8,128)(2,1)S(1)}, bf16[64,512]{1,0:T(8,128)(2,1)S(1)}, u32[]{:S(2)}, u32[]{:S(2)}) collective-permute-start(bf16[64,512]{1,0:T(8,128)(2,1)S(1)} %slice.32), channel_id=1, source_target_pairs={{0,2},{2,4},{4,6},{6,7},{7,5},{5,3},{3,1},{1,0},{8,10},{10,12},{12... | collective-permute-start | bytes 196616 | tf_op jit(solution)/shard_map/ppermute | solution.py:173
  22.7 4.4 %collective-permute-start.7 = (bf16[64,512]{1,0:T(8,128)(2,1)S(1)}, bf16[64,512]{1,0:T(8,128)(2,1)S(1)}, u32[]{:S(2)}, u32[]{:S(2)}) collective-permute-start(bf16[64,512]{1,0:T(8,128)(2,1)S(1)} %slice.33), channel_id=1, source_target_pairs={{0,1},{2,0},{4,2},{6,4},{7,6},{5,7},{3,5},{1,3},{8,9},{10,8},{12,1... | collective-permute-start | bytes 196616 | tf_op jit(solution)/shard_map/ppermute | solution.py:173
  23.1 5.8 %collective-permute-start.15 = (bf16[256,128]{1,0:T(8,128)(2,1)S(1)}, bf16[256,128]{1,0:T(8,128)(2,1)S(1)}, u32[]{:S(2)}, u32[]{:S(2)}) collective-permute-start(bf16[256,128]{1,0:T(8,128)(2,1)S(1)} %slice.30), channel_id=1, source_target_pairs={{0,2},{2,4},{4,6},{6,7},{7,5},{5,3},{3,1},{1,0},{8,10},{10,12},{12... | collective-permute-start | bytes 196616 | tf_op jit(solution)/shard_map/ppermute | solution.py:173
  25.1 4.3 %collective-permute-start.16 = (bf16[256,128]{1,0:T(8,128)(2,1)S(1)}, bf16[256,128]{1,0:T(8,128)(2,1)S(1)}, u32[]{:S(2)}, u32[]{:S(2)}) collective-permute-start(bf16[256,128]{1,0:T(8,128)(2,1)S(1)} %slice.34), channel_id=1, source_target_pairs={{0,1},{2,0},{4,2},{6,4},{7,6},{5,7},{3,5},{1,3},{8,9},{10,8},{12,1... | collective-permute-start | bytes 196616 | tf_op jit(solution)/shard_map/ppermute | solution.py:173

commit v12 on v11

--- a/solution.py
+++ b/solution.py
@@ -23,7 +23,7 @@
 
 
 def first_run(pos_ref):
-    return lax.div(jnp.min(pos_ref[:, :TOK_DEV]).astype(jnp.int32), RUN)
+    return lax.div(pos_ref[:, :TOK_DEV][0, 0].astype(jnp.int32), RUN)
 
 
 def first_in_reach(runs, pos_ref, run):
@@ -39,7 +39,7 @@
 def run_numbers(runs, pos_ref, tagged_refs):
     firsts = [first_run(pos_ref)]
     for ref in tagged_refs:
-        firsts.append(jnp.min(ref[VALUE_ROWS:, :].astype(jnp.float32)).astype(jnp.int32))
+        firsts.append(ref[VALUE_ROWS:, :].astype(jnp.float32)[0, 0].astype(jnp.int32))
     places = runs // 2
     firsts.append(places * (places - 1) // 2 - sum(firsts))
     return [(first, runs - 1 - first) for first in firsts]
@@ -121,18 +121,17 @@
 
 
 def values_kernel(runs, pos_ref, weights_ref, sorted_ref, *refs):
-    tagged_refs, last_refs, (out_ref, result_buf, out_sems) = refs[:-5], refs[-5:-3], refs[-3:]
+    tagged_refs, (last_ref, out_ref, result_buf, out_sems) = refs[:-4], refs[-4:]
     numbers = run_numbers(runs, pos_ref, tagged_refs)
 
     def half_values(half, start, count):
         ones = jnp.ones((count * RUN, HEAD_SIZE), jnp.bfloat16)
         for kv in range(KEY_VALUE_HEADS):
-            last_ref = last_refs[kv * 2 // KEY_VALUE_HEADS]
             parts = []
             for i in range(count):
                 part = sorted_ref[kv, start + i]
                 for last_half, number in enumerate(numbers[-1]):
-                    row = kv % (KEY_VALUE_HEADS // 2) * TOK_DEV + last_half * RUN
+                    row = kv * TOK_DEV + last_half * RUN
                     part = jnp.where(start + i == number, last_ref[row : row + RUN, :], part)
                 parts.append(part)
             summed = jnp.dot(
@@ -140,7 +139,10 @@
                 jnp.concatenate([jnp.concatenate(parts, axis=0), ones], axis=1),
                 preferred_element_type=jnp.float32,
             )
-            result = (summed[:, :HEAD_SIZE] / summed[:, HEAD_SIZE:]).astype(jnp.bfloat16)
+            total = summed[:, HEAD_SIZE:]
+            inverse = pl.reciprocal(total, approx=True)
+            inverse = inverse * (2.0 - total * inverse)
+            result = (summed[:, :HEAD_SIZE] * inverse).astype(jnp.bfloat16)
             for i in range(GROUP):
                 h = kv * GROUP + i
                 result_buf[half, :, h * HEAD_SIZE : (h + 1) * HEAD_SIZE] = result[i * RUN : (i + 1) * RUN]
@@ -172,15 +174,13 @@
                 pairs.append((s * places + ring[i], target))
         return lax.ppermute(block, ("section", "ctx"), pairs)
 
-    def around(block, rows, before_last=None):
+    def around(block):
         ahead, back = shift(block, 1, 1), shift(block, 1, -1)
         held = [ahead, back]
         for _ in range(2, places // 2):
             ahead, back = shift(ahead, 0, 1), shift(back, 0, -1)
             held.extend([ahead, back])
-        if before_last is not None:
-            ahead, _ = lax.optimization_barrier((ahead, before_last))
-        return held + [shift(ahead[: rows // 2], 0, 1), shift(back[rows // 2 : rows], 0, -1)]
+        return held
 
     own = shift(jnp.concatenate([queries[0], keys[0], values[0]], axis=1), 1, 0)
     vmem = pl.BlockSpec(memory_space=pltpu.VMEM)
@@ -203,8 +203,11 @@
         compiler_params=pltpu.CompilerParams(vmem_limit_bytes=8 * 1024 * 1024),
         cost_estimate=pl.CostEstimate(flops=1 << 20, bytes_accessed=1 << 10, transcendentals=0),
     )(pos)
-    all_keys = around(keys[0], TOK_DEV)
-    all_values = around(tagged, VALUE_ROWS, bias)
+    all_keys, all_values = around(keys[0]), around(tagged)
+    ahead, back = all_keys[-2:]
+    all_keys.extend([shift(ahead[:RUN], 0, 1), shift(back[RUN:], 0, -1)])
+    ahead, back, _ = lax.optimization_barrier((*all_values[-2:], bias))
+    all_values.append(shift(back[:VALUE_ROWS], 0, -1))
     params = pltpu.CompilerParams(vmem_limit_bytes=(12 + runs // 4) * 1024 * 1024)
     mark = pl.pallas_call(
         blank_kernel,
@@ -220,12 +223,12 @@
             jax.ShapeDtypeStruct((2 * KEY_VALUE_HEADS, GROUP * RUN, (runs // 4 + 1) * RUN), jnp.bfloat16),
             jax.ShapeDtypeStruct((KEY_VALUE_HEADS, runs, RUN, HEAD_SIZE), jnp.bfloat16),
         ),
-        in_specs=[vmem] * (4 + len(all_keys) + len(all_values[:-2])),
+        in_specs=[vmem] * (4 + len(all_keys) + len(all_values[:-1])),
         out_specs=(vmem,) * 2,
         scratch_shapes=[pltpu.VMEM((runs, RUN, KV_COLUMNS), jnp.bfloat16)],
         compiler_params=params,
         cost_estimate=pl.CostEstimate(flops=1 << 26, bytes_accessed=1 << 20, transcendentals=0),
-    )(pos, bias, mark, own, *all_keys, *all_values[:-2])
+    )(pos, bias, mark, own, *all_keys, *all_values[:-1])
     out = pl.pallas_call(
         functools.partial(values_kernel, runs),
         out_shape=jax.ShapeDtypeStruct((TOK_DEV, QUERY_COLUMNS), jnp.bfloat16),

time: 31.7 us -> 32.3 us (1.019)
  waiting for transfers between devices: 6.9 us -> 9.8 us
  starting transfers between devices: 20.1 us -> 18.1 us
    ppermute x17 -> x16, waiting for transfers between devices: 6.9 us -> 9.8 us  [shift(): return lax.ppermute(block, ('section', 'ctx'), pairs)]
    ppermute x17 -> x16, starting transfers between devices: 20.1 us -> 18.1 us  [shift(): return lax.ppermute(block, ('section', 'ctx'), pairs)]
  transfers between devices with their start and end apart: 17 -> 16, of which waited for: 10 -> 11; matrix products, arithmetic and copies ran while one was open for 1% -> 1% of each run, Pallas kernels for 7% -> 6%
where the time goes in v12:
time: 32.3 us; the launch traced here: 32.2 us
  starting transfers between devices  18.1 us (56%)
  waiting for transfers between devices  9.8 us (30%)
  Pallas kernels  3.95 us (12%)
    ppermute x16, starting transfers between devices, shift(): return lax.ppermute(block, ('section', 'ctx'), pairs)  18.1 us
    ppermute x16, waiting for transfers between devices, shift(): return lax.ppermute(block, ('section', 'ctx'), pairs)  9.8 us
    pallas_call x1, Pallas kernels, per_device(): pl.pallas_call(functools.partial(values_kernel, runs), out_shape=jax.Shap...  2.04 us
    pallas_call x1, Pallas kernels, per_device(): pl.pallas_call(functools.partial(weights_kernel, runs), out_shape=(jax.Sh...  1.64 us
  transfers between devices with their start and end apart: 16, of which 11 were waited for; matrix products, arithmetic and copies ran while one was open for 1% of the time, Pallas kernels for 6%

profile of v12, /device:TPU:0, one launch (start us, length us, event | category | flops | bytes accessed | tf_op | source)
XLA Modules:
  0.0 32.2 jit_solution(3604613482842244612)
XLA Ops:
  0.0 0.0 copy-start.2
  0.0 0.0 copy-start.1
  0.0 0.0 copy-start.4
  0.0 0.0 copy-start
  0.0 0.0 copy-start.3
  0.0 2.5 %collective-permute-start = (bf16[128,512]{1,0:T(8,128)(2,1)}, bf16[128,512]{1,0:T(8,128)(2,1)S(1)}, u32[]{:S(2)}, u32[]{:S(2)}) collective-permute-start(bf16[128,512]{1,0:T(8,128)(2,1)} %bitcast.16), channel_id=1, source_target_pairs={{0,10},{2,12},{4,14},{6,15},{7,13},{5,11},{3,9},{1,8},{8,18},{10,2... | collective-permute-start | bytes 393224 | tf_op jit(solution)/shard_map/ppermute | solution.py:175
  2.5 1.7 %collective-permute-start.4 = (bf16[128,512]{1,0:T(8,128)(2,1)}, bf16[128,512]{1,0:T(8,128)(2,1)S(1)}, u32[]{:S(2)}, u32[]{:S(2)}) collective-permute-start(bf16[128,512]{1,0:T(8,128)(2,1)} %bitcast.17), channel_id=1, source_target_pairs={{0,9},{2,8},{4,10},{6,12},{7,14},{5,15},{3,13},{1,11},{8,17},{10,1... | collective-permute-start | bytes 393224 | tf_op jit(solution)/shard_map/ppermute | solution.py:175
  4.2 0.0 copy-done.1
  4.3 0.0 copy-done.4
  4.3 1.2 %collective-permute-start.9 = (bf16[528,128]{1,0:T(8,128)(2,1)S(1)}, bf16[528,128]{1,0:T(8,128)(2,1)S(1)}, u32[]{:S(2)}, u32[]{:S(2)}) collective-permute-start(bf16[528,128]{1,0:T(8,128)(2,1)S(1)} %constant_dynamic-update-slice_fusion), channel_id=1, source_target_pairs={{0,10},{2,12},{4,14},{6,15},{7,13},{5,11},{3,9},{1,8},{8,18},{10,2... | collective-permute-start | bytes 405512 | tf_op jit(solution)/shard_map/ppermute | solution.py:175
  5.5 0.1 collective-permute-start.10
  5.6 0.0 copy-done.2
  5.6 0.0 copy-done
  5.6 0.1 pad_maximum_fusion
  5.7 0.5 %collective-permute-start.8 = (bf16[128,5120]{1,0:T(8,128)(2,1)S(1)}, bf16[128,5120]{1,0:T(8,128)(2,1)S(1)}, u32[]{:S(2)}, u32[]{:S(2)}) collective-permute-start(bf16[128,5120]{1,0:T(8,128)(2,1)S(1)} %pad_maximum_fusion), channel_id=1, source_target_pairs={{0,8},{2,10},{4,12},{6,14},{7,15},{5,13},{3,11},{1,9},{8,16},{10,1... | collective-permute-start | bytes 3932168 | tf_op jit(solution)/shard_map/ppermute | solution.py:175
  6.2 0.2 collective-permute-done.refs_0_
  6.4 3.9 %collective-permute-start.1 = (bf16[128,512]{1,0:T(8,128)(2,1)S(1)}, bf16[128,512]{1,0:T(8,128)(2,1)S(1)}, u32[]{:S(2)}, u32[]{:S(2)}) collective-permute-start(bf16[128,512]{1,0:T(8,128)(2,1)S(1)} %collective-permute-done.refs_0_), channel_id=1, source_target_pairs={{0,2},{2,4},{4,6},{6,7},{7,5},{5,3},{3,1},{1,0},{8,10},{10,12},{12... | collective-permute-start | bytes 393224 | tf_op jit(solution)/shard_map/ppermute | solution.py:175
  10.3 0.0 collective-permute-done.4.refs_1_
  10.3 0.0 collective-permute-start.5
  10.3 0.8 %collective-permute-done.9.refs_8_.refs_0_ = bf16[528,128]{1,0:T(8,128)(2,1)S(1)} collective-permute-done((bf16[528,128]{1,0:T(8,128)(2,1)S(1)}, bf16[528,128]{1,0:T(8,128)(2,1)S(1)}, u32[]{:S(2)}, u32[]{:S(2)}) %collective-permute-start.9) | collective-permute-done | bytes 135200 | tf_op jit(solution)/shard_map/ppermute | solution.py:175
  11.1 2.1 %collective-permute-start.11 = (bf16[528,128]{1,0:T(8,128)(2,1)S(1)}, bf16[528,128]{1,0:T(8,128)(2,1)S(1)}, u32[]{:S(2)}, u32[]{:S(2)}) collective-permute-start(bf16[528,128]{1,0:T(8,128)(2,1)S(1)} %collective-permute-done.9.refs_8_.refs_0_), channel_id=1, source_target_pairs={{0,2},{2,4},{4,6},{6,7},{7,5},{5,3},{3,1},{1,0},{8,10},{10,12},{12... | collective-permute-start | bytes 405512 | tf_op jit(solution)/shard_map/ppermute | solution.py:175
  13.2 0.0 collective-permute-done.10.refs_9_.refs_1_
  13.2 0.0 collective-permute-start.12
  13.2 0.9 %collective-permute-done.1.refs_2_ = bf16[128,512]{1,0:T(8,128)(2,1)S(1)} collective-permute-done((bf16[128,512]{1,0:T(8,128)(2,1)S(1)}, bf16[128,512]{1,0:T(8,128)(2,1)S(1)}, u32[]{:S(2)}, u32[]{:S(2)}) %collective-permute-start.1) | collective-permute-done | bytes 131104 | tf_op jit(solution)/shard_map/ppermute | solution.py:175
  14.1 1.7 %collective-permute-start.2 = (bf16[128,512]{1,0:T(8,128)(2,1)S(1)}, bf16[128,512]{1,0:T(8,128)(2,1)S(1)}, u32[]{:S(2)}, u32[]{:S(2)}) collective-permute-start(bf16[128,512]{1,0:T(8,128)(2,1)S(1)} %collective-permute-done.1.refs_2_), channel_id=1, source_target_pairs={{0,2},{2,4},{4,6},{6,7},{7,5},{5,3},{3,1},{1,0},{8,10},{10,12},{12... | collective-permute-start | bytes 393224 | tf_op jit(solution)/shard_map/ppermute | solution.py:175
  15.8 0.5 %collective-permute-done.5.refs_3_ = bf16[128,512]{1,0:T(8,128)(2,1)S(1)} collective-permute-done((bf16[128,512]{1,0:T(8,128)(2,1)S(1)}, bf16[128,512]{1,0:T(8,128)(2,1)S(1)}, u32[]{:S(2)}, u32[]{:S(2)}) %collective-permute-start.5) | collective-permute-done | bytes 131104 | tf_op jit(solution)/shard_map/ppermute | solution.py:175
  16.3 0.1 collective-permute-start.6
  16.5 0.7 %collective-permute-done.11.refs_10_.refs_2_ = bf16[528,128]{1,0:T(8,128)(2,1)S(1)} collective-permute-done((bf16[528,128]{1,0:T(8,128)(2,1)S(1)}, bf16[528,128]{1,0:T(8,128)(2,1)S(1)}, u32[]{:S(2)}, u32[]{:S(2)}) %collective-permute-start.11) | collective-permute-done | bytes 135200 | tf_op jit(solution)/shard_map/ppermute | solution.py:175
  17.2 2.2 %collective-permute-start.13 = (bf16[528,128]{1,0:T(8,128)(2,1)S(1)}, bf16[528,128]{1,0:T(8,128)(2,1)S(1)}, u32[]{:S(2)}, u32[]{:S(2)}) collective-permute-start(bf16[528,128]{1,0:T(8,128)(2,1)S(1)} %collective-permute-done.11.refs_10_.refs_2_), channel_id=1, source_target_pairs={{0,2},{2,4},{4,6},{6,7},{7,5},{5,3},{3,1},{1,0},{8,10},{10,12},{12... | collective-permute-start | bytes 405512 | tf_op jit(solution)/shard_map/ppermute | solution.py:175
  19.4 0.3 collective-permute-done.12.refs_11_.refs_3_
  19.7 0.0 collective-permute-start.14
  19.7 0.8 %collective-permute-done.2.refs_4_ = bf16[128,512]{1,0:T(8,128)(2,1)S(1)} collective-permute-done((bf16[128,512]{1,0:T(8,128)(2,1)S(1)}, bf16[128,512]{1,0:T(8,128)(2,1)S(1)}, u32[]{:S(2)}, u32[]{:S(2)}) %collective-permute-start.2) | collective-permute-done | bytes 131104 | tf_op jit(solution)/shard_map/ppermute | solution.py:175
  20.5 1.7 %collective-permute-start.3 = (bf16[64,512]{1,0:T(8,128)(2,1)S(1)}, bf16[64,512]{1,0:T(8,128)(2,1)S(1)}, u32[]{:S(2)}, u32[]{:S(2)}) collective-permute-start(bf16[64,512]{1,0:T(8,128)(2,1)S(1)} %slice.28), channel_id=1, source_target_pairs={{0,2},{2,4},{4,6},{6,7},{7,5},{5,3},{3,1},{1,0},{8,10},{10,12},{12... | collective-permute-start | bytes 196616 | tf_op jit(solution)/shard_map/ppermute | solution.py:175
  22.3 0.4 %collective-permute-done.6.refs_5_ = bf16[128,512]{1,0:T(8,128)(2,1)S(1)} collective-permute-done((bf16[128,512]{1,0:T(8,128)(2,1)S(1)}, bf16[128,512]{1,0:T(8,128)(2,1)S(1)}, u32[]{:S(2)}, u32[]{:S(2)}) %collective-permute-start.6) | collective-permute-done | bytes 131104 | tf_op jit(solution)/shard_map/ppermute | solution.py:175
  22.7 0.0 collective-permute-start.7
  22.7 0.0 copy-done.3
  22.7 0.3 shard_map.55.bias_ref
  23.0 0.0 collective-permute-done.13.refs_12_.refs_4_
  23.0 2.2 %collective-permute-done.14.refs_13_.refs_5_ = bf16[528,128]{1,0:T(8,128)(2,1)S(1)} collective-permute-done((bf16[528,128]{1,0:T(8,128)(2,1)S(1)}, bf16[528,128]{1,0:T(8,128)(2,1)S(1)}, u32[]{:S(2)}, u32[]{:S(2)}) %collective-permute-start.14) | collective-permute-done | bytes 135200 | tf_op jit(solution)/shard_map/ppermute | solution.py:175
  25.1 0.4 %collective-permute-start.15 = (bf16[512,128]{1,0:T(8,128)(2,1)S(1)}, bf16[512,128]{1,0:T(8,128)(2,1)S(1)}, u32[]{:S(2)}, u32[]{:S(2)}) collective-permute-start(bf16[512,128]{1,0:T(8,128)(2,1)S(1)} %slice.27), channel_id=1, source_target_pairs={{0,1},{2,0},{4,2},{6,4},{7,6},{5,7},{3,5},{1,3},{8,9},{10,8},{12,1... | collective-permute-start | bytes 393224 | tf_op jit(solution)/shard_map/ppermute | solution.py:175
  25.5 0.0 collective-permute-done.3.refs_0_.refs_6_
  25.5 2.0 %collective-permute-done.7.refs_1_.refs_7_ = bf16[64,512]{1,0:T(8,128)(2,1)S(1)} collective-permute-done((bf16[64,512]{1,0:T(8,128)(2,1)S(1)}, bf16[64,512]{1,0:T(8,128)(2,1)S(1)}, u32[]{:S(2)}, u32[]{:S(2)}) %collective-permute-start.7) | collective-permute-done | bytes 65568 | tf_op jit(solution)/shard_map/ppermute | solution.py:175
  27.5 0.0 collective-permute-done.8.own_ref
  27.5 1.6 %shard_map.58 = (bf16[8,512,320]{2,1,0:T(8,128)(2,1)S(1)}, bf16[4,16,64,128]{3,2,1,0:T(8,128)(2,1)S(1)}) custom-call(f32[1,1152]{1,0:T(1,128)S(1)} %add_convert_fusion.pos_ref, f32[2,64,320]{2,1,0:T(8,128)S(1)} %shard_map.55.bias_ref, f32[8,128]{1,0:T(8,128)S(1)} %shard_map.56.mark_ref, bf16[128,5120]{1,0:T(8,128)(2,1)S(1)} %collective-permute-done.8.own_ref, ...), custom_call_target="tpu_custom_call" | custom-call | flops 67108864 | bytes 1048576 | tf_op jit(solution)/shard_map/pallas_call | solution.py:220
  29.2 1.0 %collective-permute-done.15.refs_6_ = bf16[512,128]{1,0:T(8,128)(2,1)S(1)} collective-permute-done((bf16[512,128]{1,0:T(8,128)(2,1)S(1)}, bf16[512,128]{1,0:T(8,128)(2,1)S(1)}, u32[]{:S(2)}, u32[]{:S(2)}) %collective-permute-start.15) | collective-permute-done | bytes 131104 | tf_op jit(solution)/shard_map/ppermute | solution.py:175
  30.2 2.0 %shard_map.59 = bf16[128,4096]{1,0:T(8,128)(2,1)} custom-call(f32[1,1152]{1,0:T(1,128)S(1)} %add_convert_fusion.pos_ref, bf16[8,512,320]{2,1,0:T(8,128)(2,1)S(1)} %get-tuple-element.8.weights_ref, bf16[4,16,64,128]{3,2,1,0:T(8,128)(2,1)S(1)} %get-tuple-element.9.sorted_ref, bf16[528,128]{1,0:T(8,128)(2,1)S(1)} %collective-permute-done.9.refs_8_.refs_0_, ...), custom_call_target="tpu_custom_call" | custom-call | flops 67108864 | bytes 1048576 | tf_op jit(solution)/shard_map/pallas_call | solution.py:232
  (12 shorter events, 0.1 us)
Async XLA Ops:
  0.0 5.6 %copy-start.2 = (bf16[1,128,512]{2,1,0:T(8,128)(2,1)S(1)}, bf16[1,128,512]{2,1,0:T(8,128)(2,1)}, u32[]{:S(2)}) copy-start(bf16[1,128,512]{2,1,0:T(8,128)(2,1)} %param.6) | copy-start | bytes 393220
  0.0 4.2 %copy-start.1 = (bf16[1,128,512]{2,1,0:T(8,128)(2,1)S(1)}, bf16[1,128,512]{2,1,0:T(8,128)(2,1)}, u32[]{:S(2)}) copy-start(bf16[1,128,512]{2,1,0:T(8,128)(2,1)} %param.7) | copy-start | bytes 393220
  0.0 4.3 %copy-start.4 = (s32[128]{0:T(128)S(1)}, s32[128]{0:T(128)}, u32[]{:S(2)}) copy-start(s32[128]{0:T(128)} %param.8) | copy-start | bytes 1540
  0.0 5.6 %copy-start = (bf16[1,128,4096]{2,1,0:T(8,128)(2,1)S(1)}, bf16[1,128,4096]{2,1,0:T(8,128)(2,1)}, u32[]{:S(2)}) copy-start(bf16[1,128,4096]{2,1,0:T(8,128)(2,1)} %param.5) | copy-start | bytes 3145732
  0.0 22.7 %copy-start.3 = (s32[1024]{0:T(1024)S(1)}, s32[1024]{0:T(1024)}, u32[]{:S(2)}) copy-start(s32[1024]{0:T(1024)} %param.9) | copy-start | bytes 12292
  0.0 6.4 %collective-permute-start = (bf16[128,512]{1,0:T(8,128)(2,1)}, bf16[128,512]{1,0:T(8,128)(2,1)S(1)}, u32[]{:S(2)}, u32[]{:S(2)}) collective-permute-start(bf16[128,512]{1,0:T(8,128)(2,1)} %bitcast.16), channel_id=1, source_target_pairs={{0,10},{2,12},{4,14},{6,15},{7,13},{5,11},{3,9},{1,8},{8,18},{10,2... | collective-permute-start | bytes 393224 | tf_op jit(solution)/shard_map/ppermute | solution.py:175
  2.5 7.8 %collective-permute-start.4 = (bf16[128,512]{1,0:T(8,128)(2,1)}, bf16[128,512]{1,0:T(8,128)(2,1)S(1)}, u32[]{:S(2)}, u32[]{:S(2)}) collective-permute-start(bf16[128,512]{1,0:T(8,128)(2,1)} %bitcast.17), channel_id=1, source_target_pairs={{0,9},{2,8},{4,10},{6,12},{7,14},{5,15},{3,13},{1,11},{8,17},{10,1... | collective-permute-start | bytes 393224 | tf_op jit(solution)/shard_map/ppermute | solution.py:175
  4.3 6.8 %collective-permute-start.9 = (bf16[528,128]{1,0:T(8,128)(2,1)S(1)}, bf16[528,128]{1,0:T(8,128)(2,1)S(1)}, u32[]{:S(2)}, u32[]{:S(2)}) collective-permute-start(bf16[528,128]{1,0:T(8,128)(2,1)S(1)} %constant_dynamic-update-slice_fusion), channel_id=1, source_target_pairs={{0,10},{2,12},{4,14},{6,15},{7,13},{5,11},{3,9},{1,8},{8,18},{10,2... | collective-permute-start | bytes 405512 | tf_op jit(solution)/shard_map/ppermute | solution.py:175
  5.5 7.7 %collective-permute-start.10 = (bf16[528,128]{1,0:T(8,128)(2,1)S(1)}, bf16[528,128]{1,0:T(8,128)(2,1)S(1)}, u32[]{:S(2)}, u32[]{:S(2)}) collective-permute-start(bf16[528,128]{1,0:T(8,128)(2,1)S(1)} %constant_dynamic-update-slice_fusion), channel_id=1, source_target_pairs={{0,9},{2,8},{4,10},{6,12},{7,14},{5,15},{3,13},{1,11},{8,17},{10,1... | collective-permute-start | bytes 405512 | tf_op jit(solution)/shard_map/ppermute | solution.py:175
  5.7 21.9 %collective-permute-start.8 = (bf16[128,5120]{1,0:T(8,128)(2,1)S(1)}, bf16[128,5120]{1,0:T(8,128)(2,1)S(1)}, u32[]{:S(2)}, u32[]{:S(2)}) collective-permute-start(bf16[128,5120]{1,0:T(8,128)(2,1)S(1)} %pad_maximum_fusion), channel_id=1, source_target_pairs={{0,8},{2,10},{4,12},{6,14},{7,15},{5,13},{3,11},{1,9},{8,16},{10,1... | collective-permute-start | bytes 3932168 | tf_op jit(solution)/shard_map/ppermute | solution.py:175
  6.4 7.7 %collective-permute-start.1 = (bf16[128,512]{1,0:T(8,128)(2,1)S(1)}, bf16[128,512]{1,0:T(8,128)(2,1)S(1)}, u32[]{:S(2)}, u32[]{:S(2)}) collective-permute-start(bf16[128,512]{1,0:T(8,128)(2,1)S(1)} %collective-permute-done.refs_0_), channel_id=1, source_target_pairs={{0,2},{2,4},{4,6},{6,7},{7,5},{5,3},{3,1},{1,0},{8,10},{10,12},{12... | collective-permute-start | bytes 393224 | tf_op jit(solution)/shard_map/ppermute | solution.py:175
  10.3 6.0 %collective-permute-start.5 = (bf16[128,512]{1,0:T(8,128)(2,1)S(1)}, bf16[128,512]{1,0:T(8,128)(2,1)S(1)}, u32[]{:S(2)}, u32[]{:S(2)}) collective-permute-start(bf16[128,512]{1,0:T(8,128)(2,1)S(1)} %collective-permute-done.4.refs_1_), channel_id=1, source_target_pairs={{0,1},{2,0},{4,2},{6,4},{7,6},{5,7},{3,5},{1,3},{8,9},{10,8},{12,1... | collective-permute-start | bytes 393224 | tf_op jit(solution)/shard_map/ppermute | solution.py:175
  11.1 6.1 %collective-permute-start.11 = (bf16[528,128]{1,0:T(8,128)(2,1)S(1)}, bf16[528,128]{1,0:T(8,128)(2,1)S(1)}, u32[]{:S(2)}, u32[]{:S(2)}) collective-permute-start(bf16[528,128]{1,0:T(8,128)(2,1)S(1)} %collective-permute-done.9.refs_8_.refs_0_), channel_id=1, source_target_pairs={{0,2},{2,4},{4,6},{6,7},{7,5},{5,3},{3,1},{1,0},{8,10},{10,12},{12... | collective-permute-start | bytes 405512 | tf_op jit(solution)/shard_map/ppermute | solution.py:175
  13.2 6.5 %collective-permute-start.12 = (bf16[528,128]{1,0:T(8,128)(2,1)S(1)}, bf16[528,128]{1,0:T(8,128)(2,1)S(1)}, u32[]{:S(2)}, u32[]{:S(2)}) collective-permute-start(bf16[528,128]{1,0:T(8,128)(2,1)S(1)} %collective-permute-done.10.refs_9_.refs_1_), channel_id=1, source_target_pairs={{0,1},{2,0},{4,2},{6,4},{7,6},{5,7},{3,5},{1,3},{8,9},{10,8},{12,1... | collective-permute-start | bytes 405512 | tf_op jit(solution)/shard_map/ppermute | solution.py:175
  14.1 6.4 %collective-permute-start.2 = (bf16[128,512]{1,0:T(8,128)(2,1)S(1)}, bf16[128,512]{1,0:T(8,128)(2,1)S(1)}, u32[]{:S(2)}, u32[]{:S(2)}) collective-permute-start(bf16[128,512]{1,0:T(8,128)(2,1)S(1)} %collective-permute-done.1.refs_2_), channel_id=1, source_target_pairs={{0,2},{2,4},{4,6},{6,7},{7,5},{5,3},{3,1},{1,0},{8,10},{10,12},{12... | collective-permute-start | bytes 393224 | tf_op jit(solution)/shard_map/ppermute | solution.py:175
  16.3 6.3 %collective-permute-start.6 = (bf16[128,512]{1,0:T(8,128)(2,1)S(1)}, bf16[128,512]{1,0:T(8,128)(2,1)S(1)}, u32[]{:S(2)}, u32[]{:S(2)}) collective-permute-start(bf16[128,512]{1,0:T(8,128)(2,1)S(1)} %collective-permute-done.5.refs_3_), channel_id=1, source_target_pairs={{0,1},{2,0},{4,2},{6,4},{7,6},{5,7},{3,5},{1,3},{8,9},{10,8},{12,1... | collective-permute-start | bytes 393224 | tf_op jit(solution)/shard_map/ppermute | solution.py:175
  17.2 5.8 %collective-permute-start.13 = (bf16[528,128]{1,0:T(8,128)(2,1)S(1)}, bf16[528,128]{1,0:T(8,128)(2,1)S(1)}, u32[]{:S(2)}, u32[]{:S(2)}) collective-permute-start(bf16[528,128]{1,0:T(8,128)(2,1)S(1)} %collective-permute-done.11.refs_10_.refs_2_), channel_id=1, source_target_pairs={{0,2},{2,4},{4,6},{6,7},{7,5},{5,3},{3,1},{1,0},{8,10},{10,12},{12... | collective-permute-start | bytes 405512 | tf_op jit(solution)/shard_map/ppermute | solution.py:175
  19.7 5.4 %collective-permute-start.14 = (bf16[528,128]{1,0:T(8,128)(2,1)S(1)}, bf16[528,128]{1,0:T(8,128)(2,1)S(1)}, u32[]{:S(2)}, u32[]{:S(2)}) collective-permute-start(bf16[528,128]{1,0:T(8,128)(2,1)S(1)} %collective-permute-done.12.refs_11_.refs_3_), channel_id=1, source_target_pairs={{0,1},{2,0},{4,2},{6,4},{7,6},{5,7},{3,5},{1,3},{8,9},{10,8},{12,1... | collective-permute-start | bytes 405512 | tf_op jit(solution)/shard_map/ppermute | solution.py:175
  20.5 5.0 %collective-permute-start.3 = (bf16[64,512]{1,0:T(8,128)(2,1)S(1)}, bf16[64,512]{1,0:T(8,128)(2,1)S(1)}, u32[]{:S(2)}, u32[]{:S(2)}) collective-permute-start(bf16[64,512]{1,0:T(8,128)(2,1)S(1)} %slice.28), channel_id=1, source_target_pairs={{0,2},{2,4},{4,6},{6,7},{7,5},{5,3},{3,1},{1,0},{8,10},{10,12},{12... | collective-permute-start | bytes 196616 | tf_op jit(solution)/shard_map/ppermute | solution.py:175
  22.7 4.9 %collective-permute-start.7 = (bf16[64,512]{1,0:T(8,128)(2,1)S(1)}, bf16[64,512]{1,0:T(8,128)(2,1)S(1)}, u32[]{:S(2)}, u32[]{:S(2)}) collective-permute-start(bf16[64,512]{1,0:T(8,128)(2,1)S(1)} %slice.29), channel_id=1, source_target_pairs={{0,1},{2,0},{4,2},{6,4},{7,6},{5,7},{3,5},{1,3},{8,9},{10,8},{12,1... | collective-permute-start | bytes 196616 | tf_op jit(solution)/shard_map/ppermute | solution.py:175
  25.1 5.0 %collective-permute-start.15 = (bf16[512,128]{1,0:T(8,128)(2,1)S(1)}, bf16[512,128]{1,0:T(8,128)(2,1)S(1)}, u32[]{:S(2)}, u32[]{:S(2)}) collective-permute-start(bf16[512,128]{1,0:T(8,128)(2,1)S(1)} %slice.27), channel_id=1, source_target_pairs={{0,1},{2,0},{4,2},{6,4},{7,6},{5,7},{3,5},{1,3},{8,9},{10,8},{12,1... | collective-permute-start | bytes 393224 | tf_op jit(solution)/shard_map/ppermute | solution.py:175

commit v13 on v11

--- a/solution.py
+++ b/solution.py
@@ -23,7 +23,7 @@
 
 
 def first_run(pos_ref):
-    return lax.div(jnp.min(pos_ref[:, :TOK_DEV]).astype(jnp.int32), RUN)
+    return lax.div(pos_ref[:, :TOK_DEV][0, 0].astype(jnp.int32), RUN)
 
 
 def first_in_reach(runs, pos_ref, run):
@@ -39,7 +39,7 @@
 def run_numbers(runs, pos_ref, tagged_refs):
     firsts = [first_run(pos_ref)]
     for ref in tagged_refs:
-        firsts.append(jnp.min(ref[VALUE_ROWS:, :].astype(jnp.float32)).astype(jnp.int32))
+        firsts.append(ref[VALUE_ROWS:, :].astype(jnp.float32)[0, 0].astype(jnp.int32))
     places = runs // 2
     firsts.append(places * (places - 1) // 2 - sum(firsts))
     return [(first, runs - 1 - first) for first in firsts]
@@ -140,20 +140,34 @@
                 jnp.concatenate([jnp.concatenate(parts, axis=0), ones], axis=1),
                 preferred_element_type=jnp.float32,
             )
-            result = (summed[:, :HEAD_SIZE] / summed[:, HEAD_SIZE:]).astype(jnp.bfloat16)
+            total = summed[:, HEAD_SIZE:]
+            inverse = pl.reciprocal(total, approx=True)
+            inverse = inverse * (2.0 - total * inverse)
+            result = (summed[:, :HEAD_SIZE] * inverse).astype(jnp.bfloat16)
             for i in range(GROUP):
                 h = kv * GROUP + i
                 result_buf[half, :, h * HEAD_SIZE : (h + 1) * HEAD_SIZE] = result[i * RUN : (i + 1) * RUN]
+            copies[half * KEY_VALUE_HEADS + kv].start()
 
     copies = []
     for half in range(2):
+        for kv in range(KEY_VALUE_HEADS):
+            columns = pl.ds(kv * GROUP * HEAD_SIZE, GROUP * HEAD_SIZE)
+            copies.append(
+                pltpu.make_async_copy(
+                    result_buf.at[half, :, columns],
+                    out_ref.at[pl.ds(half * RUN, RUN), columns],
+                    out_sems.at[half * KEY_VALUE_HEADS + kv],
+                )
+            )
+    for half in range(2):
         start, far = first_in_reach(runs, pos_ref, numbers[0][half])
-        pl.when(far)(functools.partial(half_values, half, start, runs // 4 + 1))
-        pl.when(jnp.logical_not(far))(functools.partial(half_values, half, start, runs // 4))
-        copies.append(
-            pltpu.make_async_copy(result_buf.at[half], out_ref.at[pl.ds(half * RUN, RUN), :], out_sems.at[half])
+        reach = runs // 4
+        lax.cond(
+            far,
+            functools.partial(half_values, half, start, reach + 1),
+            functools.partial(half_values, half, start, reach),
         )
-        copies[-1].start()
     for copy in copies:
         copy.wait()
 
@@ -172,14 +186,14 @@
                 pairs.append((s * places + ring[i], target))
         return lax.ppermute(block, ("section", "ctx"), pairs)
 
-    def around(block, rows, before_last=None):
+    def around(block, rows, early=None):
         ahead, back = shift(block, 1, 1), shift(block, 1, -1)
         held = [ahead, back]
-        for _ in range(2, places // 2):
+        for step in range(2, places // 2):
+            if early is not None and step == places // 2 - 1:
+                ahead, _ = lax.optimization_barrier((ahead, early))
             ahead, back = shift(ahead, 0, 1), shift(back, 0, -1)
             held.extend([ahead, back])
-        if before_last is not None:
-            ahead, _ = lax.optimization_barrier((ahead, before_last))
         return held + [shift(ahead[: rows // 2], 0, 1), shift(back[rows // 2 : rows], 0, -1)]
 
     own = shift(jnp.concatenate([queries[0], keys[0], values[0]], axis=1), 1, 0)
@@ -233,7 +247,7 @@
         out_specs=pl.BlockSpec(memory_space=pl.ANY),
         scratch_shapes=[
             pltpu.VMEM((2, RUN, QUERY_COLUMNS), jnp.bfloat16),
-            pltpu.SemaphoreType.DMA((2,)),
+            pltpu.SemaphoreType.DMA((2 * KEY_VALUE_HEADS,)),
         ],
         compiler_params=params,
         cost_estimate=pl.CostEstimate(flops=1 << 26, bytes_accessed=1 << 20, transcendentals=0),

time: 31.7 us -> 31.7 us (level)
  transfers between devices with their start and end apart: 17 -> 17, of which waited for: 10 -> 12; matrix products, arithmetic and copies ran while one was open for 1% -> 1% of each run, Pallas kernels for 7% -> 6%
where the time goes in v13:
time: 31.7 us; the launch traced here: 31.5 us
  starting transfers between devices  20.2 us (64%)
  waiting for transfers between devices  6.99 us (22%)
  Pallas kernels  3.96 us (12%)
    ppermute x17, starting transfers between devices, shift(): return lax.ppermute(block, ('section', 'ctx'), pairs)  20.2 us
    ppermute x17, waiting for transfers between devices, shift(): return lax.ppermute(block, ('section', 'ctx'), pairs)  6.99 us
    pallas_call x1, Pallas kernels, per_device(): pl.pallas_call(functools.partial(values_kernel, runs), out_shape=jax.Shap...  2.06 us
    pallas_call x1, Pallas kernels, per_device(): pl.pallas_call(functools.partial(weights_kernel, runs), out_shape=(jax.Sh...  1.63 us
  transfers between devices with their start and end apart: 17, of which 12 were waited for; matrix products, arithmetic and copies ran while one was open for 1% of the time, Pallas kernels for 6%

profile of v13, /device:TPU:0, one launch (start us, length us, event | category | flops | bytes accessed | tf_op | source)
XLA Modules:
  0.0 31.5 jit_solution(13763957892361568168)
XLA Ops:
  0.0 0.0 copy-start.2
  0.0 0.0 copy-start.1
  0.0 0.0 copy-start.4
  0.0 0.0 copy-start
  0.0 0.0 copy-start.3
  0.0 2.5 %collective-permute-start = (bf16[128,512]{1,0:T(8,128)(2,1)}, bf16[128,512]{1,0:T(8,128)(2,1)S(1)}, u32[]{:S(2)}, u32[]{:S(2)}) collective-permute-start(bf16[128,512]{1,0:T(8,128)(2,1)} %bitcast.16), channel_id=1, source_target_pairs={{0,10},{2,12},{4,14},{6,15},{7,13},{5,11},{3,9},{1,8},{8,18},{10,2... | collective-permute-start | bytes 393224 | tf_op jit(solution)/shard_map/ppermute | solution.py:187
  2.5 1.7 %collective-permute-start.4 = (bf16[128,512]{1,0:T(8,128)(2,1)}, bf16[128,512]{1,0:T(8,128)(2,1)S(1)}, u32[]{:S(2)}, u32[]{:S(2)}) collective-permute-start(bf16[128,512]{1,0:T(8,128)(2,1)} %bitcast.17), channel_id=1, source_target_pairs={{0,9},{2,8},{4,10},{6,12},{7,14},{5,15},{3,13},{1,11},{8,17},{10,1... | collective-permute-start | bytes 393224 | tf_op jit(solution)/shard_map/ppermute | solution.py:187
  4.2 0.0 copy-done.1
  4.3 0.0 copy-done.4
  4.3 1.2 %collective-permute-start.9 = (bf16[528,128]{1,0:T(8,128)(2,1)S(1)}, bf16[528,128]{1,0:T(8,128)(2,1)S(1)}, u32[]{:S(2)}, u32[]{:S(2)}) collective-permute-start(bf16[528,128]{1,0:T(8,128)(2,1)S(1)} %constant_dynamic-update-slice_fusion), channel_id=1, source_target_pairs={{0,10},{2,12},{4,14},{6,15},{7,13},{5,11},{3,9},{1,8},{8,18},{10,2... | collective-permute-start | bytes 405512 | tf_op jit(solution)/shard_map/ppermute | solution.py:187
  5.5 0.1 collective-permute-start.10
  5.6 0.0 copy-done.2
  5.6 0.0 copy-done
  5.6 0.1 pad_maximum_fusion
  5.7 0.5 %collective-permute-start.8 = (bf16[128,5120]{1,0:T(8,128)(2,1)S(1)}, bf16[128,5120]{1,0:T(8,128)(2,1)S(1)}, u32[]{:S(2)}, u32[]{:S(2)}) collective-permute-start(bf16[128,5120]{1,0:T(8,128)(2,1)S(1)} %pad_maximum_fusion), channel_id=1, source_target_pairs={{0,8},{2,10},{4,12},{6,14},{7,15},{5,13},{3,11},{1,9},{8,16},{10,1... | collective-permute-start | bytes 3932168 | tf_op jit(solution)/shard_map/ppermute | solution.py:187
  6.2 0.2 collective-permute-done.refs_0_
  6.4 3.9 %collective-permute-start.1 = (bf16[128,512]{1,0:T(8,128)(2,1)S(1)}, bf16[128,512]{1,0:T(8,128)(2,1)S(1)}, u32[]{:S(2)}, u32[]{:S(2)}) collective-permute-start(bf16[128,512]{1,0:T(8,128)(2,1)S(1)} %collective-permute-done.refs_0_), channel_id=1, source_target_pairs={{0,2},{2,4},{4,6},{6,7},{7,5},{5,3},{3,1},{1,0},{8,10},{10,12},{12... | collective-permute-start | bytes 393224 | tf_op jit(solution)/shard_map/ppermute | solution.py:187
  10.3 0.0 collective-permute-done.4.refs_1_
  10.3 0.0 collective-permute-start.5
  10.3 0.8 %collective-permute-done.9.refs_8_.refs_0_ = bf16[528,128]{1,0:T(8,128)(2,1)S(1)} collective-permute-done((bf16[528,128]{1,0:T(8,128)(2,1)S(1)}, bf16[528,128]{1,0:T(8,128)(2,1)S(1)}, u32[]{:S(2)}, u32[]{:S(2)}) %collective-permute-start.9) | collective-permute-done | bytes 135200 | tf_op jit(solution)/shard_map/ppermute | solution.py:187
  11.1 2.1 %collective-permute-start.11 = (bf16[528,128]{1,0:T(8,128)(2,1)S(1)}, bf16[528,128]{1,0:T(8,128)(2,1)S(1)}, u32[]{:S(2)}, u32[]{:S(2)}) collective-permute-start(bf16[528,128]{1,0:T(8,128)(2,1)S(1)} %collective-permute-done.9.refs_8_.refs_0_), channel_id=1, source_target_pairs={{0,2},{2,4},{4,6},{6,7},{7,5},{5,3},{3,1},{1,0},{8,10},{10,12},{12... | collective-permute-start | bytes 405512 | tf_op jit(solution)/shard_map/ppermute | solution.py:187
  13.2 0.0 collective-permute-done.10.refs_9_.refs_1_
  13.2 0.0 collective-permute-start.12
  13.2 0.9 %collective-permute-done.1.refs_2_ = bf16[128,512]{1,0:T(8,128)(2,1)S(1)} collective-permute-done((bf16[128,512]{1,0:T(8,128)(2,1)S(1)}, bf16[128,512]{1,0:T(8,128)(2,1)S(1)}, u32[]{:S(2)}, u32[]{:S(2)}) %collective-permute-start.1) | collective-permute-done | bytes 131104 | tf_op jit(solution)/shard_map/ppermute | solution.py:187
  14.1 1.7 %collective-permute-start.2 = (bf16[128,512]{1,0:T(8,128)(2,1)S(1)}, bf16[128,512]{1,0:T(8,128)(2,1)S(1)}, u32[]{:S(2)}, u32[]{:S(2)}) collective-permute-start(bf16[128,512]{1,0:T(8,128)(2,1)S(1)} %collective-permute-done.1.refs_2_), channel_id=1, source_target_pairs={{0,2},{2,4},{4,6},{6,7},{7,5},{5,3},{3,1},{1,0},{8,10},{10,12},{12... | collective-permute-start | bytes 393224 | tf_op jit(solution)/shard_map/ppermute | solution.py:187
  15.8 0.5 %collective-permute-done.5.refs_3_ = bf16[128,512]{1,0:T(8,128)(2,1)S(1)} collective-permute-done((bf16[128,512]{1,0:T(8,128)(2,1)S(1)}, bf16[128,512]{1,0:T(8,128)(2,1)S(1)}, u32[]{:S(2)}, u32[]{:S(2)}) %collective-permute-start.5) | collective-permute-done | bytes 131104 | tf_op jit(solution)/shard_map/ppermute | solution.py:187
  16.3 0.1 collective-permute-start.6
  16.5 0.0 copy-done.3
  16.5 0.3 shard_map.55.bias_ref
  16.7 0.5 %collective-permute-done.11.refs_10_.refs_2_ = bf16[528,128]{1,0:T(8,128)(2,1)S(1)} collective-permute-done((bf16[528,128]{1,0:T(8,128)(2,1)S(1)}, bf16[528,128]{1,0:T(8,128)(2,1)S(1)}, u32[]{:S(2)}, u32[]{:S(2)}) %collective-permute-start.11) | collective-permute-done | bytes 135200 | tf_op jit(solution)/shard_map/ppermute | solution.py:187
  17.2 2.2 %collective-permute-start.13 = (bf16[528,128]{1,0:T(8,128)(2,1)S(1)}, bf16[528,128]{1,0:T(8,128)(2,1)S(1)}, u32[]{:S(2)}, u32[]{:S(2)}) collective-permute-start(bf16[528,128]{1,0:T(8,128)(2,1)S(1)} %collective-permute-done.11.refs_10_.refs_2_), channel_id=1, source_target_pairs={{0,2},{2,4},{4,6},{6,7},{7,5},{5,3},{3,1},{1,0},{8,10},{10,12},{12... | collective-permute-start | bytes 405512 | tf_op jit(solution)/shard_map/ppermute | solution.py:187
  19.4 0.3 collective-permute-done.12.refs_11_.refs_3_
  19.7 0.0 collective-permute-start.14
  19.7 0.5 %collective-permute-done.2.refs_4_ = bf16[128,512]{1,0:T(8,128)(2,1)S(1)} collective-permute-done((bf16[128,512]{1,0:T(8,128)(2,1)S(1)}, bf16[128,512]{1,0:T(8,128)(2,1)S(1)}, u32[]{:S(2)}, u32[]{:S(2)}) %collective-permute-start.2) | collective-permute-done | bytes 131104 | tf_op jit(solution)/shard_map/ppermute | solution.py:187
  20.2 2.1 %collective-permute-start.3 = (bf16[64,512]{1,0:T(8,128)(2,1)S(1)}, bf16[64,512]{1,0:T(8,128)(2,1)S(1)}, u32[]{:S(2)}, u32[]{:S(2)}) collective-permute-start(bf16[64,512]{1,0:T(8,128)(2,1)S(1)} %slice.32), channel_id=1, source_target_pairs={{0,2},{2,4},{4,6},{6,7},{7,5},{5,3},{3,1},{1,0},{8,10},{10,12},{12... | collective-permute-start | bytes 196616 | tf_op jit(solution)/shard_map/ppermute | solution.py:187
  22.3 0.4 %collective-permute-done.6.refs_5_ = bf16[128,512]{1,0:T(8,128)(2,1)S(1)} collective-permute-done((bf16[128,512]{1,0:T(8,128)(2,1)S(1)}, bf16[128,512]{1,0:T(8,128)(2,1)S(1)}, u32[]{:S(2)}, u32[]{:S(2)}) %collective-permute-start.6) | collective-permute-done | bytes 131104 | tf_op jit(solution)/shard_map/ppermute | solution.py:187
  22.7 0.0 collective-permute-start.7
  22.7 0.3 collective-permute-done.13.refs_12_.refs_4_
  22.9 1.8 %collective-permute-start.15 = (bf16[256,128]{1,0:T(8,128)(2,1)S(1)}, bf16[256,128]{1,0:T(8,128)(2,1)S(1)}, u32[]{:S(2)}, u32[]{:S(2)}) collective-permute-start(bf16[256,128]{1,0:T(8,128)(2,1)S(1)} %slice.34), channel_id=1, source_target_pairs={{0,2},{2,4},{4,6},{6,7},{7,5},{5,3},{3,1},{1,0},{8,10},{10,12},{12... | collective-permute-start | bytes 196616 | tf_op jit(solution)/shard_map/ppermute | solution.py:187
  24.7 0.4 %collective-permute-done.14.refs_13_.refs_5_ = bf16[528,128]{1,0:T(8,128)(2,1)S(1)} collective-permute-done((bf16[528,128]{1,0:T(8,128)(2,1)S(1)}, bf16[528,128]{1,0:T(8,128)(2,1)S(1)}, u32[]{:S(2)}, u32[]{:S(2)}) %collective-permute-start.14) | collective-permute-done | bytes 135200 | tf_op jit(solution)/shard_map/ppermute | solution.py:187
  25.1 0.3 %collective-permute-start.16 = (bf16[256,128]{1,0:T(8,128)(2,1)S(1)}, bf16[256,128]{1,0:T(8,128)(2,1)S(1)}, u32[]{:S(2)}, u32[]{:S(2)}) collective-permute-start(bf16[256,128]{1,0:T(8,128)(2,1)S(1)} %slice.35), channel_id=1, source_target_pairs={{0,1},{2,0},{4,2},{6,4},{7,6},{5,7},{3,5},{1,3},{8,9},{10,8},{12,1... | collective-permute-start | bytes 196616 | tf_op jit(solution)/shard_map/ppermute | solution.py:187
  25.5 0.0 collective-permute-done.3.refs_0_.refs_6_
  25.5 1.6 %collective-permute-done.7.refs_1_.refs_7_ = bf16[64,512]{1,0:T(8,128)(2,1)S(1)} collective-permute-done((bf16[64,512]{1,0:T(8,128)(2,1)S(1)}, bf16[64,512]{1,0:T(8,128)(2,1)S(1)}, u32[]{:S(2)}, u32[]{:S(2)}) %collective-permute-start.7) | collective-permute-done | bytes 65568 | tf_op jit(solution)/shard_map/ppermute | solution.py:187
  27.1 0.0 collective-permute-done.8.own_ref
  27.1 1.6 %shard_map.58 = (bf16[8,512,320]{2,1,0:T(8,128)(2,1)S(1)}, bf16[4,16,64,128]{3,2,1,0:T(8,128)(2,1)S(1)}) custom-call(f32[1,1152]{1,0:T(1,128)S(1)} %add_convert_fusion.pos_ref, f32[2,64,320]{2,1,0:T(8,128)S(1)} %shard_map.55.bias_ref, f32[8,128]{1,0:T(8,128)S(1)} %shard_map.56.mark_ref, bf16[128,5120]{1,0:T(8,128)(2,1)S(1)} %collective-permute-done.8.own_ref, ...), custom_call_target="tpu_custom_call" | custom-call | flops 67108864 | bytes 1048576 | tf_op jit(solution)/shard_map/pallas_call | solution.py:231
  28.7 0.0 collective-permute-done.15.refs_6_
  28.8 0.6 %collective-permute-done.16.refs_7_ = bf16[256,128]{1,0:T(8,128)(2,1)S(1)} collective-permute-done((bf16[256,128]{1,0:T(8,128)(2,1)S(1)}, bf16[256,128]{1,0:T(8,128)(2,1)S(1)}, u32[]{:S(2)}, u32[]{:S(2)}) %collective-permute-start.16) | collective-permute-done | bytes 65568 | tf_op jit(solution)/shard_map/ppermute | solution.py:187
  29.4 2.1 %shard_map.59 = bf16[128,4096]{1,0:T(8,128)(2,1)} custom-call(f32[1,1152]{1,0:T(1,128)S(1)} %add_convert_fusion.pos_ref, bf16[8,512,320]{2,1,0:T(8,128)(2,1)S(1)} %get-tuple-element.9.weights_ref, bf16[4,16,64,128]{3,2,1,0:T(8,128)(2,1)S(1)} %get-tuple-element.10.sorted_ref, bf16[528,128]{1,0:T(8,128)(2,1)S(1)} %collective-permute-done.9.refs_8_.refs_0_, ...), custom_call_target="tpu_custom_call" | custom-call | flops 67108864 | bytes 1048576 | tf_op jit(solution)/shard_map/pallas_call | solution.py:243
  (13 shorter events, 0.1 us)
Async XLA Ops:
  0.0 5.6 %copy-start.2 = (bf16[1,128,512]{2,1,0:T(8,128)(2,1)S(1)}, bf16[1,128,512]{2,1,0:T(8,128)(2,1)}, u32[]{:S(2)}) copy-start(bf16[1,128,512]{2,1,0:T(8,128)(2,1)} %param.6) | copy-start | bytes 393220
  0.0 4.2 %copy-start.1 = (bf16[1,128,512]{2,1,0:T(8,128)(2,1)S(1)}, bf16[1,128,512]{2,1,0:T(8,128)(2,1)}, u32[]{:S(2)}) copy-start(bf16[1,128,512]{2,1,0:T(8,128)(2,1)} %param.7) | copy-start | bytes 393220
  0.0 4.3 %copy-start.4 = (s32[128]{0:T(128)S(1)}, s32[128]{0:T(128)}, u32[]{:S(2)}) copy-start(s32[128]{0:T(128)} %param.8) | copy-start | bytes 1540
  0.0 5.6 %copy-start = (bf16[1,128,4096]{2,1,0:T(8,128)(2,1)S(1)}, bf16[1,128,4096]{2,1,0:T(8,128)(2,1)}, u32[]{:S(2)}) copy-start(bf16[1,128,4096]{2,1,0:T(8,128)(2,1)} %param.5) | copy-start | bytes 3145732
  0.0 16.4 %copy-start.3 = (s32[1024]{0:T(1024)S(1)}, s32[1024]{0:T(1024)}, u32[]{:S(2)}) copy-start(s32[1024]{0:T(1024)} %param.9) | copy-start | bytes 12292
  0.0 6.4 %collective-permute-start = (bf16[128,512]{1,0:T(8,128)(2,1)}, bf16[128,512]{1,0:T(8,128)(2,1)S(1)}, u32[]{:S(2)}, u32[]{:S(2)}) collective-permute-start(bf16[128,512]{1,0:T(8,128)(2,1)} %bitcast.16), channel_id=1, source_target_pairs={{0,10},{2,12},{4,14},{6,15},{7,13},{5,11},{3,9},{1,8},{8,18},{10,2... | collective-permute-start | bytes 393224 | tf_op jit(solution)/shard_map/ppermute | solution.py:187
  2.5 7.8 %collective-permute-start.4 = (bf16[128,512]{1,0:T(8,128)(2,1)}, bf16[128,512]{1,0:T(8,128)(2,1)S(1)}, u32[]{:S(2)}, u32[]{:S(2)}) collective-permute-start(bf16[128,512]{1,0:T(8,128)(2,1)} %bitcast.17), channel_id=1, source_target_pairs={{0,9},{2,8},{4,10},{6,12},{7,14},{5,15},{3,13},{1,11},{8,17},{10,1... | collective-permute-start | bytes 393224 | tf_op jit(solution)/shard_map/ppermute | solution.py:187
  4.3 6.8 %collective-permute-start.9 = (bf16[528,128]{1,0:T(8,128)(2,1)S(1)}, bf16[528,128]{1,0:T(8,128)(2,1)S(1)}, u32[]{:S(2)}, u32[]{:S(2)}) collective-permute-start(bf16[528,128]{1,0:T(8,128)(2,1)S(1)} %constant_dynamic-update-slice_fusion), channel_id=1, source_target_pairs={{0,10},{2,12},{4,14},{6,15},{7,13},{5,11},{3,9},{1,8},{8,18},{10,2... | collective-permute-start | bytes 405512 | tf_op jit(solution)/shard_map/ppermute | solution.py:187
  5.5 7.7 %collective-permute-start.10 = (bf16[528,128]{1,0:T(8,128)(2,1)S(1)}, bf16[528,128]{1,0:T(8,128)(2,1)S(1)}, u32[]{:S(2)}, u32[]{:S(2)}) collective-permute-start(bf16[528,128]{1,0:T(8,128)(2,1)S(1)} %constant_dynamic-update-slice_fusion), channel_id=1, source_target_pairs={{0,9},{2,8},{4,10},{6,12},{7,14},{5,15},{3,13},{1,11},{8,17},{10,1... | collective-permute-start | bytes 405512 | tf_op jit(solution)/shard_map/ppermute | solution.py:187
  5.7 21.4 %collective-permute-start.8 = (bf16[128,5120]{1,0:T(8,128)(2,1)S(1)}, bf16[128,5120]{1,0:T(8,128)(2,1)S(1)}, u32[]{:S(2)}, u32[]{:S(2)}) collective-permute-start(bf16[128,5120]{1,0:T(8,128)(2,1)S(1)} %pad_maximum_fusion), channel_id=1, source_target_pairs={{0,8},{2,10},{4,12},{6,14},{7,15},{5,13},{3,11},{1,9},{8,16},{10,1... | collective-permute-start | bytes 3932168 | tf_op jit(solution)/shard_map/ppermute | solution.py:187
  6.4 7.7 %collective-permute-start.1 = (bf16[128,512]{1,0:T(8,128)(2,1)S(1)}, bf16[128,512]{1,0:T(8,128)(2,1)S(1)}, u32[]{:S(2)}, u32[]{:S(2)}) collective-permute-start(bf16[128,512]{1,0:T(8,128)(2,1)S(1)} %collective-permute-done.refs_0_), channel_id=1, source_target_pairs={{0,2},{2,4},{4,6},{6,7},{7,5},{5,3},{3,1},{1,0},{8,10},{10,12},{12... | collective-permute-start | bytes 393224 | tf_op jit(solution)/shard_map/ppermute | solution.py:187
  10.3 6.0 %collective-permute-start.5 = (bf16[128,512]{1,0:T(8,128)(2,1)S(1)}, bf16[128,512]{1,0:T(8,128)(2,1)S(1)}, u32[]{:S(2)}, u32[]{:S(2)}) collective-permute-start(bf16[128,512]{1,0:T(8,128)(2,1)S(1)} %collective-permute-done.4.refs_1_), channel_id=1, source_target_pairs={{0,1},{2,0},{4,2},{6,4},{7,6},{5,7},{3,5},{1,3},{8,9},{10,8},{12,1... | collective-permute-start | bytes 393224 | tf_op jit(solution)/shard_map/ppermute | solution.py:187
  11.1 6.1 %collective-permute-start.11 = (bf16[528,128]{1,0:T(8,128)(2,1)S(1)}, bf16[528,128]{1,0:T(8,128)(2,1)S(1)}, u32[]{:S(2)}, u32[]{:S(2)}) collective-permute-start(bf16[528,128]{1,0:T(8,128)(2,1)S(1)} %collective-permute-done.9.refs_8_.refs_0_), channel_id=1, source_target_pairs={{0,2},{2,4},{4,6},{6,7},{7,5},{5,3},{3,1},{1,0},{8,10},{10,12},{12... | collective-permute-start | bytes 405512 | tf_op jit(solution)/shard_map/ppermute | solution.py:187
  13.2 6.5 %collective-permute-start.12 = (bf16[528,128]{1,0:T(8,128)(2,1)S(1)}, bf16[528,128]{1,0:T(8,128)(2,1)S(1)}, u32[]{:S(2)}, u32[]{:S(2)}) collective-permute-start(bf16[528,128]{1,0:T(8,128)(2,1)S(1)} %collective-permute-done.10.refs_9_.refs_1_), channel_id=1, source_target_pairs={{0,1},{2,0},{4,2},{6,4},{7,6},{5,7},{3,5},{1,3},{8,9},{10,8},{12,1... | collective-permute-start | bytes 405512 | tf_op jit(solution)/shard_map/ppermute | solution.py:187
  14.1 6.1 %collective-permute-start.2 = (bf16[128,512]{1,0:T(8,128)(2,1)S(1)}, bf16[128,512]{1,0:T(8,128)(2,1)S(1)}, u32[]{:S(2)}, u32[]{:S(2)}) collective-permute-start(bf16[128,512]{1,0:T(8,128)(2,1)S(1)} %collective-permute-done.1.refs_2_), channel_id=1, source_target_pairs={{0,2},{2,4},{4,6},{6,7},{7,5},{5,3},{3,1},{1,0},{8,10},{10,12},{12... | collective-permute-start | bytes 393224 | tf_op jit(solution)/shard_map/ppermute | solution.py:187
  16.3 6.3 %collective-permute-start.6 = (bf16[128,512]{1,0:T(8,128)(2,1)S(1)}, bf16[128,512]{1,0:T(8,128)(2,1)S(1)}, u32[]{:S(2)}, u32[]{:S(2)}) collective-permute-start(bf16[128,512]{1,0:T(8,128)(2,1)S(1)} %collective-permute-done.5.refs_3_), channel_id=1, source_target_pairs={{0,1},{2,0},{4,2},{6,4},{7,6},{5,7},{3,5},{1,3},{8,9},{10,8},{12,1... | collective-permute-start | bytes 393224 | tf_op jit(solution)/shard_map/ppermute | solution.py:187
  17.2 5.7 %collective-permute-start.13 = (bf16[528,128]{1,0:T(8,128)(2,1)S(1)}, bf16[528,128]{1,0:T(8,128)(2,1)S(1)}, u32[]{:S(2)}, u32[]{:S(2)}) collective-permute-start(bf16[528,128]{1,0:T(8,128)(2,1)S(1)} %collective-permute-done.11.refs_10_.refs_2_), channel_id=1, source_target_pairs={{0,2},{2,4},{4,6},{6,7},{7,5},{5,3},{3,1},{1,0},{8,10},{10,12},{12... | collective-permute-start | bytes 405512 | tf_op jit(solution)/shard_map/ppermute | solution.py:187
  19.7 5.4 %collective-permute-start.14 = (bf16[528,128]{1,0:T(8,128)(2,1)S(1)}, bf16[528,128]{1,0:T(8,128)(2,1)S(1)}, u32[]{:S(2)}, u32[]{:S(2)}) collective-permute-start(bf16[528,128]{1,0:T(8,128)(2,1)S(1)} %collective-permute-done.12.refs_11_.refs_3_), channel_id=1, source_target_pairs={{0,1},{2,0},{4,2},{6,4},{7,6},{5,7},{3,5},{1,3},{8,9},{10,8},{12,1... | collective-permute-start | bytes 405512 | tf_op jit(solution)/shard_map/ppermute | solution.py:187
  20.2 5.3 %collective-permute-start.3 = (bf16[64,512]{1,0:T(8,128)(2,1)S(1)}, bf16[64,512]{1,0:T(8,128)(2,1)S(1)}, u32[]{:S(2)}, u32[]{:S(2)}) collective-permute-start(bf16[64,512]{1,0:T(8,128)(2,1)S(1)} %slice.32), channel_id=1, source_target_pairs={{0,2},{2,4},{4,6},{6,7},{7,5},{5,3},{3,1},{1,0},{8,10},{10,12},{12... | collective-permute-start | bytes 196616 | tf_op jit(solution)/shard_map/ppermute | solution.py:187
  22.7 4.4 %collective-permute-start.7 = (bf16[64,512]{1,0:T(8,128)(2,1)S(1)}, bf16[64,512]{1,0:T(8,128)(2,1)S(1)}, u32[]{:S(2)}, u32[]{:S(2)}) collective-permute-start(bf16[64,512]{1,0:T(8,128)(2,1)S(1)} %slice.33), channel_id=1, source_target_pairs={{0,1},{2,0},{4,2},{6,4},{7,6},{5,7},{3,5},{1,3},{8,9},{10,8},{12,1... | collective-permute-start | bytes 196616 | tf_op jit(solution)/shard_map/ppermute | solution.py:187
  22.9 5.8 %collective-permute-start.15 = (bf16[256,128]{1,0:T(8,128)(2,1)S(1)}, bf16[256,128]{1,0:T(8,128)(2,1)S(1)}, u32[]{:S(2)}, u32[]{:S(2)}) collective-permute-start(bf16[256,128]{1,0:T(8,128)(2,1)S(1)} %slice.34), channel_id=1, source_target_pairs={{0,2},{2,4},{4,6},{6,7},{7,5},{5,3},{3,1},{1,0},{8,10},{10,12},{12... | collective-permute-start | bytes 196616 | tf_op jit(solution)/shard_map/ppermute | solution.py:187
  25.1 4.3 %collective-permute-start.16 = (bf16[256,128]{1,0:T(8,128)(2,1)S(1)}, bf16[256,128]{1,0:T(8,128)(2,1)S(1)}, u32[]{:S(2)}, u32[]{:S(2)}) collective-permute-start(bf16[256,128]{1,0:T(8,128)(2,1)S(1)} %slice.35), channel_id=1, source_target_pairs={{0,1},{2,0},{4,2},{6,4},{7,6},{5,7},{3,5},{1,3},{8,9},{10,8},{12,1... | collective-permute-start | bytes 196616 | tf_op jit(solution)/shard_map/ppermute | solution.py:187

commit v14 on v13

--- a/solution.py
+++ b/solution.py
@@ -36,8 +36,16 @@
     return jnp.where(far, run - reach, jnp.maximum(run - reach + 1, 0)), far
 
 
-def run_numbers(runs, pos_ref, tagged_refs):
-    firsts = [first_run(pos_ref)]
+def write_number(ref, row, number):
+    ref[row : row + 1, :] = jnp.full((1, ref.shape[1]), number.astype(jnp.float32))
+
+
+def read_number(ref, row):
+    return ref[row : row + 1, :].astype(jnp.float32)[0, 0].astype(jnp.int32)
+
+
+def run_numbers(runs, first, tagged_refs):
+    firsts = [first]
     for ref in tagged_refs:
         firsts.append(ref[VALUE_ROWS:, :].astype(jnp.float32)[0, 0].astype(jnp.int32))
     places = runs // 2
@@ -70,24 +78,29 @@
     refs[-1][...] = jnp.zeros_like(refs[-1])
 
 
-def bias_kernel(runs, pos_ref, bias_ref):
+def bias_kernel(runs, pos_ref, bias_ref, plan_ref):
     segment = pos_ref[:, TOK_DEV:]
     first = first_run(pos_ref)
+    write_number(plan_ref, 0, first)
     for half, run in enumerate((first, runs - 1 - first)):
         row_pos = run * RUN + lax.broadcasted_iota(jnp.int32, (RUN, 1), 0)
         at = lax.broadcasted_iota(jnp.int32, (RUN, runs * RUN), 1) == row_pos
         row_doc = jnp.sum(jnp.where(at, segment, 0.0), axis=1, keepdims=True)
         doc_start = jnp.sum(jnp.where(segment < row_doc, 1.0, 0.0), axis=1, keepdims=True).astype(jnp.int32)
-        start, _ = first_in_reach(runs, pos_ref, run)
+        start, far = first_in_reach(runs, pos_ref, run)
+        write_number(plan_ref, 1 + 2 * half, start)
+        write_number(plan_ref, 2 + 2 * half, jnp.where(far, 1, 0))
         key_pos = start * RUN + lax.broadcasted_iota(jnp.int32, bias_ref.shape[1:], 1)
         bias_ref[half] = jnp.where((key_pos <= row_pos) & (key_pos >= doc_start), 0.0, masked_fill)
 
 
-def weights_kernel(runs, pos_ref, bias_ref, mark_ref, own_ref, *refs):
+def weights_kernel(runs, plan_ref, bias_ref, mark_ref, own_ref, *refs):
     blocks = runs // 2
-    key_refs, tagged_refs = refs[:blocks], refs[blocks:-3]
-    weights_ref, sorted_ref, key_buf = refs[-3:]
-    numbers = run_numbers(runs, pos_ref, tagged_refs)
+    key_refs, tagged_refs = refs[:blocks], refs[blocks:-4]
+    weights_ref, sorted_ref, last_run_ref, key_buf = refs[-4:]
+    numbers = run_numbers(runs, read_number(plan_ref, 0), tagged_refs)
+    write_number(last_run_ref, 0, numbers[-1][0])
+    plan = [(read_number(plan_ref, 1 + 2 * half), read_number(plan_ref, 2 + 2 * half) > 0) for half in range(2)]
     sort_keys(numbers, own_ref, key_refs[:-2], key_refs[-2:], key_buf)
     sort_values(numbers, own_ref, tagged_refs, sorted_ref)
     scale = math.log2(math.e) / math.sqrt(HEAD_SIZE)
@@ -115,14 +128,16 @@
             weights_ref[half * KEY_VALUE_HEADS + kv, :, :span] = weights
 
     for half in range(2):
-        start, far = first_in_reach(runs, pos_ref, numbers[0][half])
+        start, far = plan[half]
         pl.when(far)(functools.partial(half_weights, half, start, runs // 4 + 1))
         pl.when(jnp.logical_not(far))(functools.partial(half_weights, half, start, runs // 4))
 
 
-def values_kernel(runs, pos_ref, weights_ref, sorted_ref, *refs):
-    tagged_refs, last_refs, (out_ref, result_buf, out_sems) = refs[:-5], refs[-5:-3], refs[-3:]
-    numbers = run_numbers(runs, pos_ref, tagged_refs)
+def values_kernel(runs, plan_ref, last_run_ref, weights_ref, sorted_ref, *refs):
+    last_refs, (out_ref, result_buf, out_sems) = refs[:2], refs[2:]
+    last_run = read_number(last_run_ref, 0)
+    last_runs = (last_run, runs - 1 - last_run)
+    plan = [(read_number(plan_ref, 1 + 2 * half), read_number(plan_ref, 2 + 2 * half) > 0) for half in range(2)]
 
     def half_values(half, start, count):
         ones = jnp.ones((count * RUN, HEAD_SIZE), jnp.bfloat16)
@@ -131,7 +146,7 @@
             parts = []
             for i in range(count):
                 part = sorted_ref[kv, start + i]
-                for last_half, number in enumerate(numbers[-1]):
+                for last_half, number in enumerate(last_runs):
                     row = kv % (KEY_VALUE_HEADS // 2) * TOK_DEV + last_half * RUN
                     part = jnp.where(start + i == number, last_ref[row : row + RUN, :], part)
                 parts.append(part)
@@ -161,7 +176,7 @@
                 )
             )
     for half in range(2):
-        start, far = first_in_reach(runs, pos_ref, numbers[0][half])
+        start, far = plan[half]
         reach = runs // 4
         lax.cond(
             far,
@@ -209,11 +224,14 @@
     by_head = [values[0, :, kv * HEAD_SIZE : (kv + 1) * HEAD_SIZE] for kv in range(KEY_VALUE_HEADS)]
     tagged = jnp.concatenate([*by_head, blank + tag[None]], axis=0)
     pos = lax.optimization_barrier(jnp.concatenate([token_pos, segment]).astype(jnp.float32)[None])
-    bias = pl.pallas_call(
+    bias, plan = pl.pallas_call(
         functools.partial(bias_kernel, runs),
-        out_shape=jax.ShapeDtypeStruct((2, RUN, (runs // 4 + 1) * RUN), jnp.float32),
+        out_shape=(
+            jax.ShapeDtypeStruct((2, RUN, (runs // 4 + 1) * RUN), jnp.float32),
+            jax.ShapeDtypeStruct((8, HEAD_SIZE), jnp.float32),
+        ),
         in_specs=[vmem],
-        out_specs=vmem,
+        out_specs=(vmem,) * 2,
         compiler_params=pltpu.CompilerParams(vmem_limit_bytes=8 * 1024 * 1024),
         cost_estimate=pl.CostEstimate(flops=1 << 20, bytes_accessed=1 << 10, transcendentals=0),
     )(pos)
@@ -228,22 +246,23 @@
         compiler_params=pltpu.CompilerParams(vmem_limit_bytes=8 * 1024 * 1024),
         cost_estimate=pl.CostEstimate(flops=65 << 27, bytes_accessed=0, transcendentals=0),
     )(*all_keys[-2:])
-    weights, sorted_values = pl.pallas_call(
+    weights, sorted_values, last_run = pl.pallas_call(
         functools.partial(weights_kernel, runs),
         out_shape=(
             jax.ShapeDtypeStruct((2 * KEY_VALUE_HEADS, GROUP * RUN, (runs // 4 + 1) * RUN), jnp.bfloat16),
             jax.ShapeDtypeStruct((KEY_VALUE_HEADS, runs, RUN, HEAD_SIZE), jnp.bfloat16),
+            jax.ShapeDtypeStruct((8, HEAD_SIZE), jnp.float32),
         ),
         in_specs=[vmem] * (4 + len(all_keys) + len(all_values[:-2])),
-        out_specs=(vmem,) * 2,
+        out_specs=(vmem,) * 3,
         scratch_shapes=[pltpu.VMEM((runs, RUN, KV_COLUMNS), jnp.bfloat16)],
         compiler_params=params,
         cost_estimate=pl.CostEstimate(flops=1 << 26, bytes_accessed=1 << 20, transcendentals=0),
-    )(pos, bias, mark, own, *all_keys, *all_values[:-2])
+    )(plan, bias, mark, own, *all_keys, *all_values[:-2])
     out = pl.pallas_call(
         functools.partial(values_kernel, runs),
         out_shape=jax.ShapeDtypeStruct((TOK_DEV, QUERY_COLUMNS), jnp.bfloat16),
-        in_specs=[vmem] * (3 + len(all_values)),
+        in_specs=[vmem] * 6,
         out_specs=pl.BlockSpec(memory_space=pl.ANY),
         scratch_shapes=[
             pltpu.VMEM((2, RUN, QUERY_COLUMNS), jnp.bfloat16),
@@ -251,7 +270,7 @@
         ],
         compiler_params=params,
         cost_estimate=pl.CostEstimate(flops=1 << 26, bytes_accessed=1 << 20, transcendentals=0),
-    )(pos, weights, sorted_values, *all_values)
+    )(plan, last_run, weights, sorted_values, *all_values[-2:])
     return out[None]
 
 

time: 31.7 us -> 31.3 us (0.987)
  Pallas kernels: 3.96 us -> 3.54 us
where the time goes in v14:
time: 31.3 us; the launch traced here: 31.2 us
  starting transfers between devices  20.2 us (65%)
  waiting for transfers between devices  7.17 us (23%)
  Pallas kernels  3.54 us (11%)
    ppermute x17, starting transfers between devices, shift(): return lax.ppermute(block, ('section', 'ctx'), pairs)  20.2 us
    ppermute x17, waiting for transfers between devices, shift(): return lax.ppermute(block, ('section', 'ctx'), pairs)  7.17 us
    pallas_call x1, Pallas kernels, per_device(): pl.pallas_call(functools.partial(values_kernel, runs), out_shape=jax.Shap...  1.81 us
    pallas_call x1, Pallas kernels, per_device(): pl.pallas_call(functools.partial(weights_kernel, runs), out_shape=(jax.Sh...  1.46 us
  transfers between devices with their start and end apart: 17, of which 12 were waited for; matrix products, arithmetic and copies ran while one was open for 1% of the time, Pallas kernels for 6%

profile of v14, /device:TPU:0, one launch (start us, length us, event | category | flops | bytes accessed | tf_op | source)
XLA Modules:
  0.0 31.2 jit_solution(12040546830672114640)
XLA Ops:
  0.0 0.0 copy-start.2
  0.0 0.0 copy-start.1
  0.0 0.0 copy-start.4
  0.0 0.0 copy-start
  0.0 0.0 copy-start.3
  0.0 2.5 %collective-permute-start = (bf16[128,512]{1,0:T(8,128)(2,1)}, bf16[128,512]{1,0:T(8,128)(2,1)S(1)}, u32[]{:S(2)}, u32[]{:S(2)}) collective-permute-start(bf16[128,512]{1,0:T(8,128)(2,1)} %bitcast.16), channel_id=1, source_target_pairs={{0,10},{2,12},{4,14},{6,15},{7,13},{5,11},{3,9},{1,8},{8,18},{10,2... | collective-permute-start | bytes 393224 | tf_op jit(solution)/shard_map/ppermute | solution.py:202
  2.5 1.7 %collective-permute-start.4 = (bf16[128,512]{1,0:T(8,128)(2,1)}, bf16[128,512]{1,0:T(8,128)(2,1)S(1)}, u32[]{:S(2)}, u32[]{:S(2)}) collective-permute-start(bf16[128,512]{1,0:T(8,128)(2,1)} %bitcast.17), channel_id=1, source_target_pairs={{0,9},{2,8},{4,10},{6,12},{7,14},{5,15},{3,13},{1,11},{8,17},{10,1... | collective-permute-start | bytes 393224 | tf_op jit(solution)/shard_map/ppermute | solution.py:202
  4.2 0.0 copy-done.1
  4.3 0.0 copy-done.4
  4.3 1.2 %collective-permute-start.9 = (bf16[528,128]{1,0:T(8,128)(2,1)S(1)}, bf16[528,128]{1,0:T(8,128)(2,1)S(1)}, u32[]{:S(2)}, u32[]{:S(2)}) collective-permute-start(bf16[528,128]{1,0:T(8,128)(2,1)S(1)} %constant_dynamic-update-slice_fusion), channel_id=1, source_target_pairs={{0,10},{2,12},{4,14},{6,15},{7,13},{5,11},{3,9},{1,8},{8,18},{10,2... | collective-permute-start | bytes 405512 | tf_op jit(solution)/shard_map/ppermute | solution.py:202
  5.5 0.1 collective-permute-start.10
  5.6 0.0 copy-done.2
  5.6 0.0 copy-done
  5.6 0.1 pad_maximum_fusion
  5.7 0.5 %collective-permute-start.8 = (bf16[128,5120]{1,0:T(8,128)(2,1)S(1)}, bf16[128,5120]{1,0:T(8,128)(2,1)S(1)}, u32[]{:S(2)}, u32[]{:S(2)}) collective-permute-start(bf16[128,5120]{1,0:T(8,128)(2,1)S(1)} %pad_maximum_fusion), channel_id=1, source_target_pairs={{0,8},{2,10},{4,12},{6,14},{7,15},{5,13},{3,11},{1,9},{8,16},{10,1... | collective-permute-start | bytes 3932168 | tf_op jit(solution)/shard_map/ppermute | solution.py:202
  6.2 0.2 collective-permute-done.refs_0_
  6.4 3.9 %collective-permute-start.1 = (bf16[128,512]{1,0:T(8,128)(2,1)S(1)}, bf16[128,512]{1,0:T(8,128)(2,1)S(1)}, u32[]{:S(2)}, u32[]{:S(2)}) collective-permute-start(bf16[128,512]{1,0:T(8,128)(2,1)S(1)} %collective-permute-done.refs_0_), channel_id=1, source_target_pairs={{0,2},{2,4},{4,6},{6,7},{7,5},{5,3},{3,1},{1,0},{8,10},{10,12},{12... | collective-permute-start | bytes 393224 | tf_op jit(solution)/shard_map/ppermute | solution.py:202
  10.3 0.0 collective-permute-done.4.refs_1_
  10.3 0.0 collective-permute-start.5
  10.3 0.8 %collective-permute-done.9.refs_8_ = bf16[528,128]{1,0:T(8,128)(2,1)S(1)} collective-permute-done((bf16[528,128]{1,0:T(8,128)(2,1)S(1)}, bf16[528,128]{1,0:T(8,128)(2,1)S(1)}, u32[]{:S(2)}, u32[]{:S(2)}) %collective-permute-start.9) | collective-permute-done | bytes 135200 | tf_op jit(solution)/shard_map/ppermute | solution.py:202
  11.1 2.1 %collective-permute-start.11 = (bf16[528,128]{1,0:T(8,128)(2,1)S(1)}, bf16[528,128]{1,0:T(8,128)(2,1)S(1)}, u32[]{:S(2)}, u32[]{:S(2)}) collective-permute-start(bf16[528,128]{1,0:T(8,128)(2,1)S(1)} %collective-permute-done.9.refs_8_), channel_id=1, source_target_pairs={{0,2},{2,4},{4,6},{6,7},{7,5},{5,3},{3,1},{1,0},{8,10},{10,12},{12... | collective-permute-start | bytes 405512 | tf_op jit(solution)/shard_map/ppermute | solution.py:202
  13.2 0.0 collective-permute-done.10.refs_9_
  13.2 0.0 collective-permute-start.12
  13.2 0.9 %collective-permute-done.1.refs_2_ = bf16[128,512]{1,0:T(8,128)(2,1)S(1)} collective-permute-done((bf16[128,512]{1,0:T(8,128)(2,1)S(1)}, bf16[128,512]{1,0:T(8,128)(2,1)S(1)}, u32[]{:S(2)}, u32[]{:S(2)}) %collective-permute-start.1) | collective-permute-done | bytes 131104 | tf_op jit(solution)/shard_map/ppermute | solution.py:202
  14.1 1.7 %collective-permute-start.2 = (bf16[128,512]{1,0:T(8,128)(2,1)S(1)}, bf16[128,512]{1,0:T(8,128)(2,1)S(1)}, u32[]{:S(2)}, u32[]{:S(2)}) collective-permute-start(bf16[128,512]{1,0:T(8,128)(2,1)S(1)} %collective-permute-done.1.refs_2_), channel_id=1, source_target_pairs={{0,2},{2,4},{4,6},{6,7},{7,5},{5,3},{3,1},{1,0},{8,10},{10,12},{12... | collective-permute-start | bytes 393224 | tf_op jit(solution)/shard_map/ppermute | solution.py:202
  15.8 0.5 %collective-permute-done.5.refs_3_ = bf16[128,512]{1,0:T(8,128)(2,1)S(1)} collective-permute-done((bf16[128,512]{1,0:T(8,128)(2,1)S(1)}, bf16[128,512]{1,0:T(8,128)(2,1)S(1)}, u32[]{:S(2)}, u32[]{:S(2)}) %collective-permute-start.5) | collective-permute-done | bytes 131104 | tf_op jit(solution)/shard_map/ppermute | solution.py:202
  16.3 0.1 collective-permute-start.6
  16.5 0.0 copy-done.3
  16.5 0.3 shard_map.55
  16.7 0.5 %collective-permute-done.11.refs_10_ = bf16[528,128]{1,0:T(8,128)(2,1)S(1)} collective-permute-done((bf16[528,128]{1,0:T(8,128)(2,1)S(1)}, bf16[528,128]{1,0:T(8,128)(2,1)S(1)}, u32[]{:S(2)}, u32[]{:S(2)}) %collective-permute-start.11) | collective-permute-done | bytes 135200 | tf_op jit(solution)/shard_map/ppermute | solution.py:202
  17.2 2.2 %collective-permute-start.13 = (bf16[528,128]{1,0:T(8,128)(2,1)S(1)}, bf16[528,128]{1,0:T(8,128)(2,1)S(1)}, u32[]{:S(2)}, u32[]{:S(2)}) collective-permute-start(bf16[528,128]{1,0:T(8,128)(2,1)S(1)} %collective-permute-done.11.refs_10_), channel_id=1, source_target_pairs={{0,2},{2,4},{4,6},{6,7},{7,5},{5,3},{3,1},{1,0},{8,10},{10,12},{12... | collective-permute-start | bytes 405512 | tf_op jit(solution)/shard_map/ppermute | solution.py:202
  19.4 0.3 collective-permute-done.12.refs_11_
  19.7 0.0 collective-permute-start.14
  19.7 0.5 %collective-permute-done.2.refs_4_ = bf16[128,512]{1,0:T(8,128)(2,1)S(1)} collective-permute-done((bf16[128,512]{1,0:T(8,128)(2,1)S(1)}, bf16[128,512]{1,0:T(8,128)(2,1)S(1)}, u32[]{:S(2)}, u32[]{:S(2)}) %collective-permute-start.2) | collective-permute-done | bytes 131104 | tf_op jit(solution)/shard_map/ppermute | solution.py:202
  20.2 2.1 %collective-permute-start.3 = (bf16[64,512]{1,0:T(8,128)(2,1)S(1)}, bf16[64,512]{1,0:T(8,128)(2,1)S(1)}, u32[]{:S(2)}, u32[]{:S(2)}) collective-permute-start(bf16[64,512]{1,0:T(8,128)(2,1)S(1)} %slice.32), channel_id=1, source_target_pairs={{0,2},{2,4},{4,6},{6,7},{7,5},{5,3},{3,1},{1,0},{8,10},{10,12},{12... | collective-permute-start | bytes 196616 | tf_op jit(solution)/shard_map/ppermute | solution.py:202
  22.3 0.4 %collective-permute-done.6.refs_5_ = bf16[128,512]{1,0:T(8,128)(2,1)S(1)} collective-permute-done((bf16[128,512]{1,0:T(8,128)(2,1)S(1)}, bf16[128,512]{1,0:T(8,128)(2,1)S(1)}, u32[]{:S(2)}, u32[]{:S(2)}) %collective-permute-start.6) | collective-permute-done | bytes 131104 | tf_op jit(solution)/shard_map/ppermute | solution.py:202
  22.7 0.0 collective-permute-start.7
  22.7 0.3 collective-permute-done.13.refs_12_
  22.9 1.8 %collective-permute-start.15 = (bf16[256,128]{1,0:T(8,128)(2,1)S(1)}, bf16[256,128]{1,0:T(8,128)(2,1)S(1)}, u32[]{:S(2)}, u32[]{:S(2)}) collective-permute-start(bf16[256,128]{1,0:T(8,128)(2,1)S(1)} %slice.34), channel_id=1, source_target_pairs={{0,2},{2,4},{4,6},{6,7},{7,5},{5,3},{3,1},{1,0},{8,10},{10,12},{12... | collective-permute-start | bytes 196616 | tf_op jit(solution)/shard_map/ppermute | solution.py:202
  24.7 0.4 %collective-permute-done.14.refs_13_ = bf16[528,128]{1,0:T(8,128)(2,1)S(1)} collective-permute-done((bf16[528,128]{1,0:T(8,128)(2,1)S(1)}, bf16[528,128]{1,0:T(8,128)(2,1)S(1)}, u32[]{:S(2)}, u32[]{:S(2)}) %collective-permute-start.14) | collective-permute-done | bytes 135200 | tf_op jit(solution)/shard_map/ppermute | solution.py:202
  25.1 0.3 %collective-permute-start.16 = (bf16[256,128]{1,0:T(8,128)(2,1)S(1)}, bf16[256,128]{1,0:T(8,128)(2,1)S(1)}, u32[]{:S(2)}, u32[]{:S(2)}) collective-permute-start(bf16[256,128]{1,0:T(8,128)(2,1)S(1)} %slice.35), channel_id=1, source_target_pairs={{0,1},{2,0},{4,2},{6,4},{7,6},{5,7},{3,5},{1,3},{8,9},{10,8},{12,1... | collective-permute-start | bytes 196616 | tf_op jit(solution)/shard_map/ppermute | solution.py:202
  25.5 0.0 collective-permute-done.3.refs_0_.refs_6_
  25.5 1.6 %collective-permute-done.7.refs_1_.refs_7_ = bf16[64,512]{1,0:T(8,128)(2,1)S(1)} collective-permute-done((bf16[64,512]{1,0:T(8,128)(2,1)S(1)}, bf16[64,512]{1,0:T(8,128)(2,1)S(1)}, u32[]{:S(2)}, u32[]{:S(2)}) %collective-permute-start.7) | collective-permute-done | bytes 65568 | tf_op jit(solution)/shard_map/ppermute | solution.py:202
  27.1 0.0 collective-permute-done.8.own_ref
  27.1 1.5 %shard_map.58 = (bf16[8,512,320]{2,1,0:T(8,128)(2,1)S(1)}, bf16[4,16,64,128]{3,2,1,0:T(8,128)(2,1)S(1)}, f32[8,128]{1,0:T(8,128)S(1)}) custom-call(f32[8,128]{1,0:T(8,128)S(1)} %get-tuple-element.11.plan_ref, f32[2,64,320]{2,1,0:T(8,128)S(1)} %get-tuple-element.12.bias_ref, f32[8,128]{1,0:T(8,128)S(1)} %shard_map.56.mark_ref, ...), custom_call_target="tpu_custom_call" | custom-call | flops 67108864 | bytes 1048576 | tf_op jit(solution)/shard_map/pallas_call | solution.py:249
  28.6 0.0 collective-permute-done.15.refs_0_
  28.6 0.8 %collective-permute-done.16.refs_1_ = bf16[256,128]{1,0:T(8,128)(2,1)S(1)} collective-permute-done((bf16[256,128]{1,0:T(8,128)(2,1)S(1)}, bf16[256,128]{1,0:T(8,128)(2,1)S(1)}, u32[]{:S(2)}, u32[]{:S(2)}) %collective-permute-start.16) | collective-permute-done | bytes 65568 | tf_op jit(solution)/shard_map/ppermute | solution.py:202
  29.4 1.8 %shard_map.59 = bf16[128,4096]{1,0:T(8,128)(2,1)} custom-call(f32[8,128]{1,0:T(8,128)S(1)} %get-tuple-element.11.plan_ref, f32[8,128]{1,0:T(8,128)S(1)} %get-tuple-element.14.last_run_ref, bf16[8,512,320]{2,1,0:T(8,128)(2,1)S(1)} %get-tuple-element.15.weights_ref, bf16[4,16,64,128]{3,2,1,0:T(8,128)(2,1)S(1)} %get-tuple-element.16.sorted_ref, ...), custom_call_target="tpu_custom_call" | custom-call | flops 67108864 | bytes 1048576 | tf_op jit(solution)/shard_map/pallas_call | solution.py:262
  (13 shorter events, 0.1 us)
Async XLA Ops:
  0.0 5.6 %copy-start.2 = (bf16[1,128,512]{2,1,0:T(8,128)(2,1)S(1)}, bf16[1,128,512]{2,1,0:T(8,128)(2,1)}, u32[]{:S(2)}) copy-start(bf16[1,128,512]{2,1,0:T(8,128)(2,1)} %param.6) | copy-start | bytes 393220
  0.0 4.2 %copy-start.1 = (bf16[1,128,512]{2,1,0:T(8,128)(2,1)S(1)}, bf16[1,128,512]{2,1,0:T(8,128)(2,1)}, u32[]{:S(2)}) copy-start(bf16[1,128,512]{2,1,0:T(8,128)(2,1)} %param.7) | copy-start | bytes 393220
  0.0 4.3 %copy-start.4 = (s32[128]{0:T(128)S(1)}, s32[128]{0:T(128)}, u32[]{:S(2)}) copy-start(s32[128]{0:T(128)} %param.8) | copy-start | bytes 1540
  0.0 5.6 %copy-start = (bf16[1,128,4096]{2,1,0:T(8,128)(2,1)S(1)}, bf16[1,128,4096]{2,1,0:T(8,128)(2,1)}, u32[]{:S(2)}) copy-start(bf16[1,128,4096]{2,1,0:T(8,128)(2,1)} %param.5) | copy-start | bytes 3145732
  0.0 16.4 %copy-start.3 = (s32[1024]{0:T(1024)S(1)}, s32[1024]{0:T(1024)}, u32[]{:S(2)}) copy-start(s32[1024]{0:T(1024)} %param.9) | copy-start | bytes 12292
  0.0 6.4 %collective-permute-start = (bf16[128,512]{1,0:T(8,128)(2,1)}, bf16[128,512]{1,0:T(8,128)(2,1)S(1)}, u32[]{:S(2)}, u32[]{:S(2)}) collective-permute-start(bf16[128,512]{1,0:T(8,128)(2,1)} %bitcast.16), channel_id=1, source_target_pairs={{0,10},{2,12},{4,14},{6,15},{7,13},{5,11},{3,9},{1,8},{8,18},{10,2... | collective-permute-start | bytes 393224 | tf_op jit(solution)/shard_map/ppermute | solution.py:202
  2.5 7.8 %collective-permute-start.4 = (bf16[128,512]{1,0:T(8,128)(2,1)}, bf16[128,512]{1,0:T(8,128)(2,1)S(1)}, u32[]{:S(2)}, u32[]{:S(2)}) collective-permute-start(bf16[128,512]{1,0:T(8,128)(2,1)} %bitcast.17), channel_id=1, source_target_pairs={{0,9},{2,8},{4,10},{6,12},{7,14},{5,15},{3,13},{1,11},{8,17},{10,1... | collective-permute-start | bytes 393224 | tf_op jit(solution)/shard_map/ppermute | solution.py:202
  4.3 6.8 %collective-permute-start.9 = (bf16[528,128]{1,0:T(8,128)(2,1)S(1)}, bf16[528,128]{1,0:T(8,128)(2,1)S(1)}, u32[]{:S(2)}, u32[]{:S(2)}) collective-permute-start(bf16[528,128]{1,0:T(8,128)(2,1)S(1)} %constant_dynamic-update-slice_fusion), channel_id=1, source_target_pairs={{0,10},{2,12},{4,14},{6,15},{7,13},{5,11},{3,9},{1,8},{8,18},{10,2... | collective-permute-start | bytes 405512 | tf_op jit(solution)/shard_map/ppermute | solution.py:202
  5.5 7.7 %collective-permute-start.10 = (bf16[528,128]{1,0:T(8,128)(2,1)S(1)}, bf16[528,128]{1,0:T(8,128)(2,1)S(1)}, u32[]{:S(2)}, u32[]{:S(2)}) collective-permute-start(bf16[528,128]{1,0:T(8,128)(2,1)S(1)} %constant_dynamic-update-slice_fusion), channel_id=1, source_target_pairs={{0,9},{2,8},{4,10},{6,12},{7,14},{5,15},{3,13},{1,11},{8,17},{10,1... | collective-permute-start | bytes 405512 | tf_op jit(solution)/shard_map/ppermute | solution.py:202
  5.7 21.4 %collective-permute-start.8 = (bf16[128,5120]{1,0:T(8,128)(2,1)S(1)}, bf16[128,5120]{1,0:T(8,128)(2,1)S(1)}, u32[]{:S(2)}, u32[]{:S(2)}) collective-permute-start(bf16[128,5120]{1,0:T(8,128)(2,1)S(1)} %pad_maximum_fusion), channel_id=1, source_target_pairs={{0,8},{2,10},{4,12},{6,14},{7,15},{5,13},{3,11},{1,9},{8,16},{10,1... | collective-permute-start | bytes 3932168 | tf_op jit(solution)/shard_map/ppermute | solution.py:202
  6.4 7.7 %collective-permute-start.1 = (bf16[128,512]{1,0:T(8,128)(2,1)S(1)}, bf16[128,512]{1,0:T(8,128)(2,1)S(1)}, u32[]{:S(2)}, u32[]{:S(2)}) collective-permute-start(bf16[128,512]{1,0:T(8,128)(2,1)S(1)} %collective-permute-done.refs_0_), channel_id=1, source_target_pairs={{0,2},{2,4},{4,6},{6,7},{7,5},{5,3},{3,1},{1,0},{8,10},{10,12},{12... | collective-permute-start | bytes 393224 | tf_op jit(solution)/shard_map/ppermute | solution.py:202
  10.3 6.0 %collective-permute-start.5 = (bf16[128,512]{1,0:T(8,128)(2,1)S(1)}, bf16[128,512]{1,0:T(8,128)(2,1)S(1)}, u32[]{:S(2)}, u32[]{:S(2)}) collective-permute-start(bf16[128,512]{1,0:T(8,128)(2,1)S(1)} %collective-permute-done.4.refs_1_), channel_id=1, source_target_pairs={{0,1},{2,0},{4,2},{6,4},{7,6},{5,7},{3,5},{1,3},{8,9},{10,8},{12,1... | collective-permute-start | bytes 393224 | tf_op jit(solution)/shard_map/ppermute | solution.py:202
  11.1 6.1 %collective-permute-start.11 = (bf16[528,128]{1,0:T(8,128)(2,1)S(1)}, bf16[528,128]{1,0:T(8,128)(2,1)S(1)}, u32[]{:S(2)}, u32[]{:S(2)}) collective-permute-start(bf16[528,128]{1,0:T(8,128)(2,1)S(1)} %collective-permute-done.9.refs_8_), channel_id=1, source_target_pairs={{0,2},{2,4},{4,6},{6,7},{7,5},{5,3},{3,1},{1,0},{8,10},{10,12},{12... | collective-permute-start | bytes 405512 | tf_op jit(solution)/shard_map/ppermute | solution.py:202
  13.2 6.5 %collective-permute-start.12 = (bf16[528,128]{1,0:T(8,128)(2,1)S(1)}, bf16[528,128]{1,0:T(8,128)(2,1)S(1)}, u32[]{:S(2)}, u32[]{:S(2)}) collective-permute-start(bf16[528,128]{1,0:T(8,128)(2,1)S(1)} %collective-permute-done.10.refs_9_), channel_id=1, source_target_pairs={{0,1},{2,0},{4,2},{6,4},{7,6},{5,7},{3,5},{1,3},{8,9},{10,8},{12,1... | collective-permute-start | bytes 405512 | tf_op jit(solution)/shard_map/ppermute | solution.py:202
  14.1 6.1 %collective-permute-start.2 = (bf16[128,512]{1,0:T(8,128)(2,1)S(1)}, bf16[128,512]{1,0:T(8,128)(2,1)S(1)}, u32[]{:S(2)}, u32[]{:S(2)}) collective-permute-start(bf16[128,512]{1,0:T(8,128)(2,1)S(1)} %collective-permute-done.1.refs_2_), channel_id=1, source_target_pairs={{0,2},{2,4},{4,6},{6,7},{7,5},{5,3},{3,1},{1,0},{8,10},{10,12},{12... | collective-permute-start | bytes 393224 | tf_op jit(solution)/shard_map/ppermute | solution.py:202
  16.3 6.3 %collective-permute-start.6 = (bf16[128,512]{1,0:T(8,128)(2,1)S(1)}, bf16[128,512]{1,0:T(8,128)(2,1)S(1)}, u32[]{:S(2)}, u32[]{:S(2)}) collective-permute-start(bf16[128,512]{1,0:T(8,128)(2,1)S(1)} %collective-permute-done.5.refs_3_), channel_id=1, source_target_pairs={{0,1},{2,0},{4,2},{6,4},{7,6},{5,7},{3,5},{1,3},{8,9},{10,8},{12,1... | collective-permute-start | bytes 393224 | tf_op jit(solution)/shard_map/ppermute | solution.py:202
  17.2 5.7 %collective-permute-start.13 = (bf16[528,128]{1,0:T(8,128)(2,1)S(1)}, bf16[528,128]{1,0:T(8,128)(2,1)S(1)}, u32[]{:S(2)}, u32[]{:S(2)}) collective-permute-start(bf16[528,128]{1,0:T(8,128)(2,1)S(1)} %collective-permute-done.11.refs_10_), channel_id=1, source_target_pairs={{0,2},{2,4},{4,6},{6,7},{7,5},{5,3},{3,1},{1,0},{8,10},{10,12},{12... | collective-permute-start | bytes 405512 | tf_op jit(solution)/shard_map/ppermute | solution.py:202
  19.7 5.4 %collective-permute-start.14 = (bf16[528,128]{1,0:T(8,128)(2,1)S(1)}, bf16[528,128]{1,0:T(8,128)(2,1)S(1)}, u32[]{:S(2)}, u32[]{:S(2)}) collective-permute-start(bf16[528,128]{1,0:T(8,128)(2,1)S(1)} %collective-permute-done.12.refs_11_), channel_id=1, source_target_pairs={{0,1},{2,0},{4,2},{6,4},{7,6},{5,7},{3,5},{1,3},{8,9},{10,8},{12,1... | collective-permute-start | bytes 405512 | tf_op jit(solution)/shard_map/ppermute | solution.py:202
  20.2 5.3 %collective-permute-start.3 = (bf16[64,512]{1,0:T(8,128)(2,1)S(1)}, bf16[64,512]{1,0:T(8,128)(2,1)S(1)}, u32[]{:S(2)}, u32[]{:S(2)}) collective-permute-start(bf16[64,512]{1,0:T(8,128)(2,1)S(1)} %slice.32), channel_id=1, source_target_pairs={{0,2},{2,4},{4,6},{6,7},{7,5},{5,3},{3,1},{1,0},{8,10},{10,12},{12... | collective-permute-start | bytes 196616 | tf_op jit(solution)/shard_map/ppermute | solution.py:202
  22.7 4.4 %collective-permute-start.7 = (bf16[64,512]{1,0:T(8,128)(2,1)S(1)}, bf16[64,512]{1,0:T(8,128)(2,1)S(1)}, u32[]{:S(2)}, u32[]{:S(2)}) collective-permute-start(bf16[64,512]{1,0:T(8,128)(2,1)S(1)} %slice.33), channel_id=1, source_target_pairs={{0,1},{2,0},{4,2},{6,4},{7,6},{5,7},{3,5},{1,3},{8,9},{10,8},{12,1... | collective-permute-start | bytes 196616 | tf_op jit(solution)/shard_map/ppermute | solution.py:202
  22.9 5.6 %collective-permute-start.15 = (bf16[256,128]{1,0:T(8,128)(2,1)S(1)}, bf16[256,128]{1,0:T(8,128)(2,1)S(1)}, u32[]{:S(2)}, u32[]{:S(2)}) collective-permute-start(bf16[256,128]{1,0:T(8,128)(2,1)S(1)} %slice.34), channel_id=1, source_target_pairs={{0,2},{2,4},{4,6},{6,7},{7,5},{5,3},{3,1},{1,0},{8,10},{10,12},{12... | collective-permute-start | bytes 196616 | tf_op jit(solution)/shard_map/ppermute | solution.py:202
  25.1 4.3 %collective-permute-start.16 = (bf16[256,128]{1,0:T(8,128)(2,1)S(1)}, bf16[256,128]{1,0:T(8,128)(2,1)S(1)}, u32[]{:S(2)}, u32[]{:S(2)}) collective-permute-start(bf16[256,128]{1,0:T(8,128)(2,1)S(1)} %slice.35), channel_id=1, source_target_pairs={{0,1},{2,0},{4,2},{6,4},{7,6},{5,7},{3,5},{1,3},{8,9},{10,8},{12,1... | collective-permute-start | bytes 196616 | tf_op jit(solution)/shard_map/ppermute | solution.py:202

commit v15 on v14

--- a/solution.py
+++ b/solution.py
@@ -59,8 +59,11 @@
     for (first, second), ref in zip(numbers[1:], block_refs):
         sorted_ref[first] = ref[:RUN, :]
         sorted_ref[second] = ref[RUN:, :]
-    for number, ref in zip(numbers[-1], last_refs):
-        sorted_ref[number] = ref[...]
+    cut = last_refs[0].shape[0] - RUN
+    first, second = numbers[-1]
+    sorted_ref[first] = last_refs[0][:RUN, :]
+    sorted_ref[second, :cut] = last_refs[0][RUN:, :]
+    sorted_ref[second, cut:] = last_refs[1][...]
 
 
 def sort_values(numbers, own_ref, block_refs, sorted_ref):
@@ -142,12 +145,13 @@
     def half_values(half, start, count):
         ones = jnp.ones((count * RUN, HEAD_SIZE), jnp.bfloat16)
         for kv in range(KEY_VALUE_HEADS):
-            last_ref = last_refs[kv * 2 // KEY_VALUE_HEADS]
+            which, place = divmod(kv, KEY_VALUE_HEADS * 3 // 4)
+            last_ref = last_refs[which]
             parts = []
             for i in range(count):
                 part = sorted_ref[kv, start + i]
                 for last_half, number in enumerate(last_runs):
-                    row = kv % (KEY_VALUE_HEADS // 2) * TOK_DEV + last_half * RUN
+                    row = place * TOK_DEV + last_half * RUN
                     part = jnp.where(start + i == number, last_ref[row : row + RUN, :], part)
                 parts.append(part)
             summed = jnp.dot(
@@ -209,7 +213,8 @@
                 ahead, _ = lax.optimization_barrier((ahead, early))
             ahead, back = shift(ahead, 0, 1), shift(back, 0, -1)
             held.extend([ahead, back])
-        return held + [shift(ahead[: rows // 2], 0, 1), shift(back[rows // 2 : rows], 0, -1)]
+        cut = rows * 3 // 4
+        return held + [shift(ahead[:cut], 0, 1), shift(back[cut:rows], 0, -1)]
 
     own = shift(jnp.concatenate([queries[0], keys[0], values[0]], axis=1), 1, 0)
     vmem = pl.BlockSpec(memory_space=pltpu.VMEM)

time: 31.3 us -> 31 us (level)
  waiting for transfers between devices: 7.17 us -> 6.84 us
    ppermute x17, waiting for transfers between devices: 7.17 us -> 6.84 us  [shift(): return lax.ppermute(block, ('section', 'ctx'), pairs)]
  transfers between devices with their start and end apart: 17 -> 17, of which waited for: 12 -> 11; matrix products, arithmetic and copies ran while one was open for 1% -> 1% of each run, Pallas kernels for 6% -> 6%
where the time goes in v15:
time: 31 us; the launch traced here: 30.8 us
  starting transfers between devices  20.2 us (65%)
  waiting for transfers between devices  6.84 us (22%)
  Pallas kernels  3.5 us (11%)
    ppermute x17, starting transfers between devices, shift(): return lax.ppermute(block, ('section', 'ctx'), pairs)  20.2 us
    ppermute x17, waiting for transfers between devices, shift(): return lax.ppermute(block, ('section', 'ctx'), pairs)  6.84 us
    pallas_call x1, Pallas kernels, per_device(): pl.pallas_call(functools.partial(values_kernel, runs), out_shape=jax.Shap...  1.77 us
    pallas_call x1, Pallas kernels, per_device(): pl.pallas_call(functools.partial(weights_kernel, runs), out_shape=(jax.Sh...  1.46 us
  transfers between devices with their start and end apart: 17, of which 11 were waited for; matrix products, arithmetic and copies ran while one was open for 1% of the time, Pallas kernels for 6%

profile of v15, /device:TPU:0, one launch (start us, length us, event | category | flops | bytes accessed | tf_op | source)
XLA Modules:
  0.0 30.8 jit_solution(14280576967199386199)
XLA Ops:
  0.0 0.0 copy-start.2
  0.0 0.0 copy-start.1
  0.0 0.0 copy-start.4
  0.0 0.0 copy-start
  0.0 0.0 copy-start.3
  0.0 2.5 %collective-permute-start = (bf16[128,512]{1,0:T(8,128)(2,1)}, bf16[128,512]{1,0:T(8,128)(2,1)S(1)}, u32[]{:S(2)}, u32[]{:S(2)}) collective-permute-start(bf16[128,512]{1,0:T(8,128)(2,1)} %bitcast.16), channel_id=1, source_target_pairs={{0,10},{2,12},{4,14},{6,15},{7,13},{5,11},{3,9},{1,8},{8,18},{10,2... | collective-permute-start | bytes 393224 | tf_op jit(solution)/shard_map/ppermute | solution.py:206
  2.5 1.7 %collective-permute-start.4 = (bf16[128,512]{1,0:T(8,128)(2,1)}, bf16[128,512]{1,0:T(8,128)(2,1)S(1)}, u32[]{:S(2)}, u32[]{:S(2)}) collective-permute-start(bf16[128,512]{1,0:T(8,128)(2,1)} %bitcast.17), channel_id=1, source_target_pairs={{0,9},{2,8},{4,10},{6,12},{7,14},{5,15},{3,13},{1,11},{8,17},{10,1... | collective-permute-start | bytes 393224 | tf_op jit(solution)/shard_map/ppermute | solution.py:206
  4.2 0.0 copy-done.1
  4.3 0.0 copy-done.4
  4.3 1.2 %collective-permute-start.9 = (bf16[528,128]{1,0:T(8,128)(2,1)S(1)}, bf16[528,128]{1,0:T(8,128)(2,1)S(1)}, u32[]{:S(2)}, u32[]{:S(2)}) collective-permute-start(bf16[528,128]{1,0:T(8,128)(2,1)S(1)} %constant_dynamic-update-slice_fusion), channel_id=1, source_target_pairs={{0,10},{2,12},{4,14},{6,15},{7,13},{5,11},{3,9},{1,8},{8,18},{10,2... | collective-permute-start | bytes 405512 | tf_op jit(solution)/shard_map/ppermute | solution.py:206
  5.5 0.1 collective-permute-start.10
  5.6 0.0 copy-done.2
  5.6 0.0 copy-done
  5.6 0.1 pad_maximum_fusion
  5.7 0.5 %collective-permute-start.8 = (bf16[128,5120]{1,0:T(8,128)(2,1)S(1)}, bf16[128,5120]{1,0:T(8,128)(2,1)S(1)}, u32[]{:S(2)}, u32[]{:S(2)}) collective-permute-start(bf16[128,5120]{1,0:T(8,128)(2,1)S(1)} %pad_maximum_fusion), channel_id=1, source_target_pairs={{0,8},{2,10},{4,12},{6,14},{7,15},{5,13},{3,11},{1,9},{8,16},{10,1... | collective-permute-start | bytes 3932168 | tf_op jit(solution)/shard_map/ppermute | solution.py:206
  6.2 0.2 collective-permute-done.refs_0_
  6.4 3.9 %collective-permute-start.1 = (bf16[128,512]{1,0:T(8,128)(2,1)S(1)}, bf16[128,512]{1,0:T(8,128)(2,1)S(1)}, u32[]{:S(2)}, u32[]{:S(2)}) collective-permute-start(bf16[128,512]{1,0:T(8,128)(2,1)S(1)} %collective-permute-done.refs_0_), channel_id=1, source_target_pairs={{0,2},{2,4},{4,6},{6,7},{7,5},{5,3},{3,1},{1,0},{8,10},{10,12},{12... | collective-permute-start | bytes 393224 | tf_op jit(solution)/shard_map/ppermute | solution.py:206
  10.3 0.0 collective-permute-done.4.refs_1_
  10.3 0.0 collective-permute-start.5
  10.3 0.8 %collective-permute-done.9.refs_8_ = bf16[528,128]{1,0:T(8,128)(2,1)S(1)} collective-permute-done((bf16[528,128]{1,0:T(8,128)(2,1)S(1)}, bf16[528,128]{1,0:T(8,128)(2,1)S(1)}, u32[]{:S(2)}, u32[]{:S(2)}) %collective-permute-start.9) | collective-permute-done | bytes 135200 | tf_op jit(solution)/shard_map/ppermute | solution.py:206
  11.1 2.1 %collective-permute-start.11 = (bf16[528,128]{1,0:T(8,128)(2,1)S(1)}, bf16[528,128]{1,0:T(8,128)(2,1)S(1)}, u32[]{:S(2)}, u32[]{:S(2)}) collective-permute-start(bf16[528,128]{1,0:T(8,128)(2,1)S(1)} %collective-permute-done.9.refs_8_), channel_id=1, source_target_pairs={{0,2},{2,4},{4,6},{6,7},{7,5},{5,3},{3,1},{1,0},{8,10},{10,12},{12... | collective-permute-start | bytes 405512 | tf_op jit(solution)/shard_map/ppermute | solution.py:206
  13.2 0.0 collective-permute-done.10.refs_9_
  13.2 0.0 collective-permute-start.12
  13.2 0.9 %collective-permute-done.1.refs_2_ = bf16[128,512]{1,0:T(8,128)(2,1)S(1)} collective-permute-done((bf16[128,512]{1,0:T(8,128)(2,1)S(1)}, bf16[128,512]{1,0:T(8,128)(2,1)S(1)}, u32[]{:S(2)}, u32[]{:S(2)}) %collective-permute-start.1) | collective-permute-done | bytes 131104 | tf_op jit(solution)/shard_map/ppermute | solution.py:206
  14.1 1.7 %collective-permute-start.2 = (bf16[128,512]{1,0:T(8,128)(2,1)S(1)}, bf16[128,512]{1,0:T(8,128)(2,1)S(1)}, u32[]{:S(2)}, u32[]{:S(2)}) collective-permute-start(bf16[128,512]{1,0:T(8,128)(2,1)S(1)} %collective-permute-done.1.refs_2_), channel_id=1, source_target_pairs={{0,2},{2,4},{4,6},{6,7},{7,5},{5,3},{3,1},{1,0},{8,10},{10,12},{12... | collective-permute-start | bytes 393224 | tf_op jit(solution)/shard_map/ppermute | solution.py:206
  15.8 0.5 %collective-permute-done.5.refs_3_ = bf16[128,512]{1,0:T(8,128)(2,1)S(1)} collective-permute-done((bf16[128,512]{1,0:T(8,128)(2,1)S(1)}, bf16[128,512]{1,0:T(8,128)(2,1)S(1)}, u32[]{:S(2)}, u32[]{:S(2)}) %collective-permute-start.5) | collective-permute-done | bytes 131104 | tf_op jit(solution)/shard_map/ppermute | solution.py:206
  16.3 0.1 collective-permute-start.6
  16.5 0.0 copy-done.3
  16.5 0.3 shard_map.55
  16.7 0.5 %collective-permute-done.11.refs_10_ = bf16[528,128]{1,0:T(8,128)(2,1)S(1)} collective-permute-done((bf16[528,128]{1,0:T(8,128)(2,1)S(1)}, bf16[528,128]{1,0:T(8,128)(2,1)S(1)}, u32[]{:S(2)}, u32[]{:S(2)}) %collective-permute-start.11) | collective-permute-done | bytes 135200 | tf_op jit(solution)/shard_map/ppermute | solution.py:206
  17.2 2.2 %collective-permute-start.13 = (bf16[528,128]{1,0:T(8,128)(2,1)S(1)}, bf16[528,128]{1,0:T(8,128)(2,1)S(1)}, u32[]{:S(2)}, u32[]{:S(2)}) collective-permute-start(bf16[528,128]{1,0:T(8,128)(2,1)S(1)} %collective-permute-done.11.refs_10_), channel_id=1, source_target_pairs={{0,2},{2,4},{4,6},{6,7},{7,5},{5,3},{3,1},{1,0},{8,10},{10,12},{12... | collective-permute-start | bytes 405512 | tf_op jit(solution)/shard_map/ppermute | solution.py:206
  19.4 0.3 collective-permute-done.12.refs_11_
  19.7 0.0 collective-permute-start.14
  19.7 0.5 %collective-permute-done.2.refs_4_ = bf16[128,512]{1,0:T(8,128)(2,1)S(1)} collective-permute-done((bf16[128,512]{1,0:T(8,128)(2,1)S(1)}, bf16[128,512]{1,0:T(8,128)(2,1)S(1)}, u32[]{:S(2)}, u32[]{:S(2)}) %collective-permute-start.2) | collective-permute-done | bytes 131104 | tf_op jit(solution)/shard_map/ppermute | solution.py:206
  20.2 2.1 %collective-permute-start.3 = (bf16[96,512]{1,0:T(8,128)(2,1)S(1)}, bf16[96,512]{1,0:T(8,128)(2,1)S(1)}, u32[]{:S(2)}, u32[]{:S(2)}) collective-permute-start(bf16[96,512]{1,0:T(8,128)(2,1)S(1)} %slice.32), channel_id=1, source_target_pairs={{0,2},{2,4},{4,6},{6,7},{7,5},{5,3},{3,1},{1,0},{8,10},{10,12},{12... | collective-permute-start | bytes 294920 | tf_op jit(solution)/shard_map/ppermute | solution.py:206
  22.3 0.3 %collective-permute-done.6.refs_5_ = bf16[128,512]{1,0:T(8,128)(2,1)S(1)} collective-permute-done((bf16[128,512]{1,0:T(8,128)(2,1)S(1)}, bf16[128,512]{1,0:T(8,128)(2,1)S(1)}, u32[]{:S(2)}, u32[]{:S(2)}) %collective-permute-start.6) | collective-permute-done | bytes 131104 | tf_op jit(solution)/shard_map/ppermute | solution.py:206
  22.6 0.0 collective-permute-start.7
  22.7 0.6 %collective-permute-done.13.refs_12_ = bf16[528,128]{1,0:T(8,128)(2,1)S(1)} collective-permute-done((bf16[528,128]{1,0:T(8,128)(2,1)S(1)}, bf16[528,128]{1,0:T(8,128)(2,1)S(1)}, u32[]{:S(2)}, u32[]{:S(2)}) %collective-permute-start.13) | collective-permute-done | bytes 135200 | tf_op jit(solution)/shard_map/ppermute | solution.py:206
  23.3 1.8 %collective-permute-start.15 = (bf16[384,128]{1,0:T(8,128)(2,1)S(1)}, bf16[384,128]{1,0:T(8,128)(2,1)S(1)}, u32[]{:S(2)}, u32[]{:S(2)}) collective-permute-start(bf16[384,128]{1,0:T(8,128)(2,1)S(1)} %slice.34), channel_id=1, source_target_pairs={{0,2},{2,4},{4,6},{6,7},{7,5},{5,3},{3,1},{1,0},{8,10},{10,12},{12... | collective-permute-start | bytes 294920 | tf_op jit(solution)/shard_map/ppermute | solution.py:206
  25.1 0.0 collective-permute-done.14.refs_13_
  25.1 0.2 collective-permute-start.16
  25.4 1.2 %collective-permute-done.7.refs_1_.refs_7_ = bf16[32,512]{1,0:T(8,128)(2,1)S(1)} collective-permute-done((bf16[32,512]{1,0:T(8,128)(2,1)S(1)}, bf16[32,512]{1,0:T(8,128)(2,1)S(1)}, u32[]{:S(2)}, u32[]{:S(2)}) %collective-permute-start.7) | collective-permute-done | bytes 32800 | tf_op jit(solution)/shard_map/ppermute | solution.py:206
  26.6 0.0 collective-permute-done.3.refs_0_.refs_6_
  26.6 0.0 collective-permute-done.8.own_ref
  26.6 1.5 %shard_map.58 = (bf16[8,512,320]{2,1,0:T(8,128)(2,1)S(1)}, bf16[4,16,64,128]{3,2,1,0:T(8,128)(2,1)S(1)}, f32[8,128]{1,0:T(8,128)S(1)}) custom-call(f32[8,128]{1,0:T(8,128)S(1)} %get-tuple-element.11.plan_ref, f32[2,64,320]{2,1,0:T(8,128)S(1)} %get-tuple-element.12.bias_ref, f32[8,128]{1,0:T(8,128)S(1)} %shard_map.56.mark_ref, ...), custom_call_target="tpu_custom_call" | custom-call | flops 67108864 | bytes 1048576 | tf_op jit(solution)/shard_map/pallas_call | solution.py:254
  28.0 1.0 %collective-permute-done.16.refs_1_ = bf16[128,128]{1,0:T(8,128)(2,1)S(1)} collective-permute-done((bf16[128,128]{1,0:T(8,128)(2,1)S(1)}, bf16[128,128]{1,0:T(8,128)(2,1)S(1)}, u32[]{:S(2)}, u32[]{:S(2)}) %collective-permute-start.16) | collective-permute-done | bytes 32800 | tf_op jit(solution)/shard_map/ppermute | solution.py:206
  29.1 0.0 collective-permute-done.15.refs_0_
  29.1 1.8 %shard_map.59 = bf16[128,4096]{1,0:T(8,128)(2,1)} custom-call(f32[8,128]{1,0:T(8,128)S(1)} %get-tuple-element.11.plan_ref, f32[8,128]{1,0:T(8,128)S(1)} %get-tuple-element.14.last_run_ref, bf16[8,512,320]{2,1,0:T(8,128)(2,1)S(1)} %get-tuple-element.15.weights_ref, bf16[4,16,64,128]{3,2,1,0:T(8,128)(2,1)S(1)} %get-tuple-element.16.sorted_ref, ...), custom_call_target="tpu_custom_call" | custom-call | flops 67108864 | bytes 1048576 | tf_op jit(solution)/shard_map/pallas_call | solution.py:267
  (13 shorter events, 0.1 us)
Async XLA Ops:
  0.0 5.6 %copy-start.2 = (bf16[1,128,512]{2,1,0:T(8,128)(2,1)S(1)}, bf16[1,128,512]{2,1,0:T(8,128)(2,1)}, u32[]{:S(2)}) copy-start(bf16[1,128,512]{2,1,0:T(8,128)(2,1)} %param.6) | copy-start | bytes 393220
  0.0 4.2 %copy-start.1 = (bf16[1,128,512]{2,1,0:T(8,128)(2,1)S(1)}, bf16[1,128,512]{2,1,0:T(8,128)(2,1)}, u32[]{:S(2)}) copy-start(bf16[1,128,512]{2,1,0:T(8,128)(2,1)} %param.7) | copy-start | bytes 393220
  0.0 4.3 %copy-start.4 = (s32[128]{0:T(128)S(1)}, s32[128]{0:T(128)}, u32[]{:S(2)}) copy-start(s32[128]{0:T(128)} %param.8) | copy-start | bytes 1540
  0.0 5.6 %copy-start = (bf16[1,128,4096]{2,1,0:T(8,128)(2,1)S(1)}, bf16[1,128,4096]{2,1,0:T(8,128)(2,1)}, u32[]{:S(2)}) copy-start(bf16[1,128,4096]{2,1,0:T(8,128)(2,1)} %param.5) | copy-start | bytes 3145732
  0.0 16.4 %copy-start.3 = (s32[1024]{0:T(1024)S(1)}, s32[1024]{0:T(1024)}, u32[]{:S(2)}) copy-start(s32[1024]{0:T(1024)} %param.9) | copy-start | bytes 12292
  0.0 6.4 %collective-permute-start = (bf16[128,512]{1,0:T(8,128)(2,1)}, bf16[128,512]{1,0:T(8,128)(2,1)S(1)}, u32[]{:S(2)}, u32[]{:S(2)}) collective-permute-start(bf16[128,512]{1,0:T(8,128)(2,1)} %bitcast.16), channel_id=1, source_target_pairs={{0,10},{2,12},{4,14},{6,15},{7,13},{5,11},{3,9},{1,8},{8,18},{10,2... | collective-permute-start | bytes 393224 | tf_op jit(solution)/shard_map/ppermute | solution.py:206
  2.5 7.8 %collective-permute-start.4 = (bf16[128,512]{1,0:T(8,128)(2,1)}, bf16[128,512]{1,0:T(8,128)(2,1)S(1)}, u32[]{:S(2)}, u32[]{:S(2)}) collective-permute-start(bf16[128,512]{1,0:T(8,128)(2,1)} %bitcast.17), channel_id=1, source_target_pairs={{0,9},{2,8},{4,10},{6,12},{7,14},{5,15},{3,13},{1,11},{8,17},{10,1... | collective-permute-start | bytes 393224 | tf_op jit(solution)/shard_map/ppermute | solution.py:206
  4.3 6.8 %collective-permute-start.9 = (bf16[528,128]{1,0:T(8,128)(2,1)S(1)}, bf16[528,128]{1,0:T(8,128)(2,1)S(1)}, u32[]{:S(2)}, u32[]{:S(2)}) collective-permute-start(bf16[528,128]{1,0:T(8,128)(2,1)S(1)} %constant_dynamic-update-slice_fusion), channel_id=1, source_target_pairs={{0,10},{2,12},{4,14},{6,15},{7,13},{5,11},{3,9},{1,8},{8,18},{10,2... | collective-permute-start | bytes 405512 | tf_op jit(solution)/shard_map/ppermute | solution.py:206
  5.5 7.7 %collective-permute-start.10 = (bf16[528,128]{1,0:T(8,128)(2,1)S(1)}, bf16[528,128]{1,0:T(8,128)(2,1)S(1)}, u32[]{:S(2)}, u32[]{:S(2)}) collective-permute-start(bf16[528,128]{1,0:T(8,128)(2,1)S(1)} %constant_dynamic-update-slice_fusion), channel_id=1, source_target_pairs={{0,9},{2,8},{4,10},{6,12},{7,14},{5,15},{3,13},{1,11},{8,17},{10,1... | collective-permute-start | bytes 405512 | tf_op jit(solution)/shard_map/ppermute | solution.py:206
  5.7 20.9 %collective-permute-start.8 = (bf16[128,5120]{1,0:T(8,128)(2,1)S(1)}, bf16[128,5120]{1,0:T(8,128)(2,1)S(1)}, u32[]{:S(2)}, u32[]{:S(2)}) collective-permute-start(bf16[128,5120]{1,0:T(8,128)(2,1)S(1)} %pad_maximum_fusion), channel_id=1, source_target_pairs={{0,8},{2,10},{4,12},{6,14},{7,15},{5,13},{3,11},{1,9},{8,16},{10,1... | collective-permute-start | bytes 3932168 | tf_op jit(solution)/shard_map/ppermute | solution.py:206
  6.4 7.7 %collective-permute-start.1 = (bf16[128,512]{1,0:T(8,128)(2,1)S(1)}, bf16[128,512]{1,0:T(8,128)(2,1)S(1)}, u32[]{:S(2)}, u32[]{:S(2)}) collective-permute-start(bf16[128,512]{1,0:T(8,128)(2,1)S(1)} %collective-permute-done.refs_0_), channel_id=1, source_target_pairs={{0,2},{2,4},{4,6},{6,7},{7,5},{5,3},{3,1},{1,0},{8,10},{10,12},{12... | collective-permute-start | bytes 393224 | tf_op jit(solution)/shard_map/ppermute | solution.py:206
  10.3 6.0 %collective-permute-start.5 = (bf16[128,512]{1,0:T(8,128)(2,1)S(1)}, bf16[128,512]{1,0:T(8,128)(2,1)S(1)}, u32[]{:S(2)}, u32[]{:S(2)}) collective-permute-start(bf16[128,512]{1,0:T(8,128)(2,1)S(1)} %collective-permute-done.4.refs_1_), channel_id=1, source_target_pairs={{0,1},{2,0},{4,2},{6,4},{7,6},{5,7},{3,5},{1,3},{8,9},{10,8},{12,1... | collective-permute-start | bytes 393224 | tf_op jit(solution)/shard_map/ppermute | solution.py:206
  11.1 6.1 %collective-permute-start.11 = (bf16[528,128]{1,0:T(8,128)(2,1)S(1)}, bf16[528,128]{1,0:T(8,128)(2,1)S(1)}, u32[]{:S(2)}, u32[]{:S(2)}) collective-permute-start(bf16[528,128]{1,0:T(8,128)(2,1)S(1)} %collective-permute-done.9.refs_8_), channel_id=1, source_target_pairs={{0,2},{2,4},{4,6},{6,7},{7,5},{5,3},{3,1},{1,0},{8,10},{10,12},{12... | collective-permute-start | bytes 405512 | tf_op jit(solution)/shard_map/ppermute | solution.py:206
  13.2 6.5 %collective-permute-start.12 = (bf16[528,128]{1,0:T(8,128)(2,1)S(1)}, bf16[528,128]{1,0:T(8,128)(2,1)S(1)}, u32[]{:S(2)}, u32[]{:S(2)}) collective-permute-start(bf16[528,128]{1,0:T(8,128)(2,1)S(1)} %collective-permute-done.10.refs_9_), channel_id=1, source_target_pairs={{0,1},{2,0},{4,2},{6,4},{7,6},{5,7},{3,5},{1,3},{8,9},{10,8},{12,1... | collective-permute-start | bytes 405512 | tf_op jit(solution)/shard_map/ppermute | solution.py:206
  14.1 6.1 %collective-permute-start.2 = (bf16[128,512]{1,0:T(8,128)(2,1)S(1)}, bf16[128,512]{1,0:T(8,128)(2,1)S(1)}, u32[]{:S(2)}, u32[]{:S(2)}) collective-permute-start(bf16[128,512]{1,0:T(8,128)(2,1)S(1)} %collective-permute-done.1.refs_2_), channel_id=1, source_target_pairs={{0,2},{2,4},{4,6},{6,7},{7,5},{5,3},{3,1},{1,0},{8,10},{10,12},{12... | collective-permute-start | bytes 393224 | tf_op jit(solution)/shard_map/ppermute | solution.py:206
  16.3 6.3 %collective-permute-start.6 = (bf16[128,512]{1,0:T(8,128)(2,1)S(1)}, bf16[128,512]{1,0:T(8,128)(2,1)S(1)}, u32[]{:S(2)}, u32[]{:S(2)}) collective-permute-start(bf16[128,512]{1,0:T(8,128)(2,1)S(1)} %collective-permute-done.5.refs_3_), channel_id=1, source_target_pairs={{0,1},{2,0},{4,2},{6,4},{7,6},{5,7},{3,5},{1,3},{8,9},{10,8},{12,1... | collective-permute-start | bytes 393224 | tf_op jit(solution)/shard_map/ppermute | solution.py:206
  17.2 6.1 %collective-permute-start.13 = (bf16[528,128]{1,0:T(8,128)(2,1)S(1)}, bf16[528,128]{1,0:T(8,128)(2,1)S(1)}, u32[]{:S(2)}, u32[]{:S(2)}) collective-permute-start(bf16[528,128]{1,0:T(8,128)(2,1)S(1)} %collective-permute-done.11.refs_10_), channel_id=1, source_target_pairs={{0,2},{2,4},{4,6},{6,7},{7,5},{5,3},{3,1},{1,0},{8,10},{10,12},{12... | collective-permute-start | bytes 405512 | tf_op jit(solution)/shard_map/ppermute | solution.py:206
  19.7 5.4 %collective-permute-start.14 = (bf16[528,128]{1,0:T(8,128)(2,1)S(1)}, bf16[528,128]{1,0:T(8,128)(2,1)S(1)}, u32[]{:S(2)}, u32[]{:S(2)}) collective-permute-start(bf16[528,128]{1,0:T(8,128)(2,1)S(1)} %collective-permute-done.12.refs_11_), channel_id=1, source_target_pairs={{0,1},{2,0},{4,2},{6,4},{7,6},{5,7},{3,5},{1,3},{8,9},{10,8},{12,1... | collective-permute-start | bytes 405512 | tf_op jit(solution)/shard_map/ppermute | solution.py:206
  20.2 6.4 %collective-permute-start.3 = (bf16[96,512]{1,0:T(8,128)(2,1)S(1)}, bf16[96,512]{1,0:T(8,128)(2,1)S(1)}, u32[]{:S(2)}, u32[]{:S(2)}) collective-permute-start(bf16[96,512]{1,0:T(8,128)(2,1)S(1)} %slice.32), channel_id=1, source_target_pairs={{0,2},{2,4},{4,6},{6,7},{7,5},{5,3},{3,1},{1,0},{8,10},{10,12},{12... | collective-permute-start | bytes 294920 | tf_op jit(solution)/shard_map/ppermute | solution.py:206
  22.6 3.9 %collective-permute-start.7 = (bf16[32,512]{1,0:T(8,128)(2,1)S(1)}, bf16[32,512]{1,0:T(8,128)(2,1)S(1)}, u32[]{:S(2)}, u32[]{:S(2)}) collective-permute-start(bf16[32,512]{1,0:T(8,128)(2,1)S(1)} %slice.33), channel_id=1, source_target_pairs={{0,1},{2,0},{4,2},{6,4},{7,6},{5,7},{3,5},{1,3},{8,9},{10,8},{12,1... | collective-permute-start | bytes 98312 | tf_op jit(solution)/shard_map/ppermute | solution.py:206
  23.3 5.8 %collective-permute-start.15 = (bf16[384,128]{1,0:T(8,128)(2,1)S(1)}, bf16[384,128]{1,0:T(8,128)(2,1)S(1)}, u32[]{:S(2)}, u32[]{:S(2)}) collective-permute-start(bf16[384,128]{1,0:T(8,128)(2,1)S(1)} %slice.34), channel_id=1, source_target_pairs={{0,2},{2,4},{4,6},{6,7},{7,5},{5,3},{3,1},{1,0},{8,10},{10,12},{12... | collective-permute-start | bytes 294920 | tf_op jit(solution)/shard_map/ppermute | solution.py:206
  25.1 3.9 %collective-permute-start.16 = (bf16[128,128]{1,0:T(8,128)(2,1)S(1)}, bf16[128,128]{1,0:T(8,128)(2,1)S(1)}, u32[]{:S(2)}, u32[]{:S(2)}) collective-permute-start(bf16[128,128]{1,0:T(8,128)(2,1)S(1)} %slice.35), channel_id=1, source_target_pairs={{0,1},{2,0},{4,2},{6,4},{7,6},{5,7},{3,5},{1,3},{8,9},{10,8},{12,1... | collective-permute-start | bytes 98312 | tf_op jit(solution)/shard_map/ppermute | solution.py:206

commit v16 on v15

--- a/solution.py
+++ b/solution.py
@@ -99,8 +99,8 @@
 
 def weights_kernel(runs, plan_ref, bias_ref, mark_ref, own_ref, *refs):
     blocks = runs // 2
-    key_refs, tagged_refs = refs[:blocks], refs[blocks:-4]
-    weights_ref, sorted_ref, last_run_ref, key_buf = refs[-4:]
+    key_refs, tagged_refs = refs[:blocks], refs[blocks:-5]
+    weights_ref, inverse_ref, sorted_ref, last_run_ref, key_buf = refs[-5:]
     numbers = run_numbers(runs, read_number(plan_ref, 0), tagged_refs)
     write_number(last_run_ref, 0, numbers[-1][0])
     plan = [(read_number(plan_ref, 1 + 2 * half), read_number(plan_ref, 2 + 2 * half) > 0) for half in range(2)]
@@ -127,8 +127,12 @@
                 preferred_element_type=jnp.float32,
             )
             row_max = jnp.max(scores, axis=1, keepdims=True)
-            weights = jnp.exp2((scores - row_max) * scale).astype(jnp.bfloat16)
-            weights_ref[half * KEY_VALUE_HEADS + kv, :, :span] = weights
+            weights = jnp.exp2((scores - row_max) * scale)
+            total = jnp.sum(weights, axis=1, keepdims=True)
+            inverse = pl.reciprocal(total, approx=True)
+            inverse = inverse * (2.0 - total * inverse)
+            weights_ref[half * KEY_VALUE_HEADS + kv, :, :span] = weights.astype(jnp.bfloat16)
+            inverse_ref[half * KEY_VALUE_HEADS + kv] = jnp.broadcast_to(inverse, (GROUP * RUN, HEAD_SIZE))
 
     for half in range(2):
         start, far = plan[half]
@@ -136,14 +140,13 @@
         pl.when(jnp.logical_not(far))(functools.partial(half_weights, half, start, runs // 4))
 
 
-def values_kernel(runs, plan_ref, last_run_ref, weights_ref, sorted_ref, *refs):
+def values_kernel(runs, plan_ref, last_run_ref, weights_ref, inverse_ref, sorted_ref, *refs):
     last_refs, (out_ref, result_buf, out_sems) = refs[:2], refs[2:]
     last_run = read_number(last_run_ref, 0)
     last_runs = (last_run, runs - 1 - last_run)
     plan = [(read_number(plan_ref, 1 + 2 * half), read_number(plan_ref, 2 + 2 * half) > 0) for half in range(2)]
 
     def half_values(half, start, count):
-        ones = jnp.ones((count * RUN, HEAD_SIZE), jnp.bfloat16)
         for kv in range(KEY_VALUE_HEADS):
             which, place = divmod(kv, KEY_VALUE_HEADS * 3 // 4)
             last_ref = last_refs[which]
@@ -156,13 +159,10 @@
                 parts.append(part)
             summed = jnp.dot(
                 weights_ref[half * KEY_VALUE_HEADS + kv, :, : count * RUN],
-                jnp.concatenate([jnp.concatenate(parts, axis=0), ones], axis=1),
+                jnp.concatenate(parts, axis=0),
                 preferred_element_type=jnp.float32,
             )
-            total = summed[:, HEAD_SIZE:]
-            inverse = pl.reciprocal(total, approx=True)
-            inverse = inverse * (2.0 - total * inverse)
-            result = (summed[:, :HEAD_SIZE] * inverse).astype(jnp.bfloat16)
+            result = (summed * inverse_ref[half * KEY_VALUE_HEADS + kv]).astype(jnp.bfloat16)
             for i in range(GROUP):
                 h = kv * GROUP + i
                 result_buf[half, :, h * HEAD_SIZE : (h + 1) * HEAD_SIZE] = result[i * RUN : (i + 1) * RUN]
@@ -251,15 +251,16 @@
         compiler_params=pltpu.CompilerParams(vmem_limit_bytes=8 * 1024 * 1024),
         cost_estimate=pl.CostEstimate(flops=65 << 27, bytes_accessed=0, transcendentals=0),
     )(*all_keys[-2:])
-    weights, sorted_values, last_run = pl.pallas_call(
+    weights, inverse, sorted_values, last_run = pl.pallas_call(
         functools.partial(weights_kernel, runs),
         out_shape=(
             jax.ShapeDtypeStruct((2 * KEY_VALUE_HEADS, GROUP * RUN, (runs // 4 + 1) * RUN), jnp.bfloat16),
+            jax.ShapeDtypeStruct((2 * KEY_VALUE_HEADS, GROUP * RUN, HEAD_SIZE), jnp.float32),
             jax.ShapeDtypeStruct((KEY_VALUE_HEADS, runs, RUN, HEAD_SIZE), jnp.bfloat16),
             jax.ShapeDtypeStruct((8, HEAD_SIZE), jnp.float32),
         ),
         in_specs=[vmem] * (4 + len(all_keys) + len(all_values[:-2])),
-        out_specs=(vmem,) * 3,
+        out_specs=(vmem,) * 4,
         scratch_shapes=[pltpu.VMEM((runs, RUN, KV_COLUMNS), jnp.bfloat16)],
         compiler_params=params,
         cost_estimate=pl.CostEstimate(flops=1 << 26, bytes_accessed=1 << 20, transcendentals=0),
@@ -267,7 +268,7 @@
     out = pl.pallas_call(
         functools.partial(values_kernel, runs),
         out_shape=jax.ShapeDtypeStruct((TOK_DEV, QUERY_COLUMNS), jnp.bfloat16),
-        in_specs=[vmem] * 6,
+        in_specs=[vmem] * 7,
         out_specs=pl.BlockSpec(memory_space=pl.ANY),
         scratch_shapes=[
             pltpu.VMEM((2, RUN, QUERY_COLUMNS), jnp.bfloat16),
@@ -275,7 +276,7 @@
         ],
         compiler_params=params,
         cost_estimate=pl.CostEstimate(flops=1 << 26, bytes_accessed=1 << 20, transcendentals=0),
-    )(plan, last_run, weights, sorted_values, *all_values[-2:])
+    )(plan, last_run, weights, inverse, sorted_values, *all_values[-2:])
     return out[None]
 
 

time: 31 us -> 30.9 us (level)
  waiting for transfers between devices: 6.84 us -> 6.35 us
  Pallas kernels: 3.5 us -> 3.98 us
    pallas_call x1, Pallas kernels: 1.46 us -> 1.95 us  [per_device(): pl.pallas_call(functools.partial(weights_kernel, runs), out_shape=(jax.Sh...]
    ppermute x17, waiting for transfers between devices: 6.84 us -> 6.35 us  [shift(): return lax.ppermute(block, ('section', 'ctx'), pairs)]
  transfers between devices with their start and end apart: 17 -> 17, of which waited for: 11 -> 11; matrix products, arithmetic and copies ran while one was open for 1% -> 1% of each run, Pallas kernels for 6% -> 7%
where the time goes in v16:
time: 30.9 us; the launch traced here: 30.8 us
  starting transfers between devices  20.2 us (65%)
  waiting for transfers between devices  6.35 us (21%)
  Pallas kernels  3.98 us (13%)
    ppermute x17, starting transfers between devices, shift(): return lax.ppermute(block, ('section', 'ctx'), pairs)  20.2 us
    ppermute x17, waiting for transfers between devices, shift(): return lax.ppermute(block, ('section', 'ctx'), pairs)  6.35 us
    pallas_call x1, Pallas kernels, per_device(): pl.pallas_call(functools.partial(weights_kernel, runs), out_shape=(jax.Sh...  1.95 us
    pallas_call x1, Pallas kernels, per_device(): pl.pallas_call(functools.partial(values_kernel, runs), out_shape=jax.Shap...  1.75 us
  transfers between devices with their start and end apart: 17, of which 11 were waited for; matrix products, arithmetic and copies ran while one was open for 1% of the time, Pallas kernels for 7%

profile of v16, /device:TPU:0, one launch (start us, length us, event | category | flops | bytes accessed | tf_op | source)
XLA Modules:
  0.0 30.8 jit_solution(2215468347158469019)
XLA Ops:
  0.0 0.0 copy-start.1
  0.0 0.0 copy-start.4
  0.0 0.0 copy-start
  0.0 0.0 copy-start.2
  0.0 2.5 %collective-permute-start = (bf16[128,512]{1,0:T(8,128)(2,1)}, bf16[128,512]{1,0:T(8,128)(2,1)S(1)}, u32[]{:S(2)}, u32[]{:S(2)}) collective-permute-start(bf16[128,512]{1,0:T(8,128)(2,1)} %bitcast.16), channel_id=1, source_target_pairs={{0,10},{2,12},{4,14},{6,15},{7,13},{5,11},{3,9},{1,8},{8,18},{10,2... | collective-permute-start | bytes 393224 | tf_op jit(solution)/shard_map/ppermute | solution.py:206
  2.5 1.7 %collective-permute-start.4 = (bf16[128,512]{1,0:T(8,128)(2,1)}, bf16[128,512]{1,0:T(8,128)(2,1)S(1)}, u32[]{:S(2)}, u32[]{:S(2)}) collective-permute-start(bf16[128,512]{1,0:T(8,128)(2,1)} %bitcast.17), channel_id=1, source_target_pairs={{0,9},{2,8},{4,10},{6,12},{7,14},{5,15},{3,13},{1,11},{8,17},{10,1... | collective-permute-start | bytes 393224 | tf_op jit(solution)/shard_map/ppermute | solution.py:206
  4.2 0.0 copy-done.1
  4.2 0.0 copy-start.3
  4.3 0.0 copy-done.4
  4.3 1.2 %collective-permute-start.9 = (bf16[528,128]{1,0:T(8,128)(2,1)S(1)}, bf16[528,128]{1,0:T(8,128)(2,1)S(1)}, u32[]{:S(2)}, u32[]{:S(2)}) collective-permute-start(bf16[528,128]{1,0:T(8,128)(2,1)S(1)} %constant_dynamic-update-slice_fusion), channel_id=1, source_target_pairs={{0,10},{2,12},{4,14},{6,15},{7,13},{5,11},{3,9},{1,8},{8,18},{10,2... | collective-permute-start | bytes 405512 | tf_op jit(solution)/shard_map/ppermute | solution.py:206
  5.5 0.1 collective-permute-start.10
  5.6 0.0 copy-done
  5.6 0.0 copy-done.2
  5.6 0.1 pad_maximum_fusion
  5.7 0.5 %collective-permute-start.8 = (bf16[128,5120]{1,0:T(8,128)(2,1)S(1)}, bf16[128,5120]{1,0:T(8,128)(2,1)S(1)}, u32[]{:S(2)}, u32[]{:S(2)}) collective-permute-start(bf16[128,5120]{1,0:T(8,128)(2,1)S(1)} %pad_maximum_fusion), channel_id=1, source_target_pairs={{0,8},{2,10},{4,12},{6,14},{7,15},{5,13},{3,11},{1,9},{8,16},{10,1... | collective-permute-start | bytes 3932168 | tf_op jit(solution)/shard_map/ppermute | solution.py:206
  6.2 0.2 collective-permute-done.refs_0_
  6.4 3.9 %collective-permute-start.1 = (bf16[128,512]{1,0:T(8,128)(2,1)S(1)}, bf16[128,512]{1,0:T(8,128)(2,1)S(1)}, u32[]{:S(2)}, u32[]{:S(2)}) collective-permute-start(bf16[128,512]{1,0:T(8,128)(2,1)S(1)} %collective-permute-done.refs_0_), channel_id=1, source_target_pairs={{0,2},{2,4},{4,6},{6,7},{7,5},{5,3},{3,1},{1,0},{8,10},{10,12},{12... | collective-permute-start | bytes 393224 | tf_op jit(solution)/shard_map/ppermute | solution.py:206
  10.3 0.0 collective-permute-done.4.refs_1_
  10.3 0.0 collective-permute-start.5
  10.3 0.8 %collective-permute-done.9.refs_8_ = bf16[528,128]{1,0:T(8,128)(2,1)S(1)} collective-permute-done((bf16[528,128]{1,0:T(8,128)(2,1)S(1)}, bf16[528,128]{1,0:T(8,128)(2,1)S(1)}, u32[]{:S(2)}, u32[]{:S(2)}) %collective-permute-start.9) | collective-permute-done | bytes 135200 | tf_op jit(solution)/shard_map/ppermute | solution.py:206
  11.1 2.1 %collective-permute-start.11 = (bf16[528,128]{1,0:T(8,128)(2,1)S(1)}, bf16[528,128]{1,0:T(8,128)(2,1)S(1)}, u32[]{:S(2)}, u32[]{:S(2)}) collective-permute-start(bf16[528,128]{1,0:T(8,128)(2,1)S(1)} %collective-permute-done.9.refs_8_), channel_id=1, source_target_pairs={{0,2},{2,4},{4,6},{6,7},{7,5},{5,3},{3,1},{1,0},{8,10},{10,12},{12... | collective-permute-start | bytes 405512 | tf_op jit(solution)/shard_map/ppermute | solution.py:206
  13.2 0.0 collective-permute-done.10.refs_9_
  13.2 0.0 collective-permute-start.12
  13.2 0.9 %collective-permute-done.1.refs_2_ = bf16[128,512]{1,0:T(8,128)(2,1)S(1)} collective-permute-done((bf16[128,512]{1,0:T(8,128)(2,1)S(1)}, bf16[128,512]{1,0:T(8,128)(2,1)S(1)}, u32[]{:S(2)}, u32[]{:S(2)}) %collective-permute-start.1) | collective-permute-done | bytes 131104 | tf_op jit(solution)/shard_map/ppermute | solution.py:206
  14.1 1.7 %collective-permute-start.2 = (bf16[128,512]{1,0:T(8,128)(2,1)S(1)}, bf16[128,512]{1,0:T(8,128)(2,1)S(1)}, u32[]{:S(2)}, u32[]{:S(2)}) collective-permute-start(bf16[128,512]{1,0:T(8,128)(2,1)S(1)} %collective-permute-done.1.refs_2_), channel_id=1, source_target_pairs={{0,2},{2,4},{4,6},{6,7},{7,5},{5,3},{3,1},{1,0},{8,10},{10,12},{12... | collective-permute-start | bytes 393224 | tf_op jit(solution)/shard_map/ppermute | solution.py:206
  15.8 0.5 %collective-permute-done.5.refs_3_ = bf16[128,512]{1,0:T(8,128)(2,1)S(1)} collective-permute-done((bf16[128,512]{1,0:T(8,128)(2,1)S(1)}, bf16[128,512]{1,0:T(8,128)(2,1)S(1)}, u32[]{:S(2)}, u32[]{:S(2)}) %collective-permute-start.5) | collective-permute-done | bytes 131104 | tf_op jit(solution)/shard_map/ppermute | solution.py:206
  16.3 0.1 collective-permute-start.6
  16.4 0.0 copy-done.3
  16.5 0.3 shard_map.55
  16.7 0.5 %collective-permute-done.11.refs_10_ = bf16[528,128]{1,0:T(8,128)(2,1)S(1)} collective-permute-done((bf16[528,128]{1,0:T(8,128)(2,1)S(1)}, bf16[528,128]{1,0:T(8,128)(2,1)S(1)}, u32[]{:S(2)}, u32[]{:S(2)}) %collective-permute-start.11) | collective-permute-done | bytes 135200 | tf_op jit(solution)/shard_map/ppermute | solution.py:206
  17.2 2.2 %collective-permute-start.13 = (bf16[528,128]{1,0:T(8,128)(2,1)S(1)}, bf16[528,128]{1,0:T(8,128)(2,1)S(1)}, u32[]{:S(2)}, u32[]{:S(2)}) collective-permute-start(bf16[528,128]{1,0:T(8,128)(2,1)S(1)} %collective-permute-done.11.refs_10_), channel_id=1, source_target_pairs={{0,2},{2,4},{4,6},{6,7},{7,5},{5,3},{3,1},{1,0},{8,10},{10,12},{12... | collective-permute-start | bytes 405512 | tf_op jit(solution)/shard_map/ppermute | solution.py:206
  19.4 0.3 collective-permute-done.12.refs_11_
  19.7 0.0 collective-permute-start.14
  19.7 0.5 %collective-permute-done.2.refs_4_ = bf16[128,512]{1,0:T(8,128)(2,1)S(1)} collective-permute-done((bf16[128,512]{1,0:T(8,128)(2,1)S(1)}, bf16[128,512]{1,0:T(8,128)(2,1)S(1)}, u32[]{:S(2)}, u32[]{:S(2)}) %collective-permute-start.2) | collective-permute-done | bytes 131104 | tf_op jit(solution)/shard_map/ppermute | solution.py:206
  20.2 2.1 %collective-permute-start.3 = (bf16[96,512]{1,0:T(8,128)(2,1)S(1)}, bf16[96,512]{1,0:T(8,128)(2,1)S(1)}, u32[]{:S(2)}, u32[]{:S(2)}) collective-permute-start(bf16[96,512]{1,0:T(8,128)(2,1)S(1)} %slice.32), channel_id=1, source_target_pairs={{0,2},{2,4},{4,6},{6,7},{7,5},{5,3},{3,1},{1,0},{8,10},{10,12},{12... | collective-permute-start | bytes 294920 | tf_op jit(solution)/shard_map/ppermute | solution.py:206
  22.3 0.3 %collective-permute-done.6.refs_5_ = bf16[128,512]{1,0:T(8,128)(2,1)S(1)} collective-permute-done((bf16[128,512]{1,0:T(8,128)(2,1)S(1)}, bf16[128,512]{1,0:T(8,128)(2,1)S(1)}, u32[]{:S(2)}, u32[]{:S(2)}) %collective-permute-start.6) | collective-permute-done | bytes 131104 | tf_op jit(solution)/shard_map/ppermute | solution.py:206
  22.6 0.0 collective-permute-start.7
  22.6 0.6 %collective-permute-done.13.refs_12_ = bf16[528,128]{1,0:T(8,128)(2,1)S(1)} collective-permute-done((bf16[528,128]{1,0:T(8,128)(2,1)S(1)}, bf16[528,128]{1,0:T(8,128)(2,1)S(1)}, u32[]{:S(2)}, u32[]{:S(2)}) %collective-permute-start.13) | collective-permute-done | bytes 135200 | tf_op jit(solution)/shard_map/ppermute | solution.py:206
  23.3 1.8 %collective-permute-start.15 = (bf16[384,128]{1,0:T(8,128)(2,1)S(1)}, bf16[384,128]{1,0:T(8,128)(2,1)S(1)}, u32[]{:S(2)}, u32[]{:S(2)}) collective-permute-start(bf16[384,128]{1,0:T(8,128)(2,1)S(1)} %slice.34), channel_id=1, source_target_pairs={{0,2},{2,4},{4,6},{6,7},{7,5},{5,3},{3,1},{1,0},{8,10},{10,12},{12... | collective-permute-start | bytes 294920 | tf_op jit(solution)/shard_map/ppermute | solution.py:206
  25.1 0.0 collective-permute-done.14.refs_13_
  25.1 0.2 collective-permute-start.16
  25.4 1.2 %collective-permute-done.7.refs_1_.refs_7_ = bf16[32,512]{1,0:T(8,128)(2,1)S(1)} collective-permute-done((bf16[32,512]{1,0:T(8,128)(2,1)S(1)}, bf16[32,512]{1,0:T(8,128)(2,1)S(1)}, u32[]{:S(2)}, u32[]{:S(2)}) %collective-permute-start.7) | collective-permute-done | bytes 32800 | tf_op jit(solution)/shard_map/ppermute | solution.py:206
  26.6 0.0 collective-permute-done.3.refs_0_.refs_6_
  26.6 0.0 collective-permute-done.8.own_ref
  26.6 2.0 %shard_map.58 = (bf16[8,512,320]{2,1,0:T(8,128)(2,1)S(1)}, f32[8,512,128]{2,1,0:T(8,128)S(1)}, bf16[4,16,64,128]{3,2,1,0:T(8,128)(2,1)S(1)}, f32[8,128]{1,0:T(8,128)S(1)}) custom-call(f32[8,128]{1,0:T(8,128)S(1)} %get-tuple-element.12.plan_ref, f32[2,64,320]{2,1,0:T(8,128)S(1)} %get-tuple-element.13.bias_ref, f32[8,128]{1,0:T(8,128)S(1)} %shard_map.56.mark_ref, ...), custom_call_target="tpu_custom_call" | custom-call | flops 67108864 | bytes 1048576 | tf_op jit(solution)/shard_map/pallas_call | solution.py:254
  28.5 0.5 %collective-permute-done.16.refs_1_ = bf16[128,128]{1,0:T(8,128)(2,1)S(1)} collective-permute-done((bf16[128,128]{1,0:T(8,128)(2,1)S(1)}, bf16[128,128]{1,0:T(8,128)(2,1)S(1)}, u32[]{:S(2)}, u32[]{:S(2)}) %collective-permute-start.16) | collective-permute-done | bytes 32800 | tf_op jit(solution)/shard_map/ppermute | solution.py:206
  29.0 0.0 collective-permute-done.15.refs_0_
  29.0 1.8 %shard_map.59 = bf16[128,4096]{1,0:T(8,128)(2,1)} custom-call(f32[8,128]{1,0:T(8,128)S(1)} %get-tuple-element.12.plan_ref, f32[8,128]{1,0:T(8,128)S(1)} %get-tuple-element.15.last_run_ref, bf16[8,512,320]{2,1,0:T(8,128)(2,1)S(1)} %get-tuple-element.16.weights_ref, f32[8,512,128]{2,1,0:T(8,128)S(1)} %get-tuple-element.17.inverse_ref, ...), custom_call_target="tpu_custom_call" | custom-call | flops 67108864 | bytes 1048576 | tf_op jit(solution)/shard_map/pallas_call | solution.py:268
  (13 shorter events, 0.1 us)
Async XLA Ops:
  0.0 4.2 %copy-start.1 = (bf16[1,128,512]{2,1,0:T(8,128)(2,1)S(1)}, bf16[1,128,512]{2,1,0:T(8,128)(2,1)}, u32[]{:S(2)}) copy-start(bf16[1,128,512]{2,1,0:T(8,128)(2,1)} %param.7) | copy-start | bytes 393220
  0.0 4.3 %copy-start.4 = (s32[128]{0:T(128)S(1)}, s32[128]{0:T(128)}, u32[]{:S(2)}) copy-start(s32[128]{0:T(128)} %param.8) | copy-start | bytes 1540
  0.0 5.5 %copy-start = (bf16[1,128,4096]{2,1,0:T(8,128)(2,1)S(1)}, bf16[1,128,4096]{2,1,0:T(8,128)(2,1)}, u32[]{:S(2)}) copy-start(bf16[1,128,4096]{2,1,0:T(8,128)(2,1)} %param.5) | copy-start | bytes 3145732
  0.0 5.5 %copy-start.2 = (bf16[1,128,512]{2,1,0:T(8,128)(2,1)S(1)}, bf16[1,128,512]{2,1,0:T(8,128)(2,1)}, u32[]{:S(2)}) copy-start(bf16[1,128,512]{2,1,0:T(8,128)(2,1)} %param.6) | copy-start | bytes 393220
  0.0 6.4 %collective-permute-start = (bf16[128,512]{1,0:T(8,128)(2,1)}, bf16[128,512]{1,0:T(8,128)(2,1)S(1)}, u32[]{:S(2)}, u32[]{:S(2)}) collective-permute-start(bf16[128,512]{1,0:T(8,128)(2,1)} %bitcast.16), channel_id=1, source_target_pairs={{0,10},{2,12},{4,14},{6,15},{7,13},{5,11},{3,9},{1,8},{8,18},{10,2... | collective-permute-start | bytes 393224 | tf_op jit(solution)/shard_map/ppermute | solution.py:206
  2.5 7.8 %collective-permute-start.4 = (bf16[128,512]{1,0:T(8,128)(2,1)}, bf16[128,512]{1,0:T(8,128)(2,1)S(1)}, u32[]{:S(2)}, u32[]{:S(2)}) collective-permute-start(bf16[128,512]{1,0:T(8,128)(2,1)} %bitcast.17), channel_id=1, source_target_pairs={{0,9},{2,8},{4,10},{6,12},{7,14},{5,15},{3,13},{1,11},{8,17},{10,1... | collective-permute-start | bytes 393224 | tf_op jit(solution)/shard_map/ppermute | solution.py:206
  4.2 12.3 %copy-start.3 = (s32[1024]{0:T(1024)S(1)}, s32[1024]{0:T(1024)}, u32[]{:S(2)}) copy-start(s32[1024]{0:T(1024)} %param.9) | copy-start | bytes 12292
  4.3 6.8 %collective-permute-start.9 = (bf16[528,128]{1,0:T(8,128)(2,1)S(1)}, bf16[528,128]{1,0:T(8,128)(2,1)S(1)}, u32[]{:S(2)}, u32[]{:S(2)}) collective-permute-start(bf16[528,128]{1,0:T(8,128)(2,1)S(1)} %constant_dynamic-update-slice_fusion), channel_id=1, source_target_pairs={{0,10},{2,12},{4,14},{6,15},{7,13},{5,11},{3,9},{1,8},{8,18},{10,2... | collective-permute-start | bytes 405512 | tf_op jit(solution)/shard_map/ppermute | solution.py:206
  5.5 7.7 %collective-permute-start.10 = (bf16[528,128]{1,0:T(8,128)(2,1)S(1)}, bf16[528,128]{1,0:T(8,128)(2,1)S(1)}, u32[]{:S(2)}, u32[]{:S(2)}) collective-permute-start(bf16[528,128]{1,0:T(8,128)(2,1)S(1)} %constant_dynamic-update-slice_fusion), channel_id=1, source_target_pairs={{0,9},{2,8},{4,10},{6,12},{7,14},{5,15},{3,13},{1,11},{8,17},{10,1... | collective-permute-start | bytes 405512 | tf_op jit(solution)/shard_map/ppermute | solution.py:206
  5.7 20.9 %collective-permute-start.8 = (bf16[128,5120]{1,0:T(8,128)(2,1)S(1)}, bf16[128,5120]{1,0:T(8,128)(2,1)S(1)}, u32[]{:S(2)}, u32[]{:S(2)}) collective-permute-start(bf16[128,5120]{1,0:T(8,128)(2,1)S(1)} %pad_maximum_fusion), channel_id=1, source_target_pairs={{0,8},{2,10},{4,12},{6,14},{7,15},{5,13},{3,11},{1,9},{8,16},{10,1... | collective-permute-start | bytes 3932168 | tf_op jit(solution)/shard_map/ppermute | solution.py:206
  6.4 7.7 %collective-permute-start.1 = (bf16[128,512]{1,0:T(8,128)(2,1)S(1)}, bf16[128,512]{1,0:T(8,128)(2,1)S(1)}, u32[]{:S(2)}, u32[]{:S(2)}) collective-permute-start(bf16[128,512]{1,0:T(8,128)(2,1)S(1)} %collective-permute-done.refs_0_), channel_id=1, source_target_pairs={{0,2},{2,4},{4,6},{6,7},{7,5},{5,3},{3,1},{1,0},{8,10},{10,12},{12... | collective-permute-start | bytes 393224 | tf_op jit(solution)/shard_map/ppermute | solution.py:206
  10.3 6.0 %collective-permute-start.5 = (bf16[128,512]{1,0:T(8,128)(2,1)S(1)}, bf16[128,512]{1,0:T(8,128)(2,1)S(1)}, u32[]{:S(2)}, u32[]{:S(2)}) collective-permute-start(bf16[128,512]{1,0:T(8,128)(2,1)S(1)} %collective-permute-done.4.refs_1_), channel_id=1, source_target_pairs={{0,1},{2,0},{4,2},{6,4},{7,6},{5,7},{3,5},{1,3},{8,9},{10,8},{12,1... | collective-permute-start | bytes 393224 | tf_op jit(solution)/shard_map/ppermute | solution.py:206
  11.1 6.1 %collective-permute-start.11 = (bf16[528,128]{1,0:T(8,128)(2,1)S(1)}, bf16[528,128]{1,0:T(8,128)(2,1)S(1)}, u32[]{:S(2)}, u32[]{:S(2)}) collective-permute-start(bf16[528,128]{1,0:T(8,128)(2,1)S(1)} %collective-permute-done.9.refs_8_), channel_id=1, source_target_pairs={{0,2},{2,4},{4,6},{6,7},{7,5},{5,3},{3,1},{1,0},{8,10},{10,12},{12... | collective-permute-start | bytes 405512 | tf_op jit(solution)/shard_map/ppermute | solution.py:206
  13.2 6.5 %collective-permute-start.12 = (bf16[528,128]{1,0:T(8,128)(2,1)S(1)}, bf16[528,128]{1,0:T(8,128)(2,1)S(1)}, u32[]{:S(2)}, u32[]{:S(2)}) collective-permute-start(bf16[528,128]{1,0:T(8,128)(2,1)S(1)} %collective-permute-done.10.refs_9_), channel_id=1, source_target_pairs={{0,1},{2,0},{4,2},{6,4},{7,6},{5,7},{3,5},{1,3},{8,9},{10,8},{12,1... | collective-permute-start | bytes 405512 | tf_op jit(solution)/shard_map/ppermute | solution.py:206
  14.1 6.1 %collective-permute-start.2 = (bf16[128,512]{1,0:T(8,128)(2,1)S(1)}, bf16[128,512]{1,0:T(8,128)(2,1)S(1)}, u32[]{:S(2)}, u32[]{:S(2)}) collective-permute-start(bf16[128,512]{1,0:T(8,128)(2,1)S(1)} %collective-permute-done.1.refs_2_), channel_id=1, source_target_pairs={{0,2},{2,4},{4,6},{6,7},{7,5},{5,3},{3,1},{1,0},{8,10},{10,12},{12... | collective-permute-start | bytes 393224 | tf_op jit(solution)/shard_map/ppermute | solution.py:206
  16.3 6.3 %collective-permute-start.6 = (bf16[128,512]{1,0:T(8,128)(2,1)S(1)}, bf16[128,512]{1,0:T(8,128)(2,1)S(1)}, u32[]{:S(2)}, u32[]{:S(2)}) collective-permute-start(bf16[128,512]{1,0:T(8,128)(2,1)S(1)} %collective-permute-done.5.refs_3_), channel_id=1, source_target_pairs={{0,1},{2,0},{4,2},{6,4},{7,6},{5,7},{3,5},{1,3},{8,9},{10,8},{12,1... | collective-permute-start | bytes 393224 | tf_op jit(solution)/shard_map/ppermute | solution.py:206
  17.2 6.1 %collective-permute-start.13 = (bf16[528,128]{1,0:T(8,128)(2,1)S(1)}, bf16[528,128]{1,0:T(8,128)(2,1)S(1)}, u32[]{:S(2)}, u32[]{:S(2)}) collective-permute-start(bf16[528,128]{1,0:T(8,128)(2,1)S(1)} %collective-permute-done.11.refs_10_), channel_id=1, source_target_pairs={{0,2},{2,4},{4,6},{6,7},{7,5},{5,3},{3,1},{1,0},{8,10},{10,12},{12... | collective-permute-start | bytes 405512 | tf_op jit(solution)/shard_map/ppermute | solution.py:206
  19.7 5.4 %collective-permute-start.14 = (bf16[528,128]{1,0:T(8,128)(2,1)S(1)}, bf16[528,128]{1,0:T(8,128)(2,1)S(1)}, u32[]{:S(2)}, u32[]{:S(2)}) collective-permute-start(bf16[528,128]{1,0:T(8,128)(2,1)S(1)} %collective-permute-done.12.refs_11_), channel_id=1, source_target_pairs={{0,1},{2,0},{4,2},{6,4},{7,6},{5,7},{3,5},{1,3},{8,9},{10,8},{12,1... | collective-permute-start | bytes 405512 | tf_op jit(solution)/shard_map/ppermute | solution.py:206
  20.2 6.4 %collective-permute-start.3 = (bf16[96,512]{1,0:T(8,128)(2,1)S(1)}, bf16[96,512]{1,0:T(8,128)(2,1)S(1)}, u32[]{:S(2)}, u32[]{:S(2)}) collective-permute-start(bf16[96,512]{1,0:T(8,128)(2,1)S(1)} %slice.32), channel_id=1, source_target_pairs={{0,2},{2,4},{4,6},{6,7},{7,5},{5,3},{3,1},{1,0},{8,10},{10,12},{12... | collective-permute-start | bytes 294920 | tf_op jit(solution)/shard_map/ppermute | solution.py:206
  22.6 3.9 %collective-permute-start.7 = (bf16[32,512]{1,0:T(8,128)(2,1)S(1)}, bf16[32,512]{1,0:T(8,128)(2,1)S(1)}, u32[]{:S(2)}, u32[]{:S(2)}) collective-permute-start(bf16[32,512]{1,0:T(8,128)(2,1)S(1)} %slice.33), channel_id=1, source_target_pairs={{0,1},{2,0},{4,2},{6,4},{7,6},{5,7},{3,5},{1,3},{8,9},{10,8},{12,1... | collective-permute-start | bytes 98312 | tf_op jit(solution)/shard_map/ppermute | solution.py:206
  23.3 5.8 %collective-permute-start.15 = (bf16[384,128]{1,0:T(8,128)(2,1)S(1)}, bf16[384,128]{1,0:T(8,128)(2,1)S(1)}, u32[]{:S(2)}, u32[]{:S(2)}) collective-permute-start(bf16[384,128]{1,0:T(8,128)(2,1)S(1)} %slice.34), channel_id=1, source_target_pairs={{0,2},{2,4},{4,6},{6,7},{7,5},{5,3},{3,1},{1,0},{8,10},{10,12},{12... | collective-permute-start | bytes 294920 | tf_op jit(solution)/shard_map/ppermute | solution.py:206
  25.1 3.9 %collective-permute-start.16 = (bf16[128,128]{1,0:T(8,128)(2,1)S(1)}, bf16[128,128]{1,0:T(8,128)(2,1)S(1)}, u32[]{:S(2)}, u32[]{:S(2)}) collective-permute-start(bf16[128,128]{1,0:T(8,128)(2,1)S(1)} %slice.35), channel_id=1, source_target_pairs={{0,1},{2,0},{4,2},{6,4},{7,6},{5,7},{3,5},{1,3},{8,9},{10,8},{12,1... | collective-permute-start | bytes 98312 | tf_op jit(solution)/shard_map/ppermute | solution.py:206

commit v17 on v16

--- a/solution.py
+++ b/solution.py
@@ -26,14 +26,12 @@
     return lax.div(pos_ref[:, :TOK_DEV][0, 0].astype(jnp.int32), RUN)
 
 
-def first_in_reach(runs, pos_ref, run):
-    reach = runs // 4
+def needs_far(runs, pos_ref, run):
     segment = pos_ref[:, TOK_DEV:]
     position = lax.broadcasted_iota(jnp.int32, segment.shape, 1)
     doc = jnp.max(jnp.where(position == run * RUN, segment, -1.0))
-    far_doc = jnp.max(jnp.where(position == (run - reach + 1) * RUN - 1, segment, -1.0))
-    far = doc == far_doc
-    return jnp.where(far, run - reach, jnp.maximum(run - reach + 1, 0)), far
+    far_doc = jnp.max(jnp.where(position == (run - runs // 4 + 1) * RUN - 1, segment, -1.0))
+    return doc == far_doc
 
 
 def write_number(ref, row, number):
@@ -85,14 +83,15 @@
     segment = pos_ref[:, TOK_DEV:]
     first = first_run(pos_ref)
     write_number(plan_ref, 0, first)
+    far = needs_far(runs, pos_ref, first) | needs_far(runs, pos_ref, runs - 1 - first)
+    write_number(plan_ref, 3, jnp.where(far, 1, 0))
     for half, run in enumerate((first, runs - 1 - first)):
         row_pos = run * RUN + lax.broadcasted_iota(jnp.int32, (RUN, 1), 0)
         at = lax.broadcasted_iota(jnp.int32, (RUN, runs * RUN), 1) == row_pos
         row_doc = jnp.sum(jnp.where(at, segment, 0.0), axis=1, keepdims=True)
         doc_start = jnp.sum(jnp.where(segment < row_doc, 1.0, 0.0), axis=1, keepdims=True).astype(jnp.int32)
-        start, far = first_in_reach(runs, pos_ref, run)
-        write_number(plan_ref, 1 + 2 * half, start)
-        write_number(plan_ref, 2 + 2 * half, jnp.where(far, 1, 0))
+        start = jnp.maximum(run - runs // 4 + jnp.where(far, 0, 1), 0)
+        write_number(plan_ref, 1 + half, start)
         key_pos = start * RUN + lax.broadcasted_iota(jnp.int32, bias_ref.shape[1:], 1)
         bias_ref[half] = jnp.where((key_pos <= row_pos) & (key_pos >= doc_start), 0.0, masked_fill)
 
@@ -103,7 +102,8 @@
     weights_ref, inverse_ref, sorted_ref, last_run_ref, key_buf = refs[-5:]
     numbers = run_numbers(runs, read_number(plan_ref, 0), tagged_refs)
     write_number(last_run_ref, 0, numbers[-1][0])
-    plan = [(read_number(plan_ref, 1 + 2 * half), read_number(plan_ref, 2 + 2 * half) > 0) for half in range(2)]
+    starts = [read_number(plan_ref, 1 + half) for half in range(2)]
+    far = read_number(plan_ref, 3) > 0
     sort_keys(numbers, own_ref, key_refs[:-2], key_refs[-2:], key_buf)
     sort_values(numbers, own_ref, tagged_refs, sorted_ref)
     scale = math.log2(math.e) / math.sqrt(HEAD_SIZE)
@@ -134,17 +134,19 @@
             weights_ref[half * KEY_VALUE_HEADS + kv, :, :span] = weights.astype(jnp.bfloat16)
             inverse_ref[half * KEY_VALUE_HEADS + kv] = jnp.broadcast_to(inverse, (GROUP * RUN, HEAD_SIZE))
 
-    for half in range(2):
-        start, far = plan[half]
-        pl.when(far)(functools.partial(half_weights, half, start, runs // 4 + 1))
-        pl.when(jnp.logical_not(far))(functools.partial(half_weights, half, start, runs // 4))
+    def both_weights(count):
+        for half in range(2):
+            half_weights(half, starts[half], count)
+
+    lax.cond(far, lambda: both_weights(runs // 4 + 1), lambda: both_weights(runs // 4))
 
 
 def values_kernel(runs, plan_ref, last_run_ref, weights_ref, inverse_ref, sorted_ref, *refs):
     last_refs, (out_ref, result_buf, out_sems) = refs[:2], refs[2:]
     last_run = read_number(last_run_ref, 0)
     last_runs = (last_run, runs - 1 - last_run)
-    plan = [(read_number(plan_ref, 1 + 2 * half), read_number(plan_ref, 2 + 2 * half) > 0) for half in range(2)]
+    starts = [read_number(plan_ref, 1 + half) for half in range(2)]
+    far = read_number(plan_ref, 3) > 0
 
     def half_values(half, start, count):
         for kv in range(KEY_VALUE_HEADS):
@@ -179,14 +181,12 @@
                     out_sems.at[half * KEY_VALUE_HEADS + kv],
                 )
             )
-    for half in range(2):
-        start, far = plan[half]
-        reach = runs // 4
-        lax.cond(
-            far,
-            functools.partial(half_values, half, start, reach + 1),
-            functools.partial(half_values, half, start, reach),
-        )
+
+    def both_values(count):
+        for half in range(2):
+            half_values(half, starts[half], count)
+
+    lax.cond(far, lambda: both_values(runs // 4 + 1), lambda: both_values(runs // 4))
     for copy in copies:
         copy.wait()
 

time: 30.9 us -> 30.9 us (level)
  Pallas kernels: 3.98 us -> 4.49 us
  waiting for transfers between devices: 6.35 us -> 5.84 us
    ppermute x17, waiting for transfers between devices: 6.35 us -> 5.84 us  [shift(): return lax.ppermute(block, ('section', 'ctx'), pairs)]
    pallas_call x1, Pallas kernels: 1.95 us -> 2.45 us  [per_device(): pl.pallas_call(functools.partial(weights_kernel, runs), out_shape=(jax.Sh...]
  transfers between devices with their start and end apart: 17 -> 17, of which waited for: 11 -> 10; matrix products, arithmetic and copies ran while one was open for 1% -> 1% of each run, Pallas kernels for 7% -> 9%
where the time goes in v17:
time: 30.9 us; the launch traced here: 30.8 us
  starting transfers between devices  20.2 us (65%)
  waiting for transfers between devices  5.84 us (19%)
  Pallas kernels  4.49 us (15%)
    ppermute x17, starting transfers between devices, shift(): return lax.ppermute(block, ('section', 'ctx'), pairs)  20.2 us
    ppermute x17, waiting for transfers between devices, shift(): return lax.ppermute(block, ('section', 'ctx'), pairs)  5.84 us
    pallas_call x1, Pallas kernels, per_device(): pl.pallas_call(functools.partial(weights_kernel, runs), out_shape=(jax.Sh...  2.45 us
    pallas_call x1, Pallas kernels, per_device(): pl.pallas_call(functools.partial(values_kernel, runs), out_shape=jax.Shap...  1.77 us
  transfers between devices with their start and end apart: 17, of which 10 were waited for; matrix products, arithmetic and copies ran while one was open for 1% of the time, Pallas kernels for 9%

profile of v17, /device:TPU:0, one launch (start us, length us, event | category | flops | bytes accessed | tf_op | source)
XLA Modules:
  0.0 30.8 jit_solution(7966435537749523372)
XLA Ops:
  0.0 0.0 copy-start.1
  0.0 0.0 copy-start.4
  0.0 0.0 copy-start
  0.0 0.0 copy-start.2
  0.0 2.5 %collective-permute-start = (bf16[128,512]{1,0:T(8,128)(2,1)}, bf16[128,512]{1,0:T(8,128)(2,1)S(1)}, u32[]{:S(2)}, u32[]{:S(2)}) collective-permute-start(bf16[128,512]{1,0:T(8,128)(2,1)} %bitcast.16), channel_id=1, source_target_pairs={{0,10},{2,12},{4,14},{6,15},{7,13},{5,11},{3,9},{1,8},{8,18},{10,2... | collective-permute-start | bytes 393224 | tf_op jit(solution)/shard_map/ppermute | solution.py:206
  2.5 1.7 %collective-permute-start.4 = (bf16[128,512]{1,0:T(8,128)(2,1)}, bf16[128,512]{1,0:T(8,128)(2,1)S(1)}, u32[]{:S(2)}, u32[]{:S(2)}) collective-permute-start(bf16[128,512]{1,0:T(8,128)(2,1)} %bitcast.17), channel_id=1, source_target_pairs={{0,9},{2,8},{4,10},{6,12},{7,14},{5,15},{3,13},{1,11},{8,17},{10,1... | collective-permute-start | bytes 393224 | tf_op jit(solution)/shard_map/ppermute | solution.py:206
  4.2 0.0 copy-done.1
  4.2 0.0 copy-start.3
  4.3 0.0 copy-done.4
  4.3 1.2 %collective-permute-start.9 = (bf16[528,128]{1,0:T(8,128)(2,1)S(1)}, bf16[528,128]{1,0:T(8,128)(2,1)S(1)}, u32[]{:S(2)}, u32[]{:S(2)}) collective-permute-start(bf16[528,128]{1,0:T(8,128)(2,1)S(1)} %constant_dynamic-update-slice_fusion), channel_id=1, source_target_pairs={{0,10},{2,12},{4,14},{6,15},{7,13},{5,11},{3,9},{1,8},{8,18},{10,2... | collective-permute-start | bytes 405512 | tf_op jit(solution)/shard_map/ppermute | solution.py:206
  5.5 0.1 collective-permute-start.10
  5.6 0.0 copy-done
  5.6 0.0 copy-done.2
  5.6 0.1 pad_maximum_fusion
  5.7 0.5 %collective-permute-start.8 = (bf16[128,5120]{1,0:T(8,128)(2,1)S(1)}, bf16[128,5120]{1,0:T(8,128)(2,1)S(1)}, u32[]{:S(2)}, u32[]{:S(2)}) collective-permute-start(bf16[128,5120]{1,0:T(8,128)(2,1)S(1)} %pad_maximum_fusion), channel_id=1, source_target_pairs={{0,8},{2,10},{4,12},{6,14},{7,15},{5,13},{3,11},{1,9},{8,16},{10,1... | collective-permute-start | bytes 3932168 | tf_op jit(solution)/shard_map/ppermute | solution.py:206
  6.2 0.2 collective-permute-done.refs_0_
  6.4 3.9 %collective-permute-start.1 = (bf16[128,512]{1,0:T(8,128)(2,1)S(1)}, bf16[128,512]{1,0:T(8,128)(2,1)S(1)}, u32[]{:S(2)}, u32[]{:S(2)}) collective-permute-start(bf16[128,512]{1,0:T(8,128)(2,1)S(1)} %collective-permute-done.refs_0_), channel_id=1, source_target_pairs={{0,2},{2,4},{4,6},{6,7},{7,5},{5,3},{3,1},{1,0},{8,10},{10,12},{12... | collective-permute-start | bytes 393224 | tf_op jit(solution)/shard_map/ppermute | solution.py:206
  10.3 0.0 collective-permute-done.4.refs_1_
  10.3 0.0 collective-permute-start.5
  10.3 0.8 %collective-permute-done.9.refs_8_ = bf16[528,128]{1,0:T(8,128)(2,1)S(1)} collective-permute-done((bf16[528,128]{1,0:T(8,128)(2,1)S(1)}, bf16[528,128]{1,0:T(8,128)(2,1)S(1)}, u32[]{:S(2)}, u32[]{:S(2)}) %collective-permute-start.9) | collective-permute-done | bytes 135200 | tf_op jit(solution)/shard_map/ppermute | solution.py:206
  11.1 2.1 %collective-permute-start.11 = (bf16[528,128]{1,0:T(8,128)(2,1)S(1)}, bf16[528,128]{1,0:T(8,128)(2,1)S(1)}, u32[]{:S(2)}, u32[]{:S(2)}) collective-permute-start(bf16[528,128]{1,0:T(8,128)(2,1)S(1)} %collective-permute-done.9.refs_8_), channel_id=1, source_target_pairs={{0,2},{2,4},{4,6},{6,7},{7,5},{5,3},{3,1},{1,0},{8,10},{10,12},{12... | collective-permute-start | bytes 405512 | tf_op jit(solution)/shard_map/ppermute | solution.py:206
  13.2 0.0 collective-permute-done.10.refs_9_
  13.2 0.0 collective-permute-start.12
  13.2 0.9 %collective-permute-done.1.refs_2_ = bf16[128,512]{1,0:T(8,128)(2,1)S(1)} collective-permute-done((bf16[128,512]{1,0:T(8,128)(2,1)S(1)}, bf16[128,512]{1,0:T(8,128)(2,1)S(1)}, u32[]{:S(2)}, u32[]{:S(2)}) %collective-permute-start.1) | collective-permute-done | bytes 131104 | tf_op jit(solution)/shard_map/ppermute | solution.py:206
  14.1 1.7 %collective-permute-start.2 = (bf16[128,512]{1,0:T(8,128)(2,1)S(1)}, bf16[128,512]{1,0:T(8,128)(2,1)S(1)}, u32[]{:S(2)}, u32[]{:S(2)}) collective-permute-start(bf16[128,512]{1,0:T(8,128)(2,1)S(1)} %collective-permute-done.1.refs_2_), channel_id=1, source_target_pairs={{0,2},{2,4},{4,6},{6,7},{7,5},{5,3},{3,1},{1,0},{8,10},{10,12},{12... | collective-permute-start | bytes 393224 | tf_op jit(solution)/shard_map/ppermute | solution.py:206
  15.8 0.5 %collective-permute-done.5.refs_3_ = bf16[128,512]{1,0:T(8,128)(2,1)S(1)} collective-permute-done((bf16[128,512]{1,0:T(8,128)(2,1)S(1)}, bf16[128,512]{1,0:T(8,128)(2,1)S(1)}, u32[]{:S(2)}, u32[]{:S(2)}) %collective-permute-start.5) | collective-permute-done | bytes 131104 | tf_op jit(solution)/shard_map/ppermute | solution.py:206
  16.3 0.1 collective-permute-start.6
  16.4 0.0 copy-done.3
  16.5 0.3 shard_map.55
  16.7 0.5 %collective-permute-done.11.refs_10_ = bf16[528,128]{1,0:T(8,128)(2,1)S(1)} collective-permute-done((bf16[528,128]{1,0:T(8,128)(2,1)S(1)}, bf16[528,128]{1,0:T(8,128)(2,1)S(1)}, u32[]{:S(2)}, u32[]{:S(2)}) %collective-permute-start.11) | collective-permute-done | bytes 135200 | tf_op jit(solution)/shard_map/ppermute | solution.py:206
  17.2 2.2 %collective-permute-start.13 = (bf16[528,128]{1,0:T(8,128)(2,1)S(1)}, bf16[528,128]{1,0:T(8,128)(2,1)S(1)}, u32[]{:S(2)}, u32[]{:S(2)}) collective-permute-start(bf16[528,128]{1,0:T(8,128)(2,1)S(1)} %collective-permute-done.11.refs_10_), channel_id=1, source_target_pairs={{0,2},{2,4},{4,6},{6,7},{7,5},{5,3},{3,1},{1,0},{8,10},{10,12},{12... | collective-permute-start | bytes 405512 | tf_op jit(solution)/shard_map/ppermute | solution.py:206
  19.4 0.3 collective-permute-done.12.refs_11_
  19.7 0.0 collective-permute-start.14
  19.7 0.5 %collective-permute-done.2.refs_4_ = bf16[128,512]{1,0:T(8,128)(2,1)S(1)} collective-permute-done((bf16[128,512]{1,0:T(8,128)(2,1)S(1)}, bf16[128,512]{1,0:T(8,128)(2,1)S(1)}, u32[]{:S(2)}, u32[]{:S(2)}) %collective-permute-start.2) | collective-permute-done | bytes 131104 | tf_op jit(solution)/shard_map/ppermute | solution.py:206
  20.2 2.1 %collective-permute-start.3 = (bf16[96,512]{1,0:T(8,128)(2,1)S(1)}, bf16[96,512]{1,0:T(8,128)(2,1)S(1)}, u32[]{:S(2)}, u32[]{:S(2)}) collective-permute-start(bf16[96,512]{1,0:T(8,128)(2,1)S(1)} %slice.32), channel_id=1, source_target_pairs={{0,2},{2,4},{4,6},{6,7},{7,5},{5,3},{3,1},{1,0},{8,10},{10,12},{12... | collective-permute-start | bytes 294920 | tf_op jit(solution)/shard_map/ppermute | solution.py:206
  22.3 0.3 %collective-permute-done.6.refs_5_ = bf16[128,512]{1,0:T(8,128)(2,1)S(1)} collective-permute-done((bf16[128,512]{1,0:T(8,128)(2,1)S(1)}, bf16[128,512]{1,0:T(8,128)(2,1)S(1)}, u32[]{:S(2)}, u32[]{:S(2)}) %collective-permute-start.6) | collective-permute-done | bytes 131104 | tf_op jit(solution)/shard_map/ppermute | solution.py:206
  22.6 0.0 collective-permute-start.7
  22.6 0.6 %collective-permute-done.13.refs_12_ = bf16[528,128]{1,0:T(8,128)(2,1)S(1)} collective-permute-done((bf16[528,128]{1,0:T(8,128)(2,1)S(1)}, bf16[528,128]{1,0:T(8,128)(2,1)S(1)}, u32[]{:S(2)}, u32[]{:S(2)}) %collective-permute-start.13) | collective-permute-done | bytes 135200 | tf_op jit(solution)/shard_map/ppermute | solution.py:206
  23.3 1.8 %collective-permute-start.15 = (bf16[384,128]{1,0:T(8,128)(2,1)S(1)}, bf16[384,128]{1,0:T(8,128)(2,1)S(1)}, u32[]{:S(2)}, u32[]{:S(2)}) collective-permute-start(bf16[384,128]{1,0:T(8,128)(2,1)S(1)} %slice.34), channel_id=1, source_target_pairs={{0,2},{2,4},{4,6},{6,7},{7,5},{5,3},{3,1},{1,0},{8,10},{10,12},{12... | collective-permute-start | bytes 294920 | tf_op jit(solution)/shard_map/ppermute | solution.py:206
  25.1 0.0 collective-permute-done.14.refs_13_
  25.1 0.2 collective-permute-start.16
  25.4 1.2 %collective-permute-done.7.refs_1_.refs_7_ = bf16[32,512]{1,0:T(8,128)(2,1)S(1)} collective-permute-done((bf16[32,512]{1,0:T(8,128)(2,1)S(1)}, bf16[32,512]{1,0:T(8,128)(2,1)S(1)}, u32[]{:S(2)}, u32[]{:S(2)}) %collective-permute-start.7) | collective-permute-done | bytes 32800 | tf_op jit(solution)/shard_map/ppermute | solution.py:206
  26.6 0.0 collective-permute-done.3.refs_0_.refs_6_
  26.6 0.0 collective-permute-done.8.own_ref
  26.6 2.5 %shard_map.58 = (bf16[8,512,320]{2,1,0:T(8,128)(2,1)S(1)}, f32[8,512,128]{2,1,0:T(8,128)S(1)}, bf16[4,16,64,128]{3,2,1,0:T(8,128)(2,1)S(1)}, f32[8,128]{1,0:T(8,128)S(1)}) custom-call(f32[8,128]{1,0:T(8,128)S(1)} %get-tuple-element.12.plan_ref, f32[2,64,320]{2,1,0:T(8,128)S(1)} %get-tuple-element.13.bias_ref, f32[8,128]{1,0:T(8,128)S(1)} %shard_map.56.mark_ref, ...), custom_call_target="tpu_custom_call" | custom-call | flops 67108864 | bytes 1048576 | tf_op jit(solution)/shard_map/pallas_call | solution.py:254
  29.0 0.0 collective-permute-done.16.refs_1_
  29.0 0.0 collective-permute-done.15.refs_0_
  29.0 1.8 %shard_map.59 = bf16[128,4096]{1,0:T(8,128)(2,1)} custom-call(f32[8,128]{1,0:T(8,128)S(1)} %get-tuple-element.12.plan_ref, f32[8,128]{1,0:T(8,128)S(1)} %get-tuple-element.15.last_run_ref, bf16[8,512,320]{2,1,0:T(8,128)(2,1)S(1)} %get-tuple-element.16.weights_ref, f32[8,512,128]{2,1,0:T(8,128)S(1)} %get-tuple-element.17.inverse_ref, ...), custom_call_target="tpu_custom_call" | custom-call | flops 67108864 | bytes 1048576 | tf_op jit(solution)/shard_map/pallas_call | solution.py:268
  (13 shorter events, 0.1 us)
Async XLA Ops:
  0.0 4.2 %copy-start.1 = (bf16[1,128,512]{2,1,0:T(8,128)(2,1)S(1)}, bf16[1,128,512]{2,1,0:T(8,128)(2,1)}, u32[]{:S(2)}) copy-start(bf16[1,128,512]{2,1,0:T(8,128)(2,1)} %param.7) | copy-start | bytes 393220
  0.0 4.3 %copy-start.4 = (s32[128]{0:T(128)S(1)}, s32[128]{0:T(128)}, u32[]{:S(2)}) copy-start(s32[128]{0:T(128)} %param.8) | copy-start | bytes 1540
  0.0 5.5 %copy-start = (bf16[1,128,4096]{2,1,0:T(8,128)(2,1)S(1)}, bf16[1,128,4096]{2,1,0:T(8,128)(2,1)}, u32[]{:S(2)}) copy-start(bf16[1,128,4096]{2,1,0:T(8,128)(2,1)} %param.5) | copy-start | bytes 3145732
  0.0 5.5 %copy-start.2 = (bf16[1,128,512]{2,1,0:T(8,128)(2,1)S(1)}, bf16[1,128,512]{2,1,0:T(8,128)(2,1)}, u32[]{:S(2)}) copy-start(bf16[1,128,512]{2,1,0:T(8,128)(2,1)} %param.6) | copy-start | bytes 393220
  0.0 6.4 %collective-permute-start = (bf16[128,512]{1,0:T(8,128)(2,1)}, bf16[128,512]{1,0:T(8,128)(2,1)S(1)}, u32[]{:S(2)}, u32[]{:S(2)}) collective-permute-start(bf16[128,512]{1,0:T(8,128)(2,1)} %bitcast.16), channel_id=1, source_target_pairs={{0,10},{2,12},{4,14},{6,15},{7,13},{5,11},{3,9},{1,8},{8,18},{10,2... | collective-permute-start | bytes 393224 | tf_op jit(solution)/shard_map/ppermute | solution.py:206
  2.5 7.8 %collective-permute-start.4 = (bf16[128,512]{1,0:T(8,128)(2,1)}, bf16[128,512]{1,0:T(8,128)(2,1)S(1)}, u32[]{:S(2)}, u32[]{:S(2)}) collective-permute-start(bf16[128,512]{1,0:T(8,128)(2,1)} %bitcast.17), channel_id=1, source_target_pairs={{0,9},{2,8},{4,10},{6,12},{7,14},{5,15},{3,13},{1,11},{8,17},{10,1... | collective-permute-start | bytes 393224 | tf_op jit(solution)/shard_map/ppermute | solution.py:206
  4.2 12.3 %copy-start.3 = (s32[1024]{0:T(1024)S(1)}, s32[1024]{0:T(1024)}, u32[]{:S(2)}) copy-start(s32[1024]{0:T(1024)} %param.9) | copy-start | bytes 12292
  4.3 6.8 %collective-permute-start.9 = (bf16[528,128]{1,0:T(8,128)(2,1)S(1)}, bf16[528,128]{1,0:T(8,128)(2,1)S(1)}, u32[]{:S(2)}, u32[]{:S(2)}) collective-permute-start(bf16[528,128]{1,0:T(8,128)(2,1)S(1)} %constant_dynamic-update-slice_fusion), channel_id=1, source_target_pairs={{0,10},{2,12},{4,14},{6,15},{7,13},{5,11},{3,9},{1,8},{8,18},{10,2... | collective-permute-start | bytes 405512 | tf_op jit(solution)/shard_map/ppermute | solution.py:206
  5.5 7.7 %collective-permute-start.10 = (bf16[528,128]{1,0:T(8,128)(2,1)S(1)}, bf16[528,128]{1,0:T(8,128)(2,1)S(1)}, u32[]{:S(2)}, u32[]{:S(2)}) collective-permute-start(bf16[528,128]{1,0:T(8,128)(2,1)S(1)} %constant_dynamic-update-slice_fusion), channel_id=1, source_target_pairs={{0,9},{2,8},{4,10},{6,12},{7,14},{5,15},{3,13},{1,11},{8,17},{10,1... | collective-permute-start | bytes 405512 | tf_op jit(solution)/shard_map/ppermute | solution.py:206
  5.7 20.9 %collective-permute-start.8 = (bf16[128,5120]{1,0:T(8,128)(2,1)S(1)}, bf16[128,5120]{1,0:T(8,128)(2,1)S(1)}, u32[]{:S(2)}, u32[]{:S(2)}) collective-permute-start(bf16[128,5120]{1,0:T(8,128)(2,1)S(1)} %pad_maximum_fusion), channel_id=1, source_target_pairs={{0,8},{2,10},{4,12},{6,14},{7,15},{5,13},{3,11},{1,9},{8,16},{10,1... | collective-permute-start | bytes 3932168 | tf_op jit(solution)/shard_map/ppermute | solution.py:206
  6.4 7.7 %collective-permute-start.1 = (bf16[128,512]{1,0:T(8,128)(2,1)S(1)}, bf16[128,512]{1,0:T(8,128)(2,1)S(1)}, u32[]{:S(2)}, u32[]{:S(2)}) collective-permute-start(bf16[128,512]{1,0:T(8,128)(2,1)S(1)} %collective-permute-done.refs_0_), channel_id=1, source_target_pairs={{0,2},{2,4},{4,6},{6,7},{7,5},{5,3},{3,1},{1,0},{8,10},{10,12},{12... | collective-permute-start | bytes 393224 | tf_op jit(solution)/shard_map/ppermute | solution.py:206
  10.3 6.0 %collective-permute-start.5 = (bf16[128,512]{1,0:T(8,128)(2,1)S(1)}, bf16[128,512]{1,0:T(8,128)(2,1)S(1)}, u32[]{:S(2)}, u32[]{:S(2)}) collective-permute-start(bf16[128,512]{1,0:T(8,128)(2,1)S(1)} %collective-permute-done.4.refs_1_), channel_id=1, source_target_pairs={{0,1},{2,0},{4,2},{6,4},{7,6},{5,7},{3,5},{1,3},{8,9},{10,8},{12,1... | collective-permute-start | bytes 393224 | tf_op jit(solution)/shard_map/ppermute | solution.py:206
  11.1 6.1 %collective-permute-start.11 = (bf16[528,128]{1,0:T(8,128)(2,1)S(1)}, bf16[528,128]{1,0:T(8,128)(2,1)S(1)}, u32[]{:S(2)}, u32[]{:S(2)}) collective-permute-start(bf16[528,128]{1,0:T(8,128)(2,1)S(1)} %collective-permute-done.9.refs_8_), channel_id=1, source_target_pairs={{0,2},{2,4},{4,6},{6,7},{7,5},{5,3},{3,1},{1,0},{8,10},{10,12},{12... | collective-permute-start | bytes 405512 | tf_op jit(solution)/shard_map/ppermute | solution.py:206
  13.2 6.5 %collective-permute-start.12 = (bf16[528,128]{1,0:T(8,128)(2,1)S(1)}, bf16[528,128]{1,0:T(8,128)(2,1)S(1)}, u32[]{:S(2)}, u32[]{:S(2)}) collective-permute-start(bf16[528,128]{1,0:T(8,128)(2,1)S(1)} %collective-permute-done.10.refs_9_), channel_id=1, source_target_pairs={{0,1},{2,0},{4,2},{6,4},{7,6},{5,7},{3,5},{1,3},{8,9},{10,8},{12,1... | collective-permute-start | bytes 405512 | tf_op jit(solution)/shard_map/ppermute | solution.py:206
  14.1 6.1 %collective-permute-start.2 = (bf16[128,512]{1,0:T(8,128)(2,1)S(1)}, bf16[128,512]{1,0:T(8,128)(2,1)S(1)}, u32[]{:S(2)}, u32[]{:S(2)}) collective-permute-start(bf16[128,512]{1,0:T(8,128)(2,1)S(1)} %collective-permute-done.1.refs_2_), channel_id=1, source_target_pairs={{0,2},{2,4},{4,6},{6,7},{7,5},{5,3},{3,1},{1,0},{8,10},{10,12},{12... | collective-permute-start | bytes 393224 | tf_op jit(solution)/shard_map/ppermute | solution.py:206
  16.3 6.3 %collective-permute-start.6 = (bf16[128,512]{1,0:T(8,128)(2,1)S(1)}, bf16[128,512]{1,0:T(8,128)(2,1)S(1)}, u32[]{:S(2)}, u32[]{:S(2)}) collective-permute-start(bf16[128,512]{1,0:T(8,128)(2,1)S(1)} %collective-permute-done.5.refs_3_), channel_id=1, source_target_pairs={{0,1},{2,0},{4,2},{6,4},{7,6},{5,7},{3,5},{1,3},{8,9},{10,8},{12,1... | collective-permute-start | bytes 393224 | tf_op jit(solution)/shard_map/ppermute | solution.py:206
  17.2 6.1 %collective-permute-start.13 = (bf16[528,128]{1,0:T(8,128)(2,1)S(1)}, bf16[528,128]{1,0:T(8,128)(2,1)S(1)}, u32[]{:S(2)}, u32[]{:S(2)}) collective-permute-start(bf16[528,128]{1,0:T(8,128)(2,1)S(1)} %collective-permute-done.11.refs_10_), channel_id=1, source_target_pairs={{0,2},{2,4},{4,6},{6,7},{7,5},{5,3},{3,1},{1,0},{8,10},{10,12},{12... | collective-permute-start | bytes 405512 | tf_op jit(solution)/shard_map/ppermute | solution.py:206
  19.7 5.4 %collective-permute-start.14 = (bf16[528,128]{1,0:T(8,128)(2,1)S(1)}, bf16[528,128]{1,0:T(8,128)(2,1)S(1)}, u32[]{:S(2)}, u32[]{:S(2)}) collective-permute-start(bf16[528,128]{1,0:T(8,128)(2,1)S(1)} %collective-permute-done.12.refs_11_), channel_id=1, source_target_pairs={{0,1},{2,0},{4,2},{6,4},{7,6},{5,7},{3,5},{1,3},{8,9},{10,8},{12,1... | collective-permute-start | bytes 405512 | tf_op jit(solution)/shard_map/ppermute | solution.py:206
  20.2 6.4 %collective-permute-start.3 = (bf16[96,512]{1,0:T(8,128)(2,1)S(1)}, bf16[96,512]{1,0:T(8,128)(2,1)S(1)}, u32[]{:S(2)}, u32[]{:S(2)}) collective-permute-start(bf16[96,512]{1,0:T(8,128)(2,1)S(1)} %slice.32), channel_id=1, source_target_pairs={{0,2},{2,4},{4,6},{6,7},{7,5},{5,3},{3,1},{1,0},{8,10},{10,12},{12... | collective-permute-start | bytes 294920 | tf_op jit(solution)/shard_map/ppermute | solution.py:206
  22.6 3.9 %collective-permute-start.7 = (bf16[32,512]{1,0:T(8,128)(2,1)S(1)}, bf16[32,512]{1,0:T(8,128)(2,1)S(1)}, u32[]{:S(2)}, u32[]{:S(2)}) collective-permute-start(bf16[32,512]{1,0:T(8,128)(2,1)S(1)} %slice.33), channel_id=1, source_target_pairs={{0,1},{2,0},{4,2},{6,4},{7,6},{5,7},{3,5},{1,3},{8,9},{10,8},{12,1... | collective-permute-start | bytes 98312 | tf_op jit(solution)/shard_map/ppermute | solution.py:206
  23.3 5.8 %collective-permute-start.15 = (bf16[384,128]{1,0:T(8,128)(2,1)S(1)}, bf16[384,128]{1,0:T(8,128)(2,1)S(1)}, u32[]{:S(2)}, u32[]{:S(2)}) collective-permute-start(bf16[384,128]{1,0:T(8,128)(2,1)S(1)} %slice.34), channel_id=1, source_target_pairs={{0,2},{2,4},{4,6},{6,7},{7,5},{5,3},{3,1},{1,0},{8,10},{10,12},{12... | collective-permute-start | bytes 294920 | tf_op jit(solution)/shard_map/ppermute | solution.py:206
  25.1 3.9 %collective-permute-start.16 = (bf16[128,128]{1,0:T(8,128)(2,1)S(1)}, bf16[128,128]{1,0:T(8,128)(2,1)S(1)}, u32[]{:S(2)}, u32[]{:S(2)}) collective-permute-start(bf16[128,128]{1,0:T(8,128)(2,1)S(1)} %slice.35), channel_id=1, source_target_pairs={{0,1},{2,0},{4,2},{6,4},{7,6},{5,7},{3,5},{1,3},{8,9},{10,8},{12,1... | collective-permute-start | bytes 98312 | tf_op jit(solution)/shard_map/ppermute | solution.py:206

commit v18 on v17

--- a/solution.py
+++ b/solution.py
@@ -150,14 +150,13 @@
 
     def half_values(half, start, count):
         for kv in range(KEY_VALUE_HEADS):
-            which, place = divmod(kv, KEY_VALUE_HEADS * 3 // 4)
-            last_ref = last_refs[which]
             parts = []
             for i in range(count):
                 part = sorted_ref[kv, start + i]
                 for last_half, number in enumerate(last_runs):
-                    row = place * TOK_DEV + last_half * RUN
-                    part = jnp.where(start + i == number, last_ref[row : row + RUN, :], part)
+                    row = kv * TOK_DEV + last_half * RUN
+                    which, row = divmod(row, VALUE_ROWS - RUN)
+                    part = jnp.where(start + i == number, last_refs[which][row : row + RUN, :], part)
                 parts.append(part)
             summed = jnp.dot(
                 weights_ref[half * KEY_VALUE_HEADS + kv, :, : count * RUN],
@@ -205,7 +204,7 @@
                 pairs.append((s * places + ring[i], target))
         return lax.ppermute(block, ("section", "ctx"), pairs)
 
-    def around(block, rows, early=None):
+    def around(block, rows, cut, early=None):
         ahead, back = shift(block, 1, 1), shift(block, 1, -1)
         held = [ahead, back]
         for step in range(2, places // 2):
@@ -213,7 +212,6 @@
                 ahead, _ = lax.optimization_barrier((ahead, early))
             ahead, back = shift(ahead, 0, 1), shift(back, 0, -1)
             held.extend([ahead, back])
-        cut = rows * 3 // 4
         return held + [shift(ahead[:cut], 0, 1), shift(back[cut:rows], 0, -1)]
 
     own = shift(jnp.concatenate([queries[0], keys[0], values[0]], axis=1), 1, 0)
@@ -240,8 +238,8 @@
         compiler_params=pltpu.CompilerParams(vmem_limit_bytes=8 * 1024 * 1024),
         cost_estimate=pl.CostEstimate(flops=1 << 20, bytes_accessed=1 << 10, transcendentals=0),
     )(pos)
-    all_keys = around(keys[0], TOK_DEV)
-    all_values = around(tagged, VALUE_ROWS, bias)
+    all_keys = around(keys[0], TOK_DEV, TOK_DEV * 3 // 4)
+    all_values = around(tagged, VALUE_ROWS, VALUE_ROWS - RUN, bias)
     params = pltpu.CompilerParams(vmem_limit_bytes=(12 + runs // 4) * 1024 * 1024)
     mark = pl.pallas_call(
         blank_kernel,

time: 30.9 us -> 30.6 us (level)
  Pallas kernels: 4.49 us -> 3.62 us
  waiting for transfers between devices: 5.84 us -> 6.37 us
    pallas_call x1, Pallas kernels: 2.45 us -> 1.74 us  [per_device(): pl.pallas_call(functools.partial(weights_kernel, runs), out_shape=(jax.Sh...]
    ppermute x17, waiting for transfers between devices: 5.84 us -> 6.37 us  [shift(): return lax.ppermute(block, ('section', 'ctx'), pairs)]
  transfers between devices with their start and end apart: 17 -> 17, of which waited for: 10 -> 11; matrix products, arithmetic and copies ran while one was open for 1% -> 1% of each run, Pallas kernels for 9% -> 7%
where the time goes in v18:
time: 30.6 us; the launch traced here: 30.5 us
  starting transfers between devices  20.2 us (66%)
  waiting for transfers between devices  6.37 us (21%)
  Pallas kernels  3.62 us (12%)
    ppermute x17, starting transfers between devices, shift(): return lax.ppermute(block, ('section', 'ctx'), pairs)  20.2 us
    ppermute x17, waiting for transfers between devices, shift(): return lax.ppermute(block, ('section', 'ctx'), pairs)  6.37 us
    pallas_call x1, Pallas kernels, per_device(): pl.pallas_call(functools.partial(weights_kernel, runs), out_shape=(jax.Sh...  1.74 us
    pallas_call x1, Pallas kernels, per_device(): pl.pallas_call(functools.partial(values_kernel, runs), out_shape=jax.Shap...  1.6 us
  transfers between devices with their start and end apart: 17, of which 11 were waited for; matrix products, arithmetic and copies ran while one was open for 1% of the time, Pallas kernels for 7%

profile of v18, /device:TPU:0, one launch (start us, length us, event | category | flops | bytes accessed | tf_op | source)
XLA Modules:
  0.0 30.5 jit_solution(9481400527682242118)
XLA Ops:
  0.0 0.0 copy-start.1
  0.0 0.0 copy-start.4
  0.0 0.0 copy-start
  0.0 0.0 copy-start.2
  0.0 2.5 %collective-permute-start = (bf16[128,512]{1,0:T(8,128)(2,1)}, bf16[128,512]{1,0:T(8,128)(2,1)S(1)}, u32[]{:S(2)}, u32[]{:S(2)}) collective-permute-start(bf16[128,512]{1,0:T(8,128)(2,1)} %bitcast.16), channel_id=1, source_target_pairs={{0,10},{2,12},{4,14},{6,15},{7,13},{5,11},{3,9},{1,8},{8,18},{10,2... | collective-permute-start | bytes 393224 | tf_op jit(solution)/shard_map/ppermute | solution.py:205
  2.5 1.7 %collective-permute-start.4 = (bf16[128,512]{1,0:T(8,128)(2,1)}, bf16[128,512]{1,0:T(8,128)(2,1)S(1)}, u32[]{:S(2)}, u32[]{:S(2)}) collective-permute-start(bf16[128,512]{1,0:T(8,128)(2,1)} %bitcast.17), channel_id=1, source_target_pairs={{0,9},{2,8},{4,10},{6,12},{7,14},{5,15},{3,13},{1,11},{8,17},{10,1... | collective-permute-start | bytes 393224 | tf_op jit(solution)/shard_map/ppermute | solution.py:205
  4.2 0.0 copy-done.1
  4.2 0.0 copy-start.3
  4.3 0.0 copy-done.4
  4.3 1.2 %collective-permute-start.9 = (bf16[528,128]{1,0:T(8,128)(2,1)S(1)}, bf16[528,128]{1,0:T(8,128)(2,1)S(1)}, u32[]{:S(2)}, u32[]{:S(2)}) collective-permute-start(bf16[528,128]{1,0:T(8,128)(2,1)S(1)} %constant_dynamic-update-slice_fusion), channel_id=1, source_target_pairs={{0,10},{2,12},{4,14},{6,15},{7,13},{5,11},{3,9},{1,8},{8,18},{10,2... | collective-permute-start | bytes 405512 | tf_op jit(solution)/shard_map/ppermute | solution.py:205
  5.5 0.1 collective-permute-start.10
  5.6 0.0 copy-done
  5.6 0.0 copy-done.2
  5.6 0.1 pad_maximum_fusion
  5.7 0.5 %collective-permute-start.8 = (bf16[128,5120]{1,0:T(8,128)(2,1)S(1)}, bf16[128,5120]{1,0:T(8,128)(2,1)S(1)}, u32[]{:S(2)}, u32[]{:S(2)}) collective-permute-start(bf16[128,5120]{1,0:T(8,128)(2,1)S(1)} %pad_maximum_fusion), channel_id=1, source_target_pairs={{0,8},{2,10},{4,12},{6,14},{7,15},{5,13},{3,11},{1,9},{8,16},{10,1... | collective-permute-start | bytes 3932168 | tf_op jit(solution)/shard_map/ppermute | solution.py:205
  6.2 0.2 collective-permute-done.refs_0_
  6.4 3.9 %collective-permute-start.1 = (bf16[128,512]{1,0:T(8,128)(2,1)S(1)}, bf16[128,512]{1,0:T(8,128)(2,1)S(1)}, u32[]{:S(2)}, u32[]{:S(2)}) collective-permute-start(bf16[128,512]{1,0:T(8,128)(2,1)S(1)} %collective-permute-done.refs_0_), channel_id=1, source_target_pairs={{0,2},{2,4},{4,6},{6,7},{7,5},{5,3},{3,1},{1,0},{8,10},{10,12},{12... | collective-permute-start | bytes 393224 | tf_op jit(solution)/shard_map/ppermute | solution.py:205
  10.3 0.0 collective-permute-done.4.refs_1_
  10.3 0.0 collective-permute-start.5
  10.3 0.8 %collective-permute-done.9.refs_8_ = bf16[528,128]{1,0:T(8,128)(2,1)S(1)} collective-permute-done((bf16[528,128]{1,0:T(8,128)(2,1)S(1)}, bf16[528,128]{1,0:T(8,128)(2,1)S(1)}, u32[]{:S(2)}, u32[]{:S(2)}) %collective-permute-start.9) | collective-permute-done | bytes 135200 | tf_op jit(solution)/shard_map/ppermute | solution.py:205
  11.1 2.1 %collective-permute-start.11 = (bf16[528,128]{1,0:T(8,128)(2,1)S(1)}, bf16[528,128]{1,0:T(8,128)(2,1)S(1)}, u32[]{:S(2)}, u32[]{:S(2)}) collective-permute-start(bf16[528,128]{1,0:T(8,128)(2,1)S(1)} %collective-permute-done.9.refs_8_), channel_id=1, source_target_pairs={{0,2},{2,4},{4,6},{6,7},{7,5},{5,3},{3,1},{1,0},{8,10},{10,12},{12... | collective-permute-start | bytes 405512 | tf_op jit(solution)/shard_map/ppermute | solution.py:205
  13.2 0.0 collective-permute-done.10.refs_9_
  13.2 0.0 collective-permute-start.12
  13.2 0.9 %collective-permute-done.1.refs_2_ = bf16[128,512]{1,0:T(8,128)(2,1)S(1)} collective-permute-done((bf16[128,512]{1,0:T(8,128)(2,1)S(1)}, bf16[128,512]{1,0:T(8,128)(2,1)S(1)}, u32[]{:S(2)}, u32[]{:S(2)}) %collective-permute-start.1) | collective-permute-done | bytes 131104 | tf_op jit(solution)/shard_map/ppermute | solution.py:205
  14.1 1.7 %collective-permute-start.2 = (bf16[128,512]{1,0:T(8,128)(2,1)S(1)}, bf16[128,512]{1,0:T(8,128)(2,1)S(1)}, u32[]{:S(2)}, u32[]{:S(2)}) collective-permute-start(bf16[128,512]{1,0:T(8,128)(2,1)S(1)} %collective-permute-done.1.refs_2_), channel_id=1, source_target_pairs={{0,2},{2,4},{4,6},{6,7},{7,5},{5,3},{3,1},{1,0},{8,10},{10,12},{12... | collective-permute-start | bytes 393224 | tf_op jit(solution)/shard_map/ppermute | solution.py:205
  15.8 0.5 %collective-permute-done.5.refs_3_ = bf16[128,512]{1,0:T(8,128)(2,1)S(1)} collective-permute-done((bf16[128,512]{1,0:T(8,128)(2,1)S(1)}, bf16[128,512]{1,0:T(8,128)(2,1)S(1)}, u32[]{:S(2)}, u32[]{:S(2)}) %collective-permute-start.5) | collective-permute-done | bytes 131104 | tf_op jit(solution)/shard_map/ppermute | solution.py:205
  16.3 0.1 collective-permute-start.6
  16.4 0.0 copy-done.3
  16.5 0.3 shard_map.55
  16.7 0.5 %collective-permute-done.11.refs_10_ = bf16[528,128]{1,0:T(8,128)(2,1)S(1)} collective-permute-done((bf16[528,128]{1,0:T(8,128)(2,1)S(1)}, bf16[528,128]{1,0:T(8,128)(2,1)S(1)}, u32[]{:S(2)}, u32[]{:S(2)}) %collective-permute-start.11) | collective-permute-done | bytes 135200 | tf_op jit(solution)/shard_map/ppermute | solution.py:205
  17.2 2.2 %collective-permute-start.13 = (bf16[528,128]{1,0:T(8,128)(2,1)S(1)}, bf16[528,128]{1,0:T(8,128)(2,1)S(1)}, u32[]{:S(2)}, u32[]{:S(2)}) collective-permute-start(bf16[528,128]{1,0:T(8,128)(2,1)S(1)} %collective-permute-done.11.refs_10_), channel_id=1, source_target_pairs={{0,2},{2,4},{4,6},{6,7},{7,5},{5,3},{3,1},{1,0},{8,10},{10,12},{12... | collective-permute-start | bytes 405512 | tf_op jit(solution)/shard_map/ppermute | solution.py:205
  19.4 0.3 collective-permute-done.12.refs_11_
  19.7 0.0 collective-permute-start.14
  19.7 0.5 %collective-permute-done.2.refs_4_ = bf16[128,512]{1,0:T(8,128)(2,1)S(1)} collective-permute-done((bf16[128,512]{1,0:T(8,128)(2,1)S(1)}, bf16[128,512]{1,0:T(8,128)(2,1)S(1)}, u32[]{:S(2)}, u32[]{:S(2)}) %collective-permute-start.2) | collective-permute-done | bytes 131104 | tf_op jit(solution)/shard_map/ppermute | solution.py:205
  20.2 2.1 %collective-permute-start.3 = (bf16[96,512]{1,0:T(8,128)(2,1)S(1)}, bf16[96,512]{1,0:T(8,128)(2,1)S(1)}, u32[]{:S(2)}, u32[]{:S(2)}) collective-permute-start(bf16[96,512]{1,0:T(8,128)(2,1)S(1)} %slice.32), channel_id=1, source_target_pairs={{0,2},{2,4},{4,6},{6,7},{7,5},{5,3},{3,1},{1,0},{8,10},{10,12},{12... | collective-permute-start | bytes 294920 | tf_op jit(solution)/shard_map/ppermute | solution.py:205
  22.3 0.3 %collective-permute-done.6.refs_5_ = bf16[128,512]{1,0:T(8,128)(2,1)S(1)} collective-permute-done((bf16[128,512]{1,0:T(8,128)(2,1)S(1)}, bf16[128,512]{1,0:T(8,128)(2,1)S(1)}, u32[]{:S(2)}, u32[]{:S(2)}) %collective-permute-start.6) | collective-permute-done | bytes 131104 | tf_op jit(solution)/shard_map/ppermute | solution.py:205
  22.6 0.0 collective-permute-start.7
  22.6 0.6 %collective-permute-done.13.refs_12_ = bf16[528,128]{1,0:T(8,128)(2,1)S(1)} collective-permute-done((bf16[528,128]{1,0:T(8,128)(2,1)S(1)}, bf16[528,128]{1,0:T(8,128)(2,1)S(1)}, u32[]{:S(2)}, u32[]{:S(2)}) %collective-permute-start.13) | collective-permute-done | bytes 135200 | tf_op jit(solution)/shard_map/ppermute | solution.py:205
  23.3 1.8 %collective-permute-start.15 = (bf16[448,128]{1,0:T(8,128)(2,1)S(1)}, bf16[448,128]{1,0:T(8,128)(2,1)S(1)}, u32[]{:S(2)}, u32[]{:S(2)}) collective-permute-start(bf16[448,128]{1,0:T(8,128)(2,1)S(1)} %slice.34), channel_id=1, source_target_pairs={{0,2},{2,4},{4,6},{6,7},{7,5},{5,3},{3,1},{1,0},{8,10},{10,12},{12... | collective-permute-start | bytes 344072 | tf_op jit(solution)/shard_map/ppermute | solution.py:205
  25.1 0.0 collective-permute-done.14.refs_13_
  25.1 0.2 collective-permute-start.16
  25.4 1.2 %collective-permute-done.7.refs_1_.refs_7_ = bf16[32,512]{1,0:T(8,128)(2,1)S(1)} collective-permute-done((bf16[32,512]{1,0:T(8,128)(2,1)S(1)}, bf16[32,512]{1,0:T(8,128)(2,1)S(1)}, u32[]{:S(2)}, u32[]{:S(2)}) %collective-permute-start.7) | collective-permute-done | bytes 32800 | tf_op jit(solution)/shard_map/ppermute | solution.py:205
  26.6 0.0 collective-permute-done.3.refs_0_.refs_6_
  26.6 0.0 collective-permute-done.8.own_ref
  26.6 1.7 %shard_map.58 = (bf16[8,512,320]{2,1,0:T(8,128)(2,1)S(1)}, f32[8,512,128]{2,1,0:T(8,128)S(1)}, bf16[4,16,64,128]{3,2,1,0:T(8,128)(2,1)S(1)}, f32[8,128]{1,0:T(8,128)S(1)}) custom-call(f32[8,128]{1,0:T(8,128)S(1)} %get-tuple-element.12.plan_ref, f32[2,64,320]{2,1,0:T(8,128)S(1)} %get-tuple-element.13.bias_ref, f32[8,128]{1,0:T(8,128)S(1)} %shard_map.56.mark_ref, ...), custom_call_target="tpu_custom_call" | custom-call | flops 67108864 | bytes 1048576 | tf_op jit(solution)/shard_map/pallas_call | solution.py:252
  28.3 0.6 %collective-permute-done.16.refs_1_ = bf16[64,128]{1,0:T(8,128)(2,1)S(1)} collective-permute-done((bf16[64,128]{1,0:T(8,128)(2,1)S(1)}, bf16[64,128]{1,0:T(8,128)(2,1)S(1)}, u32[]{:S(2)}, u32[]{:S(2)}) %collective-permute-start.16) | collective-permute-done | bytes 16416 | tf_op jit(solution)/shard_map/ppermute | solution.py:205
  28.9 0.0 collective-permute-done.15.refs_0_
  28.9 1.6 %shard_map.59 = bf16[128,4096]{1,0:T(8,128)(2,1)} custom-call(f32[8,128]{1,0:T(8,128)S(1)} %get-tuple-element.12.plan_ref, f32[8,128]{1,0:T(8,128)S(1)} %get-tuple-element.15.last_run_ref, bf16[8,512,320]{2,1,0:T(8,128)(2,1)S(1)} %get-tuple-element.16.weights_ref, f32[8,512,128]{2,1,0:T(8,128)S(1)} %get-tuple-element.17.inverse_ref, ...), custom_call_target="tpu_custom_call" | custom-call | flops 67108864 | bytes 1048576 | tf_op jit(solution)/shard_map/pallas_call | solution.py:266
  (13 shorter events, 0.1 us)
Async XLA Ops:
  0.0 4.2 %copy-start.1 = (bf16[1,128,512]{2,1,0:T(8,128)(2,1)S(1)}, bf16[1,128,512]{2,1,0:T(8,128)(2,1)}, u32[]{:S(2)}) copy-start(bf16[1,128,512]{2,1,0:T(8,128)(2,1)} %param.7) | copy-start | bytes 393220
  0.0 4.3 %copy-start.4 = (s32[128]{0:T(128)S(1)}, s32[128]{0:T(128)}, u32[]{:S(2)}) copy-start(s32[128]{0:T(128)} %param.8) | copy-start | bytes 1540
  0.0 5.5 %copy-start = (bf16[1,128,4096]{2,1,0:T(8,128)(2,1)S(1)}, bf16[1,128,4096]{2,1,0:T(8,128)(2,1)}, u32[]{:S(2)}) copy-start(bf16[1,128,4096]{2,1,0:T(8,128)(2,1)} %param.5) | copy-start | bytes 3145732
  0.0 5.5 %copy-start.2 = (bf16[1,128,512]{2,1,0:T(8,128)(2,1)S(1)}, bf16[1,128,512]{2,1,0:T(8,128)(2,1)}, u32[]{:S(2)}) copy-start(bf16[1,128,512]{2,1,0:T(8,128)(2,1)} %param.6) | copy-start | bytes 393220
  0.0 6.4 %collective-permute-start = (bf16[128,512]{1,0:T(8,128)(2,1)}, bf16[128,512]{1,0:T(8,128)(2,1)S(1)}, u32[]{:S(2)}, u32[]{:S(2)}) collective-permute-start(bf16[128,512]{1,0:T(8,128)(2,1)} %bitcast.16), channel_id=1, source_target_pairs={{0,10},{2,12},{4,14},{6,15},{7,13},{5,11},{3,9},{1,8},{8,18},{10,2... | collective-permute-start | bytes 393224 | tf_op jit(solution)/shard_map/ppermute | solution.py:205
  2.5 7.8 %collective-permute-start.4 = (bf16[128,512]{1,0:T(8,128)(2,1)}, bf16[128,512]{1,0:T(8,128)(2,1)S(1)}, u32[]{:S(2)}, u32[]{:S(2)}) collective-permute-start(bf16[128,512]{1,0:T(8,128)(2,1)} %bitcast.17), channel_id=1, source_target_pairs={{0,9},{2,8},{4,10},{6,12},{7,14},{5,15},{3,13},{1,11},{8,17},{10,1... | collective-permute-start | bytes 393224 | tf_op jit(solution)/shard_map/ppermute | solution.py:205
  4.2 12.3 %copy-start.3 = (s32[1024]{0:T(1024)S(1)}, s32[1024]{0:T(1024)}, u32[]{:S(2)}) copy-start(s32[1024]{0:T(1024)} %param.9) | copy-start | bytes 12292
  4.3 6.8 %collective-permute-start.9 = (bf16[528,128]{1,0:T(8,128)(2,1)S(1)}, bf16[528,128]{1,0:T(8,128)(2,1)S(1)}, u32[]{:S(2)}, u32[]{:S(2)}) collective-permute-start(bf16[528,128]{1,0:T(8,128)(2,1)S(1)} %constant_dynamic-update-slice_fusion), channel_id=1, source_target_pairs={{0,10},{2,12},{4,14},{6,15},{7,13},{5,11},{3,9},{1,8},{8,18},{10,2... | collective-permute-start | bytes 405512 | tf_op jit(solution)/shard_map/ppermute | solution.py:205
  5.5 7.7 %collective-permute-start.10 = (bf16[528,128]{1,0:T(8,128)(2,1)S(1)}, bf16[528,128]{1,0:T(8,128)(2,1)S(1)}, u32[]{:S(2)}, u32[]{:S(2)}) collective-permute-start(bf16[528,128]{1,0:T(8,128)(2,1)S(1)} %constant_dynamic-update-slice_fusion), channel_id=1, source_target_pairs={{0,9},{2,8},{4,10},{6,12},{7,14},{5,15},{3,13},{1,11},{8,17},{10,1... | collective-permute-start | bytes 405512 | tf_op jit(solution)/shard_map/ppermute | solution.py:205
  5.7 20.9 %collective-permute-start.8 = (bf16[128,5120]{1,0:T(8,128)(2,1)S(1)}, bf16[128,5120]{1,0:T(8,128)(2,1)S(1)}, u32[]{:S(2)}, u32[]{:S(2)}) collective-permute-start(bf16[128,5120]{1,0:T(8,128)(2,1)S(1)} %pad_maximum_fusion), channel_id=1, source_target_pairs={{0,8},{2,10},{4,12},{6,14},{7,15},{5,13},{3,11},{1,9},{8,16},{10,1... | collective-permute-start | bytes 3932168 | tf_op jit(solution)/shard_map/ppermute | solution.py:205
  6.4 7.7 %collective-permute-start.1 = (bf16[128,512]{1,0:T(8,128)(2,1)S(1)}, bf16[128,512]{1,0:T(8,128)(2,1)S(1)}, u32[]{:S(2)}, u32[]{:S(2)}) collective-permute-start(bf16[128,512]{1,0:T(8,128)(2,1)S(1)} %collective-permute-done.refs_0_), channel_id=1, source_target_pairs={{0,2},{2,4},{4,6},{6,7},{7,5},{5,3},{3,1},{1,0},{8,10},{10,12},{12... | collective-permute-start | bytes 393224 | tf_op jit(solution)/shard_map/ppermute | solution.py:205
  10.3 6.0 %collective-permute-start.5 = (bf16[128,512]{1,0:T(8,128)(2,1)S(1)}, bf16[128,512]{1,0:T(8,128)(2,1)S(1)}, u32[]{:S(2)}, u32[]{:S(2)}) collective-permute-start(bf16[128,512]{1,0:T(8,128)(2,1)S(1)} %collective-permute-done.4.refs_1_), channel_id=1, source_target_pairs={{0,1},{2,0},{4,2},{6,4},{7,6},{5,7},{3,5},{1,3},{8,9},{10,8},{12,1... | collective-permute-start | bytes 393224 | tf_op jit(solution)/shard_map/ppermute | solution.py:205
  11.1 6.1 %collective-permute-start.11 = (bf16[528,128]{1,0:T(8,128)(2,1)S(1)}, bf16[528,128]{1,0:T(8,128)(2,1)S(1)}, u32[]{:S(2)}, u32[]{:S(2)}) collective-permute-start(bf16[528,128]{1,0:T(8,128)(2,1)S(1)} %collective-permute-done.9.refs_8_), channel_id=1, source_target_pairs={{0,2},{2,4},{4,6},{6,7},{7,5},{5,3},{3,1},{1,0},{8,10},{10,12},{12... | collective-permute-start | bytes 405512 | tf_op jit(solution)/shard_map/ppermute | solution.py:205
  13.2 6.5 %collective-permute-start.12 = (bf16[528,128]{1,0:T(8,128)(2,1)S(1)}, bf16[528,128]{1,0:T(8,128)(2,1)S(1)}, u32[]{:S(2)}, u32[]{:S(2)}) collective-permute-start(bf16[528,128]{1,0:T(8,128)(2,1)S(1)} %collective-permute-done.10.refs_9_), channel_id=1, source_target_pairs={{0,1},{2,0},{4,2},{6,4},{7,6},{5,7},{3,5},{1,3},{8,9},{10,8},{12,1... | collective-permute-start | bytes 405512 | tf_op jit(solution)/shard_map/ppermute | solution.py:205
  14.1 6.1 %collective-permute-start.2 = (bf16[128,512]{1,0:T(8,128)(2,1)S(1)}, bf16[128,512]{1,0:T(8,128)(2,1)S(1)}, u32[]{:S(2)}, u32[]{:S(2)}) collective-permute-start(bf16[128,512]{1,0:T(8,128)(2,1)S(1)} %collective-permute-done.1.refs_2_), channel_id=1, source_target_pairs={{0,2},{2,4},{4,6},{6,7},{7,5},{5,3},{3,1},{1,0},{8,10},{10,12},{12... | collective-permute-start | bytes 393224 | tf_op jit(solution)/shard_map/ppermute | solution.py:205
  16.3 6.3 %collective-permute-start.6 = (bf16[128,512]{1,0:T(8,128)(2,1)S(1)}, bf16[128,512]{1,0:T(8,128)(2,1)S(1)}, u32[]{:S(2)}, u32[]{:S(2)}) collective-permute-start(bf16[128,512]{1,0:T(8,128)(2,1)S(1)} %collective-permute-done.5.refs_3_), channel_id=1, source_target_pairs={{0,1},{2,0},{4,2},{6,4},{7,6},{5,7},{3,5},{1,3},{8,9},{10,8},{12,1... | collective-permute-start | bytes 393224 | tf_op jit(solution)/shard_map/ppermute | solution.py:205
  17.2 6.1 %collective-permute-start.13 = (bf16[528,128]{1,0:T(8,128)(2,1)S(1)}, bf16[528,128]{1,0:T(8,128)(2,1)S(1)}, u32[]{:S(2)}, u32[]{:S(2)}) collective-permute-start(bf16[528,128]{1,0:T(8,128)(2,1)S(1)} %collective-permute-done.11.refs_10_), channel_id=1, source_target_pairs={{0,2},{2,4},{4,6},{6,7},{7,5},{5,3},{3,1},{1,0},{8,10},{10,12},{12... | collective-permute-start | bytes 405512 | tf_op jit(solution)/shard_map/ppermute | solution.py:205
  19.7 5.4 %collective-permute-start.14 = (bf16[528,128]{1,0:T(8,128)(2,1)S(1)}, bf16[528,128]{1,0:T(8,128)(2,1)S(1)}, u32[]{:S(2)}, u32[]{:S(2)}) collective-permute-start(bf16[528,128]{1,0:T(8,128)(2,1)S(1)} %collective-permute-done.12.refs_11_), channel_id=1, source_target_pairs={{0,1},{2,0},{4,2},{6,4},{7,6},{5,7},{3,5},{1,3},{8,9},{10,8},{12,1... | collective-permute-start | bytes 405512 | tf_op jit(solution)/shard_map/ppermute | solution.py:205
  20.2 6.4 %collective-permute-start.3 = (bf16[96,512]{1,0:T(8,128)(2,1)S(1)}, bf16[96,512]{1,0:T(8,128)(2,1)S(1)}, u32[]{:S(2)}, u32[]{:S(2)}) collective-permute-start(bf16[96,512]{1,0:T(8,128)(2,1)S(1)} %slice.32), channel_id=1, source_target_pairs={{0,2},{2,4},{4,6},{6,7},{7,5},{5,3},{3,1},{1,0},{8,10},{10,12},{12... | collective-permute-start | bytes 294920 | tf_op jit(solution)/shard_map/ppermute | solution.py:205
  22.6 3.9 %collective-permute-start.7 = (bf16[32,512]{1,0:T(8,128)(2,1)S(1)}, bf16[32,512]{1,0:T(8,128)(2,1)S(1)}, u32[]{:S(2)}, u32[]{:S(2)}) collective-permute-start(bf16[32,512]{1,0:T(8,128)(2,1)S(1)} %slice.33), channel_id=1, source_target_pairs={{0,1},{2,0},{4,2},{6,4},{7,6},{5,7},{3,5},{1,3},{8,9},{10,8},{12,1... | collective-permute-start | bytes 98312 | tf_op jit(solution)/shard_map/ppermute | solution.py:205
  23.3 5.6 %collective-permute-start.15 = (bf16[448,128]{1,0:T(8,128)(2,1)S(1)}, bf16[448,128]{1,0:T(8,128)(2,1)S(1)}, u32[]{:S(2)}, u32[]{:S(2)}) collective-permute-start(bf16[448,128]{1,0:T(8,128)(2,1)S(1)} %slice.34), channel_id=1, source_target_pairs={{0,2},{2,4},{4,6},{6,7},{7,5},{5,3},{3,1},{1,0},{8,10},{10,12},{12... | collective-permute-start | bytes 344072 | tf_op jit(solution)/shard_map/ppermute | solution.py:205
  25.1 3.7 %collective-permute-start.16 = (bf16[64,128]{1,0:T(8,128)(2,1)S(1)}, bf16[64,128]{1,0:T(8,128)(2,1)S(1)}, u32[]{:S(2)}, u32[]{:S(2)}) collective-permute-start(bf16[64,128]{1,0:T(8,128)(2,1)S(1)} %slice.35), channel_id=1, source_target_pairs={{0,1},{2,0},{4,2},{6,4},{7,6},{5,7},{3,5},{1,3},{8,9},{10,8},{12,1... | collective-permute-start | bytes 49160 | tf_op jit(solution)/shard_map/ppermute | solution.py:205
